TPU v7x, 256 devices: a whole 4x4x8 slice. The times are simulated.
256 devices in a mesh: expert: 64 (over x_hi, y, z), dp: 4 (over x_lo, core).
Axes of the slice: x: 4 (x_hi: 2, x_lo: 2; x = x_hi * 2 + x_lo), y: 4, z: 8, core: 2. Of those that a mesh axis runs over, the one named last changes fastest.
Arguments:
- tokens: bfloat16 [8192, 2048], P(('expert', 'dp')), may hold values from -6 to 6
- cotangent: bfloat16 [8192, 2048], P(('expert', 'dp')), may hold values from -6 to 6
- routes: int32 [8192, 8], P(('expert', 'dp')), may hold values from 0 to 63, all different within a row; in each aligned block of 32 rows (0 to 31, 32 to 63, ...) at most 6 rows name the same one
- route_weights: float32 [8192, 8], P(('expert', 'dp')), may hold values from 0.05 to 0.25
- matching: int32 [64], replicated, may hold values from 0 to 63, as said below
- gate_up: bfloat16 [64, 2, 768, 2048], P('expert', None, 'dp'), may hold values from -0.125 to 0.125
- down: bfloat16 [64, 768, 2048], P('expert', 'dp'), may hold values from -0.21875 to 0.21875
- gate_up_m: bfloat16 [64, 2, 768, 2048], P('expert', None, 'dp'), may hold values from -3 to 3
- gate_up_v: bfloat16 [64, 2, 768, 2048], P('expert', None, 'dp'), may hold values from 0.0099487305 to 1
- down_m: bfloat16 [64, 768, 2048], P('expert', 'dp'), may hold values from -3 to 3
- down_v: bfloat16 [64, 768, 2048], P('expert', 'dp'), may hold values from 0.0099487305 to 1
Outputs:
- layer_out: bfloat16 [8192, 2048], P(('expert', 'dp'))
- input_grad: bfloat16 [8192, 2048], P(('expert', 'dp'))
- new_gate_up: bfloat16 [64, 2, 768, 2048], P('expert', None, 'dp')
- new_down: bfloat16 [64, 768, 2048], P('expert', 'dp')
Inputs may be any that keep to these rules, and one draw needn't show every extreme that they name: matching[i] is either i or the index that differs from i in its highest bit (32 away); matching[matching[i]] = i, and exactly 16 pairs are exchanged, among them always the pair of index 0 and the pair of index 31. `routes`: within the 32 rows of one device, each expert is named at most 6 times, and this bound is reached.
All inputs are finite; a program needn't handle non-finite values.
Results may differ from a plain program's by a relative error of at most 0.0075.
Values may be sent and summed in bfloat16 or wider, within the bound.
No kernel may reach another device: no remote copies, remote signals or barrier semaphores. Data moves between devices by JAX's collectives and lax.ppermute only.
A program may use at most 128 MiB of HBM per device.

v0:
```python
import jax
import jax.numpy as jnp
from jax import lax
from jax.sharding import PartitionSpec as P

BETA_ONE = 0.9
BETA_TWO = 0.95
STEP_RATE = 0.01
ADAM_EPS = 1e-08


def swapped_2(block, axis, distance):
    count = lax.axis_size(axis)
    route = []
    for low in range(count):
        high = low | 1 << distance
        if high != low and high < count:
            route += [(low, high), (high, low)]
    return lax.ppermute(block, axis, route)


def adam_update(weight, moment_one, moment_two, gradient):
    one_new = BETA_ONE * moment_one.astype(jnp.float32) + (1.0 - BETA_ONE) * gradient
    two_new = BETA_TWO * moment_two.astype(jnp.float32) + (1.0 - BETA_TWO) * gradient * gradient
    return (
        weight.astype(jnp.float32) - STEP_RATE * one_new / (jnp.sqrt(two_new) + ADAM_EPS)
    ).astype(jnp.bfloat16)


def contract_last(left, right):
    return lax.dot_general(
        left, right, (((1,), (1,)), ((), ())), preferred_element_type=jnp.float32
    )


def contract_first(left, right):
    return lax.dot_general(
        left, right, (((0,), (0,)), ((), ())), preferred_element_type=jnp.float32
    )


def body(
    tokens,
    cotangent,
    routes,
    route_weights,
    matching,
    gate_up,
    down,
    gate_up_m,
    gate_up_v,
    down_m,
    down_v,
):
    axis_width = lax.axis_size("expert")
    self_index = lax.axis_index("expert")
    high_bit = axis_width.bit_length() - 2
    labels = jnp.arange(axis_width, dtype=jnp.int32)
    own_partner = jnp.sum(jnp.where(labels == self_index, matching, 0))
    swapped = own_partner != self_index

    def relocate(stored):
        partner_copy = swapped_2(stored, "expert", high_bit)
        return jnp.where(swapped, partner_copy, stored)

    gate_up, down, gate_up_m, gate_up_v, down_m, down_v = [
        relocate(stored) for stored in (gate_up, down, gate_up_m, gate_up_v, down_m, down_v)
    ]
    tok_dev, top_count = routes.shape
    feature = tokens.shape[1]
    row_count = tok_dev * top_count
    capacity = min(tok_dev, row_count // axis_width + row_count // (2 * axis_width))
    flat_routes = routes.reshape(-1)
    route_hits = flat_routes[:, None] == labels[None, :]
    destination = jnp.sum(jnp.where(route_hits, matching[None, :], 0), axis=1)
    to_dest = destination[:, None] == labels[None, :]
    running = jnp.cumsum(to_dest.astype(jnp.int32), axis=0) - 1
    slot_index = jnp.sum(jnp.where(to_dest, running, 0), axis=1)
    position = destination * capacity + slot_index
    x_rows = jnp.repeat(tokens, top_count, axis=0)
    scaled = (
        (route_weights[:, :, None] * cotangent[:, None, :].astype(jnp.float32))
        .reshape(row_count, feature)
        .astype(jnp.bfloat16)
    )
    send_x = jnp.zeros((axis_width * capacity, feature), jnp.bfloat16).at[position].set(x_rows)
    send_d = jnp.zeros((axis_width * capacity, feature), jnp.bfloat16).at[position].set(scaled)
    recv_x, recv_d = (
        lax.all_to_all(
            send_x.reshape(axis_width, capacity, feature),
            "expert",
            split_axis=0,
            concat_axis=0,
            tiled=True,
        ),
        lax.all_to_all(
            send_d.reshape(axis_width, capacity, feature),
            "expert",
            split_axis=0,
            concat_axis=0,
            tiled=True,
        ),
    )
    rows_x = recv_x.reshape(axis_width * capacity, feature)
    rows_d = recv_d.reshape(axis_width * capacity, feature)
    full_gu, full_down = (
        lax.all_gather(gate_up, "dp", axis=2, tiled=True),
        lax.all_gather(down, "dp", axis=1, tiled=True),
    )
    w_gate = full_gu[0, 0]
    w_up = full_gu[0, 1]
    w_down = full_down[0]
    pre_gate = contract_last(rows_x, w_gate)
    pre_up = contract_last(rows_x, w_up)
    gate_sig = jax.nn.sigmoid(pre_gate)
    hidden = (pre_gate * gate_sig * pre_up).astype(jnp.bfloat16)
    out_rows = jnp.dot(hidden, w_down, preferred_element_type=jnp.float32).astype(jnp.bfloat16)
    d_hidden = contract_last(rows_d, w_down)
    d_gate = (d_hidden * pre_up * gate_sig * (1.0 + pre_gate * (1.0 - gate_sig))).astype(
        jnp.bfloat16
    )
    d_up = (d_hidden * pre_gate * gate_sig).astype(jnp.bfloat16)
    d_rows = (
        jnp.dot(d_gate, w_gate, preferred_element_type=jnp.float32)
        + jnp.dot(d_up, w_up, preferred_element_type=jnp.float32)
    ).astype(jnp.bfloat16)
    back_y, back_dx = (
        lax.all_to_all(
            out_rows.reshape(axis_width, capacity, feature),
            "expert",
            split_axis=0,
            concat_axis=0,
            tiled=True,
        ),
        lax.all_to_all(
            d_rows.reshape(axis_width, capacity, feature),
            "expert",
            split_axis=0,
            concat_axis=0,
            tiled=True,
        ),
    )
    picked_y = (
        back_y.reshape(axis_width * capacity, feature)[position]
        .astype(jnp.float32)
        .reshape(tok_dev, top_count, feature)
    )
    picked_dx = (
        back_dx.reshape(axis_width * capacity, feature)[position]
        .astype(jnp.float32)
        .reshape(tok_dev, top_count, feature)
    )
    layer_out = jnp.sum(route_weights[:, :, None] * picked_y, axis=1).astype(jnp.bfloat16)
    input_grad = jnp.sum(picked_dx, axis=1).astype(jnp.bfloat16)
    grad_gate = contract_first(d_gate, rows_x)
    grad_up = contract_first(d_up, rows_x)
    grad_down = contract_first(hidden, rows_d)
    grad_gu = jnp.stack([grad_gate, grad_up])[None]
    share_gu, share_down = (
        lax.psum_scatter(
            grad_gu.astype(jnp.bfloat16), "dp", scatter_dimension=2, tiled=True
        ).astype(jnp.float32),
        lax.psum_scatter(
            grad_down[None].astype(jnp.bfloat16), "dp", scatter_dimension=1, tiled=True
        ).astype(jnp.float32),
    )
    new_gate_up = adam_update(gate_up, gate_up_m, gate_up_v, share_gu)
    new_down = adam_update(down, down_m, down_v, share_down)
    return (layer_out, input_grad, new_gate_up, new_down)


def solution(mesh):
    return jax.shard_map(
        body,
        mesh=mesh,
        in_specs=(
            P(("expert", "dp"), None),
            P(("expert", "dp"), None),
            P(("expert", "dp"), None),
            P(("expert", "dp"), None),
            P(),
            P("expert", None, "dp", None),
            P("expert", "dp", None),
            P("expert", None, "dp", None),
            P("expert", None, "dp", None),
            P("expert", "dp", None),
            P("expert", "dp", None),
        ),
        out_specs=(
            P(("expert", "dp"), None),
            P(("expert", "dp"), None),
            P("expert", None, "dp", None),
            P("expert", "dp", None),
        ),
        check_vma=False,
    )
```

profile of v0, /device:TPU:1, one launch (start us, length us, event | category | flops | bytes accessed | tf_op | source)
XLA Modules:
  0.0 513.3 jit_solution(10913582714857811023)
XLA Ops:
  7.2 3.7 collective-permute-start
  10.9 1.3 fusion.43
  12.8 31.4 %collective-permute-done = bf16[1,2,192,2048]{3,2,1,0:T(8,128)(2,1)S(1)} collective-permute-done((bf16[1,2,192,2048]{3,2,1,0:T(8,128)(2,1)}, bf16[1,2,192,2048]{3,2,1,0:T(8,128)(2,1)S(1)}, u32[]{:S(2)}, u32[]{:S(2)}) %collective-permute-start) | collective-permute-done | bytes 1572896 | tf_op jit(solution)/shard_map/ppermute | solution.py:19
  44.3 1.3 broadcast_select_fusion
  47.5 2.6 scatter_custom_fusion
  50.1 1.6 reshape.130
  51.8 16.5 %all-to-all-start = ((bf16[64,6,2048]{2,1,0:T(8,128)(2,1)}), bf16[64,6,2048]{2,1,0:T(8,128)(2,1)S(1)}, u32[]{:S(2)}, u32[]{:S(2)}) async-start(bf16[64,6,2048]{2,1,0:T(8,128)(2,1)} %reshape.130), calls=%async_computation | async-start | bytes 4194304 | tf_op jit(solution)/shard_map/all_to_all | solution.py:89
  68.5 3.5 scatter_custom_fusion.1
  72.0 3.7 reshape.134
  75.7 40.8 %all-to-all-done = bf16[64,6,2048]{2,1,0:T(8,128)(2,1)S(1)} async-done(((bf16[64,6,2048]{2,1,0:T(8,128)(2,1)}), bf16[64,6,2048]{2,1,0:T(8,128)(2,1)S(1)}, u32[]{:S(2)}, u32[]{:S(2)}) %all-to-all-start) | async-done | bytes 1572896 | tf_op jit(solution)/shard_map/all_to_all | solution.py:89
  116.5 9.9 %all-to-all-start.2 = ((bf16[64,6,2048]{2,1,0:T(8,128)(2,1)}), bf16[64,6,2048]{2,1,0:T(8,128)(2,1)}, u32[]{:S(2)}, u32[]{:S(2)}) async-start(bf16[64,6,2048]{2,1,0:T(8,128)(2,1)} %reshape.134), calls=%async_computation.2 | async-start | bytes 4194304 | tf_op jit(solution)/shard_map/all_to_all | solution.py:96
  126.6 1.4 reshape.131
  128.1 46.1 %all-to-all-done.2 = bf16[64,6,2048]{2,1,0:T(8,128)(2,1)} async-done(((bf16[64,6,2048]{2,1,0:T(8,128)(2,1)}), bf16[64,6,2048]{2,1,0:T(8,128)(2,1)}, u32[]{:S(2)}, u32[]{:S(2)}) %all-to-all-start.2) | async-done | bytes 1572896 | tf_op jit(solution)/shard_map/all_to_all | solution.py:96
  174.2 2.6 reshape.135
  176.8 3.5 fusion.18
  180.6 2.5 multiply_convert_fusion.2
  183.9 3.5 fusion.14
  187.5 2.4 collective-permute-start.5
  190.6 2.3 collective-permute-start.1
  192.9 12.8 %collective-permute-done.5 = bf16[1,192,2048]{2,1,0:T(8,128)(2,1)} collective-permute-done((bf16[1,192,2048]{2,1,0:T(8,128)(2,1)}, bf16[1,192,2048]{2,1,0:T(8,128)(2,1)}, u32[]{:S(2)}, u32[]{:S(2)}) %collective-permute-start.5) | collective-permute-done | bytes 786464 | tf_op jit(solution)/shard_map/ppermute | solution.py:19
  205.7 33.7 %collective-permute-done.4 = bf16[1,192,2048]{2,1,0:T(8,128)(2,1)} collective-permute-done((bf16[1,192,2048]{2,1,0:T(8,128)(2,1)}, bf16[1,192,2048]{2,1,0:T(8,128)(2,1)}, u32[]{:S(2)}, u32[]{:S(2)}) %collective-permute-start.4) | collective-permute-done | bytes 786464 | tf_op jit(solution)/shard_map/ppermute | solution.py:19
  239.4 23.6 %collective-permute-done.1 = bf16[1,192,2048]{2,1,0:T(8,128)(2,1)} collective-permute-done((bf16[1,192,2048]{2,1,0:T(8,128)(2,1)}, bf16[1,192,2048]{2,1,0:T(8,128)(2,1)}, u32[]{:S(2)}, u32[]{:S(2)}) %collective-permute-start.1) | collective-permute-done | bytes 786464 | tf_op jit(solution)/shard_map/ppermute | solution.py:19
  263.0 4.6 fusion.30
  267.9 43.3 %all-gather.5.cloned.1.call-done = bf16[1,768,2048]{2,1,0:T(8,128)(2,1)} async-done(((bf16[1,192,2048]{2,1,0:T(8,128)(2,1)}), bf16[1,768,2048]{2,1,0:T(8,128)(2,1)}) %all-gather.5.cloned.1.call-update) | async-done | bytes 3145744 | tf_op jit(solution)/shard_map/all_gather | solution.py:108
  311.2 4.2 multiply_convert_fusion.1
  315.4 1.8 fusion.13
  317.3 1.8 fusion.12
  319.2 3.2 pad_maximum_fusion
  323.4 3.3 fusion.15
  326.7 1.6 reshape.132
  328.3 12.4 %all-to-all-start.1 = ((bf16[64,6,2048]{2,1,0:T(8,128)(2,1)}), bf16[64,6,2048]{2,1,0:T(8,128)(2,1)S(1)}, u32[]{:S(2)}, u32[]{:S(2)}) async-start(bf16[64,6,2048]{2,1,0:T(8,128)(2,1)} %reshape.132), calls=%async_computation.1 | async-start | bytes 4194304 | tf_op jit(solution)/shard_map/all_to_all | solution.py:128
  340.7 3.4 fusion.19
  344.2 4.5 add_convert_fusion
  348.6 3.7 reshape.136
  352.3 38.4 %all-to-all-done.1 = bf16[64,6,2048]{2,1,0:T(8,128)(2,1)S(1)} async-done(((bf16[64,6,2048]{2,1,0:T(8,128)(2,1)}), bf16[64,6,2048]{2,1,0:T(8,128)(2,1)S(1)}, u32[]{:S(2)}, u32[]{:S(2)}) %all-to-all-start.1) | async-done | bytes 1572896 | tf_op jit(solution)/shard_map/all_to_all | solution.py:128
  390.7 1.3 copy-done.3
  392.0 9.4 %all-to-all-start.3 = ((bf16[64,6,2048]{2,1,0:T(8,128)(2,1)}), bf16[64,6,2048]{2,1,0:T(8,128)(2,1)}, u32[]{:S(2)}, u32[]{:S(2)}) async-start(bf16[64,6,2048]{2,1,0:T(8,128)(2,1)} %reshape.136), calls=%async_computation.3 | async-start | bytes 4194304 | tf_op jit(solution)/shard_map/all_to_all | solution.py:135
  401.5 2.6 collective-permute-start.3
  404.5 2.6 reshape.133
  407.1 1.4 gather_fusion
  408.5 42.2 %all-to-all-done.3 = bf16[64,6,2048]{2,1,0:T(8,128)(2,1)} async-done(((bf16[64,6,2048]{2,1,0:T(8,128)(2,1)}), bf16[64,6,2048]{2,1,0:T(8,128)(2,1)}, u32[]{:S(2)}, u32[]{:S(2)}) %all-to-all-start.3) | async-done | bytes 1572896 | tf_op jit(solution)/shard_map/all_to_all | solution.py:135
  450.7 2.6 reshape.137
  453.3 2.3 gather_fusion.1
  455.6 2.7 bitcast_reduce_fusion
  458.3 1.6 fusion.21
  460.0 6.8 %collective-permute-done.3 = bf16[1,2,192,2048]{3,2,1,0:T(8,128)(2,1)} collective-permute-done((bf16[1,2,192,2048]{3,2,1,0:T(8,128)(2,1)}, bf16[1,2,192,2048]{3,2,1,0:T(8,128)(2,1)}, u32[]{:S(2)}, u32[]{:S(2)}) %collective-permute-start.3) | collective-permute-done | bytes 1572896 | tf_op jit(solution)/shard_map/ppermute | solution.py:19
  466.8 33.7 %collective-permute-done.2 = bf16[1,2,192,2048]{3,2,1,0:T(8,128)(2,1)} collective-permute-done((bf16[1,2,192,2048]{3,2,1,0:T(8,128)(2,1)}, bf16[1,2,192,2048]{3,2,1,0:T(8,128)(2,1)}, u32[]{:S(2)}, u32[]{:S(2)}) %collective-permute-start.2) | collective-permute-done | bytes 1572896 | tf_op jit(solution)/shard_map/ppermute | solution.py:19
  500.5 6.3 %fusion.11 = bf16[1,2,192,2048]{3,2,1,0:T(8,128)(2,1)} fusion(bf16[1,2,192,2048]{3,2,1,0:T(8,128)(2,1)} %reduce-scatter.3.cloned.1.call-done, bf16[1,2,192,2048]{3,2,1,0:T(8,128)(2,1)S(1)} %copy-done.2, bf16[1,2,192,2048]{3,2,1,0:T(8,128)(2,1)} %collective-permute-done.3, bf16[1,2,192,2048]{3,2,1,0:T(8,128)(2,1)} %param.19, ...), kind=kLoop, calls=%fused_computation.24 | loop fusion | flops 14155776 | bytes 11010049 | tf_op jit(solution)/shard_map/convert_element_type | solution.py:27
  (61 shorter events, 6.0 us)
Async XLA Ops:
  7.2 40.3 %copy-start = (bf16[32,2048]{1,0:T(8,128)(2,1)S(1)}, bf16[32,2048]{1,0:T(8,128)(2,1)}, u32[]{:S(2)}) copy-start(bf16[32,2048]{1,0:T(8,128)(2,1)} %param.11) | copy-start | bytes 393220
  7.2 169.6 %all-gather.3.cloned.1.call-start = ((), (), s32[]{:S(2)}) async-start(), calls=%async_computation.6 | async-start | bytes 7864320 | tf_op jit(solution)/shard_map/all_gather | solution.py:107
  7.2 37.0 %collective-permute-start = (bf16[1,2,192,2048]{3,2,1,0:T(8,128)(2,1)}, bf16[1,2,192,2048]{3,2,1,0:T(8,128)(2,1)S(1)}, u32[]{:S(2)}, u32[]{:S(2)}) collective-permute-start(bf16[1,2,192,2048]{3,2,1,0:T(8,128)(2,1)} %param.16), channel_id=1, source_target_pairs={{0,128},{128,0},{4,132},{132,4},{8,136},{136,8},{12,140},{140,12},... | collective-permute-start | bytes 4718600 | tf_op jit(solution)/shard_map/ppermute | solution.py:19
  45.6 0.7 copy-start.6
  45.6 0.9 copy-start.8
  51.8 16.5 %copy-start.5 = (bf16[32,2048]{1,0:T(8,128)(2,1)S(1)}, bf16[32,2048]{1,0:T(8,128)(2,1)}, u32[]{:S(2)}) copy-start(bf16[32,2048]{1,0:T(8,128)(2,1)} %param.12) | copy-start | bytes 393220
  51.8 16.5 %copy-start.7 = (f32[32,8]{0,1:T(8,128)S(1)}, f32[32,8]{0,1:T(8,128)}, u32[]{:S(2)}) copy-start(f32[32,8]{0,1:T(8,128)} %param.14) | copy-start | bytes 3076
  51.8 64.7 %all-to-all-start = ((bf16[64,6,2048]{2,1,0:T(8,128)(2,1)}), bf16[64,6,2048]{2,1,0:T(8,128)(2,1)S(1)}, u32[]{:S(2)}, u32[]{:S(2)}) async-start(bf16[64,6,2048]{2,1,0:T(8,128)(2,1)} %reshape.130), calls=%async_computation | async-start | bytes 4194304 | tf_op jit(solution)/shard_map/all_to_all | solution.py:89
  116.5 57.7 %all-to-all-start.2 = ((bf16[64,6,2048]{2,1,0:T(8,128)(2,1)}), bf16[64,6,2048]{2,1,0:T(8,128)(2,1)}, u32[]{:S(2)}, u32[]{:S(2)}) async-start(bf16[64,6,2048]{2,1,0:T(8,128)(2,1)} %reshape.134), calls=%async_computation.2 | async-start | bytes 4194304 | tf_op jit(solution)/shard_map/all_to_all | solution.py:96
  126.4 136.6 %reduce-scatter.5.cloned.1.call-start = ((), (), s32[]{:S(2)}) async-start(), calls=%async_computation.9 | async-start | bytes 3932160 | tf_op jit(solution)/shard_map/reduce_scatter | solution.py:163
  128.1 48.8 %copy-start.4 = (bf16[384,2048]{1,0:T(8,128)(2,1)S(1)}, bf16[384,2048]{1,0:T(8,128)(2,1)}, u32[]{:S(2)}) copy-start(bf16[384,2048]{1,0:T(8,128)(2,1)} %reshape.131) | copy-start | bytes 4718596
  176.8 3.7 copy-start.9
  180.6 2.5 copy-start.14
  183.0 0.8 copy-start.15
  187.5 123.7 %all-gather.5.cloned.1.call-start = ((), (), s32[]{:S(2)}) async-start(), calls=%async_computation.7 | async-start | bytes 3932160 | tf_op jit(solution)/shard_map/all_gather | solution.py:108
  187.5 18.2 %collective-permute-start.5 = (bf16[1,192,2048]{2,1,0:T(8,128)(2,1)}, bf16[1,192,2048]{2,1,0:T(8,128)(2,1)}, u32[]{:S(2)}, u32[]{:S(2)}) collective-permute-start(bf16[1,192,2048]{2,1,0:T(8,128)(2,1)} %param.21), channel_id=1, source_target_pairs={{0,128},{128,0},{4,132},{132,4},{8,136},{136,8},{12,140},{140,12},... | collective-permute-start | bytes 2359304 | tf_op jit(solution)/shard_map/ppermute | solution.py:19
  189.9 49.5 %collective-permute-start.4 = (bf16[1,192,2048]{2,1,0:T(8,128)(2,1)}, bf16[1,192,2048]{2,1,0:T(8,128)(2,1)}, u32[]{:S(2)}, u32[]{:S(2)}) collective-permute-start(bf16[1,192,2048]{2,1,0:T(8,128)(2,1)} %param.20), channel_id=1, source_target_pairs={{0,128},{128,0},{4,132},{132,4},{8,136},{136,8},{12,140},{140,12},... | collective-permute-start | bytes 2359304 | tf_op jit(solution)/shard_map/ppermute | solution.py:19
  190.6 72.4 %collective-permute-start.1 = (bf16[1,192,2048]{2,1,0:T(8,128)(2,1)}, bf16[1,192,2048]{2,1,0:T(8,128)(2,1)}, u32[]{:S(2)}, u32[]{:S(2)}) collective-permute-start(bf16[1,192,2048]{2,1,0:T(8,128)(2,1)} %param.17), channel_id=1, source_target_pairs={{0,128},{128,0},{4,132},{132,4},{8,136},{136,8},{12,140},{140,12},... | collective-permute-start | bytes 2359304 | tf_op jit(solution)/shard_map/ppermute | solution.py:19
  267.6 232.9 %reduce-scatter.3.cloned.1.call-start = ((), (), s32[]{:S(2)}) async-start(), calls=%async_computation.8 | async-start | bytes 7864320 | tf_op jit(solution)/shard_map/reduce_scatter | solution.py:160
  315.4 1.9 copy-start.10
  315.4 1.9 copy-start.12
  322.3 1.1 copy-start.16
  328.3 12.5 %copy-start.11 = (bf16[384,768]{1,0:T(8,128)(2,1)S(1)}, bf16[384,768]{1,0:T(8,128)(2,1)}, u32[]{:S(2)}) copy-start(bf16[384,768]{1,0:T(8,128)(2,1)} %copy-done.10) | copy-start | bytes 1769476
  328.3 62.4 %all-to-all-start.1 = ((bf16[64,6,2048]{2,1,0:T(8,128)(2,1)}), bf16[64,6,2048]{2,1,0:T(8,128)(2,1)S(1)}, u32[]{:S(2)}, u32[]{:S(2)}) async-start(bf16[64,6,2048]{2,1,0:T(8,128)(2,1)} %reshape.132), calls=%async_computation.1 | async-start | bytes 4194304 | tf_op jit(solution)/shard_map/all_to_all | solution.py:128
  340.7 3.4 copy-start.13
  390.7 1.3 copy-start.3
  392.0 58.7 %all-to-all-start.3 = ((bf16[64,6,2048]{2,1,0:T(8,128)(2,1)}), bf16[64,6,2048]{2,1,0:T(8,128)(2,1)}, u32[]{:S(2)}, u32[]{:S(2)}) async-start(bf16[64,6,2048]{2,1,0:T(8,128)(2,1)} %reshape.136), calls=%async_computation.3 | async-start | bytes 4194304 | tf_op jit(solution)/shard_map/all_to_all | solution.py:135
  401.5 65.3 %collective-permute-start.3 = (bf16[1,2,192,2048]{3,2,1,0:T(8,128)(2,1)}, bf16[1,2,192,2048]{3,2,1,0:T(8,128)(2,1)}, u32[]{:S(2)}, u32[]{:S(2)}) collective-permute-start(bf16[1,2,192,2048]{3,2,1,0:T(8,128)(2,1)} %param.19), channel_id=1, source_target_pairs={{0,128},{128,0},{4,132},{132,4},{8,136},{136,8},{12,140},{140,12},... | collective-permute-start | bytes 4718600 | tf_op jit(solution)/shard_map/ppermute | solution.py:19
  404.1 96.4 %collective-permute-start.2 = (bf16[1,2,192,2048]{3,2,1,0:T(8,128)(2,1)}, bf16[1,2,192,2048]{3,2,1,0:T(8,128)(2,1)}, u32[]{:S(2)}, u32[]{:S(2)}) collective-permute-start(bf16[1,2,192,2048]{3,2,1,0:T(8,128)(2,1)} %param.18), channel_id=1, source_target_pairs={{0,128},{128,0},{4,132},{132,4},{8,136},{136,8},{12,140},{140,12},... | collective-permute-start | bytes 4718600 | tf_op jit(solution)/shard_map/ppermute | solution.py:19
  455.6 44.8 %copy-start.2 = (bf16[1,2,192,2048]{3,2,1,0:T(8,128)(2,1)S(1)}, bf16[1,2,192,2048]{3,2,1,0:T(8,128)(2,1)}, u32[]{:S(2)}) copy-start(bf16[1,2,192,2048]{3,2,1,0:T(8,128)(2,1)} %broadcast_select_fusion) | copy-start | bytes 4718596
  500.5 6.3 %copy-start.1 = (bf16[32,2048]{1,0:T(8,128)(2,1)S(1)}, bf16[32,2048]{1,0:T(8,128)(2,1)}, u32[]{:S(2)}) copy-start(bf16[32,2048]{1,0:T(8,128)(2,1)} %param.11) | copy-start | bytes 393220
Sparse Core Ops, SparseCore 0:
  45.7 108.1 all-gather.2
  187.6 64.9 reduce-scatter.4
  267.7 43.4 all-gather.4
  322.5 102.7 reduce-scatter.2
where the time goes:
time: 514 us; the launch traced here: 513 us
  waiting for transfers between devices  353 us (69%)
  starting transfers between devices  60.8 us (12%)
  local copies, waits for them, and re-layouts  30.8 us (6%)
  matrix products  28.6 us (6%)
  other arithmetic  25.4 us (5%)
  between operations  14.7 us (3%)
    ppermute x6, waiting for transfers between devices, swapped_2(): return lax.ppermute(block, axis, route)  142 us
    all_to_all x1, waiting for transfers between devices, body(): lax.all_to_all(send_d.reshape(axis_width, capacity, feature), 'expert', s...  46.1 us
    all_gather x1, waiting for transfers between devices, body(): lax.all_gather(down, 'dp', axis=1, tiled=True)  43.3 us
    all_to_all x1, waiting for transfers between devices, body(): lax.all_to_all(d_rows.reshape(axis_width, capacity, feature), 'expert', s...  42.2 us
    all_to_all x1, waiting for transfers between devices, body(): lax.all_to_all(send_x.reshape(axis_width, capacity, feature), 'expert', s...  40.8 us
    all_to_all x1, waiting for transfers between devices, body(): lax.all_to_all(out_rows.reshape(axis_width, capacity, feature), 'expert',...  38.4 us
    all_to_all x1, starting transfers between devices, body(): lax.all_to_all(send_x.reshape(axis_width, capacity, feature), 'expert', s...  16.5 us
    all_to_all x1, starting transfers between devices, body(): lax.all_to_all(out_rows.reshape(axis_width, capacity, feature), 'expert',...  12.4 us
  transfers between devices with their start and end apart: 14, of which 11 were waited for; matrix products, arithmetic and copies ran while one was open for 9% of the time, Pallas kernels for 0%

commit v1 on v0

v1 whole, which is shorter than its diff:
```python
import jax
import jax.numpy as jnp
from jax import lax
from jax.experimental import pallas as pl
from jax.experimental.pallas import tpu as pltpu
from jax.sharding import Mesh, PartitionSpec as P

BETA_ONE = 0.9
BETA_TWO = 0.95
STEP_RATE = 0.01
ADAM_EPS = 1e-08

F32 = jnp.float32
BF16 = jnp.bfloat16
CAP = 6
RINGS = ("y", "z")
ALL = ("xh", "y", "z", "xl", "core")


def swap(block, axis):
    return lax.ppermute(block, axis, [(0, 1), (1, 0)])


def after(value, *earlier):
    return lax.optimization_barrier((value, *earlier))[0]


def adam_update(weight, moment_one, moment_two, gradient):
    one_new = BETA_ONE * moment_one.astype(F32) + (1.0 - BETA_ONE) * gradient
    two_new = BETA_TWO * moment_two.astype(F32) + (1.0 - BETA_TWO) * gradient * gradient
    return (weight.astype(F32) - STEP_RATE * one_new / (jnp.sqrt(two_new) + ADAM_EPS)).astype(BF16)


def dot_nt(left, right):
    return lax.dot_general(left, right, (((1,), (1,)), ((), ())), preferred_element_type=F32)


def dot_nn(left, right):
    return lax.dot_general(left, right, (((1,), (0,)), ((), ())), preferred_element_type=F32)


def dot_tn(left, right):
    return lax.dot_general(left, right, (((0,), (0,)), ((), ())), preferred_element_type=F32)


CHUNK = 256


def expert_kernel(x_ref, d_ref, w_own, w_xl, w_pair, o_ref, dx_ref, g_own, g_xl, g_pair,
                  w_all, g_all, o_acc, dx_acc, in_sem, out_sem):
    share = w_own.shape[1]
    sources = (w_own, w_xl, w_pair.at[0], w_pair.at[1])
    targets = (g_own, g_xl, g_pair.at[0], g_pair.at[1])
    loads = [
        pltpu.make_async_copy(src, w_all.at[:, pl.ds(i * share, share)], in_sem.at[i])
        for i, src in enumerate(sources)
    ]
    stores = [
        pltpu.make_async_copy(g_all.at[:, pl.ds(i * share, share)], dst, out_sem.at[i])
        for i, dst in enumerate(targets)
    ]
    for load in loads:
        load.start()
    for load in loads:
        load.wait()
    chunks = w_all.shape[1] // CHUNK

    def step(c, carry):
        rows = pl.ds(pl.multiple_of(c * CHUNK, CHUNK), CHUNK)
        x = x_ref[...]
        d = d_ref[...]
        a = dot_nt(x, w_all[0, rows, :])
        u = dot_nt(x, w_all[1, rows, :])
        s = 1.0 / (1.0 + jnp.exp(-a))
        h = (a * s * u).astype(BF16)
        dh = dot_nt(d, w_all[2, rows, :])
        da = (dh * u * s * (1.0 + a * (1.0 - s))).astype(BF16)
        du = (dh * a * s).astype(BF16)
        o = dot_nn(h, w_all[2, rows, :])
        dx = dot_nn(da, w_all[0, rows, :]) + dot_nn(du, w_all[1, rows, :])

        @pl.when(c == 0)
        def _():
            o_acc[...] = o
            dx_acc[...] = dx

        @pl.when(c > 0)
        def _():
            o_acc[...] += o
            dx_acc[...] += dx

        g_all[0, rows, :] = dot_tn(da, x).astype(BF16)
        g_all[1, rows, :] = dot_tn(du, x).astype(BF16)
        g_all[2, rows, :] = dot_tn(h, d).astype(BF16)
        return carry

    lax.fori_loop(0, chunks, step, 0)
    for store in stores:
        store.start()
    o_ref[...] = o_acc[...].astype(BF16)
    dx_ref[...] = dx_acc[...].astype(BF16)
    for store in stores:
        store.wait()


def expert_step(x, d, w_own, w_xl, w_pair):
    rows, feature = x.shape
    share = w_own.shape[1]
    any_spec = pl.BlockSpec(memory_space=pl.ANY)
    vmem_spec = pl.BlockSpec(memory_space=pltpu.VMEM)
    row_shape = jax.ShapeDtypeStruct((rows, feature), BF16)
    part_shape = jax.ShapeDtypeStruct(w_own.shape, BF16)
    pair_shape = jax.ShapeDtypeStruct(w_pair.shape, BF16)
    return pl.pallas_call(
        expert_kernel,
        out_shape=(row_shape, row_shape, part_shape, part_shape, pair_shape),
        in_specs=[vmem_spec, vmem_spec, any_spec, any_spec, any_spec],
        out_specs=(vmem_spec, vmem_spec, any_spec, any_spec, any_spec),
        scratch_shapes=[
            pltpu.VMEM((3, 4 * share, feature), BF16),
            pltpu.VMEM((3, 4 * share, feature), BF16),
            pltpu.VMEM((rows, feature), F32),
            pltpu.VMEM((rows, feature), F32),
            pltpu.SemaphoreType.DMA((4,)),
            pltpu.SemaphoreType.DMA((4,)),
        ],
        compiler_params=pltpu.CompilerParams(vmem_limit_bytes=56 * 1024 * 1024),
        cost_estimate=pl.CostEstimate(
            flops=18 * rows * feature * 4 * share,
            bytes_accessed=2 * (4 * rows * feature + 24 * share * feature),
            transcendentals=rows * 4 * share,
        ),
    )(x, d, w_own, w_xl, w_pair)


def split_three(value):
    high = value.astype(BF16)
    rest = value - high.astype(F32)
    middle = rest.astype(BF16)
    low = (rest - middle.astype(F32)).astype(BF16)
    return high, middle, low


def body(tokens, cotangent, routes, route_weights, matching, gate_up, down, gate_up_m, gate_up_v,
         down_m, down_v):
    half = lax.axis_index("xh")
    rings = lax.axis_size("y") * lax.axis_size("z")
    self_index = half * rings + lax.axis_index("y") * lax.axis_size("z") + lax.axis_index("z")
    swapped = jnp.sum(jnp.where(jnp.arange(2 * rings) == self_index, matching, 0)) != self_index
    count, feature = tokens.shape
    slots = 2 * CAP

    packed = jnp.concatenate([tokens, cotangent])
    packed_other = swap(packed, "xh")
    routes_other = swap(routes, "xh")
    weights_other = swap(route_weights, "xh")
    source = jnp.concatenate([packed, packed_other])

    w_own = jnp.concatenate([gate_up[0], down])
    w_first = after(w_own, packed_other, routes_other, weights_other)
    w_xl = swap(w_first, "xl")
    w_pair = swap(jnp.stack([w_own, w_xl]), "core")

    both_routes = jnp.stack([routes, routes_other])
    both_weights = jnp.stack([route_weights, weights_other])
    ring_ids = jnp.arange(rings, dtype=jnp.int32)
    hit = both_routes[..., None] == half * rings + ring_ids
    used = jnp.any(hit, axis=2)
    scale = jnp.sum(jnp.where(hit, both_weights[..., None], 0.0), axis=2)
    earlier = jnp.cumsum(used.astype(jnp.int32), axis=1) - used
    slot = earlier + CAP * jnp.arange(2, dtype=jnp.int32)[:, None, None]
    slot = jnp.where(used, slot, -1)
    slot_ids = jnp.arange(slots, dtype=jnp.int32)
    select = jnp.transpose(slot, (2, 0, 1))[:, None] == slot_ids[None, :, None, None]
    row_scale = jnp.sum(jnp.where(select, jnp.transpose(scale, (2, 0, 1))[:, None], 0.0), axis=(2, 3))
    select_b = select.astype(BF16)
    none = jnp.zeros_like(select_b)
    pick_x = jnp.stack([select_b, none], axis=3)
    pick_c = jnp.stack([none, select_b], axis=3)
    pick = jnp.concatenate([pick_x, pick_c], axis=1).reshape(rings * 2 * slots, 4 * count)
    factor = jnp.concatenate([jnp.ones_like(row_scale), row_scale], axis=1).reshape(-1, 1)
    send = (dot_nn(pick, source) * factor).astype(BF16).reshape(rings, 2 * slots, feature)

    recv = lax.all_to_all(send, RINGS, split_axis=0, concat_axis=0, tiled=True)
    rows_x = recv[:, :slots].reshape(rings * slots, feature)
    rows_d = recv[:, slots:].reshape(rings * slots, feature)

    out_rows, dx_rows, g_own, g_xl, g_pair = expert_step(rows_x, rows_d, w_own, w_xl, w_pair)

    g_core = swap(g_pair, "core")
    back_send = jnp.concatenate(
        [out_rows.reshape(rings, slots, feature), dx_rows.reshape(rings, slots, feature)], axis=1
    )
    back = lax.all_to_all(back_send, RINGS, split_axis=0, concat_axis=0, tiled=True)
    moments_one = (gate_up_m[0, 0], gate_up_m[0, 1], down_m[0])
    moments_two = (gate_up_v[0, 0], gate_up_v[0, 1], down_v[0])
    updated = []
    for i in range(3):
        to_other = (g_xl[i].astype(F32) + g_core[1, i].astype(F32)).astype(BF16)
        gradient = g_own[i].astype(F32) + g_core[0, i].astype(F32) + swap(to_other, "xl").astype(F32)
        new = adam_update(w_own[i], moments_one[i], moments_two[i], gradient)
        updated.append(jnp.where(swapped, swap(new, "xh"), new))

    mix = jnp.transpose(select, (2, 3, 0, 1))
    mix_y = jnp.where(mix, row_scale, 0.0)
    mix_y = jnp.concatenate([mix_y, jnp.zeros_like(mix_y)], axis=3).reshape(2 * count, -1)
    mix_d = mix.astype(BF16)
    mix_d = jnp.concatenate([jnp.zeros_like(mix_d), mix_d], axis=3).reshape(2 * count, -1)
    mixed = dot_nn(
        jnp.concatenate([*split_three(mix_y), mix_d]), back.reshape(rings * 2 * slots, feature)
    ).reshape(4, 2, count, feature)
    sum_y = mixed[0] + mixed[1] + mixed[2]
    sum_d = mixed[3]
    theirs = jnp.concatenate([sum_y[1], sum_d[1]]).astype(BF16)
    ours = swap(theirs, "xh").astype(F32)
    layer_out = (sum_y[0] + ours[:count]).astype(BF16)
    input_grad = (sum_d[0] + ours[count:]).astype(BF16)
    return layer_out, input_grad, jnp.stack(updated[:2])[None], updated[2][None]


def solution(mesh):
    wide = Mesh(mesh.devices.reshape(2, 4, 8, 2, 2), ALL)
    token_spec = P(ALL, None)
    expert, share = ("xh", "y", "z"), ("xl", "core")
    up_spec = P(expert, None, share, None)
    down_spec = P(expert, share, None)
    return jax.shard_map(
        body,
        mesh=wide,
        in_specs=(token_spec, token_spec, token_spec, token_spec, P(), up_spec, down_spec, up_spec,
                  up_spec, down_spec, down_spec),
        out_specs=(token_spec, token_spec, up_spec, down_spec),
        check_vma=False,
    )
```

time: 514 us -> 283 us (0.55)
  waiting for transfers between devices: 353 us -> 149 us
  Pallas kernels: 0 us -> 26.3 us
  matrix products: 28.6 us -> 4.74 us
  starting transfers between devices: 60.8 us -> 41.8 us
  other arithmetic: 25.4 us -> 39.6 us
  between operations: 14.7 us -> 1.56 us
  local copies, waits for them, and re-layouts: 30.8 us -> 19.6 us
    all_to_all x4 -> x2, waiting for transfers between devices: 168 us -> 27.9 us  [the longest x1 27.9 us: body(): recv = lax.all_to_all(send, RINGS, split_axis=0, concat_axis=0, tiled=True)]
    all_gather x2 -> x0, waiting for transfers between devices: 43.3 us -> none  [the longest x1 43.3 us: body(): lax.all_gather(down, 'dp', axis=1, tiled=True)]
    all_to_all x4 -> x2, starting transfers between devices: 48.2 us -> 15.4 us  [the longest x1 11.2 us: body(): recv = lax.all_to_all(send, RINGS, split_axis=0, concat_axis=0, tiled=True)]
    pallas_call x0 -> x1, Pallas kernels: none -> 26.3 us  [expert_step(): pl.pallas_call(expert_kernel, out_shape=(row_shape, row_shape, part_shape...]
    dot_general x9 -> x2, matrix products: 28.6 us -> 4.74 us  [dot_nn(): lax.dot_general(left, right, (((1,), (0,)), ((), ())), preferred_element_...]
    ppermute x6 -> x13, waiting for transfers between devices: 142 us -> 121 us  [swap(): return lax.ppermute(block, axis, [(0, 1), (1, 0)])]
    ppermute x6 -> x13, starting transfers between devices: 12.1 us -> 26.4 us  [swap(): return lax.ppermute(block, axis, [(0, 1), (1, 0)])]
    another operation x3 -> x7, other arithmetic: 3.83 us -> 11.6 us  [the longest x2 9.12 us: body(): w_pair = swap(jnp.stack([w_own, w_xl]), 'core')]
  transfers between devices with their start and end apart: 14 -> 15, of which waited for: 11 -> 9; matrix products, arithmetic and copies ran while one was open for 9% -> 22% of each run, Pallas kernels for 0% -> 0%
where the time goes in v1:
time: 283 us
  waiting for transfers between devices  149 us (53%)
  starting transfers between devices  41.8 us (15%)
  other arithmetic  39.6 us (14%)
  Pallas kernels  26.3 us (9%)
  local copies, waits for them, and re-layouts  19.6 us (7%)
  matrix products  4.74 us (2%)
    ppermute x13, waiting for transfers between devices, swap(): return lax.ppermute(block, axis, [(0, 1), (1, 0)])  121 us
    all_to_all x1, waiting for transfers between devices, body(): recv = lax.all_to_all(send, RINGS, split_axis=0, concat_axis=0, tiled=True)  27.9 us
    ppermute x13, starting transfers between devices, swap(): return lax.ppermute(block, axis, [(0, 1), (1, 0)])  26.4 us
    pallas_call x1, Pallas kernels, expert_step(): pl.pallas_call(expert_kernel, out_shape=(row_shape, row_shape, part_shape...  26.3 us
    all_to_all x1, starting transfers between devices, body(): recv = lax.all_to_all(send, RINGS, split_axis=0, concat_axis=0, tiled=True)  11.2 us
    another operation x2, other arithmetic, body(): w_pair = swap(jnp.stack([w_own, w_xl]), 'core')  9.12 us
    convert_element_type x1, other arithmetic, adam_update(): (weight.astype(F32) - STEP_RATE * one_new / (jnp.sqrt(two_new) + ADAM_EPS...  8.18 us
  transfers between devices with their start and end apart: 15, of which 9 were waited for; matrix products, arithmetic and copies ran while one was open for 22% of the time, Pallas kernels for 0%

profile of v1, /device:TPU:1, one launch (start us, length us, event | category | flops | bytes accessed | tf_op | source)
XLA Modules:
  0.0 282.6 jit_solution(1011902963610589537)
XLA Ops:
  0.6 3.7 %collective-permute-start = (s32[32,8]{0,1:T(8,128)}, s32[32,8]{0,1:T(8,128)S(1)}, u32[]{:S(2)}, u32[]{:S(2)}) collective-permute-start(s32[32,8]{0,1:T(8,128)} %param.13), channel_id=1, source_target_pairs={{0,128},{128,0},{1,129},{129,1},{2,130},{130,2},{3,131},{131,3},{4... | collective-permute-start | bytes 3080 | tf_op jit(solution)/shard_map/ppermute | solution.py:21
  4.4 1.0 pad_maximum_fusion.3
  5.4 3.0 %collective-permute-start.2 = (bf16[64,2048]{1,0:T(8,128)(2,1)S(1)}, bf16[64,2048]{1,0:T(8,128)(2,1)S(1)}, u32[]{:S(2)}, u32[]{:S(2)}) collective-permute-start(bf16[64,2048]{1,0:T(8,128)(2,1)S(1)} %pad_maximum_fusion.3), channel_id=1, source_target_pairs={{0,128},{128,0},{1,129},{129,1},{2,130},{130,2},{3,131},{131,3},{4... | collective-permute-start | bytes 786440 | tf_op jit(solution)/shard_map/ppermute | solution.py:21
  8.3 4.1 %fusion.50 = (bf16[1,3,192,2048]{3,2,1,0:T(8,128)(2,1)}, bf16[3,192,2048]{2,1,0:T(8,128)(2,1)}) fusion(bf16[1,192,2048]{2,1,0:T(8,128)(2,1)} %param.17, bf16[2,192,2048]{2,1,0:T(8,128)(2,1)} %bitcast.128), kind=kLoop, calls=%fused_computation.103 | loop fusion | flops 1179648 | bytes 7077888 | tf_op jit(solution)/shard_map/stack | solution.py:162
  13.9 1.0 collective-permute-start.3
  15.3 1.2 fusion.27
  16.9 2.6 multiply_convert_fusion
  19.5 11.2 %all-to-all-start = ((bf16[32,24,2048]{2,1,0:T(8,128)(2,1)}), bf16[32,24,2048]{2,1,0:T(8,128)(2,1)S(1)}, u32[]{:S(2)}, u32[]{:S(2)}) async-start(bf16[32,24,2048]{2,1,0:T(8,128)(2,1)} %bitcast.127), calls=%async_computation | async-start | bytes 6291456 | tf_op jit(solution)/shard_map/all_to_all | solution.py:184
  30.8 33.7 %collective-permute-done.3.w_xl = bf16[3,192,2048]{2,1,0:T(8,128)(2,1)} collective-permute-done((bf16[3,192,2048]{2,1,0:T(8,128)(2,1)}, bf16[3,192,2048]{2,1,0:T(8,128)(2,1)}, u32[]{:S(2)}, u32[]{:S(2)}) %collective-permute-start.3) | collective-permute-done | bytes 2359328 | tf_op jit(solution)/shard_map/ppermute | solution.py:21
  64.5 5.0 %pad_maximum_fusion = bf16[2,3,192,2048]{3,2,1,0:T(8,128)(2,1)} fusion(bf16[1,3,192,2048]{3,2,1,0:T(8,128)(2,1)} %bitcast.10, bf16[1,3,192,2048]{3,2,1,0:T(8,128)(2,1)} %get-tuple-element.24), kind=kLoop, calls=%fused_computation.1 | loop fusion | flops 2359296 | bytes 9437184 | tf_op jit(solution)/shard_map/stack | solution.py:162
  69.5 3.4 %collective-permute-start.4 = (bf16[2,3,192,2048]{3,2,1,0:T(8,128)(2,1)}, bf16[2,3,192,2048]{3,2,1,0:T(8,128)(2,1)}, u32[]{:S(2)}, u32[]{:S(2)}) collective-permute-start(bf16[2,3,192,2048]{3,2,1,0:T(8,128)(2,1)} %pad_maximum_fusion), channel_id=1, source_target_pairs={{0,1},{1,0},{2,3},{3,2},{4,5},{5,4},{6,7},{7,6},{8,9},{9,8},{10,11... | collective-permute-start | bytes 14155784 | tf_op jit(solution)/shard_map/ppermute | solution.py:21
  72.9 27.9 %all-to-all-done = bf16[32,24,2048]{2,1,0:T(8,128)(2,1)S(1)} async-done(((bf16[32,24,2048]{2,1,0:T(8,128)(2,1)}), bf16[32,24,2048]{2,1,0:T(8,128)(2,1)S(1)}, u32[]{:S(2)}, u32[]{:S(2)}) %all-to-all-start) | async-done | bytes 3145760 | tf_op jit(solution)/shard_map/all_to_all | solution.py:184
  100.8 2.9 %fusion.51 = (bf16[32,12,2048]{2,1,0:T(8,128)(2,1)}, bf16[32,12,2048]{2,1,0:T(8,128)(2,1)}) fusion(bf16[32,24,2048]{2,1,0:T(8,128)(2,1)S(1)} %all-to-all-done), kind=kLoop, calls=%fused_computation.104 | loop fusion | bytes 6291456 | tf_op jit(solution)/shard_map/slice | solution.py:186
  103.8 3.8 %reshape.141.x_ref = bf16[384,2048]{1,0:T(8,128)(2,1)} reshape(bf16[32,12,2048]{2,1,0:T(8,128)(2,1)} %get-tuple-element.23) | data formatting | bytes 3145728 | tf_op jit(solution)/shard_map/reshape | solution.py:185
  107.5 1.4 reshape.142.d_ref
  108.9 26.3 %shard_map.138 = (bf16[384,2048]{1,0:T(8,128)(2,1)}, bf16[384,2048]{1,0:T(8,128)(2,1)}, bf16[3,192,2048]{2,1,0:T(8,128)(2,1)}, bf16[3,192,2048]{2,1,0:T(8,128)(2,1)}, bf16[2,3,192,2048]{3,2,1,0:T(8,128)(2,1)}) custom-call(bf16[384,2048]{1,0:T(8,128)(2,1)} %reshape.141.x_ref, bf16[384,2048]{1,0:T(8,128)(2,1)} %reshape.142.d_ref, ...), custom_call_target="tpu_custom_call" | custom-call | flops 10871635968 | bytes 25165824 | tf_op jit(solution)/shard_map/pallas_call | solution.py:114
  135.2 5.5 %collective-permute-start.6 = (bf16[2,3,192,2048]{3,2,1,0:T(8,128)(2,1)}, bf16[2,3,192,2048]{3,2,1,0:T(8,128)(2,1)}, u32[]{:S(2)}, u32[]{:S(2)}) collective-permute-start(bf16[2,3,192,2048]{3,2,1,0:T(8,128)(2,1)} %get-tuple-element.14), channel_id=1, source_target_pairs={{0,1},{1,0},{2,3},{3,2},{4,5},{5,4},{6,7},{7,6},{8,9},{9,8},{10,11... | collective-permute-start | bytes 14155784 | tf_op jit(solution)/shard_map/ppermute | solution.py:21
  140.7 2.4 reshape.143
  143.1 3.6 %reshape.144 = bf16[32,12,2048]{2,1,0:T(8,128)(2,1)} reshape(bf16[384,2048]{1,0:T(8,128)(2,1)} %get-tuple-element.12) | data formatting | bytes 3145728 | tf_op jit(solution)/shard_map/reshape | solution.py:192
  146.7 4.2 %pad_maximum_fusion.1 = bf16[32,24,2048]{2,1,0:T(8,128)(2,1)} fusion(bf16[32,12,2048]{2,1,0:T(8,128)(2,1)} %reshape.144, bf16[32,12,2048]{2,1,0:T(8,128)(2,1)S(1)} %reshape.143), kind=kLoop, calls=%fused_computation.2 | loop fusion | flops 6291456 | bytes 6291456 | tf_op jit(solution)/shard_map/concatenate | solution.py:191
  150.9 4.2 %all-to-all-start.1 = ((bf16[32,24,2048]{2,1,0:T(8,128)(2,1)}), bf16[32,24,2048]{2,1,0:T(8,128)(2,1)S(1)}, u32[]{:S(2)}, u32[]{:S(2)}) async-start(bf16[32,24,2048]{2,1,0:T(8,128)(2,1)} %pad_maximum_fusion.1), calls=%async_computation.1 | async-start | bytes 6291456 | tf_op jit(solution)/shard_map/all_to_all | solution.py:194
  155.1 0.6 fusion.47
  156.6 4.5 %fusion.15 = (bf16[192,2048]{1,0:T(8,128)(2,1)}, bf16[192,2048]{1,0:T(8,128)(2,1)}, bf16[192,2048]{1,0:T(8,128)(2,1)}) fusion(bf16[2,3,192,2048]{3,2,1,0:T(8,128)(2,1)} %collective-permute-done.6, bf16[3,192,2048]{2,1,0:T(8,128)(2,1)} %get-tuple-element.15), kind=kLoop, calls=%fused_computation.26 | loop fusion | flops 4718592 | bytes 7077888 | tf_op jit(solution)/shard_map/convert_element_type | solution.py:199
  161.1 0.5 collective-permute-start.11
  161.6 0.9 collective-permute-start.7
  162.5 0.5 collective-permute-start.9
  163.5 1.1 concatenate.32
  164.7 2.4 reshape.136
  167.6 0.9 reshape.147
  168.5 2.0 fusion.52
  170.5 10.0 %collective-permute-done.11 = bf16[192,2048]{1,0:T(8,128)(2,1)} collective-permute-done((bf16[192,2048]{1,0:T(8,128)(2,1)}, bf16[192,2048]{1,0:T(8,128)(2,1)}, u32[]{:S(2)}, u32[]{:S(2)}) %collective-permute-start.11) | collective-permute-done | bytes 786464 | tf_op jit(solution)/shard_map/ppermute | solution.py:21
  180.5 16.9 %collective-permute-done.7 = bf16[192,2048]{1,0:T(8,128)(2,1)} collective-permute-done((bf16[192,2048]{1,0:T(8,128)(2,1)}, bf16[192,2048]{1,0:T(8,128)(2,1)}, u32[]{:S(2)}, u32[]{:S(2)}) %collective-permute-start.7) | collective-permute-done | bytes 786464 | tf_op jit(solution)/shard_map/ppermute | solution.py:21
  197.4 16.9 %collective-permute-done.9 = bf16[192,2048]{1,0:T(8,128)(2,1)} collective-permute-done((bf16[192,2048]{1,0:T(8,128)(2,1)}, bf16[192,2048]{1,0:T(8,128)(2,1)}, u32[]{:S(2)}, u32[]{:S(2)}) %collective-permute-start.9) | collective-permute-done | bytes 786464 | tf_op jit(solution)/shard_map/ppermute | solution.py:21
  214.2 8.2 %fusion.26 = (bf16[192,2048]{1,0:T(8,128)(2,1)}, bf16[192,2048]{1,0:T(8,128)(2,1)}, bf16[192,2048]{1,0:T(8,128)(2,1)}) fusion(bf16[192,2048]{1,0:T(8,128)(2,1)} %collective-permute-done.7, bf16[2,3,192,2048]{3,2,1,0:T(8,128)(2,1)} %collective-permute-done.6, bf16[1,2,192,2048]{3,2,1,0:T(8,128)(2,1)} %param.19, bf16[3,192,2048]{2,1,0:T(8,128)(2,1)} %get-tuple-element.13, ...), kind=kLoop, calls=%fused_computation.45 | loop fusion | flops 23592960 | bytes 16515072 | tf_op jit(solution)/shard_map/convert_element_type | solution.py:31
  222.4 2.5 collective-permute-start.12
  224.9 0.5 collective-permute-start.8
  225.5 2.4 collective-permute-start.10
  227.9 2.1 fusion.33
  230.2 2.2 collective-permute-start.5
  232.4 10.1 %collective-permute-done.12 = bf16[192,2048]{1,0:T(8,128)(2,1)} collective-permute-done((bf16[192,2048]{1,0:T(8,128)(2,1)}, bf16[192,2048]{1,0:T(8,128)(2,1)}, u32[]{:S(2)}, u32[]{:S(2)}) %collective-permute-start.12) | collective-permute-done | bytes 786464 | tf_op jit(solution)/shard_map/ppermute | solution.py:21
  242.5 2.1 select_bitcast_fusion
  244.6 14.8 %collective-permute-done.8 = bf16[192,2048]{1,0:T(8,128)(2,1)} collective-permute-done((bf16[192,2048]{1,0:T(8,128)(2,1)}, bf16[192,2048]{1,0:T(8,128)(2,1)}, u32[]{:S(2)}, u32[]{:S(2)}) %collective-permute-start.8) | collective-permute-done | bytes 786464 | tf_op jit(solution)/shard_map/ppermute | solution.py:21
  259.4 1.2 select_bitcast_fusion.2
  260.6 15.6 %collective-permute-done.10 = bf16[192,2048]{1,0:T(8,128)(2,1)} collective-permute-done((bf16[192,2048]{1,0:T(8,128)(2,1)}, bf16[192,2048]{1,0:T(8,128)(2,1)}, u32[]{:S(2)}, u32[]{:S(2)}) %collective-permute-start.10) | collective-permute-done | bytes 786464 | tf_op jit(solution)/shard_map/ppermute | solution.py:21
  276.3 1.2 select_bitcast_fusion.1
  277.5 1.3 maximum_bitcast_fusion
  278.8 3.0 %collective-permute-done.5 = bf16[64,2048]{1,0:T(8,128)(2,1)S(1)} collective-permute-done((bf16[64,2048]{1,0:T(8,128)(2,1)S(1)}, bf16[64,2048]{1,0:T(8,128)(2,1)S(1)}, u32[]{:S(2)}, u32[]{:S(2)}) %collective-permute-start.5) | collective-permute-done | bytes 262176 | tf_op jit(solution)/shard_map/ppermute | solution.py:21
  281.8 0.8 fusion.43
  (51 shorter events, 3.6 us)
Async XLA Ops:
  0.6 11.9 %collective-permute-start = (s32[32,8]{0,1:T(8,128)}, s32[32,8]{0,1:T(8,128)S(1)}, u32[]{:S(2)}, u32[]{:S(2)}) collective-permute-start(s32[32,8]{0,1:T(8,128)} %param.13), channel_id=1, source_target_pairs={{0,128},{128,0},{1,129},{129,1},{2,130},{130,2},{3,131},{131,3},{4... | collective-permute-start | bytes 3080 | tf_op jit(solution)/shard_map/ppermute | solution.py:21
  4.3 8.5 %collective-permute-start.1 = (f32[32,8]{0,1:T(8,128)}, f32[32,8]{0,1:T(8,128)S(1)}, u32[]{:S(2)}, u32[]{:S(2)}) collective-permute-start(f32[32,8]{0,1:T(8,128)} %param.14), channel_id=1, source_target_pairs={{0,128},{128,0},{1,129},{129,1},{2,130},{130,2},{3,131},{131,3},{4... | collective-permute-start | bytes 3080 | tf_op jit(solution)/shard_map/ppermute | solution.py:21
  5.4 8.5 %collective-permute-start.2 = (bf16[64,2048]{1,0:T(8,128)(2,1)S(1)}, bf16[64,2048]{1,0:T(8,128)(2,1)S(1)}, u32[]{:S(2)}, u32[]{:S(2)}) collective-permute-start(bf16[64,2048]{1,0:T(8,128)(2,1)S(1)} %pad_maximum_fusion.3), channel_id=1, source_target_pairs={{0,128},{128,0},{1,129},{129,1},{2,130},{130,2},{3,131},{131,3},{4... | collective-permute-start | bytes 786440 | tf_op jit(solution)/shard_map/ppermute | solution.py:21
  8.3 4.2 %copy-start.4 = (s32[32,8]{0,1:T(8,128)S(1)}, s32[32,8]{0,1:T(8,128)}, u32[]{:S(2)}) copy-start(s32[32,8]{0,1:T(8,128)} %param.13) | copy-start | bytes 3076
  8.3 4.4 %copy-start.5 = (f32[32,8]{0,1:T(8,128)S(1)}, f32[32,8]{0,1:T(8,128)}, u32[]{:S(2)}) copy-start(f32[32,8]{0,1:T(8,128)} %param.14) | copy-start | bytes 3076
  12.9 3.9 %copy-start.2 = (bf16[32,2048]{1,0:T(8,128)(2,1)S(1)}, bf16[32,2048]{1,0:T(8,128)(2,1)}, u32[]{:S(2)}) copy-start(bf16[32,2048]{1,0:T(8,128)(2,1)} %param.12) | copy-start | bytes 393220
  13.0 3.9 %copy-start.3 = (bf16[32,2048]{1,0:T(8,128)(2,1)S(1)}, bf16[32,2048]{1,0:T(8,128)(2,1)}, u32[]{:S(2)}) copy-start(bf16[32,2048]{1,0:T(8,128)(2,1)} %param.11) | copy-start | bytes 393220
  13.9 50.6 %collective-permute-start.3 = (bf16[3,192,2048]{2,1,0:T(8,128)(2,1)}, bf16[3,192,2048]{2,1,0:T(8,128)(2,1)}, u32[]{:S(2)}, u32[]{:S(2)}) collective-permute-start(bf16[3,192,2048]{2,1,0:T(8,128)(2,1)} %get-tuple-element.10.w_own), channel_id=1, source_target_pairs={{0,2},{2,0},{1,3},{3,1},{4,6},{6,4},{5,7},{7,5},{8,10},{10,8},{9,1... | collective-permute-start | bytes 7077896 | tf_op jit(solution)/shard_map/ppermute | solution.py:21
  19.5 81.3 %all-to-all-start = ((bf16[32,24,2048]{2,1,0:T(8,128)(2,1)}), bf16[32,24,2048]{2,1,0:T(8,128)(2,1)S(1)}, u32[]{:S(2)}, u32[]{:S(2)}) async-start(bf16[32,24,2048]{2,1,0:T(8,128)(2,1)} %bitcast.127), calls=%async_computation | async-start | bytes 6291456 | tf_op jit(solution)/shard_map/all_to_all | solution.py:184
  69.5 39.4 %collective-permute-start.4 = (bf16[2,3,192,2048]{3,2,1,0:T(8,128)(2,1)}, bf16[2,3,192,2048]{3,2,1,0:T(8,128)(2,1)}, u32[]{:S(2)}, u32[]{:S(2)}) collective-permute-start(bf16[2,3,192,2048]{3,2,1,0:T(8,128)(2,1)} %pad_maximum_fusion), channel_id=1, source_target_pairs={{0,1},{1,0},{2,3},{3,2},{4,5},{5,4},{6,7},{7,6},{8,9},{9,8},{10,11... | collective-permute-start | bytes 14155784 | tf_op jit(solution)/shard_map/ppermute | solution.py:21
  103.7 3.8 %copy-start = (bf16[32,12,2048]{2,1,0:T(8,128)(2,1)S(1)}, bf16[32,12,2048]{2,1,0:T(8,128)(2,1)}, u32[]{:S(2)}) copy-start(bf16[32,12,2048]{2,1,0:T(8,128)(2,1)} %get-tuple-element.22) | copy-start | bytes 4718596
  135.2 21.4 %collective-permute-start.6 = (bf16[2,3,192,2048]{3,2,1,0:T(8,128)(2,1)}, bf16[2,3,192,2048]{3,2,1,0:T(8,128)(2,1)}, u32[]{:S(2)}, u32[]{:S(2)}) collective-permute-start(bf16[2,3,192,2048]{3,2,1,0:T(8,128)(2,1)} %get-tuple-element.14), channel_id=1, source_target_pairs={{0,1},{1,0},{2,3},{3,2},{4,5},{5,4},{6,7},{7,6},{8,9},{9,8},{10,11... | collective-permute-start | bytes 14155784 | tf_op jit(solution)/shard_map/ppermute | solution.py:21
  150.9 4.2 %copy-start.6 = (s32[64]{0:T(128)S(1)}, s32[64]{0:T(128)}, u32[]{:S(2)}) copy-start(s32[64]{0:T(128)} %param.15) | copy-start | bytes 772
  150.9 77.0 %all-to-all-start.1 = ((bf16[32,24,2048]{2,1,0:T(8,128)(2,1)}), bf16[32,24,2048]{2,1,0:T(8,128)(2,1)S(1)}, u32[]{:S(2)}, u32[]{:S(2)}) async-start(bf16[32,24,2048]{2,1,0:T(8,128)(2,1)} %pad_maximum_fusion.1), calls=%async_computation.1 | async-start | bytes 6291456 | tf_op jit(solution)/shard_map/all_to_all | solution.py:194
  161.1 19.4 %collective-permute-start.11 = (bf16[192,2048]{1,0:T(8,128)(2,1)}, bf16[192,2048]{1,0:T(8,128)(2,1)}, u32[]{:S(2)}, u32[]{:S(2)}) collective-permute-start(bf16[192,2048]{1,0:T(8,128)(2,1)} %get-tuple-element.19), channel_id=1, source_target_pairs={{0,2},{2,0},{1,3},{3,1},{4,6},{6,4},{5,7},{7,5},{8,10},{10,8},{9,1... | collective-permute-start | bytes 2359304 | tf_op jit(solution)/shard_map/ppermute | solution.py:21
  161.6 35.8 %collective-permute-start.7 = (bf16[192,2048]{1,0:T(8,128)(2,1)}, bf16[192,2048]{1,0:T(8,128)(2,1)}, u32[]{:S(2)}, u32[]{:S(2)}) collective-permute-start(bf16[192,2048]{1,0:T(8,128)(2,1)} %get-tuple-element.21), channel_id=1, source_target_pairs={{0,2},{2,0},{1,3},{3,1},{4,6},{6,4},{5,7},{7,5},{8,10},{10,8},{9,1... | collective-permute-start | bytes 2359304 | tf_op jit(solution)/shard_map/ppermute | solution.py:21
  162.5 51.7 %collective-permute-start.9 = (bf16[192,2048]{1,0:T(8,128)(2,1)}, bf16[192,2048]{1,0:T(8,128)(2,1)}, u32[]{:S(2)}, u32[]{:S(2)}) collective-permute-start(bf16[192,2048]{1,0:T(8,128)(2,1)} %get-tuple-element.20), channel_id=1, source_target_pairs={{0,2},{2,0},{1,3},{3,1},{4,6},{6,4},{5,7},{7,5},{8,10},{10,8},{9,1... | collective-permute-start | bytes 2359304 | tf_op jit(solution)/shard_map/ppermute | solution.py:21
  214.2 13.7 %copy-start.1 = (bf16[64,768]{0,1:T(8,128)(2,1)S(1)}, bf16[64,768]{0,1:T(8,128)(2,1)}, u32[]{:S(2)}) copy-start(bf16[64,768]{0,1:T(8,128)(2,1)} %reshape.147) | copy-start | bytes 294916
  222.4 20.1 %collective-permute-start.12 = (bf16[192,2048]{1,0:T(8,128)(2,1)}, bf16[192,2048]{1,0:T(8,128)(2,1)}, u32[]{:S(2)}, u32[]{:S(2)}) collective-permute-start(bf16[192,2048]{1,0:T(8,128)(2,1)} %get-tuple-element.18), channel_id=1, source_target_pairs={{0,128},{128,0},{1,129},{129,1},{2,130},{130,2},{3,131},{131,3},{4... | collective-permute-start | bytes 2359304 | tf_op jit(solution)/shard_map/ppermute | solution.py:21
  224.9 34.5 %collective-permute-start.8 = (bf16[192,2048]{1,0:T(8,128)(2,1)}, bf16[192,2048]{1,0:T(8,128)(2,1)}, u32[]{:S(2)}, u32[]{:S(2)}) collective-permute-start(bf16[192,2048]{1,0:T(8,128)(2,1)} %get-tuple-element.16), channel_id=1, source_target_pairs={{0,128},{128,0},{1,129},{129,1},{2,130},{130,2},{3,131},{131,3},{4... | collective-permute-start | bytes 2359304 | tf_op jit(solution)/shard_map/ppermute | solution.py:21
  225.5 50.8 %collective-permute-start.10 = (bf16[192,2048]{1,0:T(8,128)(2,1)}, bf16[192,2048]{1,0:T(8,128)(2,1)}, u32[]{:S(2)}, u32[]{:S(2)}) collective-permute-start(bf16[192,2048]{1,0:T(8,128)(2,1)} %get-tuple-element.17), channel_id=1, source_target_pairs={{0,128},{128,0},{1,129},{129,1},{2,130},{130,2},{3,131},{131,3},{4... | collective-permute-start | bytes 2359304 | tf_op jit(solution)/shard_map/ppermute | solution.py:21
  230.2 51.6 %collective-permute-start.5 = (bf16[64,2048]{1,0:T(8,128)(2,1)S(1)}, bf16[64,2048]{1,0:T(8,128)(2,1)S(1)}, u32[]{:S(2)}, u32[]{:S(2)}) collective-permute-start(bf16[64,2048]{1,0:T(8,128)(2,1)S(1)} %pad_maximum_fusion.4), channel_id=1, source_target_pairs={{0,128},{128,0},{1,129},{129,1},{2,130},{130,2},{3,131},{131,3},{4... | collective-permute-start | bytes 786440 | tf_op jit(solution)/shard_map/ppermute | solution.py:21

commit v2 on v1

v2 whole, which is shorter than its diff:
```python
import jax
import jax.numpy as jnp
from jax import lax
from jax.experimental import pallas as pl
from jax.experimental.pallas import tpu as pltpu
from jax.sharding import Mesh, PartitionSpec as P

BETA_ONE = 0.9
BETA_TWO = 0.95
STEP_RATE = 0.01
ADAM_EPS = 1e-08

F32 = jnp.float32
BF16 = jnp.bfloat16
CAP = 6
RINGS = ("y", "z")
ALL = ("xh", "y", "z", "xl", "core")


def swap(block, axis):
    return lax.ppermute(block, axis, [(0, 1), (1, 0)])


def after(value, *earlier):
    return lax.optimization_barrier((value, *earlier))[0]


def adam_update(weight, moment_one, moment_two, gradient):
    one_new = BETA_ONE * moment_one.astype(F32) + (1.0 - BETA_ONE) * gradient
    two_new = BETA_TWO * moment_two.astype(F32) + (1.0 - BETA_TWO) * gradient * gradient
    return (weight.astype(F32) - STEP_RATE * one_new / (jnp.sqrt(two_new) + ADAM_EPS)).astype(BF16)


def dot_nt(left, right):
    return lax.dot_general(left, right, (((1,), (1,)), ((), ())), preferred_element_type=F32)


def dot_nn(left, right):
    return lax.dot_general(left, right, (((1,), (0,)), ((), ())), preferred_element_type=F32)


def dot_tn(left, right):
    return lax.dot_general(left, right, (((0,), (0,)), ((), ())), preferred_element_type=F32)


CHUNK = 256
LANES = 512
GROUP = 16
VMEM_LIMIT = 56 * 1024 * 1024


def mixed_order(size):
    to = lax.broadcasted_iota(jnp.int32, (size, size), 0)
    at = lax.broadcasted_iota(jnp.int32, (size, size), 1)
    part = to // (size // 2)
    row = to - part * (size // 2)
    return (at == (row // 4) * 8 + part * 4 + row % 4).astype(BF16)


def rows_kernel(rows_ref, w_own, w_xl, w_pair, back_ref, xd_out, act_out, g_pair,
                w_all, xd, mixed, acts, g_all, w_sem, xd_sem, act_sem, g_sem):
    share = w_own.shape[1]
    width = 4 * share
    rows = xd.shape[1]
    pairs = rows_ref.shape[0] // (3 * GROUP)
    plain = pairs * GROUP
    sources = (w_pair.at[0], w_pair.at[1], w_own, w_xl)
    loads = [
        pltpu.make_async_copy(src, w_all.at[:, pl.ds(i * share, share)], w_sem.at[i])
        for i, src in enumerate(sources)
    ]
    for load in loads:
        load.start()

    upper = lax.broadcasted_iota(jnp.int32, (GROUP, rows_ref.shape[1]), 0) < GROUP // 2

    def part(p, carry):
        base = pl.multiple_of(p * 3 * GROUP, GROUP)
        first = rows_ref[pl.ds(base, GROUP), :]
        last = rows_ref[pl.ds(base + 2 * GROUP, GROUP), :]
        to = pl.ds(pl.multiple_of(p * GROUP, GROUP), GROUP)
        xd[0, to, :] = jnp.where(upper, first, last)
        xd[1, to, :] = rows_ref[pl.ds(base + GROUP, GROUP), :]
        mixed[to, :] = jnp.where(upper, last, first)
        return carry

    lax.fori_loop(0, pairs, part, 0)
    order = mixed_order(plain)
    for n in range(0, rows_ref.shape[1], LANES):
        sorted_rows = dot_nn(order, mixed[:, n:n + LANES]).astype(BF16)
        xd[0, plain:, n:n + LANES] = sorted_rows[:plain // 2]
        xd[1, plain:, n:n + LANES] = sorted_rows[plain // 2:]
    xd_store = pltpu.make_async_copy(xd, xd_out, xd_sem)
    xd_store.start()

    done = 0
    for f in range(0, width, CHUNK):
        while done * share < f + CHUNK:
            loads[done].wait()
            done += 1
        a = dot_nt(xd[0], w_all[0, f:f + CHUNK, :])
        u = dot_nt(xd[0], w_all[1, f:f + CHUNK, :])
        s = 1.0 / (1.0 + jnp.exp(-a))
        dh = dot_nt(xd[1], w_all[2, f:f + CHUNK, :])
        acts[2, :, f:f + CHUNK] = (a * s * u).astype(BF16)
        acts[0, :, f:f + CHUNK] = (dh * u * s * (1.0 + a * (1.0 - s))).astype(BF16)
        acts[1, :, f:f + CHUNK] = (dh * a * s).astype(BF16)
    act_store = pltpu.make_async_copy(acts.at[:, :, pl.ds(2 * share, 2 * share)], act_out, act_sem)
    act_store.start()

    stores = [
        pltpu.make_async_copy(g_all.at[:, pl.ds(i * share, share)], g_pair.at[i], g_sem.at[i])
        for i in range(2)
    ]
    for i, side in enumerate((0, 0, 1)):
        for n in range(0, rows_ref.shape[1], LANES):
            g_all[i, :, n:n + LANES] = dot_tn(
                acts[i, :, :2 * share], xd[side, :, n:n + LANES]
            ).astype(BF16)
    for store in stores:
        store.start()

    cut = lax.broadcasted_iota(jnp.int32, (GROUP, LANES), 0) < GROUP // 2
    for n in range(0, rows_ref.shape[1], LANES):
        o = dot_nn(acts[2], w_all[2, :, n:n + LANES]).astype(BF16)
        dx = (
            dot_nn(acts[0], w_all[0, :, n:n + LANES]) + dot_nn(acts[1], w_all[1, :, n:n + LANES])
        ).astype(BF16)
        blend = dot_tn(order, jnp.concatenate([o[plain:], dx[plain:]])).astype(BF16)
        for p in range(pairs):
            o_part = o[p * GROUP:(p + 1) * GROUP]
            m_part = blend[p * GROUP:(p + 1) * GROUP]
            base = p * 3 * GROUP
            back_ref[base:base + GROUP, n:n + LANES] = jnp.where(cut, o_part, m_part)
            back_ref[base + GROUP:base + 2 * GROUP, n:n + LANES] = dx[p * GROUP:(p + 1) * GROUP]
            back_ref[base + 2 * GROUP:base + 3 * GROUP, n:n + LANES] = jnp.where(cut, m_part, o_part)
    xd_store.wait()
    act_store.wait()
    for store in stores:
        store.wait()


def rows_step(rows, w_own, w_xl, w_pair):
    total, feature = rows.shape
    half = total // 2
    share = w_own.shape[1]
    any_spec = pl.BlockSpec(memory_space=pl.ANY)
    vmem_spec = pl.BlockSpec(memory_space=pltpu.VMEM)
    return pl.pallas_call(
        rows_kernel,
        out_shape=(
            jax.ShapeDtypeStruct(rows.shape, BF16),
            jax.ShapeDtypeStruct((2, half, feature), BF16),
            jax.ShapeDtypeStruct((3, half, 2 * share), BF16),
            jax.ShapeDtypeStruct(w_pair.shape, BF16),
        ),
        in_specs=[vmem_spec, any_spec, any_spec, any_spec],
        out_specs=(vmem_spec, any_spec, any_spec, any_spec),
        scratch_shapes=[
            pltpu.VMEM((3, 4 * share, feature), BF16),
            pltpu.VMEM((2, half, feature), BF16),
            pltpu.VMEM((total // 3, feature), BF16),
            pltpu.VMEM((3, half, 4 * share), BF16),
            pltpu.VMEM((3, 2 * share, feature), BF16),
            pltpu.SemaphoreType.DMA((4,)),
            pltpu.SemaphoreType.DMA,
            pltpu.SemaphoreType.DMA,
            pltpu.SemaphoreType.DMA((2,)),
        ],
        compiler_params=pltpu.CompilerParams(vmem_limit_bytes=VMEM_LIMIT),
        cost_estimate=pl.CostEstimate(
            flops=15 * half * feature * 4 * share,
            bytes_accessed=2 * (3 * total * feature + 18 * share * feature),
            transcendentals=half * 4 * share,
        ),
    )(rows, w_own, w_xl, w_pair)


def grads_kernel(flag_ref, xd_ref, act_ref, core_ref, *outs):
    share = core_ref.shape[2]
    moved = flag_ref[0] != 0
    for i, side in enumerate((0, 0, 1)):
        g = dot_tn(act_ref[i], xd_ref[side])
        own = g[:share] + core_ref[0, i].astype(F32)
        other = g[share:] + core_ref[1, i].astype(F32)
        if i < 2:
            own, other = jnp.where(moved, other, own), jnp.where(moved, own, other)
        outs[i][...] = own.astype(BF16)
        outs[3 + i][...] = other.astype(BF16)


def grads_step(flag, xd, acts, core):
    _, half, feature = xd.shape
    share = core.shape[2]
    out = jax.ShapeDtypeStruct((share, feature), BF16)
    return pl.pallas_call(
        grads_kernel,
        grid=(feature // LANES,),
        out_shape=(out,) * 6,
        in_specs=[
            pl.BlockSpec(memory_space=pltpu.SMEM),
            pl.BlockSpec((2, half, LANES), lambda n: (0, 0, n)),
            pl.BlockSpec(acts.shape, lambda n: (0, 0, 0)),
            pl.BlockSpec((2, 3, share, LANES), lambda n: (0, 0, 0, n)),
        ],
        out_specs=(pl.BlockSpec((share, LANES), lambda n: (0, n)),) * 6,
        compiler_params=pltpu.CompilerParams(vmem_limit_bytes=VMEM_LIMIT),
        cost_estimate=pl.CostEstimate(
            flops=12 * half * feature * share,
            bytes_accessed=2 * (2 * half * feature + 12 * share * feature),
            transcendentals=0,
        ),
    )(flag, xd, acts, core)


def adam_kernel(flag_ref, keep_ref, recv_ref, *refs):
    moved = flag_ref[0] != 0
    out_ref = refs[-1]
    if len(refs) == 7:
        w, m, v = [
            jnp.where(moved, refs[i + 3][...].astype(F32), refs[i][...].astype(F32)) for i in range(3)
        ]
    else:
        w, m, v = [ref[...].astype(F32) for ref in refs[:3]]
    gradient = keep_ref[...].astype(F32) + recv_ref[...].astype(F32)
    out_ref[...] = adam_update(w, m, v, gradient)


def adam_step(flag, *arrays):
    rows, feature = arrays[0].shape
    block = pl.BlockSpec((rows // 4, feature), lambda n: (n, 0))
    return pl.pallas_call(
        adam_kernel,
        grid=(4,),
        out_shape=jax.ShapeDtypeStruct((rows, feature), BF16),
        in_specs=[pl.BlockSpec(memory_space=pltpu.SMEM)] + [block] * len(arrays),
        out_specs=block,
        compiler_params=pltpu.CompilerParams(vmem_limit_bytes=VMEM_LIMIT),
        cost_estimate=pl.CostEstimate(
            flops=20 * rows * feature,
            bytes_accessed=2 * (len(arrays) + 1) * rows * feature,
            transcendentals=rows * feature,
        ),
    )(flag, *arrays)


def split_three(value):
    high = value.astype(BF16)
    rest = value - high.astype(F32)
    middle = rest.astype(BF16)
    low = (rest - middle.astype(F32)).astype(BF16)
    return high, middle, low


def body(tokens, cotangent, routes, route_weights, matching, gate_up, down, gate_up_m, gate_up_v,
         down_m, down_v):
    half = lax.axis_index("xh")
    rings = lax.axis_size("y") * lax.axis_size("z")
    ring = lax.axis_index("y") * lax.axis_size("z") + lax.axis_index("z")
    self_index = half * rings + ring
    swapped = jnp.sum(jnp.where(jnp.arange(2 * rings) == self_index, matching, 0)) != self_index
    flag = swapped.astype(jnp.int32).reshape(1)
    count, feature = tokens.shape
    slots = 2 * CAP

    top = routes.shape[1]
    named = jnp.concatenate([routes.astype(F32), route_weights], axis=1)
    named_other = swap(named, "xh")
    tokens_other = swap(tokens, "xh")
    cotangent_other = swap(cotangent, "xh")
    source = jnp.concatenate([tokens, cotangent, tokens_other, cotangent_other])

    w_own = jnp.concatenate([gate_up[0], down])
    w_first = after(w_own, tokens_other, cotangent_other, named_other)
    w_xl = swap(w_first, "xl")
    w_pair = swap(jnp.stack([w_own, w_xl]), "core")
    m_first, v_first, _ = lax.optimization_barrier((gate_up_m[0], gate_up_v[0], w_xl))
    m_xl = swap(m_first, "xl")
    v_xl = swap(v_first, "xl")

    both = jnp.stack([named, named_other])
    both_routes = both[:, :, :top].astype(jnp.int32)
    both_weights = both[:, :, top:]
    ring_ids = jnp.arange(rings, dtype=jnp.int32)[:, None, None]
    hit = [both_routes[:, :, k] == half * rings + ring_ids for k in range(top)]
    used = sum(h.astype(jnp.int32) for h in hit)
    scale = sum(jnp.where(h, both_weights[:, :, k], 0.0) for k, h in enumerate(hit))
    before = (jnp.arange(count)[:, None] < jnp.arange(count)[None, :]).astype(BF16)
    earlier = jnp.dot(used.astype(BF16), before, preferred_element_type=F32).astype(jnp.int32)
    slot = earlier + CAP * jnp.arange(2, dtype=jnp.int32)[None, :, None]
    slot = jnp.where(used > 0, slot, -1)

    def on_lanes(value):
        return jnp.concatenate([value[:, 0], value[:, 0], value[:, 1], value[:, 1]], axis=1)[:, None]

    lane_kind = jnp.arange(4 * count, dtype=jnp.int32) // count % 2
    row = jnp.arange(2 * slots, dtype=jnp.int32)
    row = jnp.where(ring % 2 == 0, row, jnp.where(row < 8, row + 16, jnp.where(row < 16, row, row - 16)))
    row_kind = (row >= 12).astype(jnp.int32)
    row_slot = jnp.where(row < 12, row, jnp.where(row < 16, row - 4, row - 16))
    pick = (on_lanes(slot) == row_slot[:, None]) & (lane_kind == row_kind[:, None])
    lane_scale = jnp.where(lane_kind == 0, on_lanes(scale), 1.0)
    row_scale = jnp.sum(jnp.where(pick, on_lanes(scale), 0.0), axis=2)
    factor = jnp.where(row_kind == 0, 1.0, row_scale).reshape(-1, 1)
    pick_b = pick.astype(BF16).reshape(rings * 2 * slots, 4 * count)
    send = (dot_nn(pick_b, source) * factor).astype(BF16).reshape(rings, 2 * slots, feature)

    recv = lax.all_to_all(send, RINGS, split_axis=0, concat_axis=0, tiled=True)
    back_send, xd, acts, g_pair = rows_step(recv.reshape(-1, feature), w_own, w_xl, w_pair)

    g_core = swap(g_pair, "core")
    back = lax.all_to_all(
        back_send.reshape(recv.shape), RINGS, split_axis=0, concat_axis=0, tiled=True
    ).reshape(-1, feature)
    parts = grads_step(flag, xd, acts, g_core)
    new_down = adam_step(flag, parts[2], swap(parts[5], "xl"), w_own[2], down_m[0], down_v[0])
    new_down = jnp.where(swapped, swap(new_down, "xh"), new_down)
    updated = []
    for i in range(2):
        new = adam_step(flag, parts[i], swap(parts[3 + i], "xl"), w_own[i], gate_up_m[0, i],
                        gate_up_v[0, i], w_xl[i], m_xl[i], v_xl[i])
        across = lax.ppermute(new, ("xh", "xl"), [(0, 3), (3, 0), (1, 2), (2, 1)])
        updated.append(jnp.where(swapped, across, new))

    mix = [
        jnp.where(pick, term, 0).reshape(rings * 2 * slots, 4 * count)
        for term in split_three(lane_scale)
    ]
    mixed = dot_tn(jnp.concatenate(mix, axis=1), back).reshape(3, 4 * count, feature)
    mixed = mixed[0] + mixed[1] + mixed[2]
    theirs = mixed[2 * count:].astype(BF16)
    ours = swap(theirs, "xh").astype(F32)
    layer_out = (mixed[:count] + ours[:count]).astype(BF16)
    input_grad = (mixed[count:2 * count] + ours[count:]).astype(BF16)
    return layer_out, input_grad, jnp.stack(updated)[None], new_down[None]


def solution(mesh):
    wide = Mesh(mesh.devices.reshape(2, 4, 8, 2, 2), ALL)
    token_spec = P(ALL, None)
    expert, share = ("xh", "y", "z"), ("xl", "core")
    up_spec = P(expert, None, share, None)
    down_spec = P(expert, share, None)
    return jax.shard_map(
        body,
        mesh=wide,
        in_specs=(token_spec, token_spec, token_spec, token_spec, P(), up_spec, down_spec, up_spec,
                  up_spec, down_spec, down_spec),
        out_specs=(token_spec, token_spec, up_spec, down_spec),
        check_vma=False,
    )
```

time: 283 us -> 302 us (1.067)
  waiting for transfers between devices: 149 us -> 176 us
  other arithmetic: 39.6 us -> 19.5 us
  Pallas kernels: 26.3 us -> 41.3 us
  local copies, waits for them, and re-layouts: 19.6 us -> 16.2 us
    ppermute x0 -> x2, waiting for transfers between devices: none -> 26.4 us  [body(): across = lax.ppermute(new, ('xh', 'xl'), [(0, 3), (3, 0), (1, 2), (2, 1)])]
    pallas_call x1 -> x5, Pallas kernels: 26.3 us -> 41.3 us  [the longest x1 19.3 us: rows_step(): pl.pallas_call(rows_kernel, out_shape=(jax.ShapeDtypeStruct(rows.shape, B...]
    reshape x7 -> x0, local copies, waits for them, and re-layouts: 14.8 us -> none  [the longest x1 3.75 us: body(): rows_x = recv[:, :slots].reshape(rings * slots, feature)]
    squeeze x0 -> x6, local copies, waits for them, and re-layouts: none -> 13.1 us  [the longest x1 3.68 us: body(): gate_up_v[0, i]]
    convert_element_type x5, other arithmetic: 13.8 us -> 1.49 us  [the longest x1 0.78 us: body(): input_grad = (mixed[count:2 * count] + ours[count:]).astype(BF16)]
    ppermute x13, starting transfers between devices: 26.4 us -> 19.9 us  [swap(): return lax.ppermute(block, axis, [(0, 1), (1, 0)])]
    concatenate x4 -> x2, other arithmetic: 6.4 us -> 0.77 us  [the longest x1 0.69 us: body(): named = jnp.concatenate([routes.astype(F32), route_weights], axis=1)]
  transfers between devices with their start and end apart: 15 -> 17, of which waited for: 9 -> 11; matrix products, arithmetic and copies ran while one was open for 22% -> 12% of each run, Pallas kernels for 0% -> 7%
where the time goes in v2:
time: 302 us; the launch traced here: 300 us
  waiting for transfers between devices  176 us (58%)
  Pallas kernels  41.3 us (14%)
  starting transfers between devices  40.9 us (14%)
  other arithmetic  19.5 us (6%)
  local copies, waits for them, and re-layouts  16.2 us (5%)
  matrix products  5.25 us (2%)
    ppermute x13, waiting for transfers between devices, swap(): return lax.ppermute(block, axis, [(0, 1), (1, 0)])  121 us
    all_to_all x1, waiting for transfers between devices, body(): recv = lax.all_to_all(send, RINGS, split_axis=0, concat_axis=0, tiled=True)  27.9 us
    ppermute x2, waiting for transfers between devices, body(): across = lax.ppermute(new, ('xh', 'xl'), [(0, 3), (3, 0), (1, 2), (2, 1)])  26.4 us
    ppermute x13, starting transfers between devices, swap(): return lax.ppermute(block, axis, [(0, 1), (1, 0)])  19.9 us
    pallas_call x1, Pallas kernels, rows_step(): pl.pallas_call(rows_kernel, out_shape=(jax.ShapeDtypeStruct(rows.shape, B...  19.3 us
    pallas_call x3, Pallas kernels, adam_step(): pl.pallas_call(adam_kernel, grid=(4,), out_shape=jax.ShapeDtypeStruct((ro...  14.8 us
    all_to_all x1, starting transfers between devices, body(): recv = lax.all_to_all(send, RINGS, split_axis=0, concat_axis=0, tiled=True)  11.3 us
    another operation x2, other arithmetic, body(): w_pair = swap(jnp.stack([w_own, w_xl]), 'core')  7.67 us
  transfers between devices with their start and end apart: 17, of which 11 were waited for; matrix products, arithmetic and copies ran while one was open for 12% of the time, Pallas kernels for 7%

profile of v2, /device:TPU:1, one launch (start us, length us, event | category | flops | bytes accessed | tf_op | source)
XLA Modules:
  0.0 300.3 jit_solution(15312112728188809014)
XLA Ops:
  1.3 0.7 pad_maximum_fusion.3
  2.0 3.6 %collective-permute-start = (f32[32,16]{0,1:T(8,128)S(1)}, f32[32,16]{0,1:T(8,128)S(1)}, u32[]{:S(2)}, u32[]{:S(2)}) collective-permute-start(f32[32,16]{0,1:T(8,128)S(1)} %get-tuple-element.73), channel_id=1, source_target_pairs={{0,128},{128,0},{1,129},{129,1},{2,130},{130,2},{3,131},{131,3},{4... | collective-permute-start | bytes 6152 | tf_op jit(solution)/shard_map/ppermute | solution.py:21
  5.6 2.9 collective-permute-start.2
  8.7 3.4 %fusion.60 = (bf16[1,3,192,2048]{3,2,1,0:T(8,128)(2,1)S(1)}, bf16[3,192,2048]{2,1,0:T(8,128)(2,1)}) fusion(bf16[1,192,2048]{2,1,0:T(8,128)(2,1)} %param.17, bf16[2,192,2048]{2,1,0:T(8,128)(2,1)} %bitcast.102), kind=kLoop, calls=%fused_computation.154 | loop fusion | flops 1179648 | bytes 7077888 | tf_op jit(solution)/shard_map/stack | solution.py:276
  12.6 1.5 collective-permute-done.2
  15.8 2.7 multiply_convert_fusion
  18.5 11.3 %all-to-all-start = ((bf16[32,24,2048]{2,1,0:T(8,128)(2,1)}), bf16[32,24,2048]{2,1,0:T(8,128)(2,1)}, u32[]{:S(2)}, u32[]{:S(2)}) async-start(bf16[32,24,2048]{2,1,0:T(8,128)(2,1)} %bitcast.28), calls=%async_computation | async-start | bytes 6291456 | tf_op jit(solution)/shard_map/all_to_all | solution.py:308
  29.8 35.5 %collective-permute-done.3.w_xl = bf16[3,192,2048]{2,1,0:T(8,128)(2,1)} collective-permute-done((bf16[3,192,2048]{2,1,0:T(8,128)(2,1)}, bf16[3,192,2048]{2,1,0:T(8,128)(2,1)}, u32[]{:S(2)}, u32[]{:S(2)}) %collective-permute-start.3) | collective-permute-done | bytes 2359328 | tf_op jit(solution)/shard_map/ppermute | solution.py:21
  65.4 4.2 %pad_maximum_fusion = bf16[2,3,192,2048]{3,2,1,0:T(8,128)(2,1)} fusion(bf16[1,3,192,2048]{3,2,1,0:T(8,128)(2,1)} %bitcast.32, bf16[1,3,192,2048]{3,2,1,0:T(8,128)(2,1)S(1)} %get-tuple-element.34), kind=kLoop, calls=%fused_computation.1 | loop fusion | flops 2359296 | bytes 9437184 | tf_op jit(solution)/shard_map/stack | solution.py:276
  69.6 2.8 collective-permute-start.4
  72.4 27.9 %all-to-all-done = bf16[32,24,2048]{2,1,0:T(8,128)(2,1)} async-done(((bf16[32,24,2048]{2,1,0:T(8,128)(2,1)}), bf16[32,24,2048]{2,1,0:T(8,128)(2,1)}, u32[]{:S(2)}, u32[]{:S(2)}) %all-to-all-start) | async-done | bytes 3145760 | tf_op jit(solution)/shard_map/all_to_all | solution.py:308
  100.3 19.3 %shard_map.138 = (bf16[768,2048]{1,0:T(8,128)(2,1)}, bf16[2,384,2048]{2,1,0:T(8,128)(2,1)}, bf16[3,384,384]{2,1,0:T(8,128)(2,1)}, bf16[2,3,192,2048]{3,2,1,0:T(8,128)(2,1)}) custom-call(bf16[768,2048]{1,0:T(8,128)(2,1)} %bitcast.29.rows_ref, bf16[3,192,2048]{2,1,0:T(8,128)(2,1)} %get-tuple-element.17.w_own, ...), custom_call_target="tpu_custom_call" | custom-call | flops 9059696640 | bytes 23592960 | tf_op jit(solution)/shard_map/pallas_call | solution.py:149
  119.5 7.1 %all-to-all-start.1 = ((bf16[32,24,2048]{2,1,0:T(8,128)(2,1)}), bf16[32,24,2048]{2,1,0:T(8,128)(2,1)S(1)}, u32[]{:S(2)}, u32[]{:S(2)}) async-start(bf16[32,24,2048]{2,1,0:T(8,128)(2,1)} %bitcast.105), calls=%async_computation.1 | async-start | bytes 6291456 | tf_op jit(solution)/shard_map/all_to_all | solution.py:312
  126.6 2.2 collective-permute-start.6
  128.8 1.2 collective-permute-start.9
  130.0 3.7 %slice_bitcast_fusion.9 = (bf16[192,2048]{1,0:T(8,128)(2,1)}, bf16[192,2048]{1,0:T(8,128)(2,1)}, bf16[192,2048]{1,0:T(8,128)(2,1)}, bf16[192,2048]{1,0:T(8,128)(2,1)}) fusion(bf16[1,2,192,2048]{3,2,1,0:T(8,128)(2,1)} %param.19, bf16[1,2,192,2048]{3,2,1,0:T(8,128)(2,1)} %param.18), kind=kLoop, calls=%fused_computation.21 | loop fusion | bytes 6291456 | tf_op jit(solution)/shard_map/squeeze | solution.py:321
  134.1 1.2 slice_bitcast_fusion.11
  136.6 1.6 bitcast_select_fusion.2
  138.2 2.8 slice_bitcast_fusion.5
  141.0 7.3 %shard_map.139 = (bf16[192,2048]{1,0:T(8,128)(2,1)}, bf16[192,2048]{1,0:T(8,128)(2,1)}, bf16[192,2048]{1,0:T(8,128)(2,1)}, bf16[192,2048]{1,0:T(8,128)(2,1)}, bf...) custom-call(s32[1]{0:T(128)} %bitcast.35.flag_ref, bf16[2,384,2048]{2,1,0:T(8,128)(2,1)} %get-tuple-element.19.xd_ref, ...), custom_call_target="tpu_custom_call" | custom-call | flops 1811939328 | bytes 12582912 | tf_op jit(solution)/shard_map/pallas_call | solution.py:196
  148.3 1.1 collective-permute-start.13
  149.8 1.0 collective-permute-start.11
  150.8 14.3 %collective-permute-done.9 = bf16[2,192,2048]{2,1,0:T(8,128)(2,1)} collective-permute-done((bf16[2,192,2048]{2,1,0:T(8,128)(2,1)}, bf16[2,192,2048]{2,1,0:T(8,128)(2,1)}, u32[]{:S(2)}, u32[]{:S(2)}) %collective-permute-start.9) | collective-permute-done | bytes 1572896 | tf_op jit(solution)/shard_map/ppermute | solution.py:21
  165.1 2.7 slice_bitcast_fusion.3
  167.8 31.0 %collective-permute-done.8 = bf16[2,192,2048]{2,1,0:T(8,128)(2,1)} collective-permute-done((bf16[2,192,2048]{2,1,0:T(8,128)(2,1)}, bf16[2,192,2048]{2,1,0:T(8,128)(2,1)}, u32[]{:S(2)}, u32[]{:S(2)}) %collective-permute-start.8) | collective-permute-done | bytes 1572896 | tf_op jit(solution)/shard_map/ppermute | solution.py:21
  198.8 2.7 slice_bitcast_fusion.4
  201.5 14.1 %collective-permute-done.13.recv_ref = bf16[192,2048]{1,0:T(8,128)(2,1)S(1)} collective-permute-done((bf16[192,2048]{1,0:T(8,128)(2,1)}, bf16[192,2048]{1,0:T(8,128)(2,1)S(1)}, u32[]{:S(2)}, u32[]{:S(2)}) %collective-permute-start.13) | collective-permute-done | bytes 786464 | tf_op jit(solution)/shard_map/ppermute | solution.py:21
  215.5 1.0 copy-done.6
  216.5 4.6 %shard_map.142 = bf16[192,2048]{1,0:T(8,128)(2,1)} custom-call(s32[1]{0:T(128)} %bitcast.35.flag_ref, bf16[192,2048]{1,0:T(8,128)(2,1)} %get-tuple-element.28.keep_ref, bf16[192,2048]{1,0:T(8,128)(2,1)} %copy-done.6, bf16[192,2048]{1,0:T(8,128)(2,1)} %bitcast.103, bf16[192,2048]{1,0:T(8,128)(2,1)} %bitcast.107, bf16[192,2048]{1,0:T(8,128)(2,1)} %bitcast.108), custom_call_target="tpu_custom_call" | custom-call | flops 7864320 | bytes 4718592 | tf_op jit(solution)/shard_map/pallas_call | solution.py:232
  221.1 2.2 collective-permute-start.14
  223.3 9.1 %collective-permute-done.7.recv_ref = bf16[192,2048]{1,0:T(8,128)(2,1)S(1)} collective-permute-done((bf16[192,2048]{1,0:T(8,128)(2,1)}, bf16[192,2048]{1,0:T(8,128)(2,1)S(1)}, u32[]{:S(2)}, u32[]{:S(2)}) %collective-permute-start.7) | collective-permute-done | bytes 786464 | tf_op jit(solution)/shard_map/ppermute | solution.py:21
  232.4 1.0 copy-done.5
  233.4 5.1 %shard_map.140 = bf16[192,2048]{1,0:T(8,128)(2,1)} custom-call(s32[1]{0:T(128)} %bitcast.35.flag_ref, bf16[192,2048]{1,0:T(8,128)(2,1)} %get-tuple-element.22.keep_ref, bf16[192,2048]{1,0:T(8,128)(2,1)} %copy-done.5, bf16[192,2048]{1,0:T(8,128)(2,1)} %get-tuple-element.44.refs_0_, bf16[192,2048]{1,0:T(8,128)(2,1)} %get-tuple-element.78.refs_1_, ...), custom_call_target="tpu_custom_call" | custom-call | flops 7864320 | bytes 7077888 | tf_op jit(solution)/shard_map/pallas_call | solution.py:232
  238.5 1.3 collective-permute-start.10
  239.8 9.6 %collective-permute-done.11.recv_ref = bf16[192,2048]{1,0:T(8,128)(2,1)S(1)} collective-permute-done((bf16[192,2048]{1,0:T(8,128)(2,1)}, bf16[192,2048]{1,0:T(8,128)(2,1)S(1)}, u32[]{:S(2)}, u32[]{:S(2)}) %collective-permute-start.11) | collective-permute-done | bytes 786464 | tf_op jit(solution)/shard_map/ppermute | solution.py:21
  249.4 0.9 copy-done.4
  250.2 5.1 %shard_map.141 = bf16[192,2048]{1,0:T(8,128)(2,1)} custom-call(s32[1]{0:T(128)} %bitcast.35.flag_ref, bf16[192,2048]{1,0:T(8,128)(2,1)} %get-tuple-element.26.keep_ref, bf16[192,2048]{1,0:T(8,128)(2,1)} %copy-done.4, bf16[192,2048]{1,0:T(8,128)(2,1)} %get-tuple-element.45.refs_0_, bf16[192,2048]{1,0:T(8,128)(2,1)} %get-tuple-element.77.refs_1_, ...), custom_call_target="tpu_custom_call" | custom-call | flops 7864320 | bytes 7077888 | tf_op jit(solution)/shard_map/pallas_call | solution.py:232
  255.4 1.3 collective-permute-start.12
  256.7 2.4 fusion.2
  259.3 1.7 collective-permute-start.5
  261.0 6.3 %collective-permute-done.14 = bf16[192,2048]{1,0:T(8,128)(2,1)} collective-permute-done((bf16[192,2048]{1,0:T(8,128)(2,1)}, bf16[192,2048]{1,0:T(8,128)(2,1)}, u32[]{:S(2)}, u32[]{:S(2)}) %collective-permute-start.14) | collective-permute-done | bytes 786464 | tf_op jit(solution)/shard_map/ppermute | solution.py:21
  267.3 2.1 select_bitcast_fusion
  269.4 10.8 %collective-permute-done.10 = bf16[192,2048]{1,0:T(8,128)(2,1)} collective-permute-done((bf16[192,2048]{1,0:T(8,128)(2,1)}, bf16[192,2048]{1,0:T(8,128)(2,1)}, u32[]{:S(2)}, u32[]{:S(2)}) %collective-permute-start.10) | collective-permute-done | bytes 786464 | tf_op jit(solution)/shard_map/ppermute | solution.py:322
  280.2 1.2 select_bitcast_fusion.2
  281.4 15.6 %collective-permute-done.12 = bf16[192,2048]{1,0:T(8,128)(2,1)} collective-permute-done((bf16[192,2048]{1,0:T(8,128)(2,1)}, bf16[192,2048]{1,0:T(8,128)(2,1)}, u32[]{:S(2)}, u32[]{:S(2)}) %collective-permute-start.12) | collective-permute-done | bytes 786464 | tf_op jit(solution)/shard_map/ppermute | solution.py:322
  297.0 1.2 select_bitcast_fusion.1
  298.2 1.3 maximum_bitcast_fusion
  299.6 0.8 fusion.16
  (59 shorter events, 4.7 us)
Async XLA Ops:
  2.0 10.2 %collective-permute-start = (f32[32,16]{0,1:T(8,128)S(1)}, f32[32,16]{0,1:T(8,128)S(1)}, u32[]{:S(2)}, u32[]{:S(2)}) collective-permute-start(f32[32,16]{0,1:T(8,128)S(1)} %get-tuple-element.73), channel_id=1, source_target_pairs={{0,128},{128,0},{1,129},{129,1},{2,130},{130,2},{3,131},{131,3},{4... | collective-permute-start | bytes 6152 | tf_op jit(solution)/shard_map/ppermute | solution.py:21
  5.6 7.0 %collective-permute-start.1 = (bf16[32,2048]{1,0:T(8,128)(2,1)}, bf16[32,2048]{1,0:T(8,128)(2,1)S(1)}, u32[]{:S(2)}, u32[]{:S(2)}) collective-permute-start(bf16[32,2048]{1,0:T(8,128)(2,1)} %param.11), channel_id=1, source_target_pairs={{0,128},{128,0},{1,129},{129,1},{2,130},{130,2},{3,131},{131,3},{4... | collective-permute-start | bytes 393224 | tf_op jit(solution)/shard_map/ppermute | solution.py:21
  5.6 8.5 %collective-permute-start.2 = (bf16[32,2048]{1,0:T(8,128)(2,1)}, bf16[32,2048]{1,0:T(8,128)(2,1)S(1)}, u32[]{:S(2)}, u32[]{:S(2)}) collective-permute-start(bf16[32,2048]{1,0:T(8,128)(2,1)} %param.12), channel_id=1, source_target_pairs={{0,128},{128,0},{1,129},{129,1},{2,130},{130,2},{3,131},{131,3},{4... | collective-permute-start | bytes 393224 | tf_op jit(solution)/shard_map/ppermute | solution.py:21
  8.7 6.9 %copy-start.9 = (pred[24,128]{1,0:T(8,128)(4,1)}, pred[24,128]{1,0:T(8,128)(4,1)S(1)}, u32[]{:S(2)}) copy-start(pred[24,128]{1,0:T(8,128)(4,1)S(1)} %broadcast_compare_fusion) | copy-start | bytes 9220
  8.7 7.1 %copy-start.7 = (bf16[32,2048]{1,0:T(8,128)(2,1)S(1)}, bf16[32,2048]{1,0:T(8,128)(2,1)}, u32[]{:S(2)}) copy-start(bf16[32,2048]{1,0:T(8,128)(2,1)} %param.12) | copy-start | bytes 393220
  8.7 7.1 %copy-start.8 = (bf16[32,2048]{1,0:T(8,128)(2,1)S(1)}, bf16[32,2048]{1,0:T(8,128)(2,1)}, u32[]{:S(2)}) copy-start(bf16[32,2048]{1,0:T(8,128)(2,1)} %param.11) | copy-start | bytes 393220
  12.2 6.3 %copy-start.10 = (s32[768]{0:T(1024)}, s32[768]{0:T(1024)S(1)}, u32[]{:S(2)}) copy-start(s32[768]{0:T(1024)S(1)} %eq.199) | copy-start | bytes 9220
  14.2 51.2 %collective-permute-start.3 = (bf16[3,192,2048]{2,1,0:T(8,128)(2,1)}, bf16[3,192,2048]{2,1,0:T(8,128)(2,1)}, u32[]{:S(2)}, u32[]{:S(2)}) collective-permute-start(bf16[3,192,2048]{2,1,0:T(8,128)(2,1)} %get-tuple-element.17.w_own), channel_id=1, source_target_pairs={{0,2},{2,0},{1,3},{3,1},{4,6},{6,4},{5,7},{7,5},{8,10},{10,8},{9,1... | collective-permute-start | bytes 7077896 | tf_op jit(solution)/shard_map/ppermute | solution.py:21
  18.5 81.8 %all-to-all-start = ((bf16[32,24,2048]{2,1,0:T(8,128)(2,1)}), bf16[32,24,2048]{2,1,0:T(8,128)(2,1)}, u32[]{:S(2)}, u32[]{:S(2)}) async-start(bf16[32,24,2048]{2,1,0:T(8,128)(2,1)} %bitcast.28), calls=%async_computation | async-start | bytes 6291456 | tf_op jit(solution)/shard_map/all_to_all | solution.py:308
  69.6 30.7 %collective-permute-start.4 = (bf16[2,3,192,2048]{3,2,1,0:T(8,128)(2,1)}, bf16[2,3,192,2048]{3,2,1,0:T(8,128)(2,1)}, u32[]{:S(2)}, u32[]{:S(2)}) collective-permute-start(bf16[2,3,192,2048]{3,2,1,0:T(8,128)(2,1)} %pad_maximum_fusion), channel_id=1, source_target_pairs={{0,1},{1,0},{2,3},{3,2},{4,5},{5,4},{6,7},{7,6},{8,9},{9,8},{10,11... | collective-permute-start | bytes 14155784 | tf_op jit(solution)/shard_map/ppermute | solution.py:21
  119.5 137.1 %all-to-all-start.1 = ((bf16[32,24,2048]{2,1,0:T(8,128)(2,1)}), bf16[32,24,2048]{2,1,0:T(8,128)(2,1)S(1)}, u32[]{:S(2)}, u32[]{:S(2)}) async-start(bf16[32,24,2048]{2,1,0:T(8,128)(2,1)} %bitcast.105), calls=%async_computation.1 | async-start | bytes 6291456 | tf_op jit(solution)/shard_map/all_to_all | solution.py:312
  126.6 14.4 %collective-permute-start.6 = (bf16[2,3,192,2048]{3,2,1,0:T(8,128)(2,1)}, bf16[2,3,192,2048]{3,2,1,0:T(8,128)(2,1)}, u32[]{:S(2)}, u32[]{:S(2)}) collective-permute-start(bf16[2,3,192,2048]{3,2,1,0:T(8,128)(2,1)} %get-tuple-element.21), channel_id=1, source_target_pairs={{0,1},{1,0},{2,3},{3,2},{4,5},{5,4},{6,7},{7,6},{8,9},{9,8},{10,11... | collective-permute-start | bytes 14155784 | tf_op jit(solution)/shard_map/ppermute | solution.py:21
  128.8 5.3 %copy-start = (bf16[1,2,192,2048]{3,2,1,0:T(8,128)(2,1)S(1)}, bf16[1,2,192,2048]{3,2,1,0:T(8,128)(2,1)}, u32[]{:S(2)}) copy-start(bf16[1,2,192,2048]{3,2,1,0:T(8,128)(2,1)} %param.16) | copy-start | bytes 4718596
  128.8 36.3 %collective-permute-start.9 = (bf16[2,192,2048]{2,1,0:T(8,128)(2,1)}, bf16[2,192,2048]{2,1,0:T(8,128)(2,1)}, u32[]{:S(2)}, u32[]{:S(2)}) collective-permute-start(bf16[2,192,2048]{2,1,0:T(8,128)(2,1)} %bitcast.106), channel_id=1, source_target_pairs={{0,2},{2,0},{1,3},{3,1},{4,6},{6,4},{5,7},{7,5},{8,10},{10,8},{9,1... | collective-permute-start | bytes 4718600 | tf_op jit(solution)/shard_map/ppermute | solution.py:21
  133.7 1.7 copy-start.11
  133.7 65.1 %collective-permute-start.8 = (bf16[2,192,2048]{2,1,0:T(8,128)(2,1)}, bf16[2,192,2048]{2,1,0:T(8,128)(2,1)}, u32[]{:S(2)}, u32[]{:S(2)}) collective-permute-start(bf16[2,192,2048]{2,1,0:T(8,128)(2,1)} %bitcast.40), channel_id=1, source_target_pairs={{0,2},{2,0},{1,3},{3,1},{4,6},{6,4},{5,7},{7,5},{8,10},{10,8},{9,1... | collective-permute-start | bytes 4718600 | tf_op jit(solution)/shard_map/ppermute | solution.py:21
  148.3 67.2 %collective-permute-start.13 = (bf16[192,2048]{1,0:T(8,128)(2,1)}, bf16[192,2048]{1,0:T(8,128)(2,1)S(1)}, u32[]{:S(2)}, u32[]{:S(2)}) collective-permute-start(bf16[192,2048]{1,0:T(8,128)(2,1)} %get-tuple-element.29), channel_id=1, source_target_pairs={{0,2},{2,0},{1,3},{3,1},{4,6},{6,4},{5,7},{7,5},{8,10},{10,8},{9,1... | collective-permute-start | bytes 2359304 | tf_op jit(solution)/shard_map/ppermute | solution.py:21
  149.4 83.0 %collective-permute-start.7 = (bf16[192,2048]{1,0:T(8,128)(2,1)}, bf16[192,2048]{1,0:T(8,128)(2,1)S(1)}, u32[]{:S(2)}, u32[]{:S(2)}) collective-permute-start(bf16[192,2048]{1,0:T(8,128)(2,1)} %get-tuple-element.23), channel_id=1, source_target_pairs={{0,2},{2,0},{1,3},{3,1},{4,6},{6,4},{5,7},{7,5},{8,10},{10,8},{9,1... | collective-permute-start | bytes 2359304 | tf_op jit(solution)/shard_map/ppermute | solution.py:21
  149.8 99.5 %collective-permute-start.11 = (bf16[192,2048]{1,0:T(8,128)(2,1)}, bf16[192,2048]{1,0:T(8,128)(2,1)S(1)}, u32[]{:S(2)}, u32[]{:S(2)}) collective-permute-start(bf16[192,2048]{1,0:T(8,128)(2,1)} %get-tuple-element.27), channel_id=1, source_target_pairs={{0,2},{2,0},{1,3},{3,1},{4,6},{6,4},{5,7},{7,5},{8,10},{10,8},{9,1... | collective-permute-start | bytes 2359304 | tf_op jit(solution)/shard_map/ppermute | solution.py:21
  215.5 1.0 copy-start.6
  221.1 46.2 %collective-permute-start.14 = (bf16[192,2048]{1,0:T(8,128)(2,1)}, bf16[192,2048]{1,0:T(8,128)(2,1)}, u32[]{:S(2)}, u32[]{:S(2)}) collective-permute-start(bf16[192,2048]{1,0:T(8,128)(2,1)} %shard_map.142), channel_id=1, source_target_pairs={{0,128},{128,0},{1,129},{129,1},{2,130},{130,2},{3,131},{131,3},{4... | collective-permute-start | bytes 2359304 | tf_op jit(solution)/shard_map/ppermute | solution.py:21
  232.4 1.0 copy-start.5
  238.5 41.7 %collective-permute-start.10 = (bf16[192,2048]{1,0:T(8,128)(2,1)}, bf16[192,2048]{1,0:T(8,128)(2,1)}, u32[]{:S(2)}, u32[]{:S(2)}) collective-permute-start(bf16[192,2048]{1,0:T(8,128)(2,1)} %shard_map.140), channel_id=1, source_target_pairs={{0,130},{130,0},{2,128},{128,2},{1,131},{131,1},{3,129},{129,3},{4... | collective-permute-start | bytes 2359304 | tf_op jit(solution)/shard_map/ppermute | solution.py:322
  249.4 0.9 copy-start.4
  255.4 41.6 %collective-permute-start.12 = (bf16[192,2048]{1,0:T(8,128)(2,1)}, bf16[192,2048]{1,0:T(8,128)(2,1)}, u32[]{:S(2)}, u32[]{:S(2)}) collective-permute-start(bf16[192,2048]{1,0:T(8,128)(2,1)} %shard_map.141), channel_id=1, source_target_pairs={{0,130},{130,0},{2,128},{128,2},{1,131},{131,1},{3,129},{129,3},{4... | collective-permute-start | bytes 2359304 | tf_op jit(solution)/shard_map/ppermute | solution.py:322
  259.0 8.2 %copy-start.1 = (bf16[192,2048]{1,0:T(8,128)(2,1)S(1)}, bf16[192,2048]{1,0:T(8,128)(2,1)}, u32[]{:S(2)}) copy-start(bf16[192,2048]{1,0:T(8,128)(2,1)} %shard_map.142) | copy-start | bytes 2359300
  259.2 20.9 %copy-start.2 = (bf16[192,2048]{1,0:T(8,128)(2,1)S(1)}, bf16[192,2048]{1,0:T(8,128)(2,1)}, u32[]{:S(2)}) copy-start(bf16[192,2048]{1,0:T(8,128)(2,1)} %shard_map.140) | copy-start | bytes 2359300
  259.3 37.7 %copy-start.3 = (bf16[192,2048]{1,0:T(8,128)(2,1)S(1)}, bf16[192,2048]{1,0:T(8,128)(2,1)}, u32[]{:S(2)}) copy-start(bf16[192,2048]{1,0:T(8,128)(2,1)} %shard_map.141) | copy-start | bytes 2359300
  259.3 40.2 %collective-permute-start.5 = (bf16[64,2048]{1,0:T(8,128)(2,1)S(1)}, bf16[64,2048]{1,0:T(8,128)(2,1)S(1)}, u32[]{:S(2)}, u32[]{:S(2)}) collective-permute-start(bf16[64,2048]{1,0:T(8,128)(2,1)S(1)} %slice.309), channel_id=1, source_target_pairs={{0,128},{128,0},{1,129},{129,1},{2,130},{130,2},{3,131},{131,3},{4... | collective-permute-start | bytes 786440 | tf_op jit(solution)/shard_map/ppermute | solution.py:21

commit v3 on v2

--- a/solution.py
+++ b/solution.py
@@ -57,7 +57,7 @@
     return (at == (row // 4) * 8 + part * 4 + row % 4).astype(BF16)
 
 
-def rows_kernel(rows_ref, w_own, w_xl, w_pair, back_ref, xd_out, act_out, g_pair,
+def rows_kernel(rows_ref, w_own, w_xl, w_pair, back_ref, xd_out, act_out, g_gate, g_up, g_down,
                 w_all, xd, mixed, acts, g_all, w_sem, xd_sem, act_sem, g_sem):
     share = w_own.shape[1]
     width = 4 * share
@@ -108,17 +108,14 @@
     act_store = pltpu.make_async_copy(acts.at[:, :, pl.ds(2 * share, 2 * share)], act_out, act_sem)
     act_store.start()
 
-    stores = [
-        pltpu.make_async_copy(g_all.at[:, pl.ds(i * share, share)], g_pair.at[i], g_sem.at[i])
-        for i in range(2)
-    ]
-    for i, side in enumerate((0, 0, 1)):
+    stores = []
+    for i, (side, target) in enumerate(zip((0, 0, 1), (g_gate, g_up, g_down))):
         for n in range(0, rows_ref.shape[1], LANES):
             g_all[i, :, n:n + LANES] = dot_tn(
                 acts[i, :, :2 * share], xd[side, :, n:n + LANES]
             ).astype(BF16)
-    for store in stores:
-        store.start()
+        stores.append(pltpu.make_async_copy(g_all.at[i], target, g_sem.at[i]))
+        stores[i].start()
 
     cut = lax.broadcasted_iota(jnp.int32, (GROUP, LANES), 0) < GROUP // 2
     for n in range(0, rows_ref.shape[1], LANES):
@@ -152,10 +149,9 @@
             jax.ShapeDtypeStruct(rows.shape, BF16),
             jax.ShapeDtypeStruct((2, half, feature), BF16),
             jax.ShapeDtypeStruct((3, half, 2 * share), BF16),
-            jax.ShapeDtypeStruct(w_pair.shape, BF16),
-        ),
+        ) + (jax.ShapeDtypeStruct((2 * share, feature), BF16),) * 3,
         in_specs=[vmem_spec, any_spec, any_spec, any_spec],
-        out_specs=(vmem_spec, any_spec, any_spec, any_spec),
+        out_specs=(vmem_spec,) + (any_spec,) * 5,
         scratch_shapes=[
             pltpu.VMEM((3, 4 * share, feature), BF16),
             pltpu.VMEM((2, half, feature), BF16),
@@ -165,33 +161,33 @@
             pltpu.SemaphoreType.DMA((4,)),
             pltpu.SemaphoreType.DMA,
             pltpu.SemaphoreType.DMA,
-            pltpu.SemaphoreType.DMA((2,)),
+            pltpu.SemaphoreType.DMA((3,)),
         ],
         compiler_params=pltpu.CompilerParams(vmem_limit_bytes=VMEM_LIMIT),
         cost_estimate=pl.CostEstimate(
-            flops=15 * half * feature * 4 * share,
-            bytes_accessed=2 * (3 * total * feature + 18 * share * feature),
-            transcendentals=half * 4 * share,
+            flops=half * feature * share,
+            bytes_accessed=half * feature,
+            transcendentals=0,
         ),
     )(rows, w_own, w_xl, w_pair)
 
 
-def grads_kernel(flag_ref, xd_ref, act_ref, core_ref, *outs):
-    share = core_ref.shape[2]
+def grads_kernel(flag_ref, xd_ref, act_ref, core_gate, core_up, core_down, _mv_ref, *outs):
+    share = core_gate.shape[0] // 2
     moved = flag_ref[0] != 0
-    for i, side in enumerate((0, 0, 1)):
-        g = dot_tn(act_ref[i], xd_ref[side])
-        own = g[:share] + core_ref[0, i].astype(F32)
-        other = g[share:] + core_ref[1, i].astype(F32)
+    for i, (side, core_ref) in enumerate(zip((0, 0, 1), (core_gate, core_up, core_down))):
+        g = dot_tn(act_ref[i], xd_ref[side]) + core_ref[...].astype(F32)
+        own = g[:share]
+        other = g[share:]
         if i < 2:
             own, other = jnp.where(moved, other, own), jnp.where(moved, own, other)
         outs[i][...] = own.astype(BF16)
         outs[3 + i][...] = other.astype(BF16)
 
 
-def grads_step(flag, xd, acts, core):
+def grads_step(flag, xd, acts, core, mv_xl):
     _, half, feature = xd.shape
-    share = core.shape[2]
+    share = core[0].shape[0] // 2
     out = jax.ShapeDtypeStruct((share, feature), BF16)
     return pl.pallas_call(
         grads_kernel,
@@ -201,7 +197,8 @@
             pl.BlockSpec(memory_space=pltpu.SMEM),
             pl.BlockSpec((2, half, LANES), lambda n: (0, 0, n)),
             pl.BlockSpec(acts.shape, lambda n: (0, 0, 0)),
-            pl.BlockSpec((2, 3, share, LANES), lambda n: (0, 0, 0, n)),
+            *[pl.BlockSpec((2 * share, LANES), lambda n: (0, n))] * 3,
+            pl.BlockSpec(memory_space=pl.ANY),
         ],
         out_specs=(pl.BlockSpec((share, LANES), lambda n: (0, n)),) * 6,
         compiler_params=pltpu.CompilerParams(vmem_limit_bytes=VMEM_LIMIT),
@@ -210,7 +207,7 @@
             bytes_accessed=2 * (2 * half * feature + 12 * share * feature),
             transcendentals=0,
         ),
-    )(flag, xd, acts, core)
+    )(flag, xd, acts, *core, mv_xl)
 
 
 def adam_kernel(flag_ref, keep_ref, recv_ref, *refs):
@@ -227,21 +224,25 @@
 
 
 def adam_step(flag, *arrays):
-    rows, feature = arrays[0].shape
-    block = pl.BlockSpec((rows // 4, feature), lambda n: (n, 0))
+    rows, feature = arrays[0][0].shape[-2:]
+    steps = 4
+
+    def spec(lead):
+        return pl.BlockSpec((None,) * len(lead) + (rows // steps, feature), lambda n: (*lead, n, 0))
+
     return pl.pallas_call(
         adam_kernel,
-        grid=(4,),
+        grid=(steps,),
         out_shape=jax.ShapeDtypeStruct((rows, feature), BF16),
-        in_specs=[pl.BlockSpec(memory_space=pltpu.SMEM)] + [block] * len(arrays),
-        out_specs=block,
+        in_specs=[pl.BlockSpec(memory_space=pltpu.SMEM)] + [spec(lead) for _, lead in arrays],
+        out_specs=spec(()),
         compiler_params=pltpu.CompilerParams(vmem_limit_bytes=VMEM_LIMIT),
         cost_estimate=pl.CostEstimate(
             flops=20 * rows * feature,
             bytes_accessed=2 * (len(arrays) + 1) * rows * feature,
             transcendentals=rows * feature,
         ),
-    )(flag, *arrays)
+    )(flag, *[array for array, _ in arrays])
 
 
 def split_three(value):
@@ -274,9 +275,7 @@
     w_first = after(w_own, tokens_other, cotangent_other, named_other)
     w_xl = swap(w_first, "xl")
     w_pair = swap(jnp.stack([w_own, w_xl]), "core")
-    m_first, v_first, _ = lax.optimization_barrier((gate_up_m[0], gate_up_v[0], w_xl))
-    m_xl = swap(m_first, "xl")
-    v_xl = swap(v_first, "xl")
+    mv_xl = swap(after(jnp.concatenate([gate_up_m[0], gate_up_v[0]]), w_xl), "xl")
 
     both = jnp.stack([named, named_other])
     both_routes = both[:, :, :top].astype(jnp.int32)
@@ -306,19 +305,21 @@
     send = (dot_nn(pick_b, source) * factor).astype(BF16).reshape(rings, 2 * slots, feature)
 
     recv = lax.all_to_all(send, RINGS, split_axis=0, concat_axis=0, tiled=True)
-    back_send, xd, acts, g_pair = rows_step(recv.reshape(-1, feature), w_own, w_xl, w_pair)
-
-    g_core = swap(g_pair, "core")
+    back_send, xd, acts, *g_pair = rows_step(recv.reshape(-1, feature), w_own, w_xl, w_pair)
+
+    g_core = [swap(g, "core") for g in g_pair]
     back = lax.all_to_all(
         back_send.reshape(recv.shape), RINGS, split_axis=0, concat_axis=0, tiled=True
     ).reshape(-1, feature)
-    parts = grads_step(flag, xd, acts, g_core)
-    new_down = adam_step(flag, parts[2], swap(parts[5], "xl"), w_own[2], down_m[0], down_v[0])
+    parts = grads_step(flag, xd, acts, g_core, mv_xl)
+    new_down = adam_step(flag, (parts[2], ()), (swap(parts[5], "xl"), ()), (down, (0,)), (down_m, (0,)),
+                         (down_v, (0,)))
     new_down = jnp.where(swapped, swap(new_down, "xh"), new_down)
     updated = []
     for i in range(2):
-        new = adam_step(flag, parts[i], swap(parts[3 + i], "xl"), w_own[i], gate_up_m[0, i],
-                        gate_up_v[0, i], w_xl[i], m_xl[i], v_xl[i])
+        new = adam_step(flag, (parts[i], ()), (swap(parts[3 + i], "xl"), ()), (gate_up, (0, i)),
+                        (gate_up_m, (0, i)), (gate_up_v, (0, i)), (w_xl, (i,)), (mv_xl, (i,)),
+                        (mv_xl, (2 + i,)))
         across = lax.ppermute(new, ("xh", "xl"), [(0, 3), (3, 0), (1, 2), (2, 1)])
         updated.append(jnp.where(swapped, across, new))
 

time: 302 us -> 263 us (0.87)
  waiting for transfers between devices: 176 us -> 150 us
  local copies, waits for them, and re-layouts: 16.2 us -> 4.6 us
  starting transfers between devices: 40.9 us -> 37.6 us
    ppermute x13 -> x14, waiting for transfers between devices: 121 us -> 103 us  [swap(): return lax.ppermute(block, axis, [(0, 1), (1, 0)])]
    squeeze x5 -> x0, local copies, waits for them, and re-layouts: 13.1 us -> none  [the longest x1 3.68 us: body(): gate_up_v[0, i]]
    ppermute x2, waiting for transfers between devices: 26.4 us -> 21.9 us  [body(): across = lax.ppermute(new, ('xh', 'xl'), [(0, 3), (3, 0), (1, 2), (2, 1)])]
    all_to_all x1, waiting for transfers between devices: 27.9 us -> 24.2 us  [body(): recv = lax.all_to_all(send, RINGS, split_axis=0, concat_axis=0, tiled=True)]
    ppermute x13 -> x14, starting transfers between devices: 19.9 us -> 16.5 us  [swap(): return lax.ppermute(block, axis, [(0, 1), (1, 0)])]
  transfers between devices with their start and end apart: 17 -> 18, of which waited for: 11 -> 11; matrix products, arithmetic and copies ran while one was open for 12% -> 7% of each run, Pallas kernels for 7% -> 16%
where the time goes in v3:
time: 263 us; the launch traced here: 259 us
  waiting for transfers between devices  150 us (57%)
  Pallas kernels  41.4 us (16%)
  starting transfers between devices  37.6 us (14%)
  other arithmetic  17.7 us (7%)
  matrix products  6.22 us (2%)
  local copies, waits for them, and re-layouts  4.6 us (2%)
    ppermute x14, waiting for transfers between devices, swap(): return lax.ppermute(block, axis, [(0, 1), (1, 0)])  103 us
    all_to_all x1, waiting for transfers between devices, body(): recv = lax.all_to_all(send, RINGS, split_axis=0, concat_axis=0, tiled=True)  24.2 us
    ppermute x2, waiting for transfers between devices, body(): across = lax.ppermute(new, ('xh', 'xl'), [(0, 3), (3, 0), (1, 2), (2, 1)])  21.9 us
    pallas_call x1, Pallas kernels, rows_step(): pl.pallas_call(rows_kernel, out_shape=(jax.ShapeDtypeStruct(rows.shape, B...  19.2 us
    ppermute x14, starting transfers between devices, swap(): return lax.ppermute(block, axis, [(0, 1), (1, 0)])  16.5 us
    pallas_call x3, Pallas kernels, adam_step(): pl.pallas_call(adam_kernel, grid=(steps,), out_shape=jax.ShapeDtypeStruct...  14.9 us
    all_to_all x1, starting transfers between devices, body(): recv = lax.all_to_all(send, RINGS, split_axis=0, concat_axis=0, tiled=True)  11.3 us
    another operation x2, other arithmetic, body(): w_pair = swap(jnp.stack([w_own, w_xl]), 'core')  9.41 us
  transfers between devices with their start and end apart: 18, of which 11 were waited for; matrix products, arithmetic and copies ran while one was open for 7% of the time, Pallas kernels for 16%

profile of v3, /device:TPU:1, one launch (start us, length us, event | category | flops | bytes accessed | tf_op | source)
XLA Modules:
  0.0 258.7 jit_solution(2419290176002694143)
XLA Ops:
  0.6 0.7 convert_element_type.115
  1.3 0.7 pad_maximum_fusion.4
  2.0 3.6 %collective-permute-start = (f32[32,16]{0,1:T(8,128)S(1)}, f32[32,16]{0,1:T(8,128)S(1)}, u32[]{:S(2)}, u32[]{:S(2)}) collective-permute-start(f32[32,16]{0,1:T(8,128)S(1)} %get-tuple-element.63), channel_id=1, source_target_pairs={{0,128},{128,0},{1,129},{129,1},{2,130},{130,2},{3,131},{131,3},{4... | collective-permute-start | bytes 6152 | tf_op jit(solution)/shard_map/ppermute | solution.py:21
  5.6 2.9 %collective-permute-start.2 = (bf16[32,2048]{1,0:T(8,128)(2,1)}, bf16[32,2048]{1,0:T(8,128)(2,1)S(1)}, u32[]{:S(2)}, u32[]{:S(2)}) collective-permute-start(bf16[32,2048]{1,0:T(8,128)(2,1)} %param.12), channel_id=1, source_target_pairs={{0,128},{128,0},{1,129},{129,1},{2,130},{130,2},{3,131},{131,3},{4... | collective-permute-start | bytes 393224 | tf_op jit(solution)/shard_map/ppermute | solution.py:21
  8.7 4.2 %fusion.60 = (bf16[1,3,192,2048]{3,2,1,0:T(8,128)(2,1)}, bf16[3,192,2048]{2,1,0:T(8,128)(2,1)}) fusion(bf16[1,192,2048]{2,1,0:T(8,128)(2,1)} %refs_0_.5, bf16[2,192,2048]{2,1,0:T(8,128)(2,1)} %bitcast.77), kind=kLoop, calls=%fused_computation.143 | loop fusion | flops 1179648 | bytes 7077888 | tf_op jit(solution)/shard_map/stack | solution.py:277
  13.1 0.2 fusion.1
  13.4 0.7 collective-permute-done.2
  14.2 0.3 collective-permute-start.3
  14.7 0.3 select_reduce_fusion
  15.2 2.7 %multiply_convert_fusion = bf16[768,2048]{1,0:T(8,128)(2,1)} fusion(pred[768,128]{1,0:T(32,128)(4,1)S(1)} %fusion.15, f32[768]{0:T(1024)S(1)} %select_n.199, bf16[32,2048]{1,0:T(8,128)(2,1)S(1)} %collective-permute-done.2, bf16[32,2048]{1,0:T(8,128)(2,1)S(1)} %collective-permute-done.1, bf16[32,2048]{1,0:T(8,128)(2,1)S(1)} %copy-done.10, ...), kind=kOutput, calls=%fused_computation | convolution fusion | flops 407896064 | bytes 3771392 | tf_op jit(solution)/shard_map/dot_general | solution.py:39
  17.9 11.3 %all-to-all-start = ((bf16[32,24,2048]{2,1,0:T(8,128)(2,1)}), bf16[32,24,2048]{2,1,0:T(8,128)(2,1)}, u32[]{:S(2)}, u32[]{:S(2)}) async-start(bf16[32,24,2048]{2,1,0:T(8,128)(2,1)} %bitcast.76), calls=%async_computation | async-start | bytes 6291456 | tf_op jit(solution)/shard_map/all_to_all | solution.py:307
  29.2 36.1 %collective-permute-done.3.w_xl.refs_3_ = bf16[3,192,2048]{2,1,0:T(8,128)(2,1)S(1)} collective-permute-done((bf16[3,192,2048]{2,1,0:T(8,128)(2,1)}, bf16[3,192,2048]{2,1,0:T(8,128)(2,1)S(1)}, u32[]{:S(2)}, u32[]{:S(2)}) %collective-permute-start.3) | collective-permute-done | bytes 2359328 | tf_op jit(solution)/shard_map/ppermute | solution.py:21
  65.4 5.2 %pad_maximum_fusion = bf16[2,3,192,2048]{3,2,1,0:T(8,128)(2,1)} fusion(bf16[1,3,192,2048]{3,2,1,0:T(8,128)(2,1)S(1)} %bitcast.75, bf16[1,3,192,2048]{3,2,1,0:T(8,128)(2,1)} %get-tuple-element.34), kind=kLoop, calls=%fused_computation.1 | loop fusion | flops 2359296 | bytes 9437184 | tf_op jit(solution)/shard_map/stack | solution.py:277
  70.5 2.7 %collective-permute-start.4 = (bf16[2,3,192,2048]{3,2,1,0:T(8,128)(2,1)}, bf16[2,3,192,2048]{3,2,1,0:T(8,128)(2,1)}, u32[]{:S(2)}, u32[]{:S(2)}) collective-permute-start(bf16[2,3,192,2048]{3,2,1,0:T(8,128)(2,1)} %pad_maximum_fusion), channel_id=1, source_target_pairs={{0,1},{1,0},{2,3},{3,2},{4,5},{5,4},{6,7},{7,6},{8,9},{9,8},{10,11... | collective-permute-start | bytes 14155784 | tf_op jit(solution)/shard_map/ppermute | solution.py:21
  73.2 1.9 pad_maximum_fusion.1
  75.1 0.3 collective-permute-start.9
  75.4 24.2 %all-to-all-done = bf16[32,24,2048]{2,1,0:T(8,128)(2,1)} async-done(((bf16[32,24,2048]{2,1,0:T(8,128)(2,1)}), bf16[32,24,2048]{2,1,0:T(8,128)(2,1)}, u32[]{:S(2)}, u32[]{:S(2)}) %all-to-all-start) | async-done | bytes 3145760 | tf_op jit(solution)/shard_map/all_to_all | solution.py:307
  99.7 19.2 %shard_map.138 = (bf16[768,2048]{1,0:T(8,128)(2,1)}, bf16[2,384,2048]{2,1,0:T(8,128)(2,1)}, bf16[3,384,384]{2,1,0:T(8,128)(2,1)}, bf16[384,2048]{1,0:T(8,128)(2,...) custom-call(bf16[768,2048]{1,0:T(8,128)(2,1)} %bitcast.29.rows_ref, ...), custom_call_target="tpu_custom_call" | custom-call | flops 150994944 | bytes 786432 | tf_op jit(solution)/shard_map/pallas_call | solution.py:146
  118.9 7.2 %all-to-all-start.1 = ((bf16[32,24,2048]{2,1,0:T(8,128)(2,1)}), bf16[32,24,2048]{2,1,0:T(8,128)(2,1)}, u32[]{:S(2)}, u32[]{:S(2)}) async-start(bf16[32,24,2048]{2,1,0:T(8,128)(2,1)} %bitcast.80), calls=%async_computation.1 | async-start | bytes 6291456 | tf_op jit(solution)/shard_map/all_to_all | solution.py:311
  126.1 2.8 %collective-permute-start.6 = (bf16[384,2048]{1,0:T(8,128)(2,1)}, bf16[384,2048]{1,0:T(8,128)(2,1)}, u32[]{:S(2)}, u32[]{:S(2)}) collective-permute-start(bf16[384,2048]{1,0:T(8,128)(2,1)} %get-tuple-element.22), channel_id=1, source_target_pairs={{0,1},{1,0},{2,3},{3,2},{4,5},{5,4},{6,7},{7,6},{8,9},{9,8},{10,11... | collective-permute-start | bytes 4718600 | tf_op jit(solution)/shard_map/ppermute | solution.py:21
  129.0 0.4 collective-permute-start.8
  129.4 0.6 fusion.55
  130.7 14.4 %collective-permute-done.9._mv_ref.refs_4_.refs_5_ = bf16[4,192,2048]{2,1,0:T(8,128)(2,1)S(1)} collective-permute-done((bf16[4,192,2048]{2,1,0:T(8,128)(2,1)}, bf16[4,192,2048]{2,1,0:T(8,128)(2,1)S(1)}, u32[]{:S(2)}, u32[]{:S(2)}) %collective-permute-start.9) | collective-permute-done | bytes 3145760 | tf_op jit(solution)/shard_map/ppermute | solution.py:21
  145.2 1.7 copy-done
  146.9 7.3 %shard_map.139 = (bf16[192,2048]{1,0:T(8,128)(2,1)}, bf16[192,2048]{1,0:T(8,128)(2,1)}, bf16[192,2048]{1,0:T(8,128)(2,1)}, bf16[192,2048]{1,0:T(8,128)(2,1)}, bf...) custom-call(s32[1]{0:T(128)} %bitcast.35.flag_ref, bf16[2,384,2048]{2,1,0:T(8,128)(2,1)} %get-tuple-element.20.xd_ref, ...), custom_call_target="tpu_custom_call" | custom-call | flops 1811939328 | bytes 12582912 | tf_op jit(solution)/shard_map/pallas_call | solution.py:192
  154.2 0.4 collective-permute-start.14
  154.6 1.2 collective-permute-start.10
  155.7 0.3 collective-permute-start.12
  156.0 16.9 %collective-permute-done.14.recv_ref = bf16[192,2048]{1,0:T(8,128)(2,1)S(1)} collective-permute-done((bf16[192,2048]{1,0:T(8,128)(2,1)}, bf16[192,2048]{1,0:T(8,128)(2,1)S(1)}, u32[]{:S(2)}, u32[]{:S(2)}) %collective-permute-start.14) | collective-permute-done | bytes 786464 | tf_op jit(solution)/shard_map/ppermute | solution.py:21
  173.0 0.9 copy-done.9
  173.8 4.6 %shard_map.142 = bf16[192,2048]{1,0:T(8,128)(2,1)} custom-call(s32[1]{0:T(128)} %bitcast.35.flag_ref, bf16[192,2048]{1,0:T(8,128)(2,1)} %get-tuple-element.30.keep_ref, bf16[192,2048]{1,0:T(8,128)(2,1)} %copy-done.9, bf16[1,192,2048]{2,1,0:T(8,128)(2,1)} %refs_0_.5, bf16[1,192,2048]{2,1,0:T(8,128)(2,1)} %refs_1_.5, bf16[1,192,2048]{2,1,0:T(8,128)(2,1)} %refs_2_.5), custom_call_target="tpu_custom_call" | custom-call | flops 7864320 | bytes 4718592 | tf_op jit(solution)/shard_map/pallas_call | solution.py:233
  178.4 1.3 collective-permute-start.15
  179.7 10.1 %collective-permute-done.10.recv_ref = bf16[192,2048]{1,0:T(8,128)(2,1)S(1)} collective-permute-done((bf16[192,2048]{1,0:T(8,128)(2,1)}, bf16[192,2048]{1,0:T(8,128)(2,1)S(1)}, u32[]{:S(2)}, u32[]{:S(2)}) %collective-permute-start.10) | collective-permute-done | bytes 786464 | tf_op jit(solution)/shard_map/ppermute | solution.py:21
  189.8 0.9 copy-done.8
  190.7 5.1 %shard_map.140 = bf16[192,2048]{1,0:T(8,128)(2,1)} custom-call(s32[1]{0:T(128)} %bitcast.35.flag_ref, bf16[192,2048]{1,0:T(8,128)(2,1)} %get-tuple-element.26.keep_ref, bf16[192,2048]{1,0:T(8,128)(2,1)} %copy-done.8, bf16[1,2,192,2048]{3,2,1,0:T(8,128)(2,1)} %refs_0_.4, bf16[1,2,192,2048]{3,2,1,0:T(8,128)(2,1)} %refs_1_.4, ...), custom_call_target="tpu_custom_call" | custom-call | flops 7864320 | bytes 7077888 | tf_op jit(solution)/shard_map/pallas_call | solution.py:233
  195.8 1.3 collective-permute-start.11
  197.3 9.2 %collective-permute-done.12.recv_ref = bf16[192,2048]{1,0:T(8,128)(2,1)S(1)} collective-permute-done((bf16[192,2048]{1,0:T(8,128)(2,1)}, bf16[192,2048]{1,0:T(8,128)(2,1)S(1)}, u32[]{:S(2)}, u32[]{:S(2)}) %collective-permute-start.12) | collective-permute-done | bytes 786464 | tf_op jit(solution)/shard_map/ppermute | solution.py:21
  206.6 0.9 copy-done.7
  207.4 5.2 %shard_map.141 = bf16[192,2048]{1,0:T(8,128)(2,1)} custom-call(s32[1]{0:T(128)} %bitcast.35.flag_ref, bf16[192,2048]{1,0:T(8,128)(2,1)} %get-tuple-element.28.keep_ref, bf16[192,2048]{1,0:T(8,128)(2,1)} %copy-done.7, bf16[1,2,192,2048]{3,2,1,0:T(8,128)(2,1)} %refs_0_.4, bf16[1,2,192,2048]{3,2,1,0:T(8,128)(2,1)} %refs_1_.4, ...), custom_call_target="tpu_custom_call" | custom-call | flops 7864320 | bytes 7077888 | tf_op jit(solution)/shard_map/pallas_call | solution.py:233
  212.6 1.4 collective-permute-start.13
  214.0 10.5 %collective-permute-done.15 = bf16[192,2048]{1,0:T(8,128)(2,1)S(1)} collective-permute-done((bf16[192,2048]{1,0:T(8,128)(2,1)}, bf16[192,2048]{1,0:T(8,128)(2,1)S(1)}, u32[]{:S(2)}, u32[]{:S(2)}) %collective-permute-start.15) | collective-permute-done | bytes 786464 | tf_op jit(solution)/shard_map/ppermute | solution.py:21
  224.5 1.0 select_bitcast_fusion
  225.4 5.1 %collective-permute-done.11 = bf16[192,2048]{1,0:T(8,128)(2,1)S(1)} collective-permute-done((bf16[192,2048]{1,0:T(8,128)(2,1)}, bf16[192,2048]{1,0:T(8,128)(2,1)S(1)}, u32[]{:S(2)}, u32[]{:S(2)}) %collective-permute-start.11) | collective-permute-done | bytes 786464 | tf_op jit(solution)/shard_map/ppermute | solution.py:323
  230.6 16.8 %collective-permute-done.13 = bf16[192,2048]{1,0:T(8,128)(2,1)S(1)} collective-permute-done((bf16[192,2048]{1,0:T(8,128)(2,1)}, bf16[192,2048]{1,0:T(8,128)(2,1)S(1)}, u32[]{:S(2)}, u32[]{:S(2)}) %collective-permute-start.13) | collective-permute-done | bytes 786464 | tf_op jit(solution)/shard_map/ppermute | solution.py:323
  247.5 3.3 %fusion.2 = f32[384,2048]{1,0:T(8,128)S(1)} fusion(bf16[768,2048]{1,0:T(8,128)(2,1)} %bitcast.34, bf16[768,128]{1,0:T(8,128)(2,1)S(1)} %get-tuple-element.44, bf16[768,128]{1,0:T(8,128)(2,1)S(1)} %get-tuple-element.43, bf16[768,128]{1,0:T(8,128)(2,1)S(1)} %get-tuple-element.42), kind=kOutput, calls=%fused_computation.13 | convolution fusion | flops 1209729024 | bytes 6881280 | tf_op jit(solution)/shard_map/dot_general | solution.py:43
  251.2 1.3 maximum_bitcast_fusion
  252.5 5.4 %collective-permute-done.5 = bf16[64,2048]{1,0:T(8,128)(2,1)S(1)} collective-permute-done((bf16[64,2048]{1,0:T(8,128)(2,1)S(1)}, bf16[64,2048]{1,0:T(8,128)(2,1)S(1)}, u32[]{:S(2)}, u32[]{:S(2)}) %collective-permute-start.5) | collective-permute-done | bytes 262176 | tf_op jit(solution)/shard_map/ppermute | solution.py:21
  257.9 0.8 fusion.16
  (59 shorter events, 1.7 us)
Async XLA Ops:
  2.0 11.0 %collective-permute-start = (f32[32,16]{0,1:T(8,128)S(1)}, f32[32,16]{0,1:T(8,128)S(1)}, u32[]{:S(2)}, u32[]{:S(2)}) collective-permute-start(f32[32,16]{0,1:T(8,128)S(1)} %get-tuple-element.63), channel_id=1, source_target_pairs={{0,128},{128,0},{1,129},{129,1},{2,130},{130,2},{3,131},{131,3},{4... | collective-permute-start | bytes 6152 | tf_op jit(solution)/shard_map/ppermute | solution.py:21
  5.6 7.8 %collective-permute-start.1 = (bf16[32,2048]{1,0:T(8,128)(2,1)}, bf16[32,2048]{1,0:T(8,128)(2,1)S(1)}, u32[]{:S(2)}, u32[]{:S(2)}) collective-permute-start(bf16[32,2048]{1,0:T(8,128)(2,1)} %param.11), channel_id=1, source_target_pairs={{0,128},{128,0},{1,129},{129,1},{2,130},{130,2},{3,131},{131,3},{4... | collective-permute-start | bytes 393224 | tf_op jit(solution)/shard_map/ppermute | solution.py:21
  5.6 8.5 %collective-permute-start.2 = (bf16[32,2048]{1,0:T(8,128)(2,1)}, bf16[32,2048]{1,0:T(8,128)(2,1)S(1)}, u32[]{:S(2)}, u32[]{:S(2)}) collective-permute-start(bf16[32,2048]{1,0:T(8,128)(2,1)} %param.12), channel_id=1, source_target_pairs={{0,128},{128,0},{1,129},{129,1},{2,130},{130,2},{3,131},{131,3},{4... | collective-permute-start | bytes 393224 | tf_op jit(solution)/shard_map/ppermute | solution.py:21
  8.7 6.5 %copy-start.10 = (bf16[32,2048]{1,0:T(8,128)(2,1)S(1)}, bf16[32,2048]{1,0:T(8,128)(2,1)}, u32[]{:S(2)}) copy-start(bf16[32,2048]{1,0:T(8,128)(2,1)} %param.12) | copy-start | bytes 393220
  8.7 6.5 %copy-start.11 = (bf16[32,2048]{1,0:T(8,128)(2,1)S(1)}, bf16[32,2048]{1,0:T(8,128)(2,1)}, u32[]{:S(2)}) copy-start(bf16[32,2048]{1,0:T(8,128)(2,1)} %param.11) | copy-start | bytes 393220
  14.2 51.2 %collective-permute-start.3 = (bf16[3,192,2048]{2,1,0:T(8,128)(2,1)}, bf16[3,192,2048]{2,1,0:T(8,128)(2,1)S(1)}, u32[]{:S(2)}, u32[]{:S(2)}) collective-permute-start(bf16[3,192,2048]{2,1,0:T(8,128)(2,1)} %get-tuple-element.18.w_own), channel_id=1, source_target_pairs={{0,2},{2,0},{1,3},{3,1},{4,6},{6,4},{5,7},{7,5},{8,10},{10,8},{9,1... | collective-permute-start | bytes 7077896 | tf_op jit(solution)/shard_map/ppermute | solution.py:21
  17.9 81.8 %all-to-all-start = ((bf16[32,24,2048]{2,1,0:T(8,128)(2,1)}), bf16[32,24,2048]{2,1,0:T(8,128)(2,1)}, u32[]{:S(2)}, u32[]{:S(2)}) async-start(bf16[32,24,2048]{2,1,0:T(8,128)(2,1)} %bitcast.76), calls=%async_computation | async-start | bytes 6291456 | tf_op jit(solution)/shard_map/all_to_all | solution.py:307
  65.4 5.2 %copy-start.1 = (bf16[3,192,2048]{2,1,0:T(8,128)(2,1)}, bf16[3,192,2048]{2,1,0:T(8,128)(2,1)S(1)}, u32[]{:S(2)}) copy-start(bf16[3,192,2048]{2,1,0:T(8,128)(2,1)S(1)} %collective-permute-done.3.w_xl.refs_3_) | copy-start | bytes 7077892
  65.4 7.9 %copy-start.2 = (bf16[1,2,192,2048]{3,2,1,0:T(8,128)(2,1)S(1)}, bf16[1,2,192,2048]{3,2,1,0:T(8,128)(2,1)}, u32[]{:S(2)}) copy-start(bf16[1,2,192,2048]{3,2,1,0:T(8,128)(2,1)} %refs_2_.4) | copy-start | bytes 4718596
  65.4 7.9 %copy-start.3 = (bf16[1,2,192,2048]{3,2,1,0:T(8,128)(2,1)S(1)}, bf16[1,2,192,2048]{3,2,1,0:T(8,128)(2,1)}, u32[]{:S(2)}) copy-start(bf16[1,2,192,2048]{3,2,1,0:T(8,128)(2,1)} %refs_1_.4) | copy-start | bytes 4718596
  70.5 29.1 %collective-permute-start.4 = (bf16[2,3,192,2048]{3,2,1,0:T(8,128)(2,1)}, bf16[2,3,192,2048]{3,2,1,0:T(8,128)(2,1)}, u32[]{:S(2)}, u32[]{:S(2)}) collective-permute-start(bf16[2,3,192,2048]{3,2,1,0:T(8,128)(2,1)} %pad_maximum_fusion), channel_id=1, source_target_pairs={{0,1},{1,0},{2,3},{3,2},{4,5},{5,4},{6,7},{7,6},{8,9},{9,8},{10,11... | collective-permute-start | bytes 14155784 | tf_op jit(solution)/shard_map/ppermute | solution.py:21
  75.1 70.0 %collective-permute-start.9 = (bf16[4,192,2048]{2,1,0:T(8,128)(2,1)}, bf16[4,192,2048]{2,1,0:T(8,128)(2,1)S(1)}, u32[]{:S(2)}, u32[]{:S(2)}) collective-permute-start(bf16[4,192,2048]{2,1,0:T(8,128)(2,1)} %pad_maximum_fusion.1), channel_id=1, source_target_pairs={{0,2},{2,0},{1,3},{3,1},{4,6},{6,4},{5,7},{7,5},{8,10},{10,8},{9,1... | collective-permute-start | bytes 9437192 | tf_op jit(solution)/shard_map/ppermute | solution.py:21
  118.9 10.5 %copy-start.12 = (s32[64]{0:T(128)S(1)}, s32[64]{0:T(128)}, u32[]{:S(2)}) copy-start(s32[64]{0:T(128)} %param.15) | copy-start | bytes 772
  118.9 128.6 %all-to-all-start.1 = ((bf16[32,24,2048]{2,1,0:T(8,128)(2,1)}), bf16[32,24,2048]{2,1,0:T(8,128)(2,1)}, u32[]{:S(2)}, u32[]{:S(2)}) async-start(bf16[32,24,2048]{2,1,0:T(8,128)(2,1)} %bitcast.80), calls=%async_computation.1 | async-start | bytes 6291456 | tf_op jit(solution)/shard_map/all_to_all | solution.py:311
  126.1 19.0 %collective-permute-start.6 = (bf16[384,2048]{1,0:T(8,128)(2,1)}, bf16[384,2048]{1,0:T(8,128)(2,1)}, u32[]{:S(2)}, u32[]{:S(2)}) collective-permute-start(bf16[384,2048]{1,0:T(8,128)(2,1)} %get-tuple-element.22), channel_id=1, source_target_pairs={{0,1},{1,0},{2,3},{3,2},{4,5},{5,4},{6,7},{7,6},{8,9},{9,8},{10,11... | collective-permute-start | bytes 4718600 | tf_op jit(solution)/shard_map/ppermute | solution.py:21
  128.9 16.2 %collective-permute-start.7 = (bf16[384,2048]{1,0:T(8,128)(2,1)}, bf16[384,2048]{1,0:T(8,128)(2,1)}, u32[]{:S(2)}, u32[]{:S(2)}) collective-permute-start(bf16[384,2048]{1,0:T(8,128)(2,1)} %get-tuple-element.23), channel_id=1, source_target_pairs={{0,1},{1,0},{2,3},{3,2},{4,5},{5,4},{6,7},{7,6},{8,9},{9,8},{10,11... | collective-permute-start | bytes 4718600 | tf_op jit(solution)/shard_map/ppermute | solution.py:21
  129.0 16.2 %collective-permute-start.8 = (bf16[384,2048]{1,0:T(8,128)(2,1)}, bf16[384,2048]{1,0:T(8,128)(2,1)}, u32[]{:S(2)}, u32[]{:S(2)}) collective-permute-start(bf16[384,2048]{1,0:T(8,128)(2,1)} %get-tuple-element.24), channel_id=1, source_target_pairs={{0,1},{1,0},{2,3},{3,2},{4,5},{5,4},{6,7},{7,6},{8,9},{9,8},{10,11... | collective-permute-start | bytes 4718600 | tf_op jit(solution)/shard_map/ppermute | solution.py:21
  145.1 1.7 copy-start
  154.2 18.8 %collective-permute-start.14 = (bf16[192,2048]{1,0:T(8,128)(2,1)}, bf16[192,2048]{1,0:T(8,128)(2,1)S(1)}, u32[]{:S(2)}, u32[]{:S(2)}) collective-permute-start(bf16[192,2048]{1,0:T(8,128)(2,1)} %get-tuple-element.31), channel_id=1, source_target_pairs={{0,2},{2,0},{1,3},{3,1},{4,6},{6,4},{5,7},{7,5},{8,10},{10,8},{9,1... | collective-permute-start | bytes 2359304 | tf_op jit(solution)/shard_map/ppermute | solution.py:21
  154.6 35.2 %collective-permute-start.10 = (bf16[192,2048]{1,0:T(8,128)(2,1)}, bf16[192,2048]{1,0:T(8,128)(2,1)S(1)}, u32[]{:S(2)}, u32[]{:S(2)}) collective-permute-start(bf16[192,2048]{1,0:T(8,128)(2,1)} %get-tuple-element.27), channel_id=1, source_target_pairs={{0,2},{2,0},{1,3},{3,1},{4,6},{6,4},{5,7},{7,5},{8,10},{10,8},{9,1... | collective-permute-start | bytes 2359304 | tf_op jit(solution)/shard_map/ppermute | solution.py:21
  155.7 50.8 %collective-permute-start.12 = (bf16[192,2048]{1,0:T(8,128)(2,1)}, bf16[192,2048]{1,0:T(8,128)(2,1)S(1)}, u32[]{:S(2)}, u32[]{:S(2)}) collective-permute-start(bf16[192,2048]{1,0:T(8,128)(2,1)} %get-tuple-element.29), channel_id=1, source_target_pairs={{0,2},{2,0},{1,3},{3,1},{4,6},{6,4},{5,7},{7,5},{8,10},{10,8},{9,1... | collective-permute-start | bytes 2359304 | tf_op jit(solution)/shard_map/ppermute | solution.py:21
  173.0 0.9 copy-start.9
  178.4 46.1 %collective-permute-start.15 = (bf16[192,2048]{1,0:T(8,128)(2,1)}, bf16[192,2048]{1,0:T(8,128)(2,1)S(1)}, u32[]{:S(2)}, u32[]{:S(2)}) collective-permute-start(bf16[192,2048]{1,0:T(8,128)(2,1)} %shard_map.142), channel_id=1, source_target_pairs={{0,128},{128,0},{1,129},{129,1},{2,130},{130,2},{3,131},{131,3},{4... | collective-permute-start | bytes 2359304 | tf_op jit(solution)/shard_map/ppermute | solution.py:21
  189.8 0.9 copy-start.8
  195.8 34.7 %collective-permute-start.11 = (bf16[192,2048]{1,0:T(8,128)(2,1)}, bf16[192,2048]{1,0:T(8,128)(2,1)S(1)}, u32[]{:S(2)}, u32[]{:S(2)}) collective-permute-start(bf16[192,2048]{1,0:T(8,128)(2,1)} %shard_map.140), channel_id=1, source_target_pairs={{0,130},{130,0},{2,128},{128,2},{1,131},{131,1},{3,129},{129,3},{4... | collective-permute-start | bytes 2359304 | tf_op jit(solution)/shard_map/ppermute | solution.py:323
  206.6 0.9 copy-start.7
  207.4 17.0 %copy-start.6 = (bf16[192,2048]{1,0:T(8,128)(2,1)S(1)}, bf16[192,2048]{1,0:T(8,128)(2,1)}, u32[]{:S(2)}) copy-start(bf16[192,2048]{1,0:T(8,128)(2,1)} %shard_map.142) | copy-start | bytes 2359300
  212.6 17.9 %copy-start.4 = (bf16[192,2048]{1,0:T(8,128)(2,1)S(1)}, bf16[192,2048]{1,0:T(8,128)(2,1)}, u32[]{:S(2)}) copy-start(bf16[192,2048]{1,0:T(8,128)(2,1)} %shard_map.140) | copy-start | bytes 2359300
  212.6 34.7 %copy-start.5 = (bf16[192,2048]{1,0:T(8,128)(2,1)S(1)}, bf16[192,2048]{1,0:T(8,128)(2,1)}, u32[]{:S(2)}) copy-start(bf16[192,2048]{1,0:T(8,128)(2,1)} %shard_map.141) | copy-start | bytes 2359300
  212.6 34.7 %collective-permute-start.13 = (bf16[192,2048]{1,0:T(8,128)(2,1)}, bf16[192,2048]{1,0:T(8,128)(2,1)S(1)}, u32[]{:S(2)}, u32[]{:S(2)}) collective-permute-start(bf16[192,2048]{1,0:T(8,128)(2,1)} %shard_map.141), channel_id=1, source_target_pairs={{0,130},{130,0},{2,128},{128,2},{1,131},{131,1},{3,129},{129,3},{4... | collective-permute-start | bytes 2359304 | tf_op jit(solution)/shard_map/ppermute | solution.py:323
  251.0 6.8 %collective-permute-start.5 = (bf16[64,2048]{1,0:T(8,128)(2,1)S(1)}, bf16[64,2048]{1,0:T(8,128)(2,1)S(1)}, u32[]{:S(2)}, u32[]{:S(2)}) collective-permute-start(bf16[64,2048]{1,0:T(8,128)(2,1)S(1)} %slice.241), channel_id=1, source_target_pairs={{0,128},{128,0},{1,129},{129,1},{2,130},{130,2},{3,131},{131,3},{4... | collective-permute-start | bytes 786440 | tf_op jit(solution)/shard_map/ppermute | solution.py:21

commit v4 on v3

--- a/solution.py
+++ b/solution.py
@@ -57,7 +57,7 @@
     return (at == (row // 4) * 8 + part * 4 + row % 4).astype(BF16)
 
 
-def rows_kernel(rows_ref, w_own, w_xl, w_pair, back_ref, xd_out, act_out, g_gate, g_up, g_down,
+def rows_kernel(rows_ref, w_own, w_xl, w_pair, _mv, back_ref, xd_out, act_out, g_gate, g_up, g_down,
                 w_all, xd, mixed, acts, g_all, w_sem, xd_sem, act_sem, g_sem):
     share = w_own.shape[1]
     width = 4 * share
@@ -137,7 +137,7 @@
         store.wait()
 
 
-def rows_step(rows, w_own, w_xl, w_pair):
+def rows_step(rows, w_own, w_xl, w_pair, mv_xl):
     total, feature = rows.shape
     half = total // 2
     share = w_own.shape[1]
@@ -150,7 +150,7 @@
             jax.ShapeDtypeStruct((2, half, feature), BF16),
             jax.ShapeDtypeStruct((3, half, 2 * share), BF16),
         ) + (jax.ShapeDtypeStruct((2 * share, feature), BF16),) * 3,
-        in_specs=[vmem_spec, any_spec, any_spec, any_spec],
+        in_specs=[vmem_spec] + [any_spec] * 4,
         out_specs=(vmem_spec,) + (any_spec,) * 5,
         scratch_shapes=[
             pltpu.VMEM((3, 4 * share, feature), BF16),
@@ -169,23 +169,23 @@
             bytes_accessed=half * feature,
             transcendentals=0,
         ),
-    )(rows, w_own, w_xl, w_pair)
-
-
-def grads_kernel(flag_ref, xd_ref, act_ref, core_gate, core_up, core_down, _mv_ref, *outs):
+    )(rows, w_own, w_xl, w_pair, mv_xl)
+
+
+def grads_kernel(flag_ref, xd_ref, act_ref, core_gate, core_up, core_down, *outs):
     share = core_gate.shape[0] // 2
     moved = flag_ref[0] != 0
     for i, (side, core_ref) in enumerate(zip((0, 0, 1), (core_gate, core_up, core_down))):
         g = dot_tn(act_ref[i], xd_ref[side]) + core_ref[...].astype(F32)
         own = g[:share]
         other = g[share:]
-        if i < 2:
+        if i < 1:
             own, other = jnp.where(moved, other, own), jnp.where(moved, own, other)
         outs[i][...] = own.astype(BF16)
         outs[3 + i][...] = other.astype(BF16)
 
 
-def grads_step(flag, xd, acts, core, mv_xl):
+def grads_step(flag, xd, acts, core):
     _, half, feature = xd.shape
     share = core[0].shape[0] // 2
     out = jax.ShapeDtypeStruct((share, feature), BF16)
@@ -198,7 +198,6 @@
             pl.BlockSpec((2, half, LANES), lambda n: (0, 0, n)),
             pl.BlockSpec(acts.shape, lambda n: (0, 0, 0)),
             *[pl.BlockSpec((2 * share, LANES), lambda n: (0, n))] * 3,
-            pl.BlockSpec(memory_space=pl.ANY),
         ],
         out_specs=(pl.BlockSpec((share, LANES), lambda n: (0, n)),) * 6,
         compiler_params=pltpu.CompilerParams(vmem_limit_bytes=VMEM_LIMIT),
@@ -207,7 +206,7 @@
             bytes_accessed=2 * (2 * half * feature + 12 * share * feature),
             transcendentals=0,
         ),
-    )(flag, xd, acts, *core, mv_xl)
+    )(flag, xd, acts, *core)
 
 
 def adam_kernel(flag_ref, keep_ref, recv_ref, *refs):
@@ -245,6 +244,31 @@
     )(flag, *[array for array, _ in arrays])
 
 
+def settle_kernel(flag_ref, *refs):
+    moved = flag_ref[0] != 0
+    for i in range(refs[-1].shape[0]):
+        refs[-1][i] = jnp.where(moved, refs[2 * i + 1][...], refs[2 * i][...])
+
+
+def settle(flag, arrays, ready):
+    rows, feature = arrays[0].shape
+    count = len(arrays) // 2
+    steps = 2
+    block = pl.BlockSpec((rows // steps, feature), lambda n: (n, 0))
+    return pl.pallas_call(
+        settle_kernel,
+        grid=(steps,),
+        out_shape=jax.ShapeDtypeStruct((count, rows, feature), BF16),
+        in_specs=[pl.BlockSpec(memory_space=pltpu.SMEM)] + [block] * len(arrays)
+        + [pl.BlockSpec(memory_space=pl.ANY)],
+        out_specs=pl.BlockSpec((count, rows // steps, feature), lambda n: (0, n, 0)),
+        compiler_params=pltpu.CompilerParams(vmem_limit_bytes=VMEM_LIMIT),
+        cost_estimate=pl.CostEstimate(
+            flops=count * rows * feature, bytes_accessed=6 * count * rows * feature, transcendentals=0
+        ),
+    )(flag, *arrays, ready)
+
+
 def split_three(value):
     high = value.astype(BF16)
     rest = value - high.astype(F32)
@@ -275,7 +299,7 @@
     w_first = after(w_own, tokens_other, cotangent_other, named_other)
     w_xl = swap(w_first, "xl")
     w_pair = swap(jnp.stack([w_own, w_xl]), "core")
-    mv_xl = swap(after(jnp.concatenate([gate_up_m[0], gate_up_v[0]]), w_xl), "xl")
+    mv_xl = swap(after(jnp.concatenate([gate_up_m[0, :1], gate_up_v[0, :1]]), w_xl), "xl")
 
     both = jnp.stack([named, named_other])
     both_routes = both[:, :, :top].astype(jnp.int32)
@@ -305,23 +329,25 @@
     send = (dot_nn(pick_b, source) * factor).astype(BF16).reshape(rings, 2 * slots, feature)
 
     recv = lax.all_to_all(send, RINGS, split_axis=0, concat_axis=0, tiled=True)
-    back_send, xd, acts, *g_pair = rows_step(recv.reshape(-1, feature), w_own, w_xl, w_pair)
+    back_send, xd, acts, *g_pair = rows_step(recv.reshape(-1, feature), w_own, w_xl, w_pair, mv_xl)
 
     g_core = [swap(g, "core") for g in g_pair]
     back = lax.all_to_all(
         back_send.reshape(recv.shape), RINGS, split_axis=0, concat_axis=0, tiled=True
     ).reshape(-1, feature)
-    parts = grads_step(flag, xd, acts, g_core, mv_xl)
-    new_down = adam_step(flag, (parts[2], ()), (swap(parts[5], "xl"), ()), (down, (0,)), (down_m, (0,)),
+    parts = grads_step(flag, xd, acts, g_core)
+    others = [swap(parts[3], "xl"), swap(parts[4], "xl")]
+    new_gate = adam_step(flag, (parts[0], ()), (others[0], ()), (gate_up, (0, 0)), (gate_up_m, (0, 0)),
+                         (gate_up_v, (0, 0)), (w_xl, (0,)), (mv_xl, (0,)), (mv_xl, (1,)))
+    others.append(swap(after(parts[5], new_gate), "xl"))
+    gate_other = lax.ppermute(new_gate, ("xh", "xl"), [(0, 3), (3, 0), (1, 2), (2, 1)])
+    new_up = adam_step(flag, (parts[1], ()), (others[1], ()), (gate_up, (0, 1)), (gate_up_m, (0, 1)),
+                       (gate_up_v, (0, 1)))
+    arrived = [new_gate, gate_other, new_up, swap(new_up, "xh")]
+    new_gate_up = settle(flag, arrived, mv_xl)
+    new_down = adam_step(flag, (parts[2], ()), (others[2], ()), (down, (0,)), (down_m, (0,)),
                          (down_v, (0,)))
-    new_down = jnp.where(swapped, swap(new_down, "xh"), new_down)
-    updated = []
-    for i in range(2):
-        new = adam_step(flag, (parts[i], ()), (swap(parts[3 + i], "xl"), ()), (gate_up, (0, i)),
-                        (gate_up_m, (0, i)), (gate_up_v, (0, i)), (w_xl, (i,)), (mv_xl, (i,)),
-                        (mv_xl, (2 + i,)))
-        across = lax.ppermute(new, ("xh", "xl"), [(0, 3), (3, 0), (1, 2), (2, 1)])
-        updated.append(jnp.where(swapped, across, new))
+    down_other = swap(new_down, "xh")
 
     mix = [
         jnp.where(pick, term, 0).reshape(rings * 2 * slots, 4 * count)
@@ -333,7 +359,8 @@
     ours = swap(theirs, "xh").astype(F32)
     layer_out = (mixed[:count] + ours[:count]).astype(BF16)
     input_grad = (mixed[count:2 * count] + ours[count:]).astype(BF16)
-    return layer_out, input_grad, jnp.stack(updated)[None], new_down[None]
+    new_down = settle(flag, [new_down, down_other], layer_out)
+    return layer_out, input_grad, new_gate_up[None], new_down
 
 
 def solution(mesh):

time: 263 us -> 254 us (0.966); the launches traced: 259 us -> 254 us
  waiting for transfers between devices: 150 us -> 141 us
  Pallas kernels: 41.4 us -> 45.8 us
  starting transfers between devices: 37.6 us -> 41.3 us
  other arithmetic: 17.7 us -> 14.7 us
    ppermute x14 -> x15, waiting for transfers between devices: 103 us -> 141 us  [swap(): return lax.ppermute(block, axis, [(0, 1), (1, 0)])]
    all_to_all x1, waiting for transfers between devices: 24.2 us -> 0.01 us  [body(): recv = lax.all_to_all(send, RINGS, split_axis=0, concat_axis=0, tiled=True)]
    ppermute x2 -> x1, waiting for transfers between devices: 21.9 us -> 0.01 us  [body(): lax.ppermute(new_gate, ('xh', 'xl'), [(0, 3), (3, 0), (1, 2), (2, 1)])]
    pallas_call x0 -> x2, Pallas kernels: none -> 4.95 us  [settle(): pl.pallas_call(settle_kernel, grid=(steps,), out_shape=jax.ShapeDtypeStru...]
    all_to_all x1, starting transfers between devices: 7.2 us -> 11.2 us  [body(): lax.all_to_all(back_send.reshape(recv.shape), RINGS, split_axis=0, concat...]
    ppermute x14 -> x15, starting transfers between devices: 16.5 us -> 17.8 us  [swap(): return lax.ppermute(block, axis, [(0, 1), (1, 0)])]
  transfers between devices with their start and end apart: 18 -> 18, of which waited for: 11 -> 11; matrix products, arithmetic and copies ran while one was open for 7% -> 7% of each run, Pallas kernels for 16% -> 10%
where the time goes in v4:
time: 254 us
  waiting for transfers between devices  141 us (56%)
  Pallas kernels  45.8 us (18%)
  starting transfers between devices  41.3 us (16%)
  other arithmetic  14.7 us (6%)
  matrix products  5.17 us (2%)
  local copies, waits for them, and re-layouts  4.17 us (2%)
    ppermute x15, waiting for transfers between devices, swap(): return lax.ppermute(block, axis, [(0, 1), (1, 0)])  141 us
    pallas_call x1, Pallas kernels, rows_step(): pl.pallas_call(rows_kernel, out_shape=(jax.ShapeDtypeStruct(rows.shape, B...  19.2 us
    ppermute x15, starting transfers between devices, swap(): return lax.ppermute(block, axis, [(0, 1), (1, 0)])  17.8 us
    pallas_call x3, Pallas kernels, adam_step(): pl.pallas_call(adam_kernel, grid=(steps,), out_shape=jax.ShapeDtypeStruct...  14.4 us
    all_to_all x1, starting transfers between devices, body(): recv = lax.all_to_all(send, RINGS, split_axis=0, concat_axis=0, tiled=True)  11.3 us
    all_to_all x1, starting transfers between devices, body(): lax.all_to_all(back_send.reshape(recv.shape), RINGS, split_axis=0, concat...  11.2 us
    another operation x2, other arithmetic, body(): w_pair = swap(jnp.stack([w_own, w_xl]), 'core')  9.27 us
    pallas_call x1, Pallas kernels, grads_step(): pl.pallas_call(grads_kernel, grid=(feature // LANES,), out_shape=(out,) *...  7.25 us
  transfers between devices with their start and end apart: 18, of which 11 were waited for; matrix products, arithmetic and copies ran while one was open for 7% of the time, Pallas kernels for 10%

profile of v4, /device:TPU:1, one launch (start us, length us, event | category | flops | bytes accessed | tf_op | source)
XLA Modules:
  0.0 253.7 jit_solution(14327479135869170205)
XLA Ops:
  0.6 0.7 convert_element_type.115
  1.3 0.7 pad_maximum_fusion.4
  2.0 3.6 %collective-permute-start = (f32[32,16]{0,1:T(8,128)S(1)}, f32[32,16]{0,1:T(8,128)S(1)}, u32[]{:S(2)}, u32[]{:S(2)}) collective-permute-start(f32[32,16]{0,1:T(8,128)S(1)} %get-tuple-element.65), channel_id=1, source_target_pairs={{0,128},{128,0},{1,129},{129,1},{2,130},{130,2},{3,131},{131,3},{4... | collective-permute-start | bytes 6152 | tf_op jit(solution)/shard_map/ppermute | solution.py:21
  5.6 2.9 %collective-permute-start.2 = (bf16[32,2048]{1,0:T(8,128)(2,1)}, bf16[32,2048]{1,0:T(8,128)(2,1)S(1)}, u32[]{:S(2)}, u32[]{:S(2)}) collective-permute-start(bf16[32,2048]{1,0:T(8,128)(2,1)} %param.12), channel_id=1, source_target_pairs={{0,128},{128,0},{1,129},{129,1},{2,130},{130,2},{3,131},{131,3},{4... | collective-permute-start | bytes 393224 | tf_op jit(solution)/shard_map/ppermute | solution.py:21
  8.7 4.1 %fusion.60 = (bf16[1,3,192,2048]{3,2,1,0:T(8,128)(2,1)}, bf16[3,192,2048]{2,1,0:T(8,128)(2,1)}) fusion(bf16[1,192,2048]{2,1,0:T(8,128)(2,1)} %refs_0_.5, bf16[2,192,2048]{2,1,0:T(8,128)(2,1)} %bitcast.71), kind=kLoop, calls=%fused_computation.141 | loop fusion | flops 1179648 | bytes 7077888 | tf_op jit(solution)/shard_map/stack | solution.py:301
  13.3 0.8 collective-permute-done.2
  14.2 0.3 collective-permute-start.3
  14.6 0.7 select_convert_fusion
  15.8 2.6 %multiply_convert_fusion = bf16[768,2048]{1,0:T(8,128)(2,1)} fusion(pred[768,128]{1,0:T(32,128)(4,1)S(1)} %fusion.15, f32[768]{0:T(1024)S(1)} %select_n.183, bf16[32,2048]{1,0:T(8,128)(2,1)S(1)} %collective-permute-done.2, bf16[32,2048]{1,0:T(8,128)(2,1)S(1)} %collective-permute-done.1, bf16[32,2048]{1,0:T(8,128)(2,1)S(1)} %copy-done.7, ...), kind=kOutput, calls=%fused_computation | convolution fusion | flops 407896064 | bytes 3771392 | tf_op jit(solution)/shard_map/dot_general | solution.py:39
  18.4 11.3 %all-to-all-start = ((bf16[32,24,2048]{2,1,0:T(8,128)(2,1)}), bf16[32,24,2048]{2,1,0:T(8,128)(2,1)}, u32[]{:S(2)}, u32[]{:S(2)}) async-start(bf16[32,24,2048]{2,1,0:T(8,128)(2,1)} %bitcast.28), calls=%async_computation | async-start | bytes 6291456 | tf_op jit(solution)/shard_map/all_to_all | solution.py:331
  29.8 35.6 %collective-permute-done.3.w_xl.refs_3_ = bf16[3,192,2048]{2,1,0:T(8,128)(2,1)S(1)} collective-permute-done((bf16[3,192,2048]{2,1,0:T(8,128)(2,1)}, bf16[3,192,2048]{2,1,0:T(8,128)(2,1)S(1)}, u32[]{:S(2)}, u32[]{:S(2)}) %collective-permute-start.3) | collective-permute-done | bytes 2359328 | tf_op jit(solution)/shard_map/ppermute | solution.py:21
  65.4 5.1 %pad_maximum_fusion = bf16[2,3,192,2048]{3,2,1,0:T(8,128)(2,1)} fusion(bf16[1,3,192,2048]{3,2,1,0:T(8,128)(2,1)S(1)} %bitcast.70, bf16[1,3,192,2048]{3,2,1,0:T(8,128)(2,1)} %get-tuple-element.36), kind=kLoop, calls=%fused_computation.1 | loop fusion | flops 2359296 | bytes 9437184 | tf_op jit(solution)/shard_map/stack | solution.py:301
  70.5 2.7 %collective-permute-start.4 = (bf16[2,3,192,2048]{3,2,1,0:T(8,128)(2,1)}, bf16[2,3,192,2048]{3,2,1,0:T(8,128)(2,1)}, u32[]{:S(2)}, u32[]{:S(2)}) collective-permute-start(bf16[2,3,192,2048]{3,2,1,0:T(8,128)(2,1)} %pad_maximum_fusion), channel_id=1, source_target_pairs={{0,1},{1,0},{2,3},{3,2},{4,5},{5,4},{6,7},{7,6},{8,9},{9,8},{10,11... | collective-permute-start | bytes 14155784 | tf_op jit(solution)/shard_map/ppermute | solution.py:21
  73.5 0.6 collective-permute-start.5
  74.0 35.7 %collective-permute-done.5._mv.refs_4_.refs_5_ = bf16[2,192,2048]{2,1,0:T(8,128)(2,1)S(1)} collective-permute-done((bf16[2,192,2048]{2,1,0:T(8,128)(2,1)S(1)}, bf16[2,192,2048]{2,1,0:T(8,128)(2,1)S(1)}, u32[]{:S(2)}, u32[]{:S(2)}) %collective-permute-start.5) | collective-permute-done | bytes 1572896 | tf_op jit(solution)/shard_map/ppermute | solution.py:21
  109.7 1.2 copy-done
  110.9 19.2 %shard_map.138 = (bf16[768,2048]{1,0:T(8,128)(2,1)}, bf16[2,384,2048]{2,1,0:T(8,128)(2,1)}, bf16[3,384,384]{2,1,0:T(8,128)(2,1)}, bf16[384,2048]{1,0:T(8,128)(2,...) custom-call(bf16[768,2048]{1,0:T(8,128)(2,1)} %bitcast.29.rows_ref, ...), custom_call_target="tpu_custom_call" | custom-call | flops 150994944 | bytes 786432 | tf_op jit(solution)/shard_map/pallas_call | solution.py:146
  130.1 11.2 %all-to-all-start.1 = ((bf16[32,24,2048]{2,1,0:T(8,128)(2,1)}), bf16[32,24,2048]{2,1,0:T(8,128)(2,1)S(1)}, u32[]{:S(2)}, u32[]{:S(2)}) async-start(bf16[32,24,2048]{2,1,0:T(8,128)(2,1)} %bitcast.73), calls=%async_computation.1 | async-start | bytes 6291456 | tf_op jit(solution)/shard_map/all_to_all | solution.py:335
  141.4 1.2 collective-permute-start.7
  142.6 0.4 collective-permute-start.9
  143.0 0.6 fusion.55
  144.3 1.6 collective-permute-done.7.core_gate
  145.9 2.2 collective-permute-done.8.core_up
  148.2 2.2 collective-permute-done.9.core_down
  150.4 7.2 %shard_map.139 = (bf16[192,2048]{1,0:T(8,128)(2,1)}, bf16[192,2048]{1,0:T(8,128)(2,1)}, bf16[192,2048]{1,0:T(8,128)(2,1)}, bf16[192,2048]{1,0:T(8,128)(2,1)}, bf...) custom-call(s32[1]{0:T(128)} %bitcast.37.flag_ref, bf16[2,384,2048]{2,1,0:T(8,128)(2,1)} %get-tuple-element.22.xd_ref, ...), custom_call_target="tpu_custom_call" | custom-call | flops 1811939328 | bytes 12582912 | tf_op jit(solution)/shard_map/pallas_call | solution.py:192
  157.7 0.4 collective-permute-start.10
  158.0 1.2 collective-permute-start.12
  159.2 17.5 %collective-permute-done.10.recv_ref = bf16[192,2048]{1,0:T(8,128)(2,1)S(1)} collective-permute-done((bf16[192,2048]{1,0:T(8,128)(2,1)}, bf16[192,2048]{1,0:T(8,128)(2,1)S(1)}, u32[]{:S(2)}, u32[]{:S(2)}) %collective-permute-start.10) | collective-permute-done | bytes 786464 | tf_op jit(solution)/shard_map/ppermute | solution.py:21
  176.7 0.9 copy-done.6
  177.6 5.2 %shard_map.140.refs_0_ = bf16[192,2048]{1,0:T(8,128)(2,1)} custom-call(s32[1]{0:T(128)} %bitcast.37.flag_ref, bf16[192,2048]{1,0:T(8,128)(2,1)} %get-tuple-element.27.keep_ref, bf16[192,2048]{1,0:T(8,128)(2,1)} %copy-done.6, bf16[1,2,192,2048]{3,2,1,0:T(8,128)(2,1)} %refs_0_.4, bf16[1,2,192,2048]{3,2,1,0:T(8,128)(2,1)} %refs_1_.4, ...), custom_call_target="tpu_custom_call" | custom-call | flops 7864320 | bytes 7077888 | tf_op jit(solution)/shard_map/pallas_call | solution.py:232
  182.8 0.4 collective-permute-start.14
  183.2 0.9 bitcast_select_fusion.2
  184.1 1.0 collective-permute-start.11
  185.1 8.5 %collective-permute-done.12.recv_ref = bf16[192,2048]{1,0:T(8,128)(2,1)S(1)} collective-permute-done((bf16[192,2048]{1,0:T(8,128)(2,1)}, bf16[192,2048]{1,0:T(8,128)(2,1)S(1)}, u32[]{:S(2)}, u32[]{:S(2)}) %collective-permute-start.12) | collective-permute-done | bytes 786464 | tf_op jit(solution)/shard_map/ppermute | solution.py:21
  193.6 0.9 copy-done.4
  194.5 4.6 %shard_map.141.refs_2_ = bf16[192,2048]{1,0:T(8,128)(2,1)} custom-call(s32[1]{0:T(128)} %bitcast.37.flag_ref, bf16[192,2048]{1,0:T(8,128)(2,1)} %get-tuple-element.29.keep_ref, bf16[192,2048]{1,0:T(8,128)(2,1)} %copy-done.4, bf16[1,2,192,2048]{3,2,1,0:T(8,128)(2,1)} %refs_0_.4, bf16[1,2,192,2048]{3,2,1,0:T(8,128)(2,1)} %refs_1_.4, ...), custom_call_target="tpu_custom_call" | custom-call | flops 7864320 | bytes 4718592 | tf_op jit(solution)/shard_map/pallas_call | solution.py:232
  199.1 1.0 collective-permute-start.13
  200.1 10.3 %collective-permute-done.14.recv_ref = bf16[192,2048]{1,0:T(8,128)(2,1)S(1)} collective-permute-done((bf16[192,2048]{1,0:T(8,128)(2,1)S(1)}, bf16[192,2048]{1,0:T(8,128)(2,1)S(1)}, u32[]{:S(2)}, u32[]{:S(2)}) %collective-permute-start.14) | collective-permute-done | bytes 786464 | tf_op jit(solution)/shard_map/ppermute | solution.py:21
  210.4 0.9 copy-done.5
  211.2 4.6 %shard_map.143.refs_0_ = bf16[192,2048]{1,0:T(8,128)(2,1)} custom-call(s32[1]{0:T(128)} %bitcast.37.flag_ref, bf16[192,2048]{1,0:T(8,128)(2,1)} %get-tuple-element.31.keep_ref, bf16[192,2048]{1,0:T(8,128)(2,1)} %copy-done.5, bf16[1,192,2048]{2,1,0:T(8,128)(2,1)} %refs_0_.5, bf16[1,192,2048]{2,1,0:T(8,128)(2,1)} %refs_1_.5, bf16[1,192,2048]{2,1,0:T(8,128)(2,1)} %refs_2_.5), custom_call_target="tpu_custom_call" | custom-call | flops 7864320 | bytes 4718592 | tf_op jit(solution)/shard_map/pallas_call | solution.py:232
  215.8 1.0 collective-permute-start.15
  216.9 2.3 fusion.2
  219.4 2.0 collective-permute-start.6
  221.5 6.9 %collective-permute-done.13.refs_3_ = bf16[192,2048]{1,0:T(8,128)(2,1)} collective-permute-done((bf16[192,2048]{1,0:T(8,128)(2,1)}, bf16[192,2048]{1,0:T(8,128)(2,1)}, u32[]{:S(2)}, u32[]{:S(2)}) %collective-permute-start.13) | collective-permute-done | bytes 786464 | tf_op jit(solution)/shard_map/ppermute | solution.py:21
  228.3 2.8 %shard_map.142 = bf16[2,192,2048]{2,1,0:T(8,128)(2,1)} custom-call(s32[1]{0:T(128)} %bitcast.37.flag_ref, bf16[192,2048]{1,0:T(8,128)(2,1)} %shard_map.140.refs_0_, bf16[192,2048]{1,0:T(8,128)(2,1)} %collective-permute-done.11.refs_1_, bf16[192,2048]{1,0:T(8,128)(2,1)} %shard_map.141.refs_2_, bf16[192,2048]{1,0:T(8,128)(2,1)} %collective-permute-done.13.refs_3_, ...), custom_call_target="tpu_custom_call" | custom-call | flops 786432 | bytes 4718592 | tf_op jit(solution)/shard_map/pallas_call | solution.py:258
  231.1 19.6 %collective-permute-done.6 = bf16[64,2048]{1,0:T(8,128)(2,1)S(1)} collective-permute-done((bf16[64,2048]{1,0:T(8,128)(2,1)S(1)}, bf16[64,2048]{1,0:T(8,128)(2,1)S(1)}, u32[]{:S(2)}, u32[]{:S(2)}) %collective-permute-start.6) | collective-permute-done | bytes 262176 | tf_op jit(solution)/shard_map/ppermute | solution.py:21
  250.7 0.8 fusion.16
  251.5 2.1 shard_map.144
  (64 shorter events, 1.9 us)
Async XLA Ops:
  2.0 10.9 %collective-permute-start = (f32[32,16]{0,1:T(8,128)S(1)}, f32[32,16]{0,1:T(8,128)S(1)}, u32[]{:S(2)}, u32[]{:S(2)}) collective-permute-start(f32[32,16]{0,1:T(8,128)S(1)} %get-tuple-element.65), channel_id=1, source_target_pairs={{0,128},{128,0},{1,129},{129,1},{2,130},{130,2},{3,131},{131,3},{4... | collective-permute-start | bytes 6152 | tf_op jit(solution)/shard_map/ppermute | solution.py:21
  5.6 7.7 %collective-permute-start.1 = (bf16[32,2048]{1,0:T(8,128)(2,1)}, bf16[32,2048]{1,0:T(8,128)(2,1)S(1)}, u32[]{:S(2)}, u32[]{:S(2)}) collective-permute-start(bf16[32,2048]{1,0:T(8,128)(2,1)} %param.11), channel_id=1, source_target_pairs={{0,128},{128,0},{1,129},{129,1},{2,130},{130,2},{3,131},{131,3},{4... | collective-permute-start | bytes 393224 | tf_op jit(solution)/shard_map/ppermute | solution.py:21
  5.6 8.5 %collective-permute-start.2 = (bf16[32,2048]{1,0:T(8,128)(2,1)}, bf16[32,2048]{1,0:T(8,128)(2,1)S(1)}, u32[]{:S(2)}, u32[]{:S(2)}) collective-permute-start(bf16[32,2048]{1,0:T(8,128)(2,1)} %param.12), channel_id=1, source_target_pairs={{0,128},{128,0},{1,129},{129,1},{2,130},{130,2},{3,131},{131,3},{4... | collective-permute-start | bytes 393224 | tf_op jit(solution)/shard_map/ppermute | solution.py:21
  8.7 6.9 %copy-start.9 = (pred[24,128]{1,0:T(8,128)(4,1)}, pred[24,128]{1,0:T(8,128)(4,1)S(1)}, u32[]{:S(2)}) copy-start(pred[24,128]{1,0:T(8,128)(4,1)S(1)} %broadcast_compare_fusion) | copy-start | bytes 9220
  8.7 7.1 %copy-start.7 = (bf16[32,2048]{1,0:T(8,128)(2,1)S(1)}, bf16[32,2048]{1,0:T(8,128)(2,1)}, u32[]{:S(2)}) copy-start(bf16[32,2048]{1,0:T(8,128)(2,1)} %param.12) | copy-start | bytes 393220
  8.7 7.1 %copy-start.8 = (bf16[32,2048]{1,0:T(8,128)(2,1)S(1)}, bf16[32,2048]{1,0:T(8,128)(2,1)}, u32[]{:S(2)}) copy-start(bf16[32,2048]{1,0:T(8,128)(2,1)} %param.11) | copy-start | bytes 393220
  12.9 5.5 %copy-start.11 = (s32[768]{0:T(1024)}, s32[768]{0:T(1024)S(1)}, u32[]{:S(2)}) copy-start(s32[768]{0:T(1024)S(1)} %eq.199) | copy-start | bytes 9220
  14.2 51.2 %collective-permute-start.3 = (bf16[3,192,2048]{2,1,0:T(8,128)(2,1)}, bf16[3,192,2048]{2,1,0:T(8,128)(2,1)S(1)}, u32[]{:S(2)}, u32[]{:S(2)}) collective-permute-start(bf16[3,192,2048]{2,1,0:T(8,128)(2,1)} %get-tuple-element.19.w_own), channel_id=1, source_target_pairs={{0,2},{2,0},{1,3},{3,1},{4,6},{6,4},{5,7},{7,5},{8,10},{10,8},{9,1... | collective-permute-start | bytes 7077896 | tf_op jit(solution)/shard_map/ppermute | solution.py:21
  18.4 91.3 %all-to-all-start = ((bf16[32,24,2048]{2,1,0:T(8,128)(2,1)}), bf16[32,24,2048]{2,1,0:T(8,128)(2,1)}, u32[]{:S(2)}, u32[]{:S(2)}) async-start(bf16[32,24,2048]{2,1,0:T(8,128)(2,1)} %bitcast.28), calls=%async_computation | async-start | bytes 6291456 | tf_op jit(solution)/shard_map/all_to_all | solution.py:331
  65.4 5.2 %copy-start.1 = (bf16[3,192,2048]{2,1,0:T(8,128)(2,1)}, bf16[3,192,2048]{2,1,0:T(8,128)(2,1)S(1)}, u32[]{:S(2)}) copy-start(bf16[3,192,2048]{2,1,0:T(8,128)(2,1)S(1)} %collective-permute-done.3.w_xl.refs_3_) | copy-start | bytes 7077892
  65.4 7.8 %copy-start.2 = (bf16[1,2,192,2048]{3,2,1,0:T(8,128)(2,1)S(1)}, bf16[1,2,192,2048]{3,2,1,0:T(8,128)(2,1)}, u32[]{:S(2)}) copy-start(bf16[1,2,192,2048]{3,2,1,0:T(8,128)(2,1)} %refs_2_.4) | copy-start | bytes 4718596
  65.4 7.8 %copy-start.3 = (bf16[1,2,192,2048]{3,2,1,0:T(8,128)(2,1)S(1)}, bf16[1,2,192,2048]{3,2,1,0:T(8,128)(2,1)}, u32[]{:S(2)}) copy-start(bf16[1,2,192,2048]{3,2,1,0:T(8,128)(2,1)} %refs_1_.4) | copy-start | bytes 4718596
  70.5 39.2 %collective-permute-start.4 = (bf16[2,3,192,2048]{3,2,1,0:T(8,128)(2,1)}, bf16[2,3,192,2048]{3,2,1,0:T(8,128)(2,1)}, u32[]{:S(2)}, u32[]{:S(2)}) collective-permute-start(bf16[2,3,192,2048]{3,2,1,0:T(8,128)(2,1)} %pad_maximum_fusion), channel_id=1, source_target_pairs={{0,1},{1,0},{2,3},{3,2},{4,5},{5,4},{6,7},{7,6},{8,9},{9,8},{10,11... | collective-permute-start | bytes 14155784 | tf_op jit(solution)/shard_map/ppermute | solution.py:21
  73.5 36.3 %collective-permute-start.5 = (bf16[2,192,2048]{2,1,0:T(8,128)(2,1)S(1)}, bf16[2,192,2048]{2,1,0:T(8,128)(2,1)S(1)}, u32[]{:S(2)}, u32[]{:S(2)}) collective-permute-start(bf16[2,192,2048]{2,1,0:T(8,128)(2,1)S(1)} %pad_maximum_fusion.2), channel_id=1, source_target_pairs={{0,2},{2,0},{1,3},{3,1},{4,6},{6,4},{5,7},{7,5},{8,10},{10,8},{9,1... | collective-permute-start | bytes 4718600 | tf_op jit(solution)/shard_map/ppermute | solution.py:21
  109.7 1.2 copy-start
  130.1 12.9 %copy-start.15 = (s32[64]{0:T(128)S(1)}, s32[64]{0:T(128)}, u32[]{:S(2)}) copy-start(s32[64]{0:T(128)} %param.15) | copy-start | bytes 772
  130.1 86.7 %all-to-all-start.1 = ((bf16[32,24,2048]{2,1,0:T(8,128)(2,1)}), bf16[32,24,2048]{2,1,0:T(8,128)(2,1)S(1)}, u32[]{:S(2)}, u32[]{:S(2)}) async-start(bf16[32,24,2048]{2,1,0:T(8,128)(2,1)} %bitcast.73), calls=%async_computation.1 | async-start | bytes 6291456 | tf_op jit(solution)/shard_map/all_to_all | solution.py:335
  141.4 4.5 %collective-permute-start.7 = (bf16[384,2048]{1,0:T(8,128)(2,1)}, bf16[384,2048]{1,0:T(8,128)(2,1)}, u32[]{:S(2)}, u32[]{:S(2)}) collective-permute-start(bf16[384,2048]{1,0:T(8,128)(2,1)} %get-tuple-element.24), channel_id=1, source_target_pairs={{0,1},{1,0},{2,3},{3,2},{4,5},{5,4},{6,7},{7,6},{8,9},{9,8},{10,11... | collective-permute-start | bytes 4718600 | tf_op jit(solution)/shard_map/ppermute | solution.py:21
  142.5 5.6 %collective-permute-start.8 = (bf16[384,2048]{1,0:T(8,128)(2,1)}, bf16[384,2048]{1,0:T(8,128)(2,1)}, u32[]{:S(2)}, u32[]{:S(2)}) collective-permute-start(bf16[384,2048]{1,0:T(8,128)(2,1)} %get-tuple-element.25), channel_id=1, source_target_pairs={{0,1},{1,0},{2,3},{3,2},{4,5},{5,4},{6,7},{7,6},{8,9},{9,8},{10,11... | collective-permute-start | bytes 4718600 | tf_op jit(solution)/shard_map/ppermute | solution.py:21
  142.6 7.8 %collective-permute-start.9 = (bf16[384,2048]{1,0:T(8,128)(2,1)}, bf16[384,2048]{1,0:T(8,128)(2,1)}, u32[]{:S(2)}, u32[]{:S(2)}) collective-permute-start(bf16[384,2048]{1,0:T(8,128)(2,1)} %get-tuple-element.26), channel_id=1, source_target_pairs={{0,1},{1,0},{2,3},{3,2},{4,5},{5,4},{6,7},{7,6},{8,9},{9,8},{10,11... | collective-permute-start | bytes 4718600 | tf_op jit(solution)/shard_map/ppermute | solution.py:21
  157.7 19.0 %collective-permute-start.10 = (bf16[192,2048]{1,0:T(8,128)(2,1)}, bf16[192,2048]{1,0:T(8,128)(2,1)S(1)}, u32[]{:S(2)}, u32[]{:S(2)}) collective-permute-start(bf16[192,2048]{1,0:T(8,128)(2,1)} %get-tuple-element.28), channel_id=1, source_target_pairs={{0,2},{2,0},{1,3},{3,1},{4,6},{6,4},{5,7},{7,5},{8,10},{10,8},{9,1... | collective-permute-start | bytes 2359304 | tf_op jit(solution)/shard_map/ppermute | solution.py:21
  158.0 35.6 %collective-permute-start.12 = (bf16[192,2048]{1,0:T(8,128)(2,1)}, bf16[192,2048]{1,0:T(8,128)(2,1)S(1)}, u32[]{:S(2)}, u32[]{:S(2)}) collective-permute-start(bf16[192,2048]{1,0:T(8,128)(2,1)} %get-tuple-element.30), channel_id=1, source_target_pairs={{0,2},{2,0},{1,3},{3,1},{4,6},{6,4},{5,7},{7,5},{8,10},{10,8},{9,1... | collective-permute-start | bytes 2359304 | tf_op jit(solution)/shard_map/ppermute | solution.py:21
  176.7 0.9 copy-start.6
  177.6 5.2 %copy-start.14 = (bf16[192,2048]{1,0:T(8,128)(2,1)S(1)}, bf16[192,2048]{1,0:T(8,128)(2,1)}, u32[]{:S(2)}) copy-start(bf16[192,2048]{1,0:T(8,128)(2,1)} %get-tuple-element.33) | copy-start | bytes 2359300
  177.6 5.6 %copy-start.10 = (pred[24,128]{1,0:T(8,128)(4,1)S(1)}, pred[24,128]{1,0:T(8,128)(4,1)}, u32[]{:S(2)}) copy-start(pred[24,128]{1,0:T(8,128)(4,1)} %copy-done.9) | copy-start | bytes 9220
  177.6 5.6 %copy-start.12 = (s32[768]{0:T(1024)S(1)}, s32[768]{0:T(1024)}, u32[]{:S(2)}) copy-start(s32[768]{0:T(1024)} %copy-done.11) | copy-start | bytes 9220
  177.6 5.6 %copy-start.13 = (bf16[32,128]{1,0:T(8,128)(2,1)S(1)}, bf16[32,128]{1,0:T(8,128)(2,1)}, u32[]{:S(2)}) copy-start(bf16[32,128]{1,0:T(8,128)(2,1)} %get-tuple-element.34) | copy-start | bytes 24580
  182.8 27.6 %collective-permute-start.14 = (bf16[192,2048]{1,0:T(8,128)(2,1)S(1)}, bf16[192,2048]{1,0:T(8,128)(2,1)S(1)}, u32[]{:S(2)}, u32[]{:S(2)}) collective-permute-start(bf16[192,2048]{1,0:T(8,128)(2,1)S(1)} %copy-done.14), channel_id=1, source_target_pairs={{0,2},{2,0},{1,3},{3,1},{4,6},{6,4},{5,7},{7,5},{8,10},{10,8},{9,1... | collective-permute-start | bytes 2359304 | tf_op jit(solution)/shard_map/ppermute | solution.py:21
  184.1 44.2 %collective-permute-start.11 = (bf16[192,2048]{1,0:T(8,128)(2,1)}, bf16[192,2048]{1,0:T(8,128)(2,1)}, u32[]{:S(2)}, u32[]{:S(2)}) collective-permute-start(bf16[192,2048]{1,0:T(8,128)(2,1)} %shard_map.140.refs_0_), channel_id=1, source_target_pairs={{0,130},{130,0},{2,128},{128,2},{1,131},{131,1},{3,129},{129,3},{4... | collective-permute-start | bytes 2359304 | tf_op jit(solution)/shard_map/ppermute | solution.py:343
  193.6 0.9 copy-start.4
  199.1 29.3 %collective-permute-start.13 = (bf16[192,2048]{1,0:T(8,128)(2,1)}, bf16[192,2048]{1,0:T(8,128)(2,1)}, u32[]{:S(2)}, u32[]{:S(2)}) collective-permute-start(bf16[192,2048]{1,0:T(8,128)(2,1)} %shard_map.141.refs_2_), channel_id=1, source_target_pairs={{0,128},{128,0},{1,129},{129,1},{2,130},{130,2},{3,131},{131,3},{4... | collective-permute-start | bytes 2359304 | tf_op jit(solution)/shard_map/ppermute | solution.py:21
  210.4 0.9 copy-start.5
  215.8 35.7 %collective-permute-start.15 = (bf16[192,2048]{1,0:T(8,128)(2,1)}, bf16[192,2048]{1,0:T(8,128)(2,1)}, u32[]{:S(2)}, u32[]{:S(2)}) collective-permute-start(bf16[192,2048]{1,0:T(8,128)(2,1)} %shard_map.143.refs_0_), channel_id=1, source_target_pairs={{0,128},{128,0},{1,129},{129,1},{2,130},{130,2},{3,131},{131,3},{4... | collective-permute-start | bytes 2359304 | tf_op jit(solution)/shard_map/ppermute | solution.py:21
  219.4 31.3 %collective-permute-start.6 = (bf16[64,2048]{1,0:T(8,128)(2,1)S(1)}, bf16[64,2048]{1,0:T(8,128)(2,1)S(1)}, u32[]{:S(2)}, u32[]{:S(2)}) collective-permute-start(bf16[64,2048]{1,0:T(8,128)(2,1)S(1)} %slice.251), channel_id=1, source_target_pairs={{0,128},{128,0},{1,129},{129,1},{2,130},{130,2},{3,131},{131,3},{4... | collective-permute-start | bytes 786440 | tf_op jit(solution)/shard_map/ppermute | solution.py:21

commit v5 on v4

--- a/solution.py
+++ b/solution.py
@@ -45,58 +45,102 @@
 
 CHUNK = 256
 LANES = 512
-GROUP = 16
 VMEM_LIMIT = 56 * 1024 * 1024
-
-
-def mixed_order(size):
-    to = lax.broadcasted_iota(jnp.int32, (size, size), 0)
-    at = lax.broadcasted_iota(jnp.int32, (size, size), 1)
-    part = to // (size // 2)
-    row = to - part * (size // 2)
-    return (at == (row // 4) * 8 + part * 4 + row % 4).astype(BF16)
-
-
-def rows_kernel(rows_ref, w_own, w_xl, w_pair, _mv, back_ref, xd_out, act_out, g_gate, g_up, g_down,
-                w_all, xd, mixed, acts, g_all, w_sem, xd_sem, act_sem, g_sem):
-    share = w_own.shape[1]
+META = 128
+
+
+def pick_kernel(place_ref, g_ref, *outs):
+    total = g_ref.shape[0]
+    feature = outs[0].shape[1] // 2
+    rows = outs[0].shape[0]
+    meta = jnp.transpose(g_ref[:, 2 * feature:].astype(F32))
+    names = meta[0:8]
+    weights = meta[8:16] + meta[16:24] + meta[24:32]
+    at = lax.broadcasted_iota(jnp.int32, (total, total), 0)
+    to = lax.broadcasted_iota(jnp.int32, (total, total), 1)
+    before = ((at < to) & ((at >> 5) == (to >> 5))).astype(BF16)
+    row = lax.broadcasted_iota(jnp.int32, (rows, total), 0)
+    source = (row * 43) >> 8
+    number = (row - CAP * source).astype(F32)
+    same = (lax.broadcasted_iota(jnp.int32, (rows, total), 1) >> 5) == source
+    picks, scales = [], []
+    for step in range(len(outs)):
+        expert = place_ref[0] + 8 * ((place_ref[1] + step) & 3)
+        hit = names == expert.astype(F32)
+        used = jnp.sum(hit.astype(F32), axis=0, keepdims=True)
+        weight = jnp.sum(jnp.where(hit, weights, 0.0), axis=0, keepdims=True)
+        rank = jnp.sum(dot_nn(hit.astype(BF16), before), axis=0, keepdims=True)
+        rank = jnp.where(used > 0, rank, -1.0)
+        pick = same & (rank == number)
+        picks.append(jnp.where(pick, 1.0, 0.0))
+        scales.append(jnp.sum(jnp.where(pick, weight, 0.0), axis=1, keepdims=True))
+    picks = jnp.concatenate(picks).astype(BF16)
+    scales = jnp.concatenate(scales)
+    for n in range(0, 2 * feature, LANES):
+        found = dot_nn(picks, g_ref[:, n:n + LANES])
+        if n >= feature:
+            found = found * scales
+        found = found.astype(BF16)
+        for i, out in enumerate(outs):
+            out[:, n:n + LANES] = found[i * rows:(i + 1) * rows]
+
+
+def pick_step(place, gathered, steps):
+    total, width = gathered.shape
+    rows = total // 32 * CAP
+    vmem_spec = pl.BlockSpec(memory_space=pltpu.VMEM)
+    wide = (width - META) // 2
+    return pl.pallas_call(
+        pick_kernel,
+        out_shape=(jax.ShapeDtypeStruct((rows, 2 * wide), BF16),) * steps,
+        in_specs=[pl.BlockSpec(memory_space=pltpu.SMEM), vmem_spec],
+        out_specs=(vmem_spec,) * steps,
+        compiler_params=pltpu.CompilerParams(vmem_limit_bytes=VMEM_LIMIT),
+        cost_estimate=pl.CostEstimate(
+            flops=4 * steps * rows * total * wide,
+            bytes_accessed=2 * (total * width + steps * rows * 2 * wide),
+            transcendentals=0,
+        ),
+    )(place, gathered)
+
+
+def rows_kernel(*refs):
+    parts, order, weights, refs = refs[:8], refs[8], refs[9:17], refs[17:]
+    (_m, back_ref, xd_out, act_out, g_gate, g_up, g_down,
+     w_all, xd, acts, g_all, r_sem, w_sem, xd_sem, act_sem, g_sem) = refs
+    share = weights[0].shape[1]
     width = 4 * share
-    rows = xd.shape[1]
-    pairs = rows_ref.shape[0] // (3 * GROUP)
-    plain = pairs * GROUP
-    sources = (w_pair.at[0], w_pair.at[1], w_own, w_xl)
-    loads = [
-        pltpu.make_async_copy(src, w_all.at[:, pl.ds(i * share, share)], w_sem.at[i])
-        for i, src in enumerate(sources)
+    feature = back_ref.shape[1]
+    size = parts[0].shape[0]
+    arrivals = [
+        pltpu.make_async_copy(
+            part.at[:, pl.ds(side * feature, feature)], xd.at[side, pl.ds(i * size, size)], r_sem.at[2 * i + side]
+        )
+        for i, part in enumerate(parts)
+        for side in range(2)
     ]
+    for arrival in arrivals:
+        arrival.start()
+    loads = []
+    for i, source in enumerate(weights):
+        first, many = (2, 1) if i % 2 else (0, 2)
+        loads.append(
+            pltpu.make_async_copy(
+                source, w_all.at[pl.ds(first, many), pl.ds(i // 2 * share, share)], w_sem.at[i]
+            )
+        )
     for load in loads:
         load.start()
-
-    upper = lax.broadcasted_iota(jnp.int32, (GROUP, rows_ref.shape[1]), 0) < GROUP // 2
-
-    def part(p, carry):
-        base = pl.multiple_of(p * 3 * GROUP, GROUP)
-        first = rows_ref[pl.ds(base, GROUP), :]
-        last = rows_ref[pl.ds(base + 2 * GROUP, GROUP), :]
-        to = pl.ds(pl.multiple_of(p * GROUP, GROUP), GROUP)
-        xd[0, to, :] = jnp.where(upper, first, last)
-        xd[1, to, :] = rows_ref[pl.ds(base + GROUP, GROUP), :]
-        mixed[to, :] = jnp.where(upper, last, first)
-        return carry
-
-    lax.fori_loop(0, pairs, part, 0)
-    order = mixed_order(plain)
-    for n in range(0, rows_ref.shape[1], LANES):
-        sorted_rows = dot_nn(order, mixed[:, n:n + LANES]).astype(BF16)
-        xd[0, plain:, n:n + LANES] = sorted_rows[:plain // 2]
-        xd[1, plain:, n:n + LANES] = sorted_rows[plain // 2:]
+    for arrival in arrivals:
+        arrival.wait()
     xd_store = pltpu.make_async_copy(xd, xd_out, xd_sem)
     xd_store.start()
 
     done = 0
     for f in range(0, width, CHUNK):
         while done * share < f + CHUNK:
-            loads[done].wait()
+            loads[2 * done].wait()
+            loads[2 * done + 1].wait()
             done += 1
         a = dot_nt(xd[0], w_all[0, f:f + CHUNK, :])
         u = dot_nt(xd[0], w_all[1, f:f + CHUNK, :])
@@ -110,55 +154,47 @@
 
     stores = []
     for i, (side, target) in enumerate(zip((0, 0, 1), (g_gate, g_up, g_down))):
-        for n in range(0, rows_ref.shape[1], LANES):
+        for n in range(0, feature, LANES):
             g_all[i, :, n:n + LANES] = dot_tn(
                 acts[i, :, :2 * share], xd[side, :, n:n + LANES]
             ).astype(BF16)
         stores.append(pltpu.make_async_copy(g_all.at[i], target, g_sem.at[i]))
         stores[i].start()
 
-    cut = lax.broadcasted_iota(jnp.int32, (GROUP, LANES), 0) < GROUP // 2
-    for n in range(0, rows_ref.shape[1], LANES):
+    for n in range(0, feature, LANES):
         o = dot_nn(acts[2], w_all[2, :, n:n + LANES]).astype(BF16)
         dx = (
             dot_nn(acts[0], w_all[0, :, n:n + LANES]) + dot_nn(acts[1], w_all[1, :, n:n + LANES])
         ).astype(BF16)
-        blend = dot_tn(order, jnp.concatenate([o[plain:], dx[plain:]])).astype(BF16)
-        for p in range(pairs):
-            o_part = o[p * GROUP:(p + 1) * GROUP]
-            m_part = blend[p * GROUP:(p + 1) * GROUP]
-            base = p * 3 * GROUP
-            back_ref[base:base + GROUP, n:n + LANES] = jnp.where(cut, o_part, m_part)
-            back_ref[base + GROUP:base + 2 * GROUP, n:n + LANES] = dx[p * GROUP:(p + 1) * GROUP]
-            back_ref[base + 2 * GROUP:base + 3 * GROUP, n:n + LANES] = jnp.where(cut, m_part, o_part)
+        back_ref[:, n:n + LANES] = dot_nn(order[...], jnp.concatenate([o, dx])).astype(BF16)
     xd_store.wait()
     act_store.wait()
     for store in stores:
         store.wait()
 
 
-def rows_step(rows, w_own, w_xl, w_pair, mv_xl):
-    total, feature = rows.shape
+def rows_step(parts, order, weights, m_xl):
+    total = order.shape[0]
+    _, share, feature = weights[0][0].shape
     half = total // 2
-    share = w_own.shape[1]
     any_spec = pl.BlockSpec(memory_space=pl.ANY)
     vmem_spec = pl.BlockSpec(memory_space=pltpu.VMEM)
     return pl.pallas_call(
         rows_kernel,
         out_shape=(
-            jax.ShapeDtypeStruct(rows.shape, BF16),
+            jax.ShapeDtypeStruct((total, feature), BF16),
             jax.ShapeDtypeStruct((2, half, feature), BF16),
             jax.ShapeDtypeStruct((3, half, 2 * share), BF16),
         ) + (jax.ShapeDtypeStruct((2 * share, feature), BF16),) * 3,
-        in_specs=[vmem_spec] + [any_spec] * 4,
+        in_specs=[any_spec] * 8 + [vmem_spec] + [any_spec] * 9,
         out_specs=(vmem_spec,) + (any_spec,) * 5,
         scratch_shapes=[
             pltpu.VMEM((3, 4 * share, feature), BF16),
             pltpu.VMEM((2, half, feature), BF16),
-            pltpu.VMEM((total // 3, feature), BF16),
             pltpu.VMEM((3, half, 4 * share), BF16),
             pltpu.VMEM((3, 2 * share, feature), BF16),
-            pltpu.SemaphoreType.DMA((4,)),
+            pltpu.SemaphoreType.DMA((16,)),
+            pltpu.SemaphoreType.DMA((8,)),
             pltpu.SemaphoreType.DMA,
             pltpu.SemaphoreType.DMA,
             pltpu.SemaphoreType.DMA((3,)),
@@ -169,10 +205,10 @@
             bytes_accessed=half * feature,
             transcendentals=0,
         ),
-    )(rows, w_own, w_xl, w_pair, mv_xl)
-
-
-def grads_kernel(flag_ref, xd_ref, act_ref, core_gate, core_up, core_down, *outs):
+    )(*parts, order, *[array for pair in weights for array in pair], m_xl)
+
+
+def grads_kernel(flag_ref, xd_ref, act_ref, core_gate, core_up, core_down, _mv, *outs):
     share = core_gate.shape[0] // 2
     moved = flag_ref[0] != 0
     for i, (side, core_ref) in enumerate(zip((0, 0, 1), (core_gate, core_up, core_down))):
@@ -185,7 +221,7 @@
         outs[3 + i][...] = other.astype(BF16)
 
 
-def grads_step(flag, xd, acts, core):
+def grads_step(flag, xd, acts, core, mv_xl):
     _, half, feature = xd.shape
     share = core[0].shape[0] // 2
     out = jax.ShapeDtypeStruct((share, feature), BF16)
@@ -198,6 +234,7 @@
             pl.BlockSpec((2, half, LANES), lambda n: (0, 0, n)),
             pl.BlockSpec(acts.shape, lambda n: (0, 0, 0)),
             *[pl.BlockSpec((2 * share, LANES), lambda n: (0, n))] * 3,
+            pl.BlockSpec(memory_space=pl.ANY),
         ],
         out_specs=(pl.BlockSpec((share, LANES), lambda n: (0, n)),) * 6,
         compiler_params=pltpu.CompilerParams(vmem_limit_bytes=VMEM_LIMIT),
@@ -206,7 +243,7 @@
             bytes_accessed=2 * (2 * half * feature + 12 * share * feature),
             transcendentals=0,
         ),
-    )(flag, xd, acts, *core)
+    )(flag, xd, acts, *core, mv_xl)
 
 
 def adam_kernel(flag_ref, keep_ref, recv_ref, *refs):
@@ -289,21 +326,41 @@
     slots = 2 * CAP
 
     top = routes.shape[1]
-    named = jnp.concatenate([routes.astype(F32), route_weights], axis=1)
-    named_other = swap(named, "xh")
-    tokens_other = swap(tokens, "xh")
-    cotangent_other = swap(cotangent, "xh")
-    source = jnp.concatenate([tokens, cotangent, tokens_other, cotangent_other])
-
-    w_own = jnp.concatenate([gate_up[0], down])
-    w_first = after(w_own, tokens_other, cotangent_other, named_other)
-    w_xl = swap(w_first, "xl")
-    w_pair = swap(jnp.stack([w_own, w_xl]), "core")
-    mv_xl = swap(after(jnp.concatenate([gate_up_m[0, :1], gate_up_v[0, :1]]), w_xl), "xl")
-
-    both = jnp.stack([named, named_other])
+    meta = jnp.concatenate([routes.astype(BF16), *split_three(route_weights)], axis=1)
+    meta = jnp.pad(meta, ((0, 0), (0, META - 4 * top)))
+    packed = jnp.concatenate([tokens, cotangent, meta], axis=1)
+    packed_other = swap(packed, "xh")
+    y_index = lax.axis_index("y")
+    place = jnp.stack([half * rings + lax.axis_index("z"), y_index]).astype(jnp.int32)
+    y_count = lax.axis_size("y")
+    up_own, down_own = gate_up[0], down
+    down_xl = swap(down_own, "xl")
+    up_xl = swap(after(up_own, down_xl), "xl")
+    parts_in, gathered = [], None
+    for tile in (packed, packed_other):
+        if gathered is not None:
+            tile = after(tile, gathered)
+        gathered = lax.all_gather(tile, "z", axis=0, tiled=True)
+        gathered = after(gathered, *(parts_in[1:] or [down_xl]))
+        picked = pick_step(place, gathered, y_count)
+        parts_in.append(picked[0])
+        for step in range(1, y_count):
+            parts_in.append(
+                lax.ppermute(picked[step], "y", [(i, (i + step) % y_count) for i in range(y_count)])
+            )
+
+    m_xl = swap(after(gate_up_m[0, :1], up_xl), "xl")
+    v_xl = swap(after(gate_up_v[0, :1], m_xl), "xl")
+    others_in = [m_xl, *parts_in[-3:]]
+    weights = (
+        (swap(up_own, "core"), swap(down_own, "core")),
+        (swap(after(up_xl, *others_in), "core"), swap(after(down_xl, *others_in), "core")),
+        (up_own, down_own),
+        (up_xl, down_xl),
+    )
+    both = jnp.stack([meta, packed_other[:, 2 * feature:]]).astype(F32)
     both_routes = both[:, :, :top].astype(jnp.int32)
-    both_weights = both[:, :, top:]
+    both_weights = both[:, :, top:2 * top] + both[:, :, 2 * top:3 * top] + both[:, :, 3 * top:4 * top]
     ring_ids = jnp.arange(rings, dtype=jnp.int32)[:, None, None]
     hit = [both_routes[:, :, k] == half * rings + ring_ids for k in range(top)]
     used = sum(h.astype(jnp.int32) for h in hit)
@@ -318,33 +375,35 @@
 
     lane_kind = jnp.arange(4 * count, dtype=jnp.int32) // count % 2
     row = jnp.arange(2 * slots, dtype=jnp.int32)
-    row = jnp.where(ring % 2 == 0, row, jnp.where(row < 8, row + 16, jnp.where(row < 16, row, row - 16)))
-    row_kind = (row >= 12).astype(jnp.int32)
-    row_slot = jnp.where(row < 12, row, jnp.where(row < 16, row - 4, row - 16))
+    row_kind = row // slots
+    row_slot = row % slots
     pick = (on_lanes(slot) == row_slot[:, None]) & (lane_kind == row_kind[:, None])
     lane_scale = jnp.where(lane_kind == 0, on_lanes(scale), 1.0)
-    row_scale = jnp.sum(jnp.where(pick, on_lanes(scale), 0.0), axis=2)
-    factor = jnp.where(row_kind == 0, 1.0, row_scale).reshape(-1, 1)
-    pick_b = pick.astype(BF16).reshape(rings * 2 * slots, 4 * count)
-    send = (dot_nn(pick_b, source) * factor).astype(BF16).reshape(rings, 2 * slots, feature)
-
-    recv = lax.all_to_all(send, RINGS, split_axis=0, concat_axis=0, tiled=True)
-    back_send, xd, acts, *g_pair = rows_step(recv.reshape(-1, feature), w_own, w_xl, w_pair, mv_xl)
+
+    place_of = jnp.arange(rings * 2 * slots, dtype=jnp.int32)
+    ring_of, within = place_of // (2 * slots), place_of % (2 * slots)
+    slot_of = within % slots
+    z_count = lax.axis_size("z")
+    step_of = (y_index - ring_of // z_count) % y_count
+    index = slot_of // CAP * y_count + step_of
+    index = (index * z_count + ring_of % z_count) * CAP + slot_of % CAP + within // slots * (rings * slots)
+    order = (index[:, None] == jnp.arange(rings * 2 * slots, dtype=jnp.int32)).astype(BF16)
+    back_send, xd, acts, *g_pair = rows_step(parts_in, order, weights, m_xl)
 
     g_core = [swap(g, "core") for g in g_pair]
     back = lax.all_to_all(
-        back_send.reshape(recv.shape), RINGS, split_axis=0, concat_axis=0, tiled=True
+        after(back_send, g_core[0]).reshape(rings, 2 * slots, feature), RINGS, split_axis=0, concat_axis=0, tiled=True
     ).reshape(-1, feature)
-    parts = grads_step(flag, xd, acts, g_core)
+    parts = grads_step(flag, xd, acts, g_core, v_xl)
     others = [swap(parts[3], "xl"), swap(parts[4], "xl")]
     new_gate = adam_step(flag, (parts[0], ()), (others[0], ()), (gate_up, (0, 0)), (gate_up_m, (0, 0)),
-                         (gate_up_v, (0, 0)), (w_xl, (0,)), (mv_xl, (0,)), (mv_xl, (1,)))
+                         (gate_up_v, (0, 0)), (up_xl, (0,)), (m_xl, (0,)), (v_xl, (0,)))
     others.append(swap(after(parts[5], new_gate), "xl"))
     gate_other = lax.ppermute(new_gate, ("xh", "xl"), [(0, 3), (3, 0), (1, 2), (2, 1)])
     new_up = adam_step(flag, (parts[1], ()), (others[1], ()), (gate_up, (0, 1)), (gate_up_m, (0, 1)),
                        (gate_up_v, (0, 1)))
     arrived = [new_gate, gate_other, new_up, swap(new_up, "xh")]
-    new_gate_up = settle(flag, arrived, mv_xl)
+    new_gate_up = settle(flag, arrived, v_xl)
     new_down = adam_step(flag, (parts[2], ()), (others[2], ()), (down, (0,)), (down_m, (0,)),
                          (down_v, (0,)))
     down_other = swap(new_down, "xh")

time: 254 us -> 299 us (1.18)
  between operations: 1.58 us -> 15 us
  waiting for transfers between devices: 141 us -> 154 us
  local copies, waits for them, and re-layouts: 4.17 us -> 15.3 us
  Pallas kernels: 45.8 us -> 55 us
  other arithmetic: 14.7 us -> 7.61 us
  starting transfers between devices: 41.3 us -> 46.6 us
    all_gather x0 -> x2, waiting for transfers between devices: none -> 31.5 us  [body(): gathered = lax.all_gather(tile, 'z', axis=0, tiled=True)]
    ppermute x15 -> x18, waiting for transfers between devices: 141 us -> 114 us  [swap(): return lax.ppermute(block, axis, [(0, 1), (1, 0)])]
    all_to_all x2 -> x1, starting transfers between devices: 22.5 us -> 6.6 us  [body(): lax.all_to_all(after(back_send, g_core[0]).reshape(rings, 2 * slots, feat...]
    ppermute x15 -> x18, starting transfers between devices: 17.8 us -> 28.4 us  [swap(): return lax.ppermute(block, axis, [(0, 1), (1, 0)])]
    ppermute x0 -> x6, starting transfers between devices: none -> 9.61 us  [body(): lax.ppermute(picked[step], 'y', [(i, (i + step) % y_count) for i in range...]
    pallas_call x1 -> x3, Pallas kernels: 19.2 us -> 28.5 us  [the longest x1 21.5 us: rows_step(): pl.pallas_call(rows_kernel, out_shape=(jax.ShapeDtypeStruct((total, featu...]
    unnamed x32 -> x59, local copies, waits for them, and re-layouts: 3.86 us -> 12.6 us
    another operation x3 -> x2, other arithmetic: 9.29 us -> 0.7 us  [the longest x1 0.62 us: body(): jnp.stack([half * rings + lax.axis_index('z'), y_index]).astype(jnp.int32)]
  transfers between devices with their start and end apart: 18 -> 28, of which waited for: 11 -> 15; matrix products, arithmetic and copies ran while one was open for 7% -> 3% of each run, Pallas kernels for 10% -> 11%
where the time goes in v5:
time: 299 us; the launch traced here: 297 us
  waiting for transfers between devices  154 us (52%)
  Pallas kernels  55 us (18%)
  starting transfers between devices  46.6 us (16%)
  local copies, waits for them, and re-layouts  15.3 us (5%)
  between operations  15 us (5%)
  other arithmetic  7.61 us (3%)
  matrix products  3.54 us (1%)
    ppermute x18, waiting for transfers between devices, swap(): return lax.ppermute(block, axis, [(0, 1), (1, 0)])  114 us
    all_gather x2, waiting for transfers between devices, body(): gathered = lax.all_gather(tile, 'z', axis=0, tiled=True)  31.5 us
    ppermute x18, starting transfers between devices, swap(): return lax.ppermute(block, axis, [(0, 1), (1, 0)])  28.4 us
    pallas_call x1, Pallas kernels, rows_step(): pl.pallas_call(rows_kernel, out_shape=(jax.ShapeDtypeStruct((total, featu...  21.5 us
    pallas_call x3, Pallas kernels, adam_step(): pl.pallas_call(adam_kernel, grid=(steps,), out_shape=jax.ShapeDtypeStruct...  14.3 us
    unnamed x59, local copies, waits for them, and re-layouts  12.6 us
    ppermute x6, starting transfers between devices, body(): lax.ppermute(picked[step], 'y', [(i, (i + step) % y_count) for i in range...  9.61 us
    ppermute x6, waiting for transfers between devices, body(): lax.ppermute(picked[step], 'y', [(i, (i + step) % y_count) for i in range...  8.16 us
  transfers between devices with their start and end apart: 28, of which 15 were waited for; matrix products, arithmetic and copies ran while one was open for 3% of the time, Pallas kernels for 11%

profile of v5, /device:TPU:1, one launch (start us, length us, event | category | flops | bytes accessed | tf_op | source)
XLA Modules:
  0.0 297.0 jit_solution(12145242146894879081)
XLA Ops:
  10.2 1.8 pad_maximum_fusion
  12.1 2.1 collective-permute-start.1
  14.3 2.5 collective-permute-start
  16.7 13.8 %collective-permute-done.1.refs_16_ = bf16[1,192,2048]{2,1,0:T(8,128)(2,1)} collective-permute-done((bf16[1,192,2048]{2,1,0:T(8,128)(2,1)}, bf16[1,192,2048]{2,1,0:T(8,128)(2,1)}, u32[]{:S(2)}, u32[]{:S(2)}) %collective-permute-start.1) | collective-permute-done | bytes 786464 | tf_op jit(solution)/shard_map/ppermute | solution.py:21
  30.5 23.1 %all-gather.3.cloned.1.call-done.g_ref = bf16[256,4224]{1,0:T(8,128)(2,1)} async-done(((bf16[32,4224]{1,0:T(8,128)(2,1)}), bf16[256,4224]{1,0:T(8,128)(2,1)}) %all-gather.3.cloned.1.call-update) | async-done | bytes 2162704 | tf_op jit(solution)/shard_map/all_gather | solution.py:343
  54.3 1.3 collective-permute-start.10
  56.2 3.5 %shard_map.138 = (bf16[48,4096]{1,0:T(8,128)(2,1)}, bf16[48,4096]{1,0:T(8,128)(2,1)}, bf16[48,4096]{1,0:T(8,128)(2,1)}, bf16[48,4096]{1,0:T(8,128)(2,1)}) custom-call(s32[2]{0:T(128)} %pad_add_fusion.1.place_ref, bf16[256,4224]{1,0:T(8,128)(2,1)} %all-gather.3.cloned.1.call-done.g_ref), custom_call_target="tpu_custom_call" | custom-call | flops 402653184 | bytes 3735552 | tf_op jit(solution)/shard_map/pallas_call | solution.py:93
  59.7 1.2 collective-permute-start.2
  60.9 2.4 collective-permute-start.3
  63.4 1.2 collective-permute-start.4
  64.5 0.9 slice_bitcast_fusion.1
  65.5 20.5 %collective-permute-done.10.refs_15_.refs_3_ = bf16[2,192,2048]{2,1,0:T(8,128)(2,1)} collective-permute-done((bf16[2,192,2048]{2,1,0:T(8,128)(2,1)}, bf16[2,192,2048]{2,1,0:T(8,128)(2,1)}, u32[]{:S(2)}, u32[]{:S(2)}) %collective-permute-start.10) | collective-permute-done | bytes 1572896 | tf_op jit(solution)/shard_map/ppermute | solution.py:21
  86.0 1.2 collective-permute-start.11
  87.2 8.4 %all-gather.5.cloned.1.call-done.g_ref = bf16[256,4224]{1,0:T(8,128)(2,1)} async-done(((bf16[32,4224]{1,0:T(8,128)(2,1)}), bf16[256,4224]{1,0:T(8,128)(2,1)}) %all-gather.5.cloned.1.call-update) | async-done | bytes 2162704 | tf_op jit(solution)/shard_map/all_gather | solution.py:343
  95.6 3.5 %shard_map.139 = (bf16[48,4096]{1,0:T(8,128)(2,1)}, bf16[48,4096]{1,0:T(8,128)(2,1)}, bf16[48,4096]{1,0:T(8,128)(2,1)}, bf16[48,4096]{1,0:T(8,128)(2,1)}) custom-call(s32[2]{0:T(128)} %pad_add_fusion.1.place_ref, bf16[256,4224]{1,0:T(8,128)(2,1)} %all-gather.5.cloned.1.call-done.g_ref), custom_call_target="tpu_custom_call" | custom-call | flops 402653184 | bytes 3735552 | tf_op jit(solution)/shard_map/pallas_call | solution.py:93
  99.1 1.2 collective-permute-start.5
  100.3 2.4 collective-permute-start.6
  102.8 1.1 collective-permute-start.7
  103.9 5.4 %collective-permute-start.8 = (bf16[2,192,2048]{2,1,0:T(8,128)(2,1)S(1)}, bf16[2,192,2048]{2,1,0:T(8,128)(2,1)S(1)}, u32[]{:S(2)}, u32[]{:S(2)}) collective-permute-start(bf16[2,192,2048]{2,1,0:T(8,128)(2,1)S(1)} %bitcast.53), channel_id=1, source_target_pairs={{0,1},{1,0},{2,3},{3,2},{4,5},{5,4},{6,7},{7,6},{8,9},{9,8},{10,11... | collective-permute-start | bytes 4718600 | tf_op jit(solution)/shard_map/ppermute | solution.py:21
  109.3 6.3 %collective-permute-done.6.refs_6_ = bf16[48,4096]{1,0:T(8,128)(2,1)S(1)} collective-permute-done((bf16[48,4096]{1,0:T(8,128)(2,1)}, bf16[48,4096]{1,0:T(8,128)(2,1)S(1)}, u32[]{:S(2)}, u32[]{:S(2)}) %collective-permute-start.6) | collective-permute-done | bytes 393248 | tf_op jit(solution)/shard_map/ppermute | solution.py:349
  115.6 1.8 collective-permute-done.7.refs_7_
  118.2 4.0 %collective-permute-start.12 = (bf16[2,192,2048]{2,1,0:T(8,128)(2,1)}, bf16[2,192,2048]{2,1,0:T(8,128)(2,1)S(1)}, u32[]{:S(2)}, u32[]{:S(2)}) collective-permute-start(bf16[2,192,2048]{2,1,0:T(8,128)(2,1)} %collective-permute-done.10.refs_15_.refs_3_), channel_id=1, source_target_pairs={{0,1},{1,0},{2,3},{3,2},{4,5},{5,4},{6,7},{7,6},{8,9},{9,8},{10,11... | collective-permute-start | bytes 4718600 | tf_op jit(solution)/shard_map/ppermute | solution.py:21
  122.8 1.3 fusion.refs_8_
  124.1 2.5 collective-permute-done.9.refs_10_
  126.6 1.1 collective-permute-done.13.refs_12_
  129.2 21.5 %shard_map.140 = (bf16[768,2048]{1,0:T(8,128)(2,1)}, bf16[2,384,2048]{2,1,0:T(8,128)(2,1)}, bf16[3,384,384]{2,1,0:T(8,128)(2,1)}, bf16[384,2048]{1,0:T(8,128)(2,...) custom-call(bf16[48,4096]{1,0:T(8,128)(2,1)} %get-tuple-element.35.refs_0_, bf16[48,4096]{1,0:T(8,128)(2,1)} %copy-done.18, ...), custom_call_target="tpu_custom_call" | custom-call | flops 150994944 | bytes 786432 | tf_op jit(solution)/shard_map/pallas_call | solution.py:182
  151.2 3.2 %collective-permute-done.14.core_gate = bf16[384,2048]{1,0:T(8,128)(2,1)S(1)} collective-permute-done((bf16[384,2048]{1,0:T(8,128)(2,1)}, bf16[384,2048]{1,0:T(8,128)(2,1)S(1)}, u32[]{:S(2)}, u32[]{:S(2)}) %collective-permute-start.14) | collective-permute-done | bytes 1572896 | tf_op jit(solution)/shard_map/ppermute | solution.py:21
  154.5 1.1 copy-done.5
  155.6 6.6 %all-to-all-start = ((bf16[32,24,2048]{2,1,0:T(8,128)(2,1)}), bf16[32,24,2048]{2,1,0:T(8,128)(2,1)}, u32[]{:S(2)}, u32[]{:S(2)}) async-start(bf16[32,24,2048]{2,1,0:T(8,128)(2,1)} %bitcast.54), calls=%async_computation | async-start | bytes 6291456 | tf_op jit(solution)/shard_map/all_to_all | solution.py:394
  164.9 1.3 collective-permute-start.18
  167.4 16.4 %collective-permute-done.18._mv.refs_5_.refs_4_ = bf16[1,192,2048]{2,1,0:T(8,128)(2,1)S(1)} collective-permute-done((bf16[1,192,2048]{2,1,0:T(8,128)(2,1)S(1)}, bf16[1,192,2048]{2,1,0:T(8,128)(2,1)S(1)}, u32[]{:S(2)}, u32[]{:S(2)}) %collective-permute-start.18) | collective-permute-done | bytes 786464 | tf_op jit(solution)/shard_map/ppermute | solution.py:21
  185.8 7.3 %shard_map.141 = (bf16[192,2048]{1,0:T(8,128)(2,1)}, bf16[192,2048]{1,0:T(8,128)(2,1)}, bf16[192,2048]{1,0:T(8,128)(2,1)}, bf16[192,2048]{1,0:T(8,128)(2,1)}, bf...) custom-call(s32[1]{0:T(128)} %bitcast.18.flag_ref, bf16[2,384,2048]{2,1,0:T(8,128)(2,1)} %get-tuple-element.52.xd_ref, ...), custom_call_target="tpu_custom_call" | custom-call | flops 1811939328 | bytes 12582912 | tf_op jit(solution)/shard_map/pallas_call | solution.py:228
  193.0 1.3 collective-permute-start.19
  195.3 16.1 %collective-permute-done.19.recv_ref = bf16[192,2048]{1,0:T(8,128)(2,1)S(1)} collective-permute-done((bf16[192,2048]{1,0:T(8,128)(2,1)}, bf16[192,2048]{1,0:T(8,128)(2,1)S(1)}, u32[]{:S(2)}, u32[]{:S(2)}) %collective-permute-start.19) | collective-permute-done | bytes 786464 | tf_op jit(solution)/shard_map/ppermute | solution.py:21
  212.2 5.2 %shard_map.142.refs_0_ = bf16[192,2048]{1,0:T(8,128)(2,1)} custom-call(s32[1]{0:T(128)} %bitcast.18.flag_ref, bf16[192,2048]{1,0:T(8,128)(2,1)} %get-tuple-element.57.keep_ref, bf16[192,2048]{1,0:T(8,128)(2,1)} %copy-done.14, bf16[1,2,192,2048]{3,2,1,0:T(8,128)(2,1)} %refs_0_.4, bf16[1,2,192,2048]{3,2,1,0:T(8,128)(2,1)} %refs_1_.4, ...), custom_call_target="tpu_custom_call" | custom-call | flops 7864320 | bytes 7077888 | tf_op jit(solution)/shard_map/pallas_call | solution.py:269
  217.4 1.3 collective-permute-start.23
  219.1 1.9 collective-permute-start.20
  220.9 7.2 %collective-permute-done.21.recv_ref = bf16[192,2048]{1,0:T(8,128)(2,1)S(1)} collective-permute-done((bf16[192,2048]{1,0:T(8,128)(2,1)}, bf16[192,2048]{1,0:T(8,128)(2,1)S(1)}, u32[]{:S(2)}, u32[]{:S(2)}) %collective-permute-start.21) | collective-permute-done | bytes 786464 | tf_op jit(solution)/shard_map/ppermute | solution.py:21
  229.0 4.5 %shard_map.143.refs_2_ = bf16[192,2048]{1,0:T(8,128)(2,1)} custom-call(s32[1]{0:T(128)} %bitcast.18.flag_ref, bf16[192,2048]{1,0:T(8,128)(2,1)} %get-tuple-element.59.keep_ref, bf16[192,2048]{1,0:T(8,128)(2,1)} %copy-done.12, bf16[1,2,192,2048]{3,2,1,0:T(8,128)(2,1)} %refs_0_.4, bf16[1,2,192,2048]{3,2,1,0:T(8,128)(2,1)} %refs_1_.4, ...), custom_call_target="tpu_custom_call" | custom-call | flops 7864320 | bytes 4718592 | tf_op jit(solution)/shard_map/pallas_call | solution.py:269
  233.6 2.7 collective-permute-start.22
  236.3 8.6 %collective-permute-done.23.recv_ref = bf16[192,2048]{1,0:T(8,128)(2,1)S(1)} collective-permute-done((bf16[192,2048]{1,0:T(8,128)(2,1)S(1)}, bf16[192,2048]{1,0:T(8,128)(2,1)S(1)}, u32[]{:S(2)}, u32[]{:S(2)}) %collective-permute-start.23) | collective-permute-done | bytes 786464 | tf_op jit(solution)/shard_map/ppermute | solution.py:21
  245.8 4.6 %shard_map.145.refs_0_ = bf16[192,2048]{1,0:T(8,128)(2,1)} custom-call(s32[1]{0:T(128)} %bitcast.18.flag_ref, bf16[192,2048]{1,0:T(8,128)(2,1)} %get-tuple-element.61.keep_ref, bf16[192,2048]{1,0:T(8,128)(2,1)} %copy-done.13, bf16[1,192,2048]{2,1,0:T(8,128)(2,1)} %refs_0_.5, bf16[1,192,2048]{2,1,0:T(8,128)(2,1)} %refs_1_.5, bf16[1,192,2048]{2,1,0:T(8,128)(2,1)} %refs_2_.5), custom_call_target="tpu_custom_call" | custom-call | flops 7864320 | bytes 4718592 | tf_op jit(solution)/shard_map/pallas_call | solution.py:269
  250.4 2.7 collective-permute-start.24
  253.1 3.3 %fusion.3 = f32[384,2048]{1,0:T(8,128)S(1)} fusion(bf16[768,2048]{1,0:T(8,128)(2,1)} %bitcast.17, bf16[768,128]{1,0:T(8,128)(2,1)S(1)} %get-tuple-element.93, bf16[768,128]{1,0:T(8,128)(2,1)S(1)} %get-tuple-element.94, bf16[768,128]{1,0:T(8,128)(2,1)S(1)} %get-tuple-element.92), kind=kOutput, calls=%fused_computation.9 | convolution fusion | flops 1209729024 | bytes 6881280 | tf_op jit(solution)/shard_map/dot_general | solution.py:43
  257.0 6.9 %collective-permute-done.22.refs_3_ = bf16[192,2048]{1,0:T(8,128)(2,1)S(1)} collective-permute-done((bf16[192,2048]{1,0:T(8,128)(2,1)}, bf16[192,2048]{1,0:T(8,128)(2,1)S(1)}, u32[]{:S(2)}, u32[]{:S(2)}) %collective-permute-start.22) | collective-permute-done | bytes 786464 | tf_op jit(solution)/shard_map/ppermute | solution.py:21
  265.7 2.8 shard_map.144
  268.5 17.9 %collective-permute-done.15 = bf16[64,2048]{1,0:T(8,128)(2,1)S(1)} collective-permute-done((bf16[64,2048]{1,0:T(8,128)(2,1)S(1)}, bf16[64,2048]{1,0:T(8,128)(2,1)S(1)}, u32[]{:S(2)}, u32[]{:S(2)}) %collective-permute-start.15) | collective-permute-done | bytes 262176 | tf_op jit(solution)/shard_map/ppermute | solution.py:21
  288.1 2.1 shard_map.146
  (119 shorter events, 20.8 us)
Async XLA Ops:
  7.2 46.4 %all-gather.3.cloned.1.call-start = ((), (), s32[]{:S(2)}) async-start(), calls=%async_computation.1 | async-start | bytes 2433024 | tf_op jit(solution)/shard_map/all_gather | solution.py:343
  10.2 54.3 %copy-start.1 = (bf16[1,2,192,2048]{3,2,1,0:T(8,128)(2,1)S(1)}, bf16[1,2,192,2048]{3,2,1,0:T(8,128)(2,1)}, u32[]{:S(2)}) copy-start(bf16[1,2,192,2048]{3,2,1,0:T(8,128)(2,1)} %refs_1_.4) | copy-start | bytes 4718596
  12.1 83.5 %all-gather.5.cloned.1.call-start = ((), (), s32[]{:S(2)}) async-start(), calls=%async_computation.2 | async-start | bytes 2433024 | tf_op jit(solution)/shard_map/all_gather | solution.py:343
  12.1 18.4 %collective-permute-start.1 = (bf16[1,192,2048]{2,1,0:T(8,128)(2,1)}, bf16[1,192,2048]{2,1,0:T(8,128)(2,1)}, u32[]{:S(2)}, u32[]{:S(2)}) collective-permute-start(bf16[1,192,2048]{2,1,0:T(8,128)(2,1)} %refs_0_.5), channel_id=1, source_target_pairs={{0,2},{2,0},{1,3},{3,1},{4,6},{6,4},{5,7},{7,5},{8,10},{10,8},{9,1... | collective-permute-start | bytes 2359304 | tf_op jit(solution)/shard_map/ppermute | solution.py:21
  14.3 39.3 %collective-permute-start = (bf16[32,4224]{1,0:T(8,128)(2,1)}, bf16[32,4224]{1,0:T(8,128)(2,1)S(1)}, u32[]{:S(2)}, u32[]{:S(2)}) collective-permute-start(bf16[32,4224]{1,0:T(8,128)(2,1)} %pad_maximum_fusion), channel_id=1, source_target_pairs={{0,128},{128,0},{1,129},{129,1},{2,130},{130,2},{3,131},{131,3},{4... | collective-permute-start | bytes 811016 | tf_op jit(solution)/shard_map/ppermute | solution.py:21
  54.3 31.6 %collective-permute-start.10 = (bf16[2,192,2048]{2,1,0:T(8,128)(2,1)}, bf16[2,192,2048]{2,1,0:T(8,128)(2,1)}, u32[]{:S(2)}, u32[]{:S(2)}) collective-permute-start(bf16[2,192,2048]{2,1,0:T(8,128)(2,1)} %bitcast.51), channel_id=1, source_target_pairs={{0,2},{2,0},{1,3},{3,1},{4,6},{6,4},{5,7},{7,5},{8,10},{10,8},{9,1... | collective-permute-start | bytes 4718600 | tf_op jit(solution)/shard_map/ppermute | solution.py:21
  59.7 27.5 %collective-permute-start.2 = (bf16[48,4096]{1,0:T(8,128)(2,1)}, bf16[48,4096]{1,0:T(8,128)(2,1)S(1)}, u32[]{:S(2)}, u32[]{:S(2)}) collective-permute-start(bf16[48,4096]{1,0:T(8,128)(2,1)} %get-tuple-element.36), channel_id=1, source_target_pairs={{0,32},{32,64},{64,96},{96,0},{1,33},{33,65},{65,97},{97,1},{2,34}... | collective-permute-start | bytes 1179656 | tf_op jit(solution)/shard_map/ppermute | solution.py:349
  60.9 26.3 %collective-permute-start.3 = (bf16[48,4096]{1,0:T(8,128)(2,1)}, bf16[48,4096]{1,0:T(8,128)(2,1)}, u32[]{:S(2)}, u32[]{:S(2)}) collective-permute-start(bf16[48,4096]{1,0:T(8,128)(2,1)} %get-tuple-element.37), channel_id=1, source_target_pairs={{0,64},{32,96},{64,0},{96,32},{1,65},{33,97},{65,1},{97,33},{2,66}... | collective-permute-start | bytes 1179656 | tf_op jit(solution)/shard_map/ppermute | solution.py:349
  63.4 40.6 %copy-start = (bf16[1,2,192,2048]{3,2,1,0:T(8,128)(2,1)S(1)}, bf16[1,2,192,2048]{3,2,1,0:T(8,128)(2,1)}, u32[]{:S(2)}) copy-start(bf16[1,2,192,2048]{3,2,1,0:T(8,128)(2,1)} %refs_0_.4) | copy-start | bytes 4718596
  63.4 23.8 %collective-permute-start.4 = (bf16[48,4096]{1,0:T(8,128)(2,1)}, bf16[48,4096]{1,0:T(8,128)(2,1)}, u32[]{:S(2)}, u32[]{:S(2)}) collective-permute-start(bf16[48,4096]{1,0:T(8,128)(2,1)} %get-tuple-element.38), channel_id=1, source_target_pairs={{0,96},{32,0},{64,32},{96,64},{1,97},{33,1},{65,33},{97,65},{2,98}... | collective-permute-start | bytes 1179656 | tf_op jit(solution)/shard_map/ppermute | solution.py:349
  86.0 23.3 %collective-permute-start.11 = (bf16[1,192,2048]{2,1,0:T(8,128)(2,1)}, bf16[1,192,2048]{2,1,0:T(8,128)(2,1)S(1)}, u32[]{:S(2)}, u32[]{:S(2)}) collective-permute-start(bf16[1,192,2048]{2,1,0:T(8,128)(2,1)} %slice_bitcast_fusion.1), channel_id=1, source_target_pairs={{0,2},{2,0},{1,3},{3,1},{4,6},{6,4},{5,7},{7,5},{8,10},{10,8},{9,1... | collective-permute-start | bytes 2359304 | tf_op jit(solution)/shard_map/ppermute | solution.py:21
  87.2 36.9 %copy-start.18 = (bf16[48,4096]{1,0:T(8,128)(2,1)}, bf16[48,4096]{1,0:T(8,128)(2,1)S(1)}, u32[]{:S(2)}) copy-start(bf16[48,4096]{1,0:T(8,128)(2,1)S(1)} %collective-permute-done.2.refs_1_) | copy-start | bytes 1179652
  99.1 10.2 %collective-permute-start.5 = (bf16[48,4096]{1,0:T(8,128)(2,1)}, bf16[48,4096]{1,0:T(8,128)(2,1)S(1)}, u32[]{:S(2)}, u32[]{:S(2)}) collective-permute-start(bf16[48,4096]{1,0:T(8,128)(2,1)} %get-tuple-element.42), channel_id=1, source_target_pairs={{0,32},{32,64},{64,96},{96,0},{1,33},{33,65},{65,97},{97,1},{2,34}... | collective-permute-start | bytes 1179656 | tf_op jit(solution)/shard_map/ppermute | solution.py:349
  100.3 15.3 %collective-permute-start.6 = (bf16[48,4096]{1,0:T(8,128)(2,1)}, bf16[48,4096]{1,0:T(8,128)(2,1)S(1)}, u32[]{:S(2)}, u32[]{:S(2)}) collective-permute-start(bf16[48,4096]{1,0:T(8,128)(2,1)} %get-tuple-element.43), channel_id=1, source_target_pairs={{0,64},{32,96},{64,0},{96,32},{1,65},{33,97},{65,1},{97,33},{2,66}... | collective-permute-start | bytes 1179656 | tf_op jit(solution)/shard_map/ppermute | solution.py:349
  102.8 14.7 %collective-permute-start.7 = (bf16[48,4096]{1,0:T(8,128)(2,1)}, bf16[48,4096]{1,0:T(8,128)(2,1)S(1)}, u32[]{:S(2)}, u32[]{:S(2)}) collective-permute-start(bf16[48,4096]{1,0:T(8,128)(2,1)} %get-tuple-element.44), channel_id=1, source_target_pairs={{0,96},{32,0},{64,32},{96,64},{1,97},{33,1},{65,33},{97,65},{2,98}... | collective-permute-start | bytes 1179656 | tf_op jit(solution)/shard_map/ppermute | solution.py:349
  103.9 22.7 %collective-permute-start.8 = (bf16[2,192,2048]{2,1,0:T(8,128)(2,1)S(1)}, bf16[2,192,2048]{2,1,0:T(8,128)(2,1)S(1)}, u32[]{:S(2)}, u32[]{:S(2)}) collective-permute-start(bf16[2,192,2048]{2,1,0:T(8,128)(2,1)S(1)} %bitcast.53), channel_id=1, source_target_pairs={{0,1},{1,0},{2,3},{3,2},{4,5},{5,4},{6,7},{7,6},{8,9},{9,8},{10,11... | collective-permute-start | bytes 4718600 | tf_op jit(solution)/shard_map/ppermute | solution.py:21
  109.3 18.5 %copy-start.4 = (bf16[1,192,2048]{2,1,0:T(8,128)(2,1)}, bf16[1,192,2048]{2,1,0:T(8,128)(2,1)S(1)}, u32[]{:S(2)}) copy-start(bf16[1,192,2048]{2,1,0:T(8,128)(2,1)S(1)} %collective-permute-done.11.refs_17_.refs_4_) | copy-start | bytes 2359300
  109.3 18.5 %copy-start.19 = (bf16[48,4096]{1,0:T(8,128)(2,1)}, bf16[48,4096]{1,0:T(8,128)(2,1)S(1)}, u32[]{:S(2)}) copy-start(bf16[48,4096]{1,0:T(8,128)(2,1)S(1)} %collective-permute-done.5.refs_5_) | copy-start | bytes 1179652
  115.6 12.2 %copy-start.20 = (bf16[48,4096]{1,0:T(8,128)(2,1)}, bf16[48,4096]{1,0:T(8,128)(2,1)S(1)}, u32[]{:S(2)}) copy-start(bf16[48,4096]{1,0:T(8,128)(2,1)S(1)} %collective-permute-done.6.refs_6_) | copy-start | bytes 1179652
  118.2 9.5 %collective-permute-start.12 = (bf16[2,192,2048]{2,1,0:T(8,128)(2,1)}, bf16[2,192,2048]{2,1,0:T(8,128)(2,1)S(1)}, u32[]{:S(2)}, u32[]{:S(2)}) collective-permute-start(bf16[2,192,2048]{2,1,0:T(8,128)(2,1)} %collective-permute-done.10.refs_15_.refs_3_), channel_id=1, source_target_pairs={{0,1},{1,0},{2,3},{3,2},{4,5},{5,4},{6,7},{7,6},{8,9},{9,8},{10,11... | collective-permute-start | bytes 4718600 | tf_op jit(solution)/shard_map/ppermute | solution.py:21
  122.3 4.4 %collective-permute-start.9 = (bf16[1,192,2048]{2,1,0:T(8,128)(2,1)}, bf16[1,192,2048]{2,1,0:T(8,128)(2,1)S(1)}, u32[]{:S(2)}, u32[]{:S(2)}) collective-permute-start(bf16[1,192,2048]{2,1,0:T(8,128)(2,1)} %refs_0_.5), channel_id=1, source_target_pairs={{0,1},{1,0},{2,3},{3,2},{4,5},{5,4},{6,7},{7,6},{8,9},{9,8},{10,11... | collective-permute-start | bytes 2359304 | tf_op jit(solution)/shard_map/ppermute | solution.py:21
  122.3 5.5 %collective-permute-start.13 = (bf16[1,192,2048]{2,1,0:T(8,128)(2,1)}, bf16[1,192,2048]{2,1,0:T(8,128)(2,1)S(1)}, u32[]{:S(2)}, u32[]{:S(2)}) collective-permute-start(bf16[1,192,2048]{2,1,0:T(8,128)(2,1)} %collective-permute-done.1.refs_16_), channel_id=1, source_target_pairs={{0,1},{1,0},{2,3},{3,2},{4,5},{5,4},{6,7},{7,6},{8,9},{9,8},{10,11... | collective-permute-start | bytes 2359304 | tf_op jit(solution)/shard_map/ppermute | solution.py:21
  126.6 1.2 copy-start.10
  126.6 1.4 copy-start.6
  127.8 0.9 copy-start.11
  127.8 1.4 copy-start.9
  150.7 3.7 %collective-permute-start.14 = (bf16[384,2048]{1,0:T(8,128)(2,1)}, bf16[384,2048]{1,0:T(8,128)(2,1)S(1)}, u32[]{:S(2)}, u32[]{:S(2)}) collective-permute-start(bf16[384,2048]{1,0:T(8,128)(2,1)} %get-tuple-element.50), channel_id=1, source_target_pairs={{0,1},{1,0},{2,3},{3,2},{4,5},{5,4},{6,7},{7,6},{8,9},{9,8},{10,11... | collective-permute-start | bytes 4718600 | tf_op jit(solution)/shard_map/ppermute | solution.py:21
  154.4 1.1 copy-start.5
  154.4 7.8 %copy-start.28 = (s32[64]{0:T(128)S(1)}, s32[64]{0:T(128)}, u32[]{:S(2)}) copy-start(s32[64]{0:T(128)} %param.15) | copy-start | bytes 772
  154.4 9.2 %copy-start.24 = (bf16[32,8]{1,0:T(8,128)(2,1)S(1)}, bf16[32,8]{1,0:T(8,128)(2,1)}, u32[]{:S(2)}) copy-start(bf16[32,8]{1,0:T(8,128)(2,1)} %copy-done.23) | copy-start | bytes 1540
  154.4 9.2 %copy-start.26 = (bf16[32,8]{1,0:T(8,128)(2,1)S(1)}, bf16[32,8]{1,0:T(8,128)(2,1)}, u32[]{:S(2)}) copy-start(bf16[32,8]{1,0:T(8,128)(2,1)} %copy-done.25) | copy-start | bytes 1540
  154.4 10.4 %copy-start.2 = (bf16[1,2,192,2048]{3,2,1,0:T(8,128)(2,1)S(1)}, bf16[1,2,192,2048]{3,2,1,0:T(8,128)(2,1)}, u32[]{:S(2)}) copy-start(bf16[1,2,192,2048]{3,2,1,0:T(8,128)(2,1)} %refs_2_.4) | copy-start | bytes 4718596
  155.6 97.5 %all-to-all-start = ((bf16[32,24,2048]{2,1,0:T(8,128)(2,1)}), bf16[32,24,2048]{2,1,0:T(8,128)(2,1)}, u32[]{:S(2)}, u32[]{:S(2)}) async-start(bf16[32,24,2048]{2,1,0:T(8,128)(2,1)} %bitcast.54), calls=%async_computation | async-start | bytes 6291456 | tf_op jit(solution)/shard_map/all_to_all | solution.py:394
  163.7 20.1 %collective-permute-start.16 = (bf16[384,2048]{1,0:T(8,128)(2,1)}, bf16[384,2048]{1,0:T(8,128)(2,1)S(1)}, u32[]{:S(2)}, u32[]{:S(2)}) collective-permute-start(bf16[384,2048]{1,0:T(8,128)(2,1)} %get-tuple-element.54), channel_id=1, source_target_pairs={{0,1},{1,0},{2,3},{3,2},{4,5},{5,4},{6,7},{7,6},{8,9},{9,8},{10,11... | collective-permute-start | bytes 4718600 | tf_op jit(solution)/shard_map/ppermute | solution.py:21
  164.7 19.2 %collective-permute-start.17 = (bf16[384,2048]{1,0:T(8,128)(2,1)}, bf16[384,2048]{1,0:T(8,128)(2,1)S(1)}, u32[]{:S(2)}, u32[]{:S(2)}) collective-permute-start(bf16[384,2048]{1,0:T(8,128)(2,1)} %get-tuple-element.55), channel_id=1, source_target_pairs={{0,1},{1,0},{2,3},{3,2},{4,5},{5,4},{6,7},{7,6},{8,9},{9,8},{10,11... | collective-permute-start | bytes 4718600 | tf_op jit(solution)/shard_map/ppermute | solution.py:21
  164.9 18.9 %collective-permute-start.18 = (bf16[1,192,2048]{2,1,0:T(8,128)(2,1)S(1)}, bf16[1,192,2048]{2,1,0:T(8,128)(2,1)S(1)}, u32[]{:S(2)}, u32[]{:S(2)}) collective-permute-start(bf16[1,192,2048]{2,1,0:T(8,128)(2,1)S(1)} %slice_bitcast_fusion), channel_id=1, source_target_pairs={{0,2},{2,0},{1,3},{3,1},{4,6},{6,4},{5,7},{7,5},{8,10},{10,8},{9,1... | collective-permute-start | bytes 2359304 | tf_op jit(solution)/shard_map/ppermute | solution.py:21
  183.8 0.9 copy-start.3
  183.8 1.4 copy-start.7
  183.8 1.9 copy-start.8
  193.0 18.3 %collective-permute-start.19 = (bf16[192,2048]{1,0:T(8,128)(2,1)}, bf16[192,2048]{1,0:T(8,128)(2,1)S(1)}, u32[]{:S(2)}, u32[]{:S(2)}) collective-permute-start(bf16[192,2048]{1,0:T(8,128)(2,1)} %get-tuple-element.58), channel_id=1, source_target_pairs={{0,2},{2,0},{1,3},{3,1},{4,6},{6,4},{5,7},{7,5},{8,10},{10,8},{9,1... | collective-permute-start | bytes 2359304 | tf_op jit(solution)/shard_map/ppermute | solution.py:21
  194.9 33.3 %collective-permute-start.21 = (bf16[192,2048]{1,0:T(8,128)(2,1)}, bf16[192,2048]{1,0:T(8,128)(2,1)S(1)}, u32[]{:S(2)}, u32[]{:S(2)}) collective-permute-start(bf16[192,2048]{1,0:T(8,128)(2,1)} %get-tuple-element.60), channel_id=1, source_target_pairs={{0,2},{2,0},{1,3},{3,1},{4,6},{6,4},{5,7},{7,5},{8,10},{10,8},{9,1... | collective-permute-start | bytes 2359304 | tf_op jit(solution)/shard_map/ppermute | solution.py:21
  212.2 5.2 %copy-start.27 = (bf16[192,2048]{1,0:T(8,128)(2,1)S(1)}, bf16[192,2048]{1,0:T(8,128)(2,1)}, u32[]{:S(2)}) copy-start(bf16[192,2048]{1,0:T(8,128)(2,1)} %get-tuple-element.63) | copy-start | bytes 2359300
  217.4 27.5 %collective-permute-start.23 = (bf16[192,2048]{1,0:T(8,128)(2,1)S(1)}, bf16[192,2048]{1,0:T(8,128)(2,1)S(1)}, u32[]{:S(2)}, u32[]{:S(2)}) collective-permute-start(bf16[192,2048]{1,0:T(8,128)(2,1)S(1)} %copy-done.27), channel_id=1, source_target_pairs={{0,2},{2,0},{1,3},{3,1},{4,6},{6,4},{5,7},{7,5},{8,10},{10,8},{9,1... | collective-permute-start | bytes 2359304 | tf_op jit(solution)/shard_map/ppermute | solution.py:21
  219.1 44.8 %collective-permute-start.20 = (bf16[192,2048]{1,0:T(8,128)(2,1)}, bf16[192,2048]{1,0:T(8,128)(2,1)S(1)}, u32[]{:S(2)}, u32[]{:S(2)}) collective-permute-start(bf16[192,2048]{1,0:T(8,128)(2,1)} %shard_map.142.refs_0_), channel_id=1, source_target_pairs={{0,130},{130,0},{2,128},{128,2},{1,131},{131,1},{3,129},{129,3},{4... | collective-permute-start | bytes 2359304 | tf_op jit(solution)/shard_map/ppermute | solution.py:402
  233.6 30.3 %collective-permute-start.22 = (bf16[192,2048]{1,0:T(8,128)(2,1)}, bf16[192,2048]{1,0:T(8,128)(2,1)S(1)}, u32[]{:S(2)}, u32[]{:S(2)}) collective-permute-start(bf16[192,2048]{1,0:T(8,128)(2,1)} %shard_map.143.refs_2_), channel_id=1, source_target_pairs={{0,128},{128,0},{1,129},{129,1},{2,130},{130,2},{3,131},{131,3},{4... | collective-permute-start | bytes 2359304 | tf_op jit(solution)/shard_map/ppermute | solution.py:21
  250.4 36.8 %collective-permute-start.24 = (bf16[192,2048]{1,0:T(8,128)(2,1)}, bf16[192,2048]{1,0:T(8,128)(2,1)S(1)}, u32[]{:S(2)}, u32[]{:S(2)}) collective-permute-start(bf16[192,2048]{1,0:T(8,128)(2,1)} %shard_map.145.refs_0_), channel_id=1, source_target_pairs={{0,128},{128,0},{1,129},{129,1},{2,130},{130,2},{3,131},{131,3},{4... | collective-permute-start | bytes 2359304 | tf_op jit(solution)/shard_map/ppermute | solution.py:21
  256.6 29.8 %collective-permute-start.15 = (bf16[64,2048]{1,0:T(8,128)(2,1)S(1)}, bf16[64,2048]{1,0:T(8,128)(2,1)S(1)}, u32[]{:S(2)}, u32[]{:S(2)}) collective-permute-start(bf16[64,2048]{1,0:T(8,128)(2,1)S(1)} %slice.224), channel_id=1, source_target_pairs={{0,128},{128,0},{1,129},{129,1},{2,130},{130,2},{3,131},{131,3},{4... | collective-permute-start | bytes 786440 | tf_op jit(solution)/shard_map/ppermute | solution.py:21
  263.9 0.9 copy-start.17
  (9 other events, 7.0 us)
Sparse Core Ops, SparseCore 0:
  12.2 41.3 all-gather.2
  55.4 40.1 all-gather.4

commit v6 on v4

--- a/solution.py
+++ b/solution.py
@@ -1,3 +1,5 @@
+import functools
+
 import jax
 import jax.numpy as jnp
 from jax import lax
@@ -14,6 +16,7 @@
 BF16 = jnp.bfloat16
 CAP = 6
 RINGS = ("y", "z")
+ACROSS = [(0, 3), (3, 0), (1, 2), (2, 1)]
 ALL = ("xh", "y", "z", "xl", "core")
 
 
@@ -57,7 +60,7 @@
     return (at == (row // 4) * 8 + part * 4 + row % 4).astype(BF16)
 
 
-def rows_kernel(rows_ref, w_own, w_xl, w_pair, _mv, back_ref, xd_out, act_out, g_gate, g_up, g_down,
+def rows_kernel(rows_ref, w_own, w_xl, w_pair, _m, _v, back_ref, xd_out, act_out, g_gate, g_up, g_down,
                 w_all, xd, mixed, acts, g_all, w_sem, xd_sem, act_sem, g_sem):
     share = w_own.shape[1]
     width = 4 * share
@@ -137,7 +140,7 @@
         store.wait()
 
 
-def rows_step(rows, w_own, w_xl, w_pair, mv_xl):
+def rows_step(rows, w_own, w_xl, w_pair, m_xl, v_xl):
     total, feature = rows.shape
     half = total // 2
     share = w_own.shape[1]
@@ -150,7 +153,7 @@
             jax.ShapeDtypeStruct((2, half, feature), BF16),
             jax.ShapeDtypeStruct((3, half, 2 * share), BF16),
         ) + (jax.ShapeDtypeStruct((2 * share, feature), BF16),) * 3,
-        in_specs=[vmem_spec] + [any_spec] * 4,
+        in_specs=[vmem_spec] + [any_spec] * 5,
         out_specs=(vmem_spec,) + (any_spec,) * 5,
         scratch_shapes=[
             pltpu.VMEM((3, 4 * share, feature), BF16),
@@ -169,44 +172,44 @@
             bytes_accessed=half * feature,
             transcendentals=0,
         ),
-    )(rows, w_own, w_xl, w_pair, mv_xl)
-
-
-def grads_kernel(flag_ref, xd_ref, act_ref, core_gate, core_up, core_down, *outs):
-    share = core_gate.shape[0] // 2
-    moved = flag_ref[0] != 0
-    for i, (side, core_ref) in enumerate(zip((0, 0, 1), (core_gate, core_up, core_down))):
-        g = dot_tn(act_ref[i], xd_ref[side]) + core_ref[...].astype(F32)
-        own = g[:share]
-        other = g[share:]
-        if i < 1:
-            own, other = jnp.where(moved, other, own), jnp.where(moved, own, other)
-        outs[i][...] = own.astype(BF16)
-        outs[3 + i][...] = other.astype(BF16)
-
-
-def grads_step(flag, xd, acts, core):
+    )(rows, w_own, w_xl, w_pair, m_xl, v_xl)
+
+
+def grads_kernel(exchange, flag_ref, rows_ref, act_ref, core_ref, *refs):
+    keep_ref, send_ref = refs[-2:]
+    share = core_ref.shape[0] // 2
+    g = dot_tn(act_ref[...], rows_ref[...]) + core_ref[...].astype(F32)
+    own, other = g[:share], g[share:]
+    if exchange:
+        moved = flag_ref[0] != 0
+        own, other = jnp.where(moved, other, own), jnp.where(moved, own, other)
+    keep_ref[...] = own.astype(BF16)
+    send_ref[...] = other.astype(BF16)
+
+
+def grads_step(exchange, flag, xd, side, acts, matrix, core, *ready):
     _, half, feature = xd.shape
-    share = core[0].shape[0] // 2
+    share = core.shape[0] // 2
     out = jax.ShapeDtypeStruct((share, feature), BF16)
+    out_spec = pl.BlockSpec((share, LANES), lambda n: (0, n))
     return pl.pallas_call(
-        grads_kernel,
+        functools.partial(grads_kernel, exchange),
         grid=(feature // LANES,),
-        out_shape=(out,) * 6,
+        out_shape=(out,) * 2,
         in_specs=[
             pl.BlockSpec(memory_space=pltpu.SMEM),
-            pl.BlockSpec((2, half, LANES), lambda n: (0, 0, n)),
-            pl.BlockSpec(acts.shape, lambda n: (0, 0, 0)),
-            *[pl.BlockSpec((2 * share, LANES), lambda n: (0, n))] * 3,
-        ],
-        out_specs=(pl.BlockSpec((share, LANES), lambda n: (0, n)),) * 6,
+            pl.BlockSpec((None, half, LANES), lambda n: (side, 0, n)),
+            pl.BlockSpec((None, *acts.shape[1:]), lambda n: (matrix, 0, 0)),
+            pl.BlockSpec((2 * share, LANES), lambda n: (0, n)),
+        ] + [pl.BlockSpec(memory_space=pl.ANY)] * len(ready),
+        out_specs=(out_spec,) * 2,
         compiler_params=pltpu.CompilerParams(vmem_limit_bytes=VMEM_LIMIT),
         cost_estimate=pl.CostEstimate(
-            flops=12 * half * feature * share,
-            bytes_accessed=2 * (2 * half * feature + 12 * share * feature),
+            flops=4 * half * feature * share,
+            bytes_accessed=2 * (half * feature + 4 * share * feature),
             transcendentals=0,
         ),
-    )(flag, xd, acts, *core)
+    )(flag, xd, acts, core, *ready)
 
 
 def adam_kernel(flag_ref, keep_ref, recv_ref, *refs):
@@ -296,10 +299,9 @@
     source = jnp.concatenate([tokens, cotangent, tokens_other, cotangent_other])
 
     w_own = jnp.concatenate([gate_up[0], down])
-    w_first = after(w_own, tokens_other, cotangent_other, named_other)
+    w_first = w_own
     w_xl = swap(w_first, "xl")
     w_pair = swap(jnp.stack([w_own, w_xl]), "core")
-    mv_xl = swap(after(jnp.concatenate([gate_up_m[0, :1], gate_up_v[0, :1]]), w_xl), "xl")
 
     both = jnp.stack([named, named_other])
     both_routes = both[:, :, :top].astype(jnp.int32)
@@ -328,23 +330,29 @@
     pick_b = pick.astype(BF16).reshape(rings * 2 * slots, 4 * count)
     send = (dot_nn(pick_b, source) * factor).astype(BF16).reshape(rings, 2 * slots, feature)
 
+    m_xl = swap(after(gate_up_m[0, :1], send), "xl")
+    v_xl = swap(after(gate_up_v[0, :1], send), "xl")
+
     recv = lax.all_to_all(send, RINGS, split_axis=0, concat_axis=0, tiled=True)
-    back_send, xd, acts, *g_pair = rows_step(recv.reshape(-1, feature), w_own, w_xl, w_pair, mv_xl)
+    back_send, xd, acts, *g_pair = rows_step(recv.reshape(-1, feature), w_own, w_xl, w_pair, m_xl, v_xl)
 
     g_core = [swap(g, "core") for g in g_pair]
+    gate = grads_step(True, flag, xd, 0, acts, 0, g_core[0])
+    up = grads_step(False, flag, xd, 0, acts, 1, g_core[1], gate[0])
+    down_g = grads_step(False, flag, xd, 1, acts, 2, g_core[2], up[0])
     back = lax.all_to_all(
-        back_send.reshape(recv.shape), RINGS, split_axis=0, concat_axis=0, tiled=True
+        after(back_send, g_core[0]).reshape(recv.shape), RINGS, split_axis=0, concat_axis=0, tiled=True
     ).reshape(-1, feature)
-    parts = grads_step(flag, xd, acts, g_core)
+    parts = (gate[0], up[0], down_g[0], gate[1], up[1], down_g[1])
     others = [swap(parts[3], "xl"), swap(parts[4], "xl")]
     new_gate = adam_step(flag, (parts[0], ()), (others[0], ()), (gate_up, (0, 0)), (gate_up_m, (0, 0)),
-                         (gate_up_v, (0, 0)), (w_xl, (0,)), (mv_xl, (0,)), (mv_xl, (1,)))
+                         (gate_up_v, (0, 0)), (w_xl, (0,)), (m_xl, (0,)), (v_xl, (0,)))
     others.append(swap(after(parts[5], new_gate), "xl"))
-    gate_other = lax.ppermute(new_gate, ("xh", "xl"), [(0, 3), (3, 0), (1, 2), (2, 1)])
+    gate_other = lax.ppermute(new_gate, ("xh", "xl"), ACROSS)
     new_up = adam_step(flag, (parts[1], ()), (others[1], ()), (gate_up, (0, 1)), (gate_up_m, (0, 1)),
                        (gate_up_v, (0, 1)))
     arrived = [new_gate, gate_other, new_up, swap(new_up, "xh")]
-    new_gate_up = settle(flag, arrived, mv_xl)
+    new_gate_up = settle(flag, arrived, m_xl)
     new_down = adam_step(flag, (parts[2], ()), (others[2], ()), (down, (0,)), (down_m, (0,)),
                          (down_v, (0,)))
     down_other = swap(new_down, "xh")

time: 254 us -> 248 us (0.976)
  waiting for transfers between devices: 141 us -> 128 us
  Pallas kernels: 45.8 us -> 52.7 us
    ppermute x15 -> x16, waiting for transfers between devices: 141 us -> 122 us  [swap(): return lax.ppermute(block, axis, [(0, 1), (1, 0)])]
    pallas_call x1 -> x3, Pallas kernels: 7.25 us -> 14.2 us  [grads_step(): pl.pallas_call(functools.partial(grads_kernel, exchange), grid=(feature /...]
    all_to_all x1, waiting for transfers between devices: 0.01 us -> 5.41 us  [body(): lax.all_to_all(after(back_send, g_core[0]).reshape(recv.shape), RINGS, sp...]
    ppermute x15 -> x16, starting transfers between devices: 17.8 us -> 17.5 us  [swap(): return lax.ppermute(block, axis, [(0, 1), (1, 0)])]
  transfers between devices with their start and end apart: 18 -> 19, of which waited for: 11 -> 10; matrix products, arithmetic and copies ran while one was open for 7% -> 8% of each run, Pallas kernels for 10% -> 13%
where the time goes in v6:
time: 248 us; the launch traced here: 247 us
  waiting for transfers between devices  128 us (52%)
  Pallas kernels  52.7 us (21%)
  starting transfers between devices  41 us (17%)
  other arithmetic  14.6 us (6%)
  matrix products  5.17 us (2%)
  local copies, waits for them, and re-layouts  3.91 us (2%)
    ppermute x16, waiting for transfers between devices, swap(): return lax.ppermute(block, axis, [(0, 1), (1, 0)])  122 us
    pallas_call x1, Pallas kernels, rows_step(): pl.pallas_call(rows_kernel, out_shape=(jax.ShapeDtypeStruct(rows.shape, B...  19.2 us
    ppermute x16, starting transfers between devices, swap(): return lax.ppermute(block, axis, [(0, 1), (1, 0)])  17.5 us
    pallas_call x3, Pallas kernels, adam_step(): pl.pallas_call(adam_kernel, grid=(steps,), out_shape=jax.ShapeDtypeStruct...  14.3 us
    pallas_call x3, Pallas kernels, grads_step(): pl.pallas_call(functools.partial(grads_kernel, exchange), grid=(feature /...  14.2 us
    all_to_all x1, starting transfers between devices, body(): lax.all_to_all(after(back_send, g_core[0]).reshape(recv.shape), RINGS, sp...  11.3 us
    all_to_all x1, starting transfers between devices, body(): recv = lax.all_to_all(send, RINGS, split_axis=0, concat_axis=0, tiled=True)  11.3 us
    another operation x2, other arithmetic, body(): w_pair = swap(jnp.stack([w_own, w_xl]), 'core')  9.3 us
  transfers between devices with their start and end apart: 19, of which 10 were waited for; matrix products, arithmetic and copies ran while one was open for 8% of the time, Pallas kernels for 13%

profile of v6, /device:TPU:1, one launch (start us, length us, event | category | flops | bytes accessed | tf_op | source)
XLA Modules:
  0.0 246.6 jit_solution(8270251199486666039)
XLA Ops:
  0.6 0.7 convert_element_type.115
  1.3 0.7 pad_maximum_fusion.3
  2.0 3.6 %collective-permute-start = (f32[32,16]{0,1:T(8,128)S(1)}, f32[32,16]{0,1:T(8,128)S(1)}, u32[]{:S(2)}, u32[]{:S(2)}) collective-permute-start(f32[32,16]{0,1:T(8,128)S(1)} %get-tuple-element.67), channel_id=1, source_target_pairs={{0,128},{128,0},{1,129},{129,1},{2,130},{130,2},{3,131},{131,3},{4... | collective-permute-start | bytes 6152 | tf_op jit(solution)/shard_map/ppermute | solution.py:24
  5.6 2.9 %collective-permute-start.2 = (bf16[32,2048]{1,0:T(8,128)(2,1)}, bf16[32,2048]{1,0:T(8,128)(2,1)S(1)}, u32[]{:S(2)}, u32[]{:S(2)}) collective-permute-start(bf16[32,2048]{1,0:T(8,128)(2,1)} %param.12), channel_id=1, source_target_pairs={{0,128},{128,0},{1,129},{129,1},{2,130},{130,2},{3,131},{131,3},{4... | collective-permute-start | bytes 393224 | tf_op jit(solution)/shard_map/ppermute | solution.py:24
  8.6 4.1 %fusion.60 = (bf16[1,3,192,2048]{3,2,1,0:T(8,128)(2,1)}, bf16[3,192,2048]{2,1,0:T(8,128)(2,1)}) fusion(bf16[1,192,2048]{2,1,0:T(8,128)(2,1)} %refs_0_.5, bf16[2,192,2048]{2,1,0:T(8,128)(2,1)} %bitcast.71), kind=kLoop, calls=%fused_computation.140 | loop fusion | flops 1179648 | bytes 7077888 | tf_op jit(solution)/shard_map/stack | solution.py:304
  13.8 0.7 select_convert_fusion
  15.0 2.6 %multiply_convert_fusion = bf16[768,2048]{1,0:T(8,128)(2,1)} fusion(pred[768,128]{1,0:T(32,128)(4,1)S(1)} %fusion.15, f32[768]{0:T(1024)S(1)} %select_n.183, bf16[32,2048]{1,0:T(8,128)(2,1)S(1)} %collective-permute-done.2, bf16[32,2048]{1,0:T(8,128)(2,1)S(1)} %collective-permute-done.1, bf16[32,2048]{1,0:T(8,128)(2,1)S(1)} %copy-done.8, ...), kind=kOutput, calls=%fused_computation | convolution fusion | flops 407896064 | bytes 3771392 | tf_op jit(solution)/shard_map/dot_general | solution.py:42
  17.6 11.3 %all-to-all-start = ((bf16[32,24,2048]{2,1,0:T(8,128)(2,1)}), bf16[32,24,2048]{2,1,0:T(8,128)(2,1)}, u32[]{:S(2)}, u32[]{:S(2)}) async-start(bf16[32,24,2048]{2,1,0:T(8,128)(2,1)} %bitcast.28), calls=%async_computation | async-start | bytes 6291456 | tf_op jit(solution)/shard_map/all_to_all | solution.py:336
  29.0 35.3 %collective-permute-done.3.w_xl.refs_3_ = bf16[3,192,2048]{2,1,0:T(8,128)(2,1)S(1)} collective-permute-done((bf16[3,192,2048]{2,1,0:T(8,128)(2,1)}, bf16[3,192,2048]{2,1,0:T(8,128)(2,1)S(1)}, u32[]{:S(2)}, u32[]{:S(2)}) %collective-permute-start.3) | collective-permute-done | bytes 2359328 | tf_op jit(solution)/shard_map/ppermute | solution.py:24
  64.2 5.2 %pad_maximum_fusion = bf16[2,3,192,2048]{3,2,1,0:T(8,128)(2,1)} fusion(bf16[1,3,192,2048]{3,2,1,0:T(8,128)(2,1)S(1)} %bitcast.70, bf16[1,3,192,2048]{3,2,1,0:T(8,128)(2,1)} %get-tuple-element.38), kind=kLoop, calls=%fused_computation.1 | loop fusion | flops 2359296 | bytes 9437184 | tf_op jit(solution)/shard_map/stack | solution.py:304
  69.4 2.3 collective-permute-start.4
  71.9 0.4 collective-permute-start.5
  72.3 1.2 collective-permute-start.6
  73.4 17.8 %collective-permute-done.5._m.refs_4_ = bf16[1,192,2048]{2,1,0:T(8,128)(2,1)S(1)} collective-permute-done((bf16[1,192,2048]{2,1,0:T(8,128)(2,1)S(1)}, bf16[1,192,2048]{2,1,0:T(8,128)(2,1)S(1)}, u32[]{:S(2)}, u32[]{:S(2)}) %collective-permute-start.5) | collective-permute-done | bytes 786464 | tf_op jit(solution)/shard_map/ppermute | solution.py:24
  91.3 16.7 %collective-permute-done.6._v.refs_5_ = bf16[1,192,2048]{2,1,0:T(8,128)(2,1)S(1)} collective-permute-done((bf16[1,192,2048]{2,1,0:T(8,128)(2,1)S(1)}, bf16[1,192,2048]{2,1,0:T(8,128)(2,1)S(1)}, u32[]{:S(2)}, u32[]{:S(2)}) %collective-permute-start.6) | collective-permute-done | bytes 786464 | tf_op jit(solution)/shard_map/ppermute | solution.py:24
  108.0 0.9 copy-done.4
  108.9 19.2 %shard_map.138 = (bf16[768,2048]{1,0:T(8,128)(2,1)}, bf16[2,384,2048]{2,1,0:T(8,128)(2,1)}, bf16[3,384,384]{2,1,0:T(8,128)(2,1)}, bf16[384,2048]{1,0:T(8,128)(2,...) custom-call(bf16[768,2048]{1,0:T(8,128)(2,1)} %bitcast.29.rows_ref, ...), custom_call_target="tpu_custom_call" | custom-call | flops 150994944 | bytes 786432 | tf_op jit(solution)/shard_map/pallas_call | solution.py:149
  128.1 0.9 collective-permute-start.7
  129.0 3.4 %collective-permute-done.7.core_ref = bf16[384,2048]{1,0:T(8,128)(2,1)} collective-permute-done((bf16[384,2048]{1,0:T(8,128)(2,1)}, bf16[384,2048]{1,0:T(8,128)(2,1)}, u32[]{:S(2)}, u32[]{:S(2)}) %collective-permute-start.7) | collective-permute-done | bytes 1572896 | tf_op jit(solution)/shard_map/ppermute | solution.py:24
  132.4 11.3 %all-to-all-start.1 = ((bf16[32,24,2048]{2,1,0:T(8,128)(2,1)}), bf16[32,24,2048]{2,1,0:T(8,128)(2,1)S(1)}, u32[]{:S(2)}, u32[]{:S(2)}) async-start(bf16[32,24,2048]{2,1,0:T(8,128)(2,1)} %bitcast.72), calls=%async_computation.1 | async-start | bytes 6291456 | tf_op jit(solution)/shard_map/all_to_all | solution.py:343
  143.7 0.7 collective-permute-start.11
  144.8 0.6 fusion.55
  146.1 4.8 %shard_map.139 = (bf16[192,2048]{1,0:T(8,128)(2,1)}, bf16[192,2048]{1,0:T(8,128)(2,1)}) custom-call(s32[1]{0:T(128)} %bitcast.37.flag_ref, bf16[2,384,2048]{2,1,0:T(8,128)(2,1)} %get-tuple-element.25.rows_ref, bf16[3,384,384]{2,1,0:T(8,128)(2,1)} %get-tuple-element.26.act_ref, bf16[384,2048]{1,0:T(8,128)(2,1)} %collective-permute-done.7.core_ref), custom_call_target="tpu_custom_call" | custom-call | flops 603979776 | bytes 4718592 | tf_op jit(solution)/shard_map/pallas_call | solution.py:195
  151.2 4.7 %shard_map.141 = (bf16[192,2048]{1,0:T(8,128)(2,1)}, bf16[192,2048]{1,0:T(8,128)(2,1)}) custom-call(s32[1]{0:T(128)} %bitcast.37.flag_ref, bf16[2,384,2048]{2,1,0:T(8,128)(2,1)} %get-tuple-element.25.rows_ref, bf16[3,384,384]{2,1,0:T(8,128)(2,1)} %get-tuple-element.26.act_ref, bf16[384,2048]{1,0:T(8,128)(2,1)} %collective-permute-done.11.core_ref, ...), custom_call_target="tpu_custom_call" | custom-call | flops 603979776 | bytes 4718592 | tf_op jit(solution)/shard_map/pallas_call | solution.py:195
  155.9 1.1 collective-permute-start.12
  157.1 4.7 %shard_map.144 = (bf16[192,2048]{1,0:T(8,128)(2,1)}, bf16[192,2048]{1,0:T(8,128)(2,1)}) custom-call(s32[1]{0:T(128)} %bitcast.37.flag_ref, bf16[2,384,2048]{2,1,0:T(8,128)(2,1)} %get-tuple-element.25.rows_ref, bf16[3,384,384]{2,1,0:T(8,128)(2,1)} %get-tuple-element.26.act_ref, bf16[384,2048]{1,0:T(8,128)(2,1)} %collective-permute-done.14.core_ref, ...), custom_call_target="tpu_custom_call" | custom-call | flops 603979776 | bytes 4718592 | tf_op jit(solution)/shard_map/pallas_call | solution.py:195
  161.8 8.3 %collective-permute-done.9.recv_ref = bf16[192,2048]{1,0:T(8,128)(2,1)S(1)} collective-permute-done((bf16[192,2048]{1,0:T(8,128)(2,1)}, bf16[192,2048]{1,0:T(8,128)(2,1)S(1)}, u32[]{:S(2)}, u32[]{:S(2)}) %collective-permute-start.9) | collective-permute-done | bytes 786464 | tf_op jit(solution)/shard_map/ppermute | solution.py:24
  170.1 0.9 copy-done.7
  171.0 5.1 %shard_map.140.refs_0_ = bf16[192,2048]{1,0:T(8,128)(2,1)} custom-call(s32[1]{0:T(128)} %bitcast.37.flag_ref, bf16[192,2048]{1,0:T(8,128)(2,1)} %get-tuple-element.27.keep_ref.refs_0_, bf16[192,2048]{1,0:T(8,128)(2,1)} %copy-done.7, bf16[1,2,192,2048]{3,2,1,0:T(8,128)(2,1)} %refs_0_.4, bf16[1,2,192,2048]{3,2,1,0:T(8,128)(2,1)} %refs_1_.4, ...), custom_call_target="tpu_custom_call" | custom-call | flops 7864320 | bytes 7077888 | tf_op jit(solution)/shard_map/pallas_call | solution.py:235
  176.1 0.4 collective-permute-start.15
  176.5 0.9 bitcast_select_fusion.2
  177.4 0.9 collective-permute-start.10
  178.3 8.7 %collective-permute-done.12.recv_ref = bf16[192,2048]{1,0:T(8,128)(2,1)S(1)} collective-permute-done((bf16[192,2048]{1,0:T(8,128)(2,1)}, bf16[192,2048]{1,0:T(8,128)(2,1)S(1)}, u32[]{:S(2)}, u32[]{:S(2)}) %collective-permute-start.12) | collective-permute-done | bytes 786464 | tf_op jit(solution)/shard_map/ppermute | solution.py:24
  187.0 0.9 copy-done.5
  187.9 4.6 %shard_map.142.refs_2_ = bf16[192,2048]{1,0:T(8,128)(2,1)} custom-call(s32[1]{0:T(128)} %bitcast.37.flag_ref, bf16[192,2048]{1,0:T(8,128)(2,1)} %get-tuple-element.30.keep_ref.refs_0_, bf16[192,2048]{1,0:T(8,128)(2,1)} %copy-done.5, bf16[1,2,192,2048]{3,2,1,0:T(8,128)(2,1)} %refs_0_.4, bf16[1,2,192,2048]{3,2,1,0:T(8,128)(2,1)} %refs_1_.4, ...), custom_call_target="tpu_custom_call" | custom-call | flops 7864320 | bytes 4718592 | tf_op jit(solution)/shard_map/pallas_call | solution.py:235
  192.5 0.9 collective-permute-start.13
  193.4 10.4 %collective-permute-done.15.recv_ref = bf16[192,2048]{1,0:T(8,128)(2,1)S(1)} collective-permute-done((bf16[192,2048]{1,0:T(8,128)(2,1)S(1)}, bf16[192,2048]{1,0:T(8,128)(2,1)S(1)}, u32[]{:S(2)}, u32[]{:S(2)}) %collective-permute-start.15) | collective-permute-done | bytes 786464 | tf_op jit(solution)/shard_map/ppermute | solution.py:24
  203.8 0.9 copy-done.6
  204.6 4.6 %shard_map.145.refs_0_ = bf16[192,2048]{1,0:T(8,128)(2,1)} custom-call(s32[1]{0:T(128)} %bitcast.37.flag_ref, bf16[192,2048]{1,0:T(8,128)(2,1)} %get-tuple-element.33.keep_ref, bf16[192,2048]{1,0:T(8,128)(2,1)} %copy-done.6, bf16[1,192,2048]{2,1,0:T(8,128)(2,1)} %refs_0_.5, bf16[1,192,2048]{2,1,0:T(8,128)(2,1)} %refs_1_.5, bf16[1,192,2048]{2,1,0:T(8,128)(2,1)} %refs_2_.5), custom_call_target="tpu_custom_call" | custom-call | flops 7864320 | bytes 4718592 | tf_op jit(solution)/shard_map/pallas_call | solution.py:235
  209.2 0.9 collective-permute-start.16
  210.2 5.4 %all-to-all-done.1 = bf16[32,24,2048]{2,1,0:T(8,128)(2,1)S(1)} async-done(((bf16[32,24,2048]{2,1,0:T(8,128)(2,1)}), bf16[32,24,2048]{2,1,0:T(8,128)(2,1)S(1)}, u32[]{:S(2)}, u32[]{:S(2)}) %all-to-all-start.1) | async-done | bytes 3145760 | tf_op jit(solution)/shard_map/all_to_all | solution.py:343
  215.6 2.3 fusion.2
  218.1 1.0 collective-permute-start.8
  219.2 2.1 collective-permute-done.13.refs_3_
  221.3 2.8 %shard_map.143 = bf16[2,192,2048]{2,1,0:T(8,128)(2,1)} custom-call(s32[1]{0:T(128)} %bitcast.37.flag_ref, bf16[192,2048]{1,0:T(8,128)(2,1)} %shard_map.140.refs_0_, bf16[192,2048]{1,0:T(8,128)(2,1)} %collective-permute-done.10.refs_1_, bf16[192,2048]{1,0:T(8,128)(2,1)} %shard_map.142.refs_2_, bf16[192,2048]{1,0:T(8,128)(2,1)} %collective-permute-done.13.refs_3_, ...), custom_call_target="tpu_custom_call" | custom-call | flops 786432 | bytes 4718592 | tf_op jit(solution)/shard_map/pallas_call | solution.py:261
  224.1 19.6 %collective-permute-done.8 = bf16[64,2048]{1,0:T(8,128)(2,1)S(1)} collective-permute-done((bf16[64,2048]{1,0:T(8,128)(2,1)S(1)}, bf16[64,2048]{1,0:T(8,128)(2,1)S(1)}, u32[]{:S(2)}, u32[]{:S(2)}) %collective-permute-start.8) | collective-permute-done | bytes 262176 | tf_op jit(solution)/shard_map/ppermute | solution.py:24
  243.7 0.8 fusion.16
  244.5 2.1 shard_map.146
  (70 shorter events, 2.6 us)
Async XLA Ops:
  2.0 11.3 %collective-permute-start = (f32[32,16]{0,1:T(8,128)S(1)}, f32[32,16]{0,1:T(8,128)S(1)}, u32[]{:S(2)}, u32[]{:S(2)}) collective-permute-start(f32[32,16]{0,1:T(8,128)S(1)} %get-tuple-element.67), channel_id=1, source_target_pairs={{0,128},{128,0},{1,129},{129,1},{2,130},{130,2},{3,131},{131,3},{4... | collective-permute-start | bytes 6152 | tf_op jit(solution)/shard_map/ppermute | solution.py:24
  5.6 9.4 %collective-permute-start.1 = (bf16[32,2048]{1,0:T(8,128)(2,1)}, bf16[32,2048]{1,0:T(8,128)(2,1)S(1)}, u32[]{:S(2)}, u32[]{:S(2)}) collective-permute-start(bf16[32,2048]{1,0:T(8,128)(2,1)} %param.11), channel_id=1, source_target_pairs={{0,128},{128,0},{1,129},{129,1},{2,130},{130,2},{3,131},{131,3},{4... | collective-permute-start | bytes 393224 | tf_op jit(solution)/shard_map/ppermute | solution.py:24
  5.6 9.4 %collective-permute-start.2 = (bf16[32,2048]{1,0:T(8,128)(2,1)}, bf16[32,2048]{1,0:T(8,128)(2,1)S(1)}, u32[]{:S(2)}, u32[]{:S(2)}) collective-permute-start(bf16[32,2048]{1,0:T(8,128)(2,1)} %param.12), channel_id=1, source_target_pairs={{0,128},{128,0},{1,129},{129,1},{2,130},{130,2},{3,131},{131,3},{4... | collective-permute-start | bytes 393224 | tf_op jit(solution)/shard_map/ppermute | solution.py:24
  8.6 6.4 %copy-start.8 = (bf16[32,2048]{1,0:T(8,128)(2,1)S(1)}, bf16[32,2048]{1,0:T(8,128)(2,1)}, u32[]{:S(2)}) copy-start(bf16[32,2048]{1,0:T(8,128)(2,1)} %param.12) | copy-start | bytes 393220
  8.6 6.5 %copy-start.9 = (bf16[32,2048]{1,0:T(8,128)(2,1)S(1)}, bf16[32,2048]{1,0:T(8,128)(2,1)}, u32[]{:S(2)}) copy-start(bf16[32,2048]{1,0:T(8,128)(2,1)} %param.11) | copy-start | bytes 393220
  12.7 51.5 %collective-permute-start.3 = (bf16[3,192,2048]{2,1,0:T(8,128)(2,1)}, bf16[3,192,2048]{2,1,0:T(8,128)(2,1)S(1)}, u32[]{:S(2)}, u32[]{:S(2)}) collective-permute-start(bf16[3,192,2048]{2,1,0:T(8,128)(2,1)} %get-tuple-element.39.w_own), channel_id=1, source_target_pairs={{0,2},{2,0},{1,3},{3,1},{4,6},{6,4},{5,7},{7,5},{8,10},{10,8},{9,1... | collective-permute-start | bytes 7077896 | tf_op jit(solution)/shard_map/ppermute | solution.py:24
  13.1 4.5 %copy-start.10 = (pred[24,128]{1,0:T(8,128)(4,1)}, pred[24,128]{1,0:T(8,128)(4,1)S(1)}, u32[]{:S(2)}) copy-start(pred[24,128]{1,0:T(8,128)(4,1)S(1)} %broadcast_compare_fusion) | copy-start | bytes 9220
  13.3 4.4 %copy-start.12 = (s32[768]{0:T(1024)}, s32[768]{0:T(1024)S(1)}, u32[]{:S(2)}) copy-start(s32[768]{0:T(1024)S(1)} %eq.199) | copy-start | bytes 9220
  17.6 90.4 %all-to-all-start = ((bf16[32,24,2048]{2,1,0:T(8,128)(2,1)}), bf16[32,24,2048]{2,1,0:T(8,128)(2,1)}, u32[]{:S(2)}, u32[]{:S(2)}) async-start(bf16[32,24,2048]{2,1,0:T(8,128)(2,1)} %bitcast.28), calls=%async_computation | async-start | bytes 6291456 | tf_op jit(solution)/shard_map/all_to_all | solution.py:336
  64.2 5.2 %copy-start = (bf16[3,192,2048]{2,1,0:T(8,128)(2,1)}, bf16[3,192,2048]{2,1,0:T(8,128)(2,1)S(1)}, u32[]{:S(2)}) copy-start(bf16[3,192,2048]{2,1,0:T(8,128)(2,1)S(1)} %collective-permute-done.3.w_xl.refs_3_) | copy-start | bytes 7077892
  64.2 7.5 %copy-start.1 = (bf16[1,2,192,2048]{3,2,1,0:T(8,128)(2,1)S(1)}, bf16[1,2,192,2048]{3,2,1,0:T(8,128)(2,1)}, u32[]{:S(2)}) copy-start(bf16[1,2,192,2048]{3,2,1,0:T(8,128)(2,1)} %refs_1_.4) | copy-start | bytes 4718596
  64.2 7.6 %copy-start.2 = (bf16[1,2,192,2048]{3,2,1,0:T(8,128)(2,1)S(1)}, bf16[1,2,192,2048]{3,2,1,0:T(8,128)(2,1)}, u32[]{:S(2)}) copy-start(bf16[1,2,192,2048]{3,2,1,0:T(8,128)(2,1)} %refs_2_.4) | copy-start | bytes 4718596
  69.4 38.6 %collective-permute-start.4 = (bf16[2,3,192,2048]{3,2,1,0:T(8,128)(2,1)}, bf16[2,3,192,2048]{3,2,1,0:T(8,128)(2,1)}, u32[]{:S(2)}, u32[]{:S(2)}) collective-permute-start(bf16[2,3,192,2048]{3,2,1,0:T(8,128)(2,1)} %pad_maximum_fusion), channel_id=1, source_target_pairs={{0,1},{1,0},{2,3},{3,2},{4,5},{5,4},{6,7},{7,6},{8,9},{9,8},{10,11... | collective-permute-start | bytes 14155784 | tf_op jit(solution)/shard_map/ppermute | solution.py:24
  71.9 19.4 %collective-permute-start.5 = (bf16[1,192,2048]{2,1,0:T(8,128)(2,1)S(1)}, bf16[1,192,2048]{2,1,0:T(8,128)(2,1)S(1)}, u32[]{:S(2)}, u32[]{:S(2)}) collective-permute-start(bf16[1,192,2048]{2,1,0:T(8,128)(2,1)S(1)} %slice_bitcast_fusion.1), channel_id=1, source_target_pairs={{0,2},{2,0},{1,3},{3,1},{4,6},{6,4},{5,7},{7,5},{8,10},{10,8},{9,1... | collective-permute-start | bytes 2359304 | tf_op jit(solution)/shard_map/ppermute | solution.py:24
  72.3 35.7 %collective-permute-start.6 = (bf16[1,192,2048]{2,1,0:T(8,128)(2,1)S(1)}, bf16[1,192,2048]{2,1,0:T(8,128)(2,1)S(1)}, u32[]{:S(2)}, u32[]{:S(2)}) collective-permute-start(bf16[1,192,2048]{2,1,0:T(8,128)(2,1)S(1)} %slice_bitcast_fusion), channel_id=1, source_target_pairs={{0,2},{2,0},{1,3},{3,1},{4,6},{6,4},{5,7},{7,5},{8,10},{10,8},{9,1... | collective-permute-start | bytes 2359304 | tf_op jit(solution)/shard_map/ppermute | solution.py:24
  91.3 16.8 %copy-start.3 = (bf16[1,192,2048]{2,1,0:T(8,128)(2,1)}, bf16[1,192,2048]{2,1,0:T(8,128)(2,1)S(1)}, u32[]{:S(2)}) copy-start(bf16[1,192,2048]{2,1,0:T(8,128)(2,1)S(1)} %collective-permute-done.5._m.refs_4_) | copy-start | bytes 2359300
  108.0 0.9 copy-start.4
  128.1 4.3 %collective-permute-start.7 = (bf16[384,2048]{1,0:T(8,128)(2,1)}, bf16[384,2048]{1,0:T(8,128)(2,1)}, u32[]{:S(2)}, u32[]{:S(2)}) collective-permute-start(bf16[384,2048]{1,0:T(8,128)(2,1)} %get-tuple-element.23), channel_id=1, source_target_pairs={{0,1},{1,0},{2,3},{3,2},{4,5},{5,4},{6,7},{7,6},{8,9},{9,8},{10,11... | collective-permute-start | bytes 4718600 | tf_op jit(solution)/shard_map/ppermute | solution.py:24
  132.4 12.4 %copy-start.16 = (s32[64]{0:T(128)S(1)}, s32[64]{0:T(128)}, u32[]{:S(2)}) copy-start(s32[64]{0:T(128)} %param.15) | copy-start | bytes 772
  132.4 83.2 %all-to-all-start.1 = ((bf16[32,24,2048]{2,1,0:T(8,128)(2,1)}), bf16[32,24,2048]{2,1,0:T(8,128)(2,1)S(1)}, u32[]{:S(2)}, u32[]{:S(2)}) async-start(bf16[32,24,2048]{2,1,0:T(8,128)(2,1)} %bitcast.72), calls=%async_computation.1 | async-start | bytes 6291456 | tf_op jit(solution)/shard_map/all_to_all | solution.py:343
  143.7 7.5 %collective-permute-start.11 = (bf16[384,2048]{1,0:T(8,128)(2,1)}, bf16[384,2048]{1,0:T(8,128)(2,1)}, u32[]{:S(2)}, u32[]{:S(2)}) collective-permute-start(bf16[384,2048]{1,0:T(8,128)(2,1)} %get-tuple-element.29), channel_id=1, source_target_pairs={{0,1},{1,0},{2,3},{3,2},{4,5},{5,4},{6,7},{7,6},{8,9},{9,8},{10,11... | collective-permute-start | bytes 4718600 | tf_op jit(solution)/shard_map/ppermute | solution.py:24
  144.5 12.6 %collective-permute-start.14 = (bf16[384,2048]{1,0:T(8,128)(2,1)}, bf16[384,2048]{1,0:T(8,128)(2,1)}, u32[]{:S(2)}, u32[]{:S(2)}) collective-permute-start(bf16[384,2048]{1,0:T(8,128)(2,1)} %get-tuple-element.32), channel_id=1, source_target_pairs={{0,1},{1,0},{2,3},{3,2},{4,5},{5,4},{6,7},{7,6},{8,9},{9,8},{10,11... | collective-permute-start | bytes 4718600 | tf_op jit(solution)/shard_map/ppermute | solution.py:24
  150.9 19.2 %collective-permute-start.9 = (bf16[192,2048]{1,0:T(8,128)(2,1)}, bf16[192,2048]{1,0:T(8,128)(2,1)S(1)}, u32[]{:S(2)}, u32[]{:S(2)}) collective-permute-start(bf16[192,2048]{1,0:T(8,128)(2,1)} %get-tuple-element.28), channel_id=1, source_target_pairs={{0,2},{2,0},{1,3},{3,1},{4,6},{6,4},{5,7},{7,5},{8,10},{10,8},{9,1... | collective-permute-start | bytes 2359304 | tf_op jit(solution)/shard_map/ppermute | solution.py:24
  155.9 31.1 %collective-permute-start.12 = (bf16[192,2048]{1,0:T(8,128)(2,1)}, bf16[192,2048]{1,0:T(8,128)(2,1)S(1)}, u32[]{:S(2)}, u32[]{:S(2)}) collective-permute-start(bf16[192,2048]{1,0:T(8,128)(2,1)} %get-tuple-element.31), channel_id=1, source_target_pairs={{0,2},{2,0},{1,3},{3,1},{4,6},{6,4},{5,7},{7,5},{8,10},{10,8},{9,1... | collective-permute-start | bytes 2359304 | tf_op jit(solution)/shard_map/ppermute | solution.py:24
  161.8 14.3 %copy-start.15 = (bf16[192,2048]{1,0:T(8,128)(2,1)S(1)}, bf16[192,2048]{1,0:T(8,128)(2,1)}, u32[]{:S(2)}) copy-start(bf16[192,2048]{1,0:T(8,128)(2,1)} %get-tuple-element.35) | copy-start | bytes 2359300
  161.8 14.7 %copy-start.11 = (pred[24,128]{1,0:T(8,128)(4,1)S(1)}, pred[24,128]{1,0:T(8,128)(4,1)}, u32[]{:S(2)}) copy-start(pred[24,128]{1,0:T(8,128)(4,1)} %copy-done.10) | copy-start | bytes 9220
  161.8 14.7 %copy-start.13 = (s32[768]{0:T(1024)S(1)}, s32[768]{0:T(1024)}, u32[]{:S(2)}) copy-start(s32[768]{0:T(1024)} %copy-done.12) | copy-start | bytes 9220
  161.8 14.7 %copy-start.14 = (bf16[32,128]{1,0:T(8,128)(2,1)S(1)}, bf16[32,128]{1,0:T(8,128)(2,1)}, u32[]{:S(2)}) copy-start(bf16[32,128]{1,0:T(8,128)(2,1)} %get-tuple-element.36) | copy-start | bytes 24580
  170.1 0.9 copy-start.7
  176.1 27.7 %collective-permute-start.15 = (bf16[192,2048]{1,0:T(8,128)(2,1)S(1)}, bf16[192,2048]{1,0:T(8,128)(2,1)S(1)}, u32[]{:S(2)}, u32[]{:S(2)}) collective-permute-start(bf16[192,2048]{1,0:T(8,128)(2,1)S(1)} %copy-done.15), channel_id=1, source_target_pairs={{0,2},{2,0},{1,3},{3,1},{4,6},{6,4},{5,7},{7,5},{8,10},{10,8},{9,1... | collective-permute-start | bytes 2359304 | tf_op jit(solution)/shard_map/ppermute | solution.py:24
  177.4 43.9 %collective-permute-start.10 = (bf16[192,2048]{1,0:T(8,128)(2,1)}, bf16[192,2048]{1,0:T(8,128)(2,1)}, u32[]{:S(2)}, u32[]{:S(2)}) collective-permute-start(bf16[192,2048]{1,0:T(8,128)(2,1)} %shard_map.140.refs_0_), channel_id=1, source_target_pairs={{0,130},{130,0},{2,128},{128,2},{1,131},{131,1},{3,129},{129,3},{4... | collective-permute-start | bytes 2359304 | tf_op jit(solution)/shard_map/ppermute | solution.py:351
  187.0 0.9 copy-start.5
  192.5 28.8 %collective-permute-start.13 = (bf16[192,2048]{1,0:T(8,128)(2,1)}, bf16[192,2048]{1,0:T(8,128)(2,1)}, u32[]{:S(2)}, u32[]{:S(2)}) collective-permute-start(bf16[192,2048]{1,0:T(8,128)(2,1)} %shard_map.142.refs_2_), channel_id=1, source_target_pairs={{0,128},{128,0},{1,129},{129,1},{2,130},{130,2},{3,131},{131,3},{4... | collective-permute-start | bytes 2359304 | tf_op jit(solution)/shard_map/ppermute | solution.py:24
  203.8 0.9 copy-start.6
  209.2 35.3 %collective-permute-start.16 = (bf16[192,2048]{1,0:T(8,128)(2,1)}, bf16[192,2048]{1,0:T(8,128)(2,1)}, u32[]{:S(2)}, u32[]{:S(2)}) collective-permute-start(bf16[192,2048]{1,0:T(8,128)(2,1)} %shard_map.145.refs_0_), channel_id=1, source_target_pairs={{0,128},{128,0},{1,129},{129,1},{2,130},{130,2},{3,131},{131,3},{4... | collective-permute-start | bytes 2359304 | tf_op jit(solution)/shard_map/ppermute | solution.py:24
  218.1 25.5 %collective-permute-start.8 = (bf16[64,2048]{1,0:T(8,128)(2,1)S(1)}, bf16[64,2048]{1,0:T(8,128)(2,1)S(1)}, u32[]{:S(2)}, u32[]{:S(2)}) collective-permute-start(bf16[64,2048]{1,0:T(8,128)(2,1)S(1)} %slice.251), channel_id=1, source_target_pairs={{0,128},{128,0},{1,129},{129,1},{2,130},{130,2},{3,131},{131,3},{4... | collective-permute-start | bytes 786440 | tf_op jit(solution)/shard_map/ppermute | solution.py:24

commit v7 on v6

--- a/solution.py
+++ b/solution.py
@@ -301,7 +301,6 @@
     w_own = jnp.concatenate([gate_up[0], down])
     w_first = w_own
     w_xl = swap(w_first, "xl")
-    w_pair = swap(jnp.stack([w_own, w_xl]), "core")
 
     both = jnp.stack([named, named_other])
     both_routes = both[:, :, :top].astype(jnp.int32)
@@ -332,6 +331,7 @@
 
     m_xl = swap(after(gate_up_m[0, :1], send), "xl")
     v_xl = swap(after(gate_up_v[0, :1], send), "xl")
+    w_pair = swap(jnp.stack([w_own, after(w_xl, m_xl)]), "core")
 
     recv = lax.all_to_all(send, RINGS, split_axis=0, concat_axis=0, tiled=True)
     back_send, xd, acts, *g_pair = rows_step(recv.reshape(-1, feature), w_own, w_xl, w_pair, m_xl, v_xl)
@@ -341,7 +341,7 @@
     up = grads_step(False, flag, xd, 0, acts, 1, g_core[1], gate[0])
     down_g = grads_step(False, flag, xd, 1, acts, 2, g_core[2], up[0])
     back = lax.all_to_all(
-        after(back_send, g_core[0]).reshape(recv.shape), RINGS, split_axis=0, concat_axis=0, tiled=True
+        after(back_send, gate[0]).reshape(recv.shape), RINGS, split_axis=0, concat_axis=0, tiled=True
     ).reshape(-1, feature)
     parts = (gate[0], up[0], down_g[0], gate[1], up[1], down_g[1])
     others = [swap(parts[3], "xl"), swap(parts[4], "xl")]

time: 248 us -> 247 us (level)
  local copies, waits for them, and re-layouts: 3.91 us -> 8.46 us
  waiting for transfers between devices: 128 us -> 124 us
    ppermute x16, waiting for transfers between devices: 122 us -> 112 us  [swap(): return lax.ppermute(block, axis, [(0, 1), (1, 0)])]
    all_to_all x1, waiting for transfers between devices: 5.41 us -> 11.5 us  [body(): lax.all_to_all(after(back_send, gate[0]).reshape(recv.shape), RINGS, spli...]
    unnamed x34 -> x38, local copies, waits for them, and re-layouts: 3.58 us -> 6.98 us
  transfers between devices with their start and end apart: 19 -> 19, of which waited for: 10 -> 9; matrix products, arithmetic and copies ran while one was open for 8% -> 8% of each run, Pallas kernels for 13% -> 11%
where the time goes in v7:
time: 247 us
  waiting for transfers between devices  124 us (50%)
  Pallas kernels  52.5 us (21%)
  starting transfers between devices  40.3 us (16%)
  other arithmetic  14.9 us (6%)
  local copies, waits for them, and re-layouts  8.46 us (3%)
  matrix products  5.19 us (2%)
    ppermute x16, waiting for transfers between devices, swap(): return lax.ppermute(block, axis, [(0, 1), (1, 0)])  112 us
    pallas_call x1, Pallas kernels, rows_step(): pl.pallas_call(rows_kernel, out_shape=(jax.ShapeDtypeStruct(rows.shape, B...  19.2 us
    ppermute x16, starting transfers between devices, swap(): return lax.ppermute(block, axis, [(0, 1), (1, 0)])  16.9 us
    pallas_call x3, Pallas kernels, adam_step(): pl.pallas_call(adam_kernel, grid=(steps,), out_shape=jax.ShapeDtypeStruct...  14.3 us
    pallas_call x3, Pallas kernels, grads_step(): pl.pallas_call(functools.partial(grads_kernel, exchange), grid=(feature /...  14.1 us
    all_to_all x1, waiting for transfers between devices, body(): lax.all_to_all(after(back_send, gate[0]).reshape(recv.shape), RINGS, spli...  11.5 us
    all_to_all x1, starting transfers between devices, body(): recv = lax.all_to_all(send, RINGS, split_axis=0, concat_axis=0, tiled=True)  11.3 us
    all_to_all x1, starting transfers between devices, body(): lax.all_to_all(after(back_send, gate[0]).reshape(recv.shape), RINGS, spli...  11.2 us
  transfers between devices with their start and end apart: 19, of which 9 were waited for; matrix products, arithmetic and copies ran while one was open for 8% of the time, Pallas kernels for 11%

profile of v7, /device:TPU:1, one launch (start us, length us, event | category | flops | bytes accessed | tf_op | source)
XLA Modules:
  0.0 246.6 jit_solution(14346473286023084342)
XLA Ops:
  0.6 0.7 convert_element_type.115
  1.3 0.7 pad_maximum_fusion.3
  2.0 3.6 %collective-permute-start = (f32[32,16]{0,1:T(8,128)S(1)}, f32[32,16]{0,1:T(8,128)S(1)}, u32[]{:S(2)}, u32[]{:S(2)}) collective-permute-start(f32[32,16]{0,1:T(8,128)S(1)} %get-tuple-element.69), channel_id=1, source_target_pairs={{0,128},{128,0},{1,129},{129,1},{2,130},{130,2},{3,131},{131,3},{4... | collective-permute-start | bytes 6152 | tf_op jit(solution)/shard_map/ppermute | solution.py:24
  5.6 2.9 %collective-permute-start.2 = (bf16[32,2048]{1,0:T(8,128)(2,1)}, bf16[32,2048]{1,0:T(8,128)(2,1)S(1)}, u32[]{:S(2)}, u32[]{:S(2)}) collective-permute-start(bf16[32,2048]{1,0:T(8,128)(2,1)} %param.12), channel_id=1, source_target_pairs={{0,128},{128,0},{1,129},{129,1},{2,130},{130,2},{3,131},{131,3},{4... | collective-permute-start | bytes 393224 | tf_op jit(solution)/shard_map/ppermute | solution.py:24
  8.6 4.1 %fusion.60 = (bf16[1,3,192,2048]{3,2,1,0:T(8,128)(2,1)}, bf16[3,192,2048]{2,1,0:T(8,128)(2,1)}) fusion(bf16[1,192,2048]{2,1,0:T(8,128)(2,1)} %refs_0_.5, bf16[2,192,2048]{2,1,0:T(8,128)(2,1)} %bitcast.71), kind=kLoop, calls=%fused_computation.140 | loop fusion | flops 1179648 | bytes 7077888 | tf_op jit(solution)/shard_map/stack | solution.py:334
  13.8 0.7 select_convert_fusion
  15.0 2.6 %multiply_convert_fusion = bf16[768,2048]{1,0:T(8,128)(2,1)} fusion(pred[768,128]{1,0:T(32,128)(4,1)S(1)} %fusion.15, f32[768]{0:T(1024)S(1)} %select_n.183, bf16[32,2048]{1,0:T(8,128)(2,1)S(1)} %collective-permute-done.2, bf16[32,2048]{1,0:T(8,128)(2,1)S(1)} %collective-permute-done.1, bf16[32,2048]{1,0:T(8,128)(2,1)S(1)} %copy-done.10, ...), kind=kOutput, calls=%fused_computation | convolution fusion | flops 407896064 | bytes 3771392 | tf_op jit(solution)/shard_map/dot_general | solution.py:42
  17.6 11.3 %all-to-all-start = ((bf16[32,24,2048]{2,1,0:T(8,128)(2,1)}), bf16[32,24,2048]{2,1,0:T(8,128)(2,1)}, u32[]{:S(2)}, u32[]{:S(2)}) async-start(bf16[32,24,2048]{2,1,0:T(8,128)(2,1)} %bitcast.28), calls=%async_computation | async-start | bytes 6291456 | tf_op jit(solution)/shard_map/all_to_all | solution.py:336
  29.0 1.2 slice_bitcast_fusion.1
  30.2 1.2 collective-permute-start.4
  31.4 49.7 %collective-permute-done.4._m.refs_4_ = bf16[1,192,2048]{2,1,0:T(8,128)(2,1)S(1)} collective-permute-done((bf16[1,192,2048]{2,1,0:T(8,128)(2,1)S(1)}, bf16[1,192,2048]{2,1,0:T(8,128)(2,1)S(1)}, u32[]{:S(2)}, u32[]{:S(2)}) %collective-permute-start.4) | collective-permute-done | bytes 786464 | tf_op jit(solution)/shard_map/ppermute | solution.py:24
  81.1 5.4 %pad_maximum_fusion = bf16[2,3,192,2048]{3,2,1,0:T(8,128)(2,1)} fusion(bf16[1,3,192,2048]{3,2,1,0:T(8,128)(2,1)S(1)} %bitcast.70, bf16[1,3,192,2048]{3,2,1,0:T(8,128)(2,1)} %get-tuple-element.40), kind=kLoop, calls=%fused_computation.1 | loop fusion | flops 2359296 | bytes 9437184 | tf_op jit(solution)/shard_map/stack | solution.py:334
  86.5 2.3 collective-permute-start.5
  89.5 18.8 %collective-permute-done.6._v.refs_5_ = bf16[1,192,2048]{2,1,0:T(8,128)(2,1)S(1)} collective-permute-done((bf16[1,192,2048]{2,1,0:T(8,128)(2,1)S(1)}, bf16[1,192,2048]{2,1,0:T(8,128)(2,1)S(1)}, u32[]{:S(2)}, u32[]{:S(2)}) %collective-permute-start.6) | collective-permute-done | bytes 786464 | tf_op jit(solution)/shard_map/ppermute | solution.py:24
  108.4 0.9 copy-done.3
  109.3 19.2 %shard_map.138 = (bf16[768,2048]{1,0:T(8,128)(2,1)}, bf16[2,384,2048]{2,1,0:T(8,128)(2,1)}, bf16[3,384,384]{2,1,0:T(8,128)(2,1)}, bf16[384,2048]{1,0:T(8,128)(2,...) custom-call(bf16[768,2048]{1,0:T(8,128)(2,1)} %bitcast.29.rows_ref, ...), custom_call_target="tpu_custom_call" | custom-call | flops 150994944 | bytes 786432 | tf_op jit(solution)/shard_map/pallas_call | solution.py:149
  128.5 0.9 collective-permute-start.7
  129.4 0.6 fusion.55
  130.7 2.0 collective-permute-done.7.core_ref
  132.6 1.1 copy-done.6
  133.8 4.8 %shard_map.139 = (bf16[192,2048]{1,0:T(8,128)(2,1)}, bf16[192,2048]{1,0:T(8,128)(2,1)}) custom-call(s32[1]{0:T(128)} %bitcast.35.flag_ref, bf16[2,384,2048]{2,1,0:T(8,128)(2,1)} %get-tuple-element.25.rows_ref, bf16[3,384,384]{2,1,0:T(8,128)(2,1)} %get-tuple-element.26.act_ref, bf16[384,2048]{1,0:T(8,128)(2,1)} %copy-done.6), custom_call_target="tpu_custom_call" | custom-call | flops 603979776 | bytes 4718592 | tf_op jit(solution)/shard_map/pallas_call | solution.py:195
  138.6 11.2 %all-to-all-start.1 = ((bf16[32,24,2048]{2,1,0:T(8,128)(2,1)}), bf16[32,24,2048]{2,1,0:T(8,128)(2,1)S(1)}, u32[]{:S(2)}, u32[]{:S(2)}) async-start(bf16[32,24,2048]{2,1,0:T(8,128)(2,1)} %bitcast.36), calls=%async_computation.1 | async-start | bytes 6291456 | tf_op jit(solution)/shard_map/all_to_all | solution.py:343
  149.8 0.7 collective-permute-start.11
  151.2 2.6 %collective-permute-done.11.core_ref = bf16[384,2048]{1,0:T(8,128)(2,1)S(1)} collective-permute-done((bf16[384,2048]{1,0:T(8,128)(2,1)}, bf16[384,2048]{1,0:T(8,128)(2,1)S(1)}, u32[]{:S(2)}, u32[]{:S(2)}) %collective-permute-start.11) | collective-permute-done | bytes 1572896 | tf_op jit(solution)/shard_map/ppermute | solution.py:24
  153.8 1.1 copy-done.5
  154.9 4.6 %shard_map.141 = (bf16[192,2048]{1,0:T(8,128)(2,1)}, bf16[192,2048]{1,0:T(8,128)(2,1)}) custom-call(s32[1]{0:T(128)} %bitcast.35.flag_ref, bf16[2,384,2048]{2,1,0:T(8,128)(2,1)} %get-tuple-element.25.rows_ref, bf16[3,384,384]{2,1,0:T(8,128)(2,1)} %get-tuple-element.26.act_ref, bf16[384,2048]{1,0:T(8,128)(2,1)} %copy-done.5, ...), custom_call_target="tpu_custom_call" | custom-call | flops 603979776 | bytes 4718592 | tf_op jit(solution)/shard_map/pallas_call | solution.py:195
  159.9 1.1 copy-done.4
  161.0 4.6 %shard_map.144 = (bf16[192,2048]{1,0:T(8,128)(2,1)}, bf16[192,2048]{1,0:T(8,128)(2,1)}) custom-call(s32[1]{0:T(128)} %bitcast.35.flag_ref, bf16[2,384,2048]{2,1,0:T(8,128)(2,1)} %get-tuple-element.25.rows_ref, bf16[3,384,384]{2,1,0:T(8,128)(2,1)} %get-tuple-element.26.act_ref, bf16[384,2048]{1,0:T(8,128)(2,1)} %copy-done.4, ...), custom_call_target="tpu_custom_call" | custom-call | flops 603979776 | bytes 4718592 | tf_op jit(solution)/shard_map/pallas_call | solution.py:195
  165.7 4.3 %collective-permute-done.9.recv_ref = bf16[192,2048]{1,0:T(8,128)(2,1)S(1)} collective-permute-done((bf16[192,2048]{1,0:T(8,128)(2,1)}, bf16[192,2048]{1,0:T(8,128)(2,1)S(1)}, u32[]{:S(2)}, u32[]{:S(2)}) %collective-permute-start.9) | collective-permute-done | bytes 786464 | tf_op jit(solution)/shard_map/ppermute | solution.py:24
  170.0 0.9 copy-done.9
  170.9 5.1 %shard_map.140.refs_0_ = bf16[192,2048]{1,0:T(8,128)(2,1)} custom-call(s32[1]{0:T(128)} %bitcast.35.flag_ref, bf16[192,2048]{1,0:T(8,128)(2,1)} %get-tuple-element.28.keep_ref.refs_0_, bf16[192,2048]{1,0:T(8,128)(2,1)} %copy-done.9, bf16[1,2,192,2048]{3,2,1,0:T(8,128)(2,1)} %refs_0_.4, bf16[1,2,192,2048]{3,2,1,0:T(8,128)(2,1)} %refs_1_.4, ...), custom_call_target="tpu_custom_call" | custom-call | flops 7864320 | bytes 7077888 | tf_op jit(solution)/shard_map/pallas_call | solution.py:235
  176.5 0.9 bitcast_select_fusion.2
  177.3 0.9 collective-permute-start.10
  178.3 8.7 %collective-permute-done.12.recv_ref = bf16[192,2048]{1,0:T(8,128)(2,1)S(1)} collective-permute-done((bf16[192,2048]{1,0:T(8,128)(2,1)}, bf16[192,2048]{1,0:T(8,128)(2,1)S(1)}, u32[]{:S(2)}, u32[]{:S(2)}) %collective-permute-start.12) | collective-permute-done | bytes 786464 | tf_op jit(solution)/shard_map/ppermute | solution.py:24
  187.0 0.9 copy-done.7
  187.9 4.6 %shard_map.142.refs_2_ = bf16[192,2048]{1,0:T(8,128)(2,1)} custom-call(s32[1]{0:T(128)} %bitcast.35.flag_ref, bf16[192,2048]{1,0:T(8,128)(2,1)} %get-tuple-element.32.keep_ref.refs_0_, bf16[192,2048]{1,0:T(8,128)(2,1)} %copy-done.7, bf16[1,2,192,2048]{3,2,1,0:T(8,128)(2,1)} %refs_0_.4, bf16[1,2,192,2048]{3,2,1,0:T(8,128)(2,1)} %refs_1_.4, ...), custom_call_target="tpu_custom_call" | custom-call | flops 7864320 | bytes 4718592 | tf_op jit(solution)/shard_map/pallas_call | solution.py:235
  192.5 0.9 collective-permute-start.13
  193.4 10.3 %collective-permute-done.15.recv_ref = bf16[192,2048]{1,0:T(8,128)(2,1)S(1)} collective-permute-done((bf16[192,2048]{1,0:T(8,128)(2,1)S(1)}, bf16[192,2048]{1,0:T(8,128)(2,1)S(1)}, u32[]{:S(2)}, u32[]{:S(2)}) %collective-permute-start.15) | collective-permute-done | bytes 786464 | tf_op jit(solution)/shard_map/ppermute | solution.py:24
  203.7 0.9 copy-done.8
  204.6 4.6 %shard_map.145.refs_0_ = bf16[192,2048]{1,0:T(8,128)(2,1)} custom-call(s32[1]{0:T(128)} %bitcast.35.flag_ref, bf16[192,2048]{1,0:T(8,128)(2,1)} %get-tuple-element.35.keep_ref, bf16[192,2048]{1,0:T(8,128)(2,1)} %copy-done.8, bf16[1,192,2048]{2,1,0:T(8,128)(2,1)} %refs_0_.5, bf16[1,192,2048]{2,1,0:T(8,128)(2,1)} %refs_1_.5, bf16[1,192,2048]{2,1,0:T(8,128)(2,1)} %refs_2_.5), custom_call_target="tpu_custom_call" | custom-call | flops 7864320 | bytes 4718592 | tf_op jit(solution)/shard_map/pallas_call | solution.py:235
  209.2 0.9 collective-permute-start.16
  210.1 11.5 %all-to-all-done.1 = bf16[32,24,2048]{2,1,0:T(8,128)(2,1)S(1)} async-done(((bf16[32,24,2048]{2,1,0:T(8,128)(2,1)}), bf16[32,24,2048]{2,1,0:T(8,128)(2,1)S(1)}, u32[]{:S(2)}, u32[]{:S(2)}) %all-to-all-start.1) | async-done | bytes 3145760 | tf_op jit(solution)/shard_map/all_to_all | solution.py:343
  221.6 2.3 fusion.2
  224.2 1.0 collective-permute-start.8
  225.3 2.8 %shard_map.143 = bf16[2,192,2048]{2,1,0:T(8,128)(2,1)} custom-call(s32[1]{0:T(128)} %bitcast.35.flag_ref, bf16[192,2048]{1,0:T(8,128)(2,1)} %shard_map.140.refs_0_, bf16[192,2048]{1,0:T(8,128)(2,1)} %collective-permute-done.10.refs_1_, bf16[192,2048]{1,0:T(8,128)(2,1)} %shard_map.142.refs_2_, bf16[192,2048]{1,0:T(8,128)(2,1)} %collective-permute-done.13.refs_3_, ...), custom_call_target="tpu_custom_call" | custom-call | flops 786432 | bytes 4718592 | tf_op jit(solution)/shard_map/pallas_call | solution.py:261
  228.1 15.6 %collective-permute-done.8 = bf16[64,2048]{1,0:T(8,128)(2,1)S(1)} collective-permute-done((bf16[64,2048]{1,0:T(8,128)(2,1)S(1)}, bf16[64,2048]{1,0:T(8,128)(2,1)S(1)}, u32[]{:S(2)}, u32[]{:S(2)}) %collective-permute-start.8) | collective-permute-done | bytes 262176 | tf_op jit(solution)/shard_map/ppermute | solution.py:24
  243.7 0.8 fusion.16
  244.5 2.1 shard_map.146
  (74 shorter events, 3.8 us)
Async XLA Ops:
  2.0 11.2 %collective-permute-start = (f32[32,16]{0,1:T(8,128)S(1)}, f32[32,16]{0,1:T(8,128)S(1)}, u32[]{:S(2)}, u32[]{:S(2)}) collective-permute-start(f32[32,16]{0,1:T(8,128)S(1)} %get-tuple-element.69), channel_id=1, source_target_pairs={{0,128},{128,0},{1,129},{129,1},{2,130},{130,2},{3,131},{131,3},{4... | collective-permute-start | bytes 6152 | tf_op jit(solution)/shard_map/ppermute | solution.py:24
  5.6 9.4 %collective-permute-start.1 = (bf16[32,2048]{1,0:T(8,128)(2,1)}, bf16[32,2048]{1,0:T(8,128)(2,1)S(1)}, u32[]{:S(2)}, u32[]{:S(2)}) collective-permute-start(bf16[32,2048]{1,0:T(8,128)(2,1)} %param.11), channel_id=1, source_target_pairs={{0,128},{128,0},{1,129},{129,1},{2,130},{130,2},{3,131},{131,3},{4... | collective-permute-start | bytes 393224 | tf_op jit(solution)/shard_map/ppermute | solution.py:24
  5.6 9.4 %collective-permute-start.2 = (bf16[32,2048]{1,0:T(8,128)(2,1)}, bf16[32,2048]{1,0:T(8,128)(2,1)S(1)}, u32[]{:S(2)}, u32[]{:S(2)}) collective-permute-start(bf16[32,2048]{1,0:T(8,128)(2,1)} %param.12), channel_id=1, source_target_pairs={{0,128},{128,0},{1,129},{129,1},{2,130},{130,2},{3,131},{131,3},{4... | collective-permute-start | bytes 393224 | tf_op jit(solution)/shard_map/ppermute | solution.py:24
  8.6 6.4 %copy-start.10 = (bf16[32,2048]{1,0:T(8,128)(2,1)S(1)}, bf16[32,2048]{1,0:T(8,128)(2,1)}, u32[]{:S(2)}) copy-start(bf16[32,2048]{1,0:T(8,128)(2,1)} %param.12) | copy-start | bytes 393220
  8.6 6.4 %copy-start.11 = (bf16[32,2048]{1,0:T(8,128)(2,1)S(1)}, bf16[32,2048]{1,0:T(8,128)(2,1)}, u32[]{:S(2)}) copy-start(bf16[32,2048]{1,0:T(8,128)(2,1)} %param.11) | copy-start | bytes 393220
  12.7 68.4 %collective-permute-start.3 = (bf16[3,192,2048]{2,1,0:T(8,128)(2,1)}, bf16[3,192,2048]{2,1,0:T(8,128)(2,1)S(1)}, u32[]{:S(2)}, u32[]{:S(2)}) collective-permute-start(bf16[3,192,2048]{2,1,0:T(8,128)(2,1)} %get-tuple-element.41.w_own), channel_id=1, source_target_pairs={{0,2},{2,0},{1,3},{3,1},{4,6},{6,4},{5,7},{7,5},{8,10},{10,8},{9,1... | collective-permute-start | bytes 7077896 | tf_op jit(solution)/shard_map/ppermute | solution.py:24
  13.1 4.5 %copy-start.12 = (pred[24,128]{1,0:T(8,128)(4,1)}, pred[24,128]{1,0:T(8,128)(4,1)S(1)}, u32[]{:S(2)}) copy-start(pred[24,128]{1,0:T(8,128)(4,1)S(1)} %broadcast_compare_fusion) | copy-start | bytes 9220
  13.2 4.4 %copy-start.14 = (s32[768]{0:T(1024)}, s32[768]{0:T(1024)S(1)}, u32[]{:S(2)}) copy-start(s32[768]{0:T(1024)S(1)} %eq.199) | copy-start | bytes 9220
  17.6 90.7 %all-to-all-start = ((bf16[32,24,2048]{2,1,0:T(8,128)(2,1)}), bf16[32,24,2048]{2,1,0:T(8,128)(2,1)}, u32[]{:S(2)}, u32[]{:S(2)}) async-start(bf16[32,24,2048]{2,1,0:T(8,128)(2,1)} %bitcast.28), calls=%async_computation | async-start | bytes 6291456 | tf_op jit(solution)/shard_map/all_to_all | solution.py:336
  30.2 50.9 %collective-permute-start.4 = (bf16[1,192,2048]{2,1,0:T(8,128)(2,1)S(1)}, bf16[1,192,2048]{2,1,0:T(8,128)(2,1)S(1)}, u32[]{:S(2)}, u32[]{:S(2)}) collective-permute-start(bf16[1,192,2048]{2,1,0:T(8,128)(2,1)S(1)} %slice_bitcast_fusion.1), channel_id=1, source_target_pairs={{0,2},{2,0},{1,3},{3,1},{4,6},{6,4},{5,7},{7,5},{8,10},{10,8},{9,1... | collective-permute-start | bytes 2359304 | tf_op jit(solution)/shard_map/ppermute | solution.py:24
  81.1 5.5 %copy-start.2 = (bf16[1,192,2048]{2,1,0:T(8,128)(2,1)}, bf16[1,192,2048]{2,1,0:T(8,128)(2,1)S(1)}, u32[]{:S(2)}) copy-start(bf16[1,192,2048]{2,1,0:T(8,128)(2,1)S(1)} %collective-permute-done.4._m.refs_4_) | copy-start | bytes 2359300
  81.1 5.5 %copy-start = (bf16[3,192,2048]{2,1,0:T(8,128)(2,1)}, bf16[3,192,2048]{2,1,0:T(8,128)(2,1)S(1)}, u32[]{:S(2)}) copy-start(bf16[3,192,2048]{2,1,0:T(8,128)(2,1)S(1)} %collective-permute-done.3.w_xl.refs_3_) | copy-start | bytes 7077892
  81.1 7.8 %copy-start.1 = (bf16[1,2,192,2048]{3,2,1,0:T(8,128)(2,1)S(1)}, bf16[1,2,192,2048]{3,2,1,0:T(8,128)(2,1)}, u32[]{:S(2)}) copy-start(bf16[1,2,192,2048]{3,2,1,0:T(8,128)(2,1)} %refs_2_.4) | copy-start | bytes 4718596
  86.5 21.9 %collective-permute-start.5 = (bf16[2,3,192,2048]{3,2,1,0:T(8,128)(2,1)}, bf16[2,3,192,2048]{3,2,1,0:T(8,128)(2,1)}, u32[]{:S(2)}, u32[]{:S(2)}) collective-permute-start(bf16[2,3,192,2048]{3,2,1,0:T(8,128)(2,1)} %pad_maximum_fusion), channel_id=1, source_target_pairs={{0,1},{1,0},{2,3},{3,2},{4,5},{5,4},{6,7},{7,6},{8,9},{9,8},{10,11... | collective-permute-start | bytes 14155784 | tf_op jit(solution)/shard_map/ppermute | solution.py:24
  89.0 19.4 %collective-permute-start.6 = (bf16[1,192,2048]{2,1,0:T(8,128)(2,1)S(1)}, bf16[1,192,2048]{2,1,0:T(8,128)(2,1)S(1)}, u32[]{:S(2)}, u32[]{:S(2)}) collective-permute-start(bf16[1,192,2048]{2,1,0:T(8,128)(2,1)S(1)} %slice_bitcast_fusion), channel_id=1, source_target_pairs={{0,2},{2,0},{1,3},{3,1},{4,6},{6,4},{5,7},{7,5},{8,10},{10,8},{9,1... | collective-permute-start | bytes 2359304 | tf_op jit(solution)/shard_map/ppermute | solution.py:24
  108.4 0.9 copy-start.3
  109.3 20.1 %copy-start.18 = (s32[64]{0:T(128)S(1)}, s32[64]{0:T(128)}, u32[]{:S(2)}) copy-start(s32[64]{0:T(128)} %param.15) | copy-start | bytes 772
  128.5 4.1 %collective-permute-start.7 = (bf16[384,2048]{1,0:T(8,128)(2,1)}, bf16[384,2048]{1,0:T(8,128)(2,1)S(1)}, u32[]{:S(2)}, u32[]{:S(2)}) collective-permute-start(bf16[384,2048]{1,0:T(8,128)(2,1)} %get-tuple-element.27), channel_id=1, source_target_pairs={{0,1},{1,0},{2,3},{3,2},{4,5},{5,4},{6,7},{7,6},{8,9},{9,8},{10,11... | collective-permute-start | bytes 4718600 | tf_op jit(solution)/shard_map/ppermute | solution.py:24
  132.6 1.1 copy-start.6
  138.6 83.1 %all-to-all-start.1 = ((bf16[32,24,2048]{2,1,0:T(8,128)(2,1)}), bf16[32,24,2048]{2,1,0:T(8,128)(2,1)S(1)}, u32[]{:S(2)}, u32[]{:S(2)}) async-start(bf16[32,24,2048]{2,1,0:T(8,128)(2,1)} %bitcast.36), calls=%async_computation.1 | async-start | bytes 6291456 | tf_op jit(solution)/shard_map/all_to_all | solution.py:343
  149.8 4.0 %collective-permute-start.11 = (bf16[384,2048]{1,0:T(8,128)(2,1)}, bf16[384,2048]{1,0:T(8,128)(2,1)S(1)}, u32[]{:S(2)}, u32[]{:S(2)}) collective-permute-start(bf16[384,2048]{1,0:T(8,128)(2,1)} %get-tuple-element.31), channel_id=1, source_target_pairs={{0,1},{1,0},{2,3},{3,2},{4,5},{5,4},{6,7},{7,6},{8,9},{9,8},{10,11... | collective-permute-start | bytes 4718600 | tf_op jit(solution)/shard_map/ppermute | solution.py:24
  150.5 9.3 %collective-permute-start.14 = (bf16[384,2048]{1,0:T(8,128)(2,1)}, bf16[384,2048]{1,0:T(8,128)(2,1)S(1)}, u32[]{:S(2)}, u32[]{:S(2)}) collective-permute-start(bf16[384,2048]{1,0:T(8,128)(2,1)} %get-tuple-element.34), channel_id=1, source_target_pairs={{0,1},{1,0},{2,3},{3,2},{4,5},{5,4},{6,7},{7,6},{8,9},{9,8},{10,11... | collective-permute-start | bytes 4718600 | tf_op jit(solution)/shard_map/ppermute | solution.py:24
  150.9 19.2 %collective-permute-start.9 = (bf16[192,2048]{1,0:T(8,128)(2,1)}, bf16[192,2048]{1,0:T(8,128)(2,1)S(1)}, u32[]{:S(2)}, u32[]{:S(2)}) collective-permute-start(bf16[192,2048]{1,0:T(8,128)(2,1)} %get-tuple-element.30), channel_id=1, source_target_pairs={{0,2},{2,0},{1,3},{3,1},{4,6},{6,4},{5,7},{7,5},{8,10},{10,8},{9,1... | collective-permute-start | bytes 2359304 | tf_op jit(solution)/shard_map/ppermute | solution.py:24
  153.8 1.1 copy-start.5
  159.6 27.4 %collective-permute-start.12 = (bf16[192,2048]{1,0:T(8,128)(2,1)}, bf16[192,2048]{1,0:T(8,128)(2,1)S(1)}, u32[]{:S(2)}, u32[]{:S(2)}) collective-permute-start(bf16[192,2048]{1,0:T(8,128)(2,1)} %get-tuple-element.33), channel_id=1, source_target_pairs={{0,2},{2,0},{1,3},{3,1},{4,6},{6,4},{5,7},{7,5},{8,10},{10,8},{9,1... | collective-permute-start | bytes 2359304 | tf_op jit(solution)/shard_map/ppermute | solution.py:24
  159.9 1.1 copy-start.4
  165.7 10.3 %copy-start.17 = (bf16[192,2048]{1,0:T(8,128)(2,1)S(1)}, bf16[192,2048]{1,0:T(8,128)(2,1)}, u32[]{:S(2)}) copy-start(bf16[192,2048]{1,0:T(8,128)(2,1)} %get-tuple-element.37) | copy-start | bytes 2359300
  165.7 10.8 %copy-start.13 = (pred[24,128]{1,0:T(8,128)(4,1)S(1)}, pred[24,128]{1,0:T(8,128)(4,1)}, u32[]{:S(2)}) copy-start(pred[24,128]{1,0:T(8,128)(4,1)} %copy-done.12) | copy-start | bytes 9220
  165.7 10.8 %copy-start.15 = (s32[768]{0:T(1024)S(1)}, s32[768]{0:T(1024)}, u32[]{:S(2)}) copy-start(s32[768]{0:T(1024)} %copy-done.14) | copy-start | bytes 9220
  165.7 10.8 %copy-start.16 = (bf16[32,128]{1,0:T(8,128)(2,1)S(1)}, bf16[32,128]{1,0:T(8,128)(2,1)}, u32[]{:S(2)}) copy-start(bf16[32,128]{1,0:T(8,128)(2,1)} %get-tuple-element.38) | copy-start | bytes 24580
  170.0 0.9 copy-start.9
  176.0 27.7 %collective-permute-start.15 = (bf16[192,2048]{1,0:T(8,128)(2,1)S(1)}, bf16[192,2048]{1,0:T(8,128)(2,1)S(1)}, u32[]{:S(2)}, u32[]{:S(2)}) collective-permute-start(bf16[192,2048]{1,0:T(8,128)(2,1)S(1)} %copy-done.17), channel_id=1, source_target_pairs={{0,2},{2,0},{1,3},{3,1},{4,6},{6,4},{5,7},{7,5},{8,10},{10,8},{9,1... | collective-permute-start | bytes 2359304 | tf_op jit(solution)/shard_map/ppermute | solution.py:24
  177.3 47.9 %collective-permute-start.10 = (bf16[192,2048]{1,0:T(8,128)(2,1)}, bf16[192,2048]{1,0:T(8,128)(2,1)}, u32[]{:S(2)}, u32[]{:S(2)}) collective-permute-start(bf16[192,2048]{1,0:T(8,128)(2,1)} %shard_map.140.refs_0_), channel_id=1, source_target_pairs={{0,130},{130,0},{2,128},{128,2},{1,131},{131,1},{3,129},{129,3},{4... | collective-permute-start | bytes 2359304 | tf_op jit(solution)/shard_map/ppermute | solution.py:351
  187.0 0.9 copy-start.7
  192.5 32.8 %collective-permute-start.13 = (bf16[192,2048]{1,0:T(8,128)(2,1)}, bf16[192,2048]{1,0:T(8,128)(2,1)}, u32[]{:S(2)}, u32[]{:S(2)}) collective-permute-start(bf16[192,2048]{1,0:T(8,128)(2,1)} %shard_map.142.refs_2_), channel_id=1, source_target_pairs={{0,128},{128,0},{1,129},{129,1},{2,130},{130,2},{3,131},{131,3},{4... | collective-permute-start | bytes 2359304 | tf_op jit(solution)/shard_map/ppermute | solution.py:24
  203.7 0.9 copy-start.8
  209.2 35.3 %collective-permute-start.16 = (bf16[192,2048]{1,0:T(8,128)(2,1)}, bf16[192,2048]{1,0:T(8,128)(2,1)}, u32[]{:S(2)}, u32[]{:S(2)}) collective-permute-start(bf16[192,2048]{1,0:T(8,128)(2,1)} %shard_map.145.refs_0_), channel_id=1, source_target_pairs={{0,128},{128,0},{1,129},{129,1},{2,130},{130,2},{3,131},{131,3},{4... | collective-permute-start | bytes 2359304 | tf_op jit(solution)/shard_map/ppermute | solution.py:24
  224.2 19.4 %collective-permute-start.8 = (bf16[64,2048]{1,0:T(8,128)(2,1)S(1)}, bf16[64,2048]{1,0:T(8,128)(2,1)S(1)}, u32[]{:S(2)}, u32[]{:S(2)}) collective-permute-start(bf16[64,2048]{1,0:T(8,128)(2,1)S(1)} %slice.251), channel_id=1, source_target_pairs={{0,128},{128,0},{1,129},{129,1},{2,130},{130,2},{3,131},{131,3},{4... | collective-permute-start | bytes 786440 | tf_op jit(solution)/shard_map/ppermute | solution.py:24

commit v8 on v7

--- a/solution.py
+++ b/solution.py
@@ -60,7 +60,7 @@
     return (at == (row // 4) * 8 + part * 4 + row % 4).astype(BF16)
 
 
-def rows_kernel(rows_ref, w_own, w_xl, w_pair, _m, _v, back_ref, xd_out, act_out, g_gate, g_up, g_down,
+def rows_kernel(rows_ref, w_own, w_xl, w_pair, _mv, back_ref, xd_out, act_out, g_gate, g_up, g_down,
                 w_all, xd, mixed, acts, g_all, w_sem, xd_sem, act_sem, g_sem):
     share = w_own.shape[1]
     width = 4 * share
@@ -140,7 +140,7 @@
         store.wait()
 
 
-def rows_step(rows, w_own, w_xl, w_pair, m_xl, v_xl):
+def rows_step(rows, w_own, w_xl, w_pair, mv_xl):
     total, feature = rows.shape
     half = total // 2
     share = w_own.shape[1]
@@ -153,7 +153,7 @@
             jax.ShapeDtypeStruct((2, half, feature), BF16),
             jax.ShapeDtypeStruct((3, half, 2 * share), BF16),
         ) + (jax.ShapeDtypeStruct((2 * share, feature), BF16),) * 3,
-        in_specs=[vmem_spec] + [any_spec] * 5,
+        in_specs=[vmem_spec] + [any_spec] * 4,
         out_specs=(vmem_spec,) + (any_spec,) * 5,
         scratch_shapes=[
             pltpu.VMEM((3, 4 * share, feature), BF16),
@@ -172,7 +172,7 @@
             bytes_accessed=half * feature,
             transcendentals=0,
         ),
-    )(rows, w_own, w_xl, w_pair, m_xl, v_xl)
+    )(rows, w_own, w_xl, w_pair, mv_xl)
 
 
 def grads_kernel(exchange, flag_ref, rows_ref, act_ref, core_ref, *refs):
@@ -299,8 +299,9 @@
     source = jnp.concatenate([tokens, cotangent, tokens_other, cotangent_other])
 
     w_own = jnp.concatenate([gate_up[0], down])
-    w_first = w_own
+    w_first = after(w_own, tokens_other, cotangent_other, named_other)
     w_xl = swap(w_first, "xl")
+    w_pair = swap(jnp.stack([w_own, w_xl]), "core")
 
     both = jnp.stack([named, named_other])
     both_routes = both[:, :, :top].astype(jnp.int32)
@@ -329,16 +330,15 @@
     pick_b = pick.astype(BF16).reshape(rings * 2 * slots, 4 * count)
     send = (dot_nn(pick_b, source) * factor).astype(BF16).reshape(rings, 2 * slots, feature)
 
-    m_xl = swap(after(gate_up_m[0, :1], send), "xl")
-    v_xl = swap(after(gate_up_v[0, :1], send), "xl")
-    w_pair = swap(jnp.stack([w_own, after(w_xl, m_xl)]), "core")
+    mv_xl = swap(after(jnp.concatenate([gate_up_m[0, :1], gate_up_v[0, :1]]), send), "xl")
+    mv_up = swap(after(jnp.concatenate([gate_up_m[0, 1:], gate_up_v[0, 1:]]), send), "xl")
 
     recv = lax.all_to_all(send, RINGS, split_axis=0, concat_axis=0, tiled=True)
-    back_send, xd, acts, *g_pair = rows_step(recv.reshape(-1, feature), w_own, w_xl, w_pair, m_xl, v_xl)
+    back_send, xd, acts, *g_pair = rows_step(recv.reshape(-1, feature), w_own, w_xl, w_pair, mv_xl)
 
     g_core = [swap(g, "core") for g in g_pair]
-    gate = grads_step(True, flag, xd, 0, acts, 0, g_core[0])
-    up = grads_step(False, flag, xd, 0, acts, 1, g_core[1], gate[0])
+    gate = grads_step(True, flag, xd, 0, acts, 0, g_core[0], mv_up)
+    up = grads_step(True, flag, xd, 0, acts, 1, g_core[1], gate[0])
     down_g = grads_step(False, flag, xd, 1, acts, 2, g_core[2], up[0])
     back = lax.all_to_all(
         after(back_send, gate[0]).reshape(recv.shape), RINGS, split_axis=0, concat_axis=0, tiled=True
@@ -346,13 +346,13 @@
     parts = (gate[0], up[0], down_g[0], gate[1], up[1], down_g[1])
     others = [swap(parts[3], "xl"), swap(parts[4], "xl")]
     new_gate = adam_step(flag, (parts[0], ()), (others[0], ()), (gate_up, (0, 0)), (gate_up_m, (0, 0)),
-                         (gate_up_v, (0, 0)), (w_xl, (0,)), (m_xl, (0,)), (v_xl, (0,)))
+                         (gate_up_v, (0, 0)), (w_xl, (0,)), (mv_xl, (0,)), (mv_xl, (1,)))
     others.append(swap(after(parts[5], new_gate), "xl"))
     gate_other = lax.ppermute(new_gate, ("xh", "xl"), ACROSS)
     new_up = adam_step(flag, (parts[1], ()), (others[1], ()), (gate_up, (0, 1)), (gate_up_m, (0, 1)),
-                       (gate_up_v, (0, 1)))
-    arrived = [new_gate, gate_other, new_up, swap(new_up, "xh")]
-    new_gate_up = settle(flag, arrived, m_xl)
+                       (gate_up_v, (0, 1)), (w_xl, (1,)), (mv_up, (0,)), (mv_up, (1,)))
+    arrived = [new_gate, gate_other, new_up, lax.ppermute(new_up, ("xh", "xl"), ACROSS)]
+    new_gate_up = settle(flag, arrived, mv_xl)
     new_down = adam_step(flag, (parts[2], ()), (others[2], ()), (down, (0,)), (down_m, (0,)),
                          (down_v, (0,)))
     down_other = swap(new_down, "xh")

time: 247 us -> 256 us (1.036)
  starting transfers between devices: 40.3 us -> 45.9 us
    ppermute x0 -> x1, waiting for transfers between devices: none -> 14.6 us  [body(): lax.ppermute(new_up, ('xh', 'xl'), ACROSS)]
    ppermute x16 -> x15, waiting for transfers between devices: 112 us -> 102 us  [swap(): return lax.ppermute(block, axis, [(0, 1), (1, 0)])]
    ppermute x16 -> x15, starting transfers between devices: 16.9 us -> 21.1 us  [swap(): return lax.ppermute(block, axis, [(0, 1), (1, 0)])]
    all_to_all x1, waiting for transfers between devices: 11.5 us -> 8.05 us  [body(): lax.all_to_all(after(back_send, gate[0]).reshape(recv.shape), RINGS, spli...]
    unnamed x38 -> x40, local copies, waits for them, and re-layouts: 6.98 us -> 7.8 us
  transfers between devices with their start and end apart: 19 -> 19, of which waited for: 9 -> 10; matrix products, arithmetic and copies ran while one was open for 8% -> 8% of each run, Pallas kernels for 11% -> 18%
where the time goes in v8:
time: 256 us; the launch traced here: 255 us
  waiting for transfers between devices  125 us (49%)
  Pallas kernels  53.2 us (21%)
  starting transfers between devices  45.9 us (18%)
  other arithmetic  16 us (6%)
  local copies, waits for them, and re-layouts  8.23 us (3%)
  matrix products  5.16 us (2%)
    ppermute x15, waiting for transfers between devices, swap(): return lax.ppermute(block, axis, [(0, 1), (1, 0)])  102 us
    ppermute x15, starting transfers between devices, swap(): return lax.ppermute(block, axis, [(0, 1), (1, 0)])  21.1 us
    pallas_call x1, Pallas kernels, rows_step(): pl.pallas_call(rows_kernel, out_shape=(jax.ShapeDtypeStruct(rows.shape, B...  19.3 us
    pallas_call x3, Pallas kernels, adam_step(): pl.pallas_call(adam_kernel, grid=(steps,), out_shape=jax.ShapeDtypeStruct...  14.8 us
    ppermute x1, waiting for transfers between devices, body(): lax.ppermute(new_up, ('xh', 'xl'), ACROSS)  14.6 us
    pallas_call x3, Pallas kernels, grads_step(): pl.pallas_call(functools.partial(grads_kernel, exchange), grid=(feature /...  14.2 us
    all_to_all x1, starting transfers between devices, body(): recv = lax.all_to_all(send, RINGS, split_axis=0, concat_axis=0, tiled=True)  11.3 us
    all_to_all x1, starting transfers between devices, body(): lax.all_to_all(after(back_send, gate[0]).reshape(recv.shape), RINGS, spli...  11.2 us
  transfers between devices with their start and end apart: 19, of which 10 were waited for; matrix products, arithmetic and copies ran while one was open for 8% of the time, Pallas kernels for 18%

profile of v8, /device:TPU:1, one launch (start us, length us, event | category | flops | bytes accessed | tf_op | source)
XLA Modules:
  0.0 255.2 jit_solution(7352800142023461104)
XLA Ops:
  0.6 0.7 convert_element_type.115
  1.3 0.7 pad_maximum_fusion.5
  2.0 3.6 %collective-permute-start = (f32[32,16]{0,1:T(8,128)S(1)}, f32[32,16]{0,1:T(8,128)S(1)}, u32[]{:S(2)}, u32[]{:S(2)}) collective-permute-start(f32[32,16]{0,1:T(8,128)S(1)} %get-tuple-element.73), channel_id=1, source_target_pairs={{0,128},{128,0},{1,129},{129,1},{2,130},{130,2},{3,131},{131,3},{4... | collective-permute-start | bytes 6152 | tf_op jit(solution)/shard_map/ppermute | solution.py:24
  5.6 2.9 %collective-permute-start.2 = (bf16[32,2048]{1,0:T(8,128)(2,1)}, bf16[32,2048]{1,0:T(8,128)(2,1)S(1)}, u32[]{:S(2)}, u32[]{:S(2)}) collective-permute-start(bf16[32,2048]{1,0:T(8,128)(2,1)} %param.12), channel_id=1, source_target_pairs={{0,128},{128,0},{1,129},{129,1},{2,130},{130,2},{3,131},{131,3},{4... | collective-permute-start | bytes 393224 | tf_op jit(solution)/shard_map/ppermute | solution.py:24
  8.7 4.1 %fusion.60 = (bf16[1,3,192,2048]{3,2,1,0:T(8,128)(2,1)}, bf16[3,192,2048]{2,1,0:T(8,128)(2,1)}) fusion(bf16[1,192,2048]{2,1,0:T(8,128)(2,1)} %refs_0_.5, bf16[2,192,2048]{2,1,0:T(8,128)(2,1)} %bitcast.76), kind=kLoop, calls=%fused_computation.144 | loop fusion | flops 1179648 | bytes 7077888 | tf_op jit(solution)/shard_map/stack | solution.py:304
  13.3 0.8 collective-permute-done.2
  14.6 0.7 select_convert_fusion
  15.8 2.6 %multiply_convert_fusion = bf16[768,2048]{1,0:T(8,128)(2,1)} fusion(pred[768,128]{1,0:T(32,128)(4,1)S(1)} %fusion.15, f32[768]{0:T(1024)S(1)} %select_n.183, bf16[32,2048]{1,0:T(8,128)(2,1)S(1)} %collective-permute-done.2, bf16[32,2048]{1,0:T(8,128)(2,1)S(1)} %collective-permute-done.1, bf16[32,2048]{1,0:T(8,128)(2,1)S(1)} %copy-done.11, ...), kind=kOutput, calls=%fused_computation | convolution fusion | flops 407896064 | bytes 3771392 | tf_op jit(solution)/shard_map/dot_general | solution.py:42
  18.4 11.3 %all-to-all-start = ((bf16[32,24,2048]{2,1,0:T(8,128)(2,1)}), bf16[32,24,2048]{2,1,0:T(8,128)(2,1)}, u32[]{:S(2)}, u32[]{:S(2)}) async-start(bf16[32,24,2048]{2,1,0:T(8,128)(2,1)} %bitcast.75), calls=%async_computation | async-start | bytes 6291456 | tf_op jit(solution)/shard_map/all_to_all | solution.py:336
  29.8 35.6 %collective-permute-done.3.w_xl.refs_3_ = bf16[3,192,2048]{2,1,0:T(8,128)(2,1)S(1)} collective-permute-done((bf16[3,192,2048]{2,1,0:T(8,128)(2,1)}, bf16[3,192,2048]{2,1,0:T(8,128)(2,1)S(1)}, u32[]{:S(2)}, u32[]{:S(2)}) %collective-permute-start.3) | collective-permute-done | bytes 2359328 | tf_op jit(solution)/shard_map/ppermute | solution.py:24
  65.4 5.2 %pad_maximum_fusion = bf16[2,3,192,2048]{3,2,1,0:T(8,128)(2,1)} fusion(bf16[1,3,192,2048]{3,2,1,0:T(8,128)(2,1)S(1)} %bitcast.74, bf16[1,3,192,2048]{3,2,1,0:T(8,128)(2,1)} %get-tuple-element.40), kind=kLoop, calls=%fused_computation.1 | loop fusion | flops 2359296 | bytes 9437184 | tf_op jit(solution)/shard_map/stack | solution.py:304
  70.5 2.7 %collective-permute-start.4 = (bf16[2,3,192,2048]{3,2,1,0:T(8,128)(2,1)}, bf16[2,3,192,2048]{3,2,1,0:T(8,128)(2,1)}, u32[]{:S(2)}, u32[]{:S(2)}) collective-permute-start(bf16[2,3,192,2048]{3,2,1,0:T(8,128)(2,1)} %pad_maximum_fusion), channel_id=1, source_target_pairs={{0,1},{1,0},{2,3},{3,2},{4,5},{5,4},{6,7},{7,6},{8,9},{9,8},{10,11... | collective-permute-start | bytes 14155784 | tf_op jit(solution)/shard_map/ppermute | solution.py:24
  73.4 1.4 pad_maximum_fusion.2
  75.2 1.2 collective-permute-start.7
  76.3 33.1 %collective-permute-done.5._mv.refs_4_.refs_5_ = bf16[2,192,2048]{2,1,0:T(8,128)(2,1)S(1)} collective-permute-done((bf16[2,192,2048]{2,1,0:T(8,128)(2,1)S(1)}, bf16[2,192,2048]{2,1,0:T(8,128)(2,1)S(1)}, u32[]{:S(2)}, u32[]{:S(2)}) %collective-permute-start.5) | collective-permute-done | bytes 1572896 | tf_op jit(solution)/shard_map/ppermute | solution.py:24
  109.5 1.2 copy-done.1
  110.7 19.3 %shard_map.138 = (bf16[768,2048]{1,0:T(8,128)(2,1)}, bf16[2,384,2048]{2,1,0:T(8,128)(2,1)}, bf16[3,384,384]{2,1,0:T(8,128)(2,1)}, bf16[384,2048]{1,0:T(8,128)(2,...) custom-call(bf16[768,2048]{1,0:T(8,128)(2,1)} %bitcast.29.rows_ref, ...), custom_call_target="tpu_custom_call" | custom-call | flops 150994944 | bytes 786432 | tf_op jit(solution)/shard_map/pallas_call | solution.py:149
  129.9 4.1 %collective-permute-start.6 = (bf16[384,2048]{1,0:T(8,128)(2,1)}, bf16[384,2048]{1,0:T(8,128)(2,1)S(1)}, u32[]{:S(2)}, u32[]{:S(2)}) collective-permute-start(bf16[384,2048]{1,0:T(8,128)(2,1)} %get-tuple-element.26), channel_id=1, source_target_pairs={{0,1},{1,0},{2,3},{3,2},{4,5},{5,4},{6,7},{7,6},{8,9},{9,8},{10,11... | collective-permute-start | bytes 4718600 | tf_op jit(solution)/shard_map/ppermute | solution.py:24
  135.3 7.9 %collective-permute-done.7.refs_0_.refs_4_.refs_5_ = bf16[2,192,2048]{2,1,0:T(8,128)(2,1)S(1)} collective-permute-done((bf16[2,192,2048]{2,1,0:T(8,128)(2,1)}, bf16[2,192,2048]{2,1,0:T(8,128)(2,1)S(1)}, u32[]{:S(2)}, u32[]{:S(2)}) %collective-permute-start.7) | collective-permute-done | bytes 1572896 | tf_op jit(solution)/shard_map/ppermute | solution.py:24
  143.2 1.1 copy-done.2
  144.8 4.8 %shard_map.139 = (bf16[192,2048]{1,0:T(8,128)(2,1)}, bf16[192,2048]{1,0:T(8,128)(2,1)}) custom-call(s32[1]{0:T(128)} %bitcast.35.flag_ref, bf16[2,384,2048]{2,1,0:T(8,128)(2,1)} %get-tuple-element.24.rows_ref, bf16[3,384,384]{2,1,0:T(8,128)(2,1)} %get-tuple-element.25.act_ref, bf16[384,2048]{1,0:T(8,128)(2,1)} %copy-done.5, bf16[2,192,2048]{2,1,0:T(8,128)(2,1)} %copy-done.2), custom_call_target="tpu_custom_call" | custom-call | flops 603979776 | bytes 4718592 | tf_op jit(solution)/shard_map/pallas_call | solution.py:195
  149.6 11.2 %all-to-all-start.1 = ((bf16[32,24,2048]{2,1,0:T(8,128)(2,1)}), bf16[32,24,2048]{2,1,0:T(8,128)(2,1)S(1)}, u32[]{:S(2)}, u32[]{:S(2)}) async-start(bf16[32,24,2048]{2,1,0:T(8,128)(2,1)} %bitcast.77), calls=%async_computation.1 | async-start | bytes 6291456 | tf_op jit(solution)/shard_map/all_to_all | solution.py:343
  160.8 2.6 %collective-permute-start.11 = (bf16[384,2048]{1,0:T(8,128)(2,1)}, bf16[384,2048]{1,0:T(8,128)(2,1)S(1)}, u32[]{:S(2)}, u32[]{:S(2)}) collective-permute-start(bf16[384,2048]{1,0:T(8,128)(2,1)} %get-tuple-element.31), channel_id=1, source_target_pairs={{0,1},{1,0},{2,3},{3,2},{4,5},{5,4},{6,7},{7,6},{8,9},{9,8},{10,11... | collective-permute-start | bytes 4718600 | tf_op jit(solution)/shard_map/ppermute | solution.py:24
  164.0 2.6 %collective-permute-done.11.core_ref = bf16[384,2048]{1,0:T(8,128)(2,1)S(1)} collective-permute-done((bf16[384,2048]{1,0:T(8,128)(2,1)}, bf16[384,2048]{1,0:T(8,128)(2,1)S(1)}, u32[]{:S(2)}, u32[]{:S(2)}) %collective-permute-start.11) | collective-permute-done | bytes 1572896 | tf_op jit(solution)/shard_map/ppermute | solution.py:24
  166.6 1.1 copy-done.7
  167.8 4.8 %shard_map.141 = (bf16[192,2048]{1,0:T(8,128)(2,1)}, bf16[192,2048]{1,0:T(8,128)(2,1)}) custom-call(s32[1]{0:T(128)} %bitcast.35.flag_ref, bf16[2,384,2048]{2,1,0:T(8,128)(2,1)} %get-tuple-element.24.rows_ref, bf16[3,384,384]{2,1,0:T(8,128)(2,1)} %get-tuple-element.25.act_ref, bf16[384,2048]{1,0:T(8,128)(2,1)} %copy-done.7, ...), custom_call_target="tpu_custom_call" | custom-call | flops 603979776 | bytes 4718592 | tf_op jit(solution)/shard_map/pallas_call | solution.py:195
  172.9 1.1 copy-done.6
  174.1 4.6 %shard_map.144 = (bf16[192,2048]{1,0:T(8,128)(2,1)}, bf16[192,2048]{1,0:T(8,128)(2,1)}) custom-call(s32[1]{0:T(128)} %bitcast.35.flag_ref, bf16[2,384,2048]{2,1,0:T(8,128)(2,1)} %get-tuple-element.24.rows_ref, bf16[3,384,384]{2,1,0:T(8,128)(2,1)} %get-tuple-element.25.act_ref, bf16[384,2048]{1,0:T(8,128)(2,1)} %copy-done.6, ...), custom_call_target="tpu_custom_call" | custom-call | flops 603979776 | bytes 4718592 | tf_op jit(solution)/shard_map/pallas_call | solution.py:195
  178.7 4.1 %collective-permute-done.9.recv_ref = bf16[192,2048]{1,0:T(8,128)(2,1)S(1)} collective-permute-done((bf16[192,2048]{1,0:T(8,128)(2,1)}, bf16[192,2048]{1,0:T(8,128)(2,1)S(1)}, u32[]{:S(2)}, u32[]{:S(2)}) %collective-permute-start.9) | collective-permute-done | bytes 786464 | tf_op jit(solution)/shard_map/ppermute | solution.py:24
  182.9 0.9 copy-done.10
  183.7 5.1 %shard_map.140.refs_0_ = bf16[192,2048]{1,0:T(8,128)(2,1)} custom-call(s32[1]{0:T(128)} %bitcast.35.flag_ref, bf16[192,2048]{1,0:T(8,128)(2,1)} %get-tuple-element.28.keep_ref.refs_0_, bf16[192,2048]{1,0:T(8,128)(2,1)} %copy-done.10, bf16[1,2,192,2048]{3,2,1,0:T(8,128)(2,1)} %refs_0_.4, bf16[1,2,192,2048]{3,2,1,0:T(8,128)(2,1)} %refs_1_.4, ...), custom_call_target="tpu_custom_call" | custom-call | flops 7864320 | bytes 7077888 | tf_op jit(solution)/shard_map/pallas_call | solution.py:235
  189.3 0.9 bitcast_select_fusion.2
  190.2 1.0 collective-permute-start.10
  191.2 8.6 %collective-permute-done.12.recv_ref = bf16[192,2048]{1,0:T(8,128)(2,1)S(1)} collective-permute-done((bf16[192,2048]{1,0:T(8,128)(2,1)}, bf16[192,2048]{1,0:T(8,128)(2,1)S(1)}, u32[]{:S(2)}, u32[]{:S(2)}) %collective-permute-start.12) | collective-permute-done | bytes 786464 | tf_op jit(solution)/shard_map/ppermute | solution.py:24
  199.8 0.9 copy-done.8
  200.7 5.1 %shard_map.142.refs_2_ = bf16[192,2048]{1,0:T(8,128)(2,1)} custom-call(s32[1]{0:T(128)} %bitcast.35.flag_ref, bf16[192,2048]{1,0:T(8,128)(2,1)} %get-tuple-element.32.keep_ref.refs_0_, bf16[192,2048]{1,0:T(8,128)(2,1)} %copy-done.8, bf16[1,2,192,2048]{3,2,1,0:T(8,128)(2,1)} %refs_0_.4, bf16[1,2,192,2048]{3,2,1,0:T(8,128)(2,1)} %refs_1_.4, ...), custom_call_target="tpu_custom_call" | custom-call | flops 7864320 | bytes 7077888 | tf_op jit(solution)/shard_map/pallas_call | solution.py:235
  205.8 1.3 collective-permute-start.13
  207.1 9.6 %collective-permute-done.15.recv_ref = bf16[192,2048]{1,0:T(8,128)(2,1)S(1)} collective-permute-done((bf16[192,2048]{1,0:T(8,128)(2,1)S(1)}, bf16[192,2048]{1,0:T(8,128)(2,1)S(1)}, u32[]{:S(2)}, u32[]{:S(2)}) %collective-permute-start.15) | collective-permute-done | bytes 786464 | tf_op jit(solution)/shard_map/ppermute | solution.py:24
  216.7 0.9 copy-done.9
  217.6 4.6 %shard_map.145.refs_0_ = bf16[192,2048]{1,0:T(8,128)(2,1)} custom-call(s32[1]{0:T(128)} %bitcast.35.flag_ref, bf16[192,2048]{1,0:T(8,128)(2,1)} %get-tuple-element.35.keep_ref, bf16[192,2048]{1,0:T(8,128)(2,1)} %copy-done.9, bf16[1,192,2048]{2,1,0:T(8,128)(2,1)} %refs_0_.5, bf16[1,192,2048]{2,1,0:T(8,128)(2,1)} %refs_1_.5, bf16[1,192,2048]{2,1,0:T(8,128)(2,1)} %refs_2_.5), custom_call_target="tpu_custom_call" | custom-call | flops 7864320 | bytes 4718592 | tf_op jit(solution)/shard_map/pallas_call | solution.py:235
  222.1 1.0 collective-permute-start.16
  223.1 8.0 %all-to-all-done.1 = bf16[32,24,2048]{2,1,0:T(8,128)(2,1)S(1)} async-done(((bf16[32,24,2048]{2,1,0:T(8,128)(2,1)}), bf16[32,24,2048]{2,1,0:T(8,128)(2,1)S(1)}, u32[]{:S(2)}, u32[]{:S(2)}) %all-to-all-start.1) | async-done | bytes 3145760 | tf_op jit(solution)/shard_map/all_to_all | solution.py:343
  231.2 2.3 fusion.2
  233.8 1.1 collective-permute-start.8
  234.8 14.6 %collective-permute-done.13.refs_3_ = bf16[192,2048]{1,0:T(8,128)(2,1)} collective-permute-done((bf16[192,2048]{1,0:T(8,128)(2,1)}, bf16[192,2048]{1,0:T(8,128)(2,1)}, u32[]{:S(2)}, u32[]{:S(2)}) %collective-permute-start.13) | collective-permute-done | bytes 786464 | tf_op jit(solution)/shard_map/ppermute | solution.py:354
  249.4 2.8 %shard_map.143 = bf16[2,192,2048]{2,1,0:T(8,128)(2,1)} custom-call(s32[1]{0:T(128)} %bitcast.35.flag_ref, bf16[192,2048]{1,0:T(8,128)(2,1)} %shard_map.140.refs_0_, bf16[192,2048]{1,0:T(8,128)(2,1)} %collective-permute-done.10.refs_1_, bf16[192,2048]{1,0:T(8,128)(2,1)} %shard_map.142.refs_2_, bf16[192,2048]{1,0:T(8,128)(2,1)} %collective-permute-done.13.refs_3_, ...), custom_call_target="tpu_custom_call" | custom-call | flops 786432 | bytes 4718592 | tf_op jit(solution)/shard_map/pallas_call | solution.py:261
  252.3 0.8 fusion.16
  253.1 2.1 shard_map.146
  (77 shorter events, 4.8 us)
Async XLA Ops:
  2.0 10.9 %collective-permute-start = (f32[32,16]{0,1:T(8,128)S(1)}, f32[32,16]{0,1:T(8,128)S(1)}, u32[]{:S(2)}, u32[]{:S(2)}) collective-permute-start(f32[32,16]{0,1:T(8,128)S(1)} %get-tuple-element.73), channel_id=1, source_target_pairs={{0,128},{128,0},{1,129},{129,1},{2,130},{130,2},{3,131},{131,3},{4... | collective-permute-start | bytes 6152 | tf_op jit(solution)/shard_map/ppermute | solution.py:24
  5.6 7.7 %collective-permute-start.1 = (bf16[32,2048]{1,0:T(8,128)(2,1)}, bf16[32,2048]{1,0:T(8,128)(2,1)S(1)}, u32[]{:S(2)}, u32[]{:S(2)}) collective-permute-start(bf16[32,2048]{1,0:T(8,128)(2,1)} %param.11), channel_id=1, source_target_pairs={{0,128},{128,0},{1,129},{129,1},{2,130},{130,2},{3,131},{131,3},{4... | collective-permute-start | bytes 393224 | tf_op jit(solution)/shard_map/ppermute | solution.py:24
  5.6 8.5 %collective-permute-start.2 = (bf16[32,2048]{1,0:T(8,128)(2,1)}, bf16[32,2048]{1,0:T(8,128)(2,1)S(1)}, u32[]{:S(2)}, u32[]{:S(2)}) collective-permute-start(bf16[32,2048]{1,0:T(8,128)(2,1)} %param.12), channel_id=1, source_target_pairs={{0,128},{128,0},{1,129},{129,1},{2,130},{130,2},{3,131},{131,3},{4... | collective-permute-start | bytes 393224 | tf_op jit(solution)/shard_map/ppermute | solution.py:24
  8.7 6.9 %copy-start.13 = (pred[24,128]{1,0:T(8,128)(4,1)}, pred[24,128]{1,0:T(8,128)(4,1)S(1)}, u32[]{:S(2)}) copy-start(pred[24,128]{1,0:T(8,128)(4,1)S(1)} %broadcast_compare_fusion) | copy-start | bytes 9220
  8.7 7.1 %copy-start.11 = (bf16[32,2048]{1,0:T(8,128)(2,1)S(1)}, bf16[32,2048]{1,0:T(8,128)(2,1)}, u32[]{:S(2)}) copy-start(bf16[32,2048]{1,0:T(8,128)(2,1)} %param.12) | copy-start | bytes 393220
  8.7 7.1 %copy-start.12 = (bf16[32,2048]{1,0:T(8,128)(2,1)S(1)}, bf16[32,2048]{1,0:T(8,128)(2,1)}, u32[]{:S(2)}) copy-start(bf16[32,2048]{1,0:T(8,128)(2,1)} %param.11) | copy-start | bytes 393220
  12.9 5.5 %copy-start.15 = (s32[768]{0:T(1024)}, s32[768]{0:T(1024)S(1)}, u32[]{:S(2)}) copy-start(s32[768]{0:T(1024)S(1)} %eq.199) | copy-start | bytes 9220
  14.2 51.2 %collective-permute-start.3 = (bf16[3,192,2048]{2,1,0:T(8,128)(2,1)}, bf16[3,192,2048]{2,1,0:T(8,128)(2,1)S(1)}, u32[]{:S(2)}, u32[]{:S(2)}) collective-permute-start(bf16[3,192,2048]{2,1,0:T(8,128)(2,1)} %get-tuple-element.21.w_own), channel_id=1, source_target_pairs={{0,2},{2,0},{1,3},{3,1},{4,6},{6,4},{5,7},{7,5},{8,10},{10,8},{9,1... | collective-permute-start | bytes 7077896 | tf_op jit(solution)/shard_map/ppermute | solution.py:24
  18.4 91.0 %all-to-all-start = ((bf16[32,24,2048]{2,1,0:T(8,128)(2,1)}), bf16[32,24,2048]{2,1,0:T(8,128)(2,1)}, u32[]{:S(2)}, u32[]{:S(2)}) async-start(bf16[32,24,2048]{2,1,0:T(8,128)(2,1)} %bitcast.75), calls=%async_computation | async-start | bytes 6291456 | tf_op jit(solution)/shard_map/all_to_all | solution.py:336
  65.4 5.2 %copy-start = (bf16[3,192,2048]{2,1,0:T(8,128)(2,1)}, bf16[3,192,2048]{2,1,0:T(8,128)(2,1)S(1)}, u32[]{:S(2)}) copy-start(bf16[3,192,2048]{2,1,0:T(8,128)(2,1)S(1)} %collective-permute-done.3.w_xl.refs_3_) | copy-start | bytes 7077892
  65.4 7.9 %copy-start.4 = (bf16[1,2,192,2048]{3,2,1,0:T(8,128)(2,1)S(1)}, bf16[1,2,192,2048]{3,2,1,0:T(8,128)(2,1)}, u32[]{:S(2)}) copy-start(bf16[1,2,192,2048]{3,2,1,0:T(8,128)(2,1)} %refs_1_.4) | copy-start | bytes 4718596
  70.5 2.8 %copy-start.3 = (bf16[1,2,192,2048]{3,2,1,0:T(8,128)(2,1)S(1)}, bf16[1,2,192,2048]{3,2,1,0:T(8,128)(2,1)}, u32[]{:S(2)}) copy-start(bf16[1,2,192,2048]{3,2,1,0:T(8,128)(2,1)} %refs_2_.4) | copy-start | bytes 4718596
  70.5 38.9 %collective-permute-start.4 = (bf16[2,3,192,2048]{3,2,1,0:T(8,128)(2,1)}, bf16[2,3,192,2048]{3,2,1,0:T(8,128)(2,1)}, u32[]{:S(2)}, u32[]{:S(2)}) collective-permute-start(bf16[2,3,192,2048]{3,2,1,0:T(8,128)(2,1)} %pad_maximum_fusion), channel_id=1, source_target_pairs={{0,1},{1,0},{2,3},{3,2},{4,5},{5,4},{6,7},{7,6},{8,9},{9,8},{10,11... | collective-permute-start | bytes 14155784 | tf_op jit(solution)/shard_map/ppermute | solution.py:24
  74.9 34.6 %collective-permute-start.5 = (bf16[2,192,2048]{2,1,0:T(8,128)(2,1)S(1)}, bf16[2,192,2048]{2,1,0:T(8,128)(2,1)S(1)}, u32[]{:S(2)}, u32[]{:S(2)}) collective-permute-start(bf16[2,192,2048]{2,1,0:T(8,128)(2,1)S(1)} %get-tuple-element.22), channel_id=1, source_target_pairs={{0,2},{2,0},{1,3},{3,1},{4,6},{6,4},{5,7},{7,5},{8,10},{10,8},{9,1... | collective-permute-start | bytes 4718600 | tf_op jit(solution)/shard_map/ppermute | solution.py:24
  75.2 68.0 %collective-permute-start.7 = (bf16[2,192,2048]{2,1,0:T(8,128)(2,1)}, bf16[2,192,2048]{2,1,0:T(8,128)(2,1)S(1)}, u32[]{:S(2)}, u32[]{:S(2)}) collective-permute-start(bf16[2,192,2048]{2,1,0:T(8,128)(2,1)} %get-tuple-element.27), channel_id=1, source_target_pairs={{0,2},{2,0},{1,3},{3,1},{4,6},{6,4},{5,7},{7,5},{8,10},{10,8},{9,1... | collective-permute-start | bytes 4718600 | tf_op jit(solution)/shard_map/ppermute | solution.py:24
  109.5 1.2 copy-start.1
  110.7 23.4 %copy-start.19 = (s32[64]{0:T(128)S(1)}, s32[64]{0:T(128)}, u32[]{:S(2)}) copy-start(s32[64]{0:T(128)} %param.15) | copy-start | bytes 772
  129.9 13.3 %collective-permute-start.6 = (bf16[384,2048]{1,0:T(8,128)(2,1)}, bf16[384,2048]{1,0:T(8,128)(2,1)S(1)}, u32[]{:S(2)}, u32[]{:S(2)}) collective-permute-start(bf16[384,2048]{1,0:T(8,128)(2,1)} %get-tuple-element.26), channel_id=1, source_target_pairs={{0,1},{1,0},{2,3},{3,2},{4,5},{5,4},{6,7},{7,6},{8,9},{9,8},{10,11... | collective-permute-start | bytes 4718600 | tf_op jit(solution)/shard_map/ppermute | solution.py:24
  143.2 1.1 copy-start.2
  143.2 1.7 copy-start.5
  149.6 81.6 %all-to-all-start.1 = ((bf16[32,24,2048]{2,1,0:T(8,128)(2,1)}), bf16[32,24,2048]{2,1,0:T(8,128)(2,1)S(1)}, u32[]{:S(2)}, u32[]{:S(2)}) async-start(bf16[32,24,2048]{2,1,0:T(8,128)(2,1)} %bitcast.77), calls=%async_computation.1 | async-start | bytes 6291456 | tf_op jit(solution)/shard_map/all_to_all | solution.py:343
  160.8 5.8 %collective-permute-start.11 = (bf16[384,2048]{1,0:T(8,128)(2,1)}, bf16[384,2048]{1,0:T(8,128)(2,1)S(1)}, u32[]{:S(2)}, u32[]{:S(2)}) collective-permute-start(bf16[384,2048]{1,0:T(8,128)(2,1)} %get-tuple-element.31), channel_id=1, source_target_pairs={{0,1},{1,0},{2,3},{3,2},{4,5},{5,4},{6,7},{7,6},{8,9},{9,8},{10,11... | collective-permute-start | bytes 4718600 | tf_op jit(solution)/shard_map/ppermute | solution.py:24
  163.4 9.5 %collective-permute-start.14 = (bf16[384,2048]{1,0:T(8,128)(2,1)}, bf16[384,2048]{1,0:T(8,128)(2,1)S(1)}, u32[]{:S(2)}, u32[]{:S(2)}) collective-permute-start(bf16[384,2048]{1,0:T(8,128)(2,1)} %get-tuple-element.34), channel_id=1, source_target_pairs={{0,1},{1,0},{2,3},{3,2},{4,5},{5,4},{6,7},{7,6},{8,9},{9,8},{10,11... | collective-permute-start | bytes 4718600 | tf_op jit(solution)/shard_map/ppermute | solution.py:24
  163.7 19.2 %collective-permute-start.9 = (bf16[192,2048]{1,0:T(8,128)(2,1)}, bf16[192,2048]{1,0:T(8,128)(2,1)S(1)}, u32[]{:S(2)}, u32[]{:S(2)}) collective-permute-start(bf16[192,2048]{1,0:T(8,128)(2,1)} %get-tuple-element.30), channel_id=1, source_target_pairs={{0,2},{2,0},{1,3},{3,1},{4,6},{6,4},{5,7},{7,5},{8,10},{10,8},{9,1... | collective-permute-start | bytes 2359304 | tf_op jit(solution)/shard_map/ppermute | solution.py:24
  166.6 1.1 copy-start.7
  172.6 27.2 %collective-permute-start.12 = (bf16[192,2048]{1,0:T(8,128)(2,1)}, bf16[192,2048]{1,0:T(8,128)(2,1)S(1)}, u32[]{:S(2)}, u32[]{:S(2)}) collective-permute-start(bf16[192,2048]{1,0:T(8,128)(2,1)} %get-tuple-element.33), channel_id=1, source_target_pairs={{0,2},{2,0},{1,3},{3,1},{4,6},{6,4},{5,7},{7,5},{8,10},{10,8},{9,1... | collective-permute-start | bytes 2359304 | tf_op jit(solution)/shard_map/ppermute | solution.py:24
  172.9 1.1 copy-start.6
  178.7 10.2 %copy-start.18 = (bf16[192,2048]{1,0:T(8,128)(2,1)S(1)}, bf16[192,2048]{1,0:T(8,128)(2,1)}, u32[]{:S(2)}) copy-start(bf16[192,2048]{1,0:T(8,128)(2,1)} %get-tuple-element.37) | copy-start | bytes 2359300
  178.7 10.6 %copy-start.14 = (pred[24,128]{1,0:T(8,128)(4,1)S(1)}, pred[24,128]{1,0:T(8,128)(4,1)}, u32[]{:S(2)}) copy-start(pred[24,128]{1,0:T(8,128)(4,1)} %copy-done.13) | copy-start | bytes 9220
  178.7 10.6 %copy-start.16 = (s32[768]{0:T(1024)S(1)}, s32[768]{0:T(1024)}, u32[]{:S(2)}) copy-start(s32[768]{0:T(1024)} %copy-done.15) | copy-start | bytes 9220
  178.7 10.6 %copy-start.17 = (bf16[32,128]{1,0:T(8,128)(2,1)S(1)}, bf16[32,128]{1,0:T(8,128)(2,1)}, u32[]{:S(2)}) copy-start(bf16[32,128]{1,0:T(8,128)(2,1)} %get-tuple-element.38) | copy-start | bytes 24580
  182.9 0.9 copy-start.10
  188.9 27.8 %collective-permute-start.15 = (bf16[192,2048]{1,0:T(8,128)(2,1)S(1)}, bf16[192,2048]{1,0:T(8,128)(2,1)S(1)}, u32[]{:S(2)}, u32[]{:S(2)}) collective-permute-start(bf16[192,2048]{1,0:T(8,128)(2,1)S(1)} %copy-done.18), channel_id=1, source_target_pairs={{0,2},{2,0},{1,3},{3,1},{4,6},{6,4},{5,7},{7,5},{8,10},{10,8},{9,1... | collective-permute-start | bytes 2359304 | tf_op jit(solution)/shard_map/ppermute | solution.py:24
  190.2 44.7 %collective-permute-start.10 = (bf16[192,2048]{1,0:T(8,128)(2,1)}, bf16[192,2048]{1,0:T(8,128)(2,1)}, u32[]{:S(2)}, u32[]{:S(2)}) collective-permute-start(bf16[192,2048]{1,0:T(8,128)(2,1)} %shard_map.140.refs_0_), channel_id=1, source_target_pairs={{0,130},{130,0},{2,128},{128,2},{1,131},{131,1},{3,129},{129,3},{4... | collective-permute-start | bytes 2359304 | tf_op jit(solution)/shard_map/ppermute | solution.py:351
  199.8 0.9 copy-start.8
  205.8 43.6 %collective-permute-start.13 = (bf16[192,2048]{1,0:T(8,128)(2,1)}, bf16[192,2048]{1,0:T(8,128)(2,1)}, u32[]{:S(2)}, u32[]{:S(2)}) collective-permute-start(bf16[192,2048]{1,0:T(8,128)(2,1)} %shard_map.142.refs_2_), channel_id=1, source_target_pairs={{0,130},{130,0},{2,128},{128,2},{1,131},{131,1},{3,129},{129,3},{4... | collective-permute-start | bytes 2359304 | tf_op jit(solution)/shard_map/ppermute | solution.py:354
  216.7 0.9 copy-start.9
  222.1 30.9 %collective-permute-start.16 = (bf16[192,2048]{1,0:T(8,128)(2,1)}, bf16[192,2048]{1,0:T(8,128)(2,1)}, u32[]{:S(2)}, u32[]{:S(2)}) collective-permute-start(bf16[192,2048]{1,0:T(8,128)(2,1)} %shard_map.145.refs_0_), channel_id=1, source_target_pairs={{0,128},{128,0},{1,129},{129,1},{2,130},{130,2},{3,131},{131,3},{4... | collective-permute-start | bytes 2359304 | tf_op jit(solution)/shard_map/ppermute | solution.py:24
  233.8 18.5 %collective-permute-start.8 = (bf16[64,2048]{1,0:T(8,128)(2,1)S(1)}, bf16[64,2048]{1,0:T(8,128)(2,1)S(1)}, u32[]{:S(2)}, u32[]{:S(2)}) collective-permute-start(bf16[64,2048]{1,0:T(8,128)(2,1)S(1)} %slice.261), channel_id=1, source_target_pairs={{0,128},{128,0},{1,129},{129,1},{2,130},{130,2},{3,131},{131,3},{4... | collective-permute-start | bytes 786440 | tf_op jit(solution)/shard_map/ppermute | solution.py:24

commit v9 on v7

--- a/solution.py
+++ b/solution.py
@@ -47,7 +47,7 @@
 
 
 CHUNK = 256
-LANES = 512
+LANES = 1024
 GROUP = 16
 VMEM_LIMIT = 56 * 1024 * 1024
 

time: 247 us -> 246 us (level)
  Pallas kernels: 52.5 us -> 49.1 us
    pallas_call x3, Pallas kernels: 14.1 us -> 11 us  [grads_step(): pl.pallas_call(functools.partial(grads_kernel, exchange), grid=(feature /...]
  transfers between devices with their start and end apart: 19 -> 19, of which waited for: 9 -> 9; matrix products, arithmetic and copies ran while one was open for 8% -> 8% of each run, Pallas kernels for 11% -> 10%
where the time goes in v9:
time: 246 us; the launch traced here: 245 us
  waiting for transfers between devices  126 us (51%)
  Pallas kernels  49.1 us (20%)
  starting transfers between devices  40.3 us (16%)
  other arithmetic  14.9 us (6%)
  local copies, waits for them, and re-layouts  8.46 us (3%)
  matrix products  5.18 us (2%)
    ppermute x16, waiting for transfers between devices, swap(): return lax.ppermute(block, axis, [(0, 1), (1, 0)])  114 us
    pallas_call x1, Pallas kernels, rows_step(): pl.pallas_call(rows_kernel, out_shape=(jax.ShapeDtypeStruct(rows.shape, B...  18.9 us
    ppermute x16, starting transfers between devices, swap(): return lax.ppermute(block, axis, [(0, 1), (1, 0)])  16.9 us
    pallas_call x3, Pallas kernels, adam_step(): pl.pallas_call(adam_kernel, grid=(steps,), out_shape=jax.ShapeDtypeStruct...  14.3 us
    all_to_all x1, waiting for transfers between devices, body(): lax.all_to_all(after(back_send, gate[0]).reshape(recv.shape), RINGS, spli...  11.5 us
    all_to_all x1, starting transfers between devices, body(): recv = lax.all_to_all(send, RINGS, split_axis=0, concat_axis=0, tiled=True)  11.3 us
    all_to_all x1, starting transfers between devices, body(): lax.all_to_all(after(back_send, gate[0]).reshape(recv.shape), RINGS, spli...  11.2 us
    pallas_call x3, Pallas kernels, grads_step(): pl.pallas_call(functools.partial(grads_kernel, exchange), grid=(feature /...  11 us
  transfers between devices with their start and end apart: 19, of which 9 were waited for; matrix products, arithmetic and copies ran while one was open for 8% of the time, Pallas kernels for 10%

profile of v9, /device:TPU:1, one launch (start us, length us, event | category | flops | bytes accessed | tf_op | source)
XLA Modules:
  0.0 245.4 jit_solution(4583741500212101688)
XLA Ops:
  0.6 0.7 convert_element_type.115
  1.3 0.7 pad_maximum_fusion.3
  2.0 3.6 %collective-permute-start = (f32[32,16]{0,1:T(8,128)S(1)}, f32[32,16]{0,1:T(8,128)S(1)}, u32[]{:S(2)}, u32[]{:S(2)}) collective-permute-start(f32[32,16]{0,1:T(8,128)S(1)} %get-tuple-element.69), channel_id=1, source_target_pairs={{0,128},{128,0},{1,129},{129,1},{2,130},{130,2},{3,131},{131,3},{4... | collective-permute-start | bytes 6152 | tf_op jit(solution)/shard_map/ppermute | solution.py:24
  5.6 2.9 %collective-permute-start.2 = (bf16[32,2048]{1,0:T(8,128)(2,1)}, bf16[32,2048]{1,0:T(8,128)(2,1)S(1)}, u32[]{:S(2)}, u32[]{:S(2)}) collective-permute-start(bf16[32,2048]{1,0:T(8,128)(2,1)} %param.12), channel_id=1, source_target_pairs={{0,128},{128,0},{1,129},{129,1},{2,130},{130,2},{3,131},{131,3},{4... | collective-permute-start | bytes 393224 | tf_op jit(solution)/shard_map/ppermute | solution.py:24
  8.6 4.1 %fusion.60 = (bf16[1,3,192,2048]{3,2,1,0:T(8,128)(2,1)}, bf16[3,192,2048]{2,1,0:T(8,128)(2,1)}) fusion(bf16[1,192,2048]{2,1,0:T(8,128)(2,1)} %refs_0_.5, bf16[2,192,2048]{2,1,0:T(8,128)(2,1)} %bitcast.71), kind=kLoop, calls=%fused_computation.140 | loop fusion | flops 1179648 | bytes 7077888 | tf_op jit(solution)/shard_map/stack | solution.py:334
  13.8 0.7 select_convert_fusion
  15.0 2.6 %multiply_convert_fusion = bf16[768,2048]{1,0:T(8,128)(2,1)} fusion(pred[768,128]{1,0:T(32,128)(4,1)S(1)} %fusion.15, f32[768]{0:T(1024)S(1)} %select_n.183, bf16[32,2048]{1,0:T(8,128)(2,1)S(1)} %collective-permute-done.2, bf16[32,2048]{1,0:T(8,128)(2,1)S(1)} %collective-permute-done.1, bf16[32,2048]{1,0:T(8,128)(2,1)S(1)} %copy-done.10, ...), kind=kOutput, calls=%fused_computation | convolution fusion | flops 407896064 | bytes 3771392 | tf_op jit(solution)/shard_map/dot_general | solution.py:42
  17.6 11.3 %all-to-all-start = ((bf16[32,24,2048]{2,1,0:T(8,128)(2,1)}), bf16[32,24,2048]{2,1,0:T(8,128)(2,1)}, u32[]{:S(2)}, u32[]{:S(2)}) async-start(bf16[32,24,2048]{2,1,0:T(8,128)(2,1)} %bitcast.28), calls=%async_computation | async-start | bytes 6291456 | tf_op jit(solution)/shard_map/all_to_all | solution.py:336
  29.0 1.2 slice_bitcast_fusion.1
  30.2 1.2 collective-permute-start.4
  31.4 49.7 %collective-permute-done.4._m.refs_4_ = bf16[1,192,2048]{2,1,0:T(8,128)(2,1)S(1)} collective-permute-done((bf16[1,192,2048]{2,1,0:T(8,128)(2,1)S(1)}, bf16[1,192,2048]{2,1,0:T(8,128)(2,1)S(1)}, u32[]{:S(2)}, u32[]{:S(2)}) %collective-permute-start.4) | collective-permute-done | bytes 786464 | tf_op jit(solution)/shard_map/ppermute | solution.py:24
  81.1 5.4 %pad_maximum_fusion = bf16[2,3,192,2048]{3,2,1,0:T(8,128)(2,1)} fusion(bf16[1,3,192,2048]{3,2,1,0:T(8,128)(2,1)S(1)} %bitcast.70, bf16[1,3,192,2048]{3,2,1,0:T(8,128)(2,1)} %get-tuple-element.40), kind=kLoop, calls=%fused_computation.1 | loop fusion | flops 2359296 | bytes 9437184 | tf_op jit(solution)/shard_map/stack | solution.py:334
  86.5 2.3 collective-permute-start.5
  89.5 18.8 %collective-permute-done.6._v.refs_5_ = bf16[1,192,2048]{2,1,0:T(8,128)(2,1)S(1)} collective-permute-done((bf16[1,192,2048]{2,1,0:T(8,128)(2,1)S(1)}, bf16[1,192,2048]{2,1,0:T(8,128)(2,1)S(1)}, u32[]{:S(2)}, u32[]{:S(2)}) %collective-permute-start.6) | collective-permute-done | bytes 786464 | tf_op jit(solution)/shard_map/ppermute | solution.py:24
  108.4 0.9 copy-done.3
  109.3 18.9 %shard_map.138 = (bf16[768,2048]{1,0:T(8,128)(2,1)}, bf16[2,384,2048]{2,1,0:T(8,128)(2,1)}, bf16[3,384,384]{2,1,0:T(8,128)(2,1)}, bf16[384,2048]{1,0:T(8,128)(2,...) custom-call(bf16[768,2048]{1,0:T(8,128)(2,1)} %bitcast.29.rows_ref, ...), custom_call_target="tpu_custom_call" | custom-call | flops 150994944 | bytes 786432 | tf_op jit(solution)/shard_map/pallas_call | solution.py:149
  128.1 0.9 collective-permute-start.7
  129.0 0.6 fusion.55
  130.3 2.0 collective-permute-done.7.core_ref
  132.3 1.1 copy-done.6
  133.4 4.0 %shard_map.139 = (bf16[192,2048]{1,0:T(8,128)(2,1)}, bf16[192,2048]{1,0:T(8,128)(2,1)}) custom-call(s32[1]{0:T(128)} %bitcast.35.flag_ref, bf16[2,384,2048]{2,1,0:T(8,128)(2,1)} %get-tuple-element.25.rows_ref, bf16[3,384,384]{2,1,0:T(8,128)(2,1)} %get-tuple-element.26.act_ref, bf16[384,2048]{1,0:T(8,128)(2,1)} %copy-done.6), custom_call_target="tpu_custom_call" | custom-call | flops 603979776 | bytes 4718592 | tf_op jit(solution)/shard_map/pallas_call | solution.py:195
  137.4 11.2 %all-to-all-start.1 = ((bf16[32,24,2048]{2,1,0:T(8,128)(2,1)}), bf16[32,24,2048]{2,1,0:T(8,128)(2,1)S(1)}, u32[]{:S(2)}, u32[]{:S(2)}) async-start(bf16[32,24,2048]{2,1,0:T(8,128)(2,1)} %bitcast.36), calls=%async_computation.1 | async-start | bytes 6291456 | tf_op jit(solution)/shard_map/all_to_all | solution.py:343
  148.6 0.7 collective-permute-start.11
  150.0 2.6 %collective-permute-done.11.core_ref = bf16[384,2048]{1,0:T(8,128)(2,1)S(1)} collective-permute-done((bf16[384,2048]{1,0:T(8,128)(2,1)}, bf16[384,2048]{1,0:T(8,128)(2,1)S(1)}, u32[]{:S(2)}, u32[]{:S(2)}) %collective-permute-start.11) | collective-permute-done | bytes 1572896 | tf_op jit(solution)/shard_map/ppermute | solution.py:24
  152.6 1.1 copy-done.5
  153.7 3.5 %shard_map.141 = (bf16[192,2048]{1,0:T(8,128)(2,1)}, bf16[192,2048]{1,0:T(8,128)(2,1)}) custom-call(s32[1]{0:T(128)} %bitcast.35.flag_ref, bf16[2,384,2048]{2,1,0:T(8,128)(2,1)} %get-tuple-element.25.rows_ref, bf16[3,384,384]{2,1,0:T(8,128)(2,1)} %get-tuple-element.26.act_ref, bf16[384,2048]{1,0:T(8,128)(2,1)} %copy-done.5, ...), custom_call_target="tpu_custom_call" | custom-call | flops 603979776 | bytes 4718592 | tf_op jit(solution)/shard_map/pallas_call | solution.py:195
  157.5 1.1 copy-done.4
  158.7 3.5 %shard_map.144 = (bf16[192,2048]{1,0:T(8,128)(2,1)}, bf16[192,2048]{1,0:T(8,128)(2,1)}) custom-call(s32[1]{0:T(128)} %bitcast.35.flag_ref, bf16[2,384,2048]{2,1,0:T(8,128)(2,1)} %get-tuple-element.25.rows_ref, bf16[3,384,384]{2,1,0:T(8,128)(2,1)} %get-tuple-element.26.act_ref, bf16[384,2048]{1,0:T(8,128)(2,1)} %copy-done.4, ...), custom_call_target="tpu_custom_call" | custom-call | flops 603979776 | bytes 4718592 | tf_op jit(solution)/shard_map/pallas_call | solution.py:195
  162.3 6.6 %collective-permute-done.9.recv_ref = bf16[192,2048]{1,0:T(8,128)(2,1)S(1)} collective-permute-done((bf16[192,2048]{1,0:T(8,128)(2,1)}, bf16[192,2048]{1,0:T(8,128)(2,1)S(1)}, u32[]{:S(2)}, u32[]{:S(2)}) %collective-permute-start.9) | collective-permute-done | bytes 786464 | tf_op jit(solution)/shard_map/ppermute | solution.py:24
  168.8 0.9 copy-done.9
  169.7 5.1 %shard_map.140.refs_0_ = bf16[192,2048]{1,0:T(8,128)(2,1)} custom-call(s32[1]{0:T(128)} %bitcast.35.flag_ref, bf16[192,2048]{1,0:T(8,128)(2,1)} %get-tuple-element.28.keep_ref.refs_0_, bf16[192,2048]{1,0:T(8,128)(2,1)} %copy-done.9, bf16[1,2,192,2048]{3,2,1,0:T(8,128)(2,1)} %refs_0_.4, bf16[1,2,192,2048]{3,2,1,0:T(8,128)(2,1)} %refs_1_.4, ...), custom_call_target="tpu_custom_call" | custom-call | flops 7864320 | bytes 7077888 | tf_op jit(solution)/shard_map/pallas_call | solution.py:235
  175.3 0.9 bitcast_select_fusion.2
  176.2 0.9 collective-permute-start.10
  177.1 8.7 %collective-permute-done.12.recv_ref = bf16[192,2048]{1,0:T(8,128)(2,1)S(1)} collective-permute-done((bf16[192,2048]{1,0:T(8,128)(2,1)}, bf16[192,2048]{1,0:T(8,128)(2,1)S(1)}, u32[]{:S(2)}, u32[]{:S(2)}) %collective-permute-start.12) | collective-permute-done | bytes 786464 | tf_op jit(solution)/shard_map/ppermute | solution.py:24
  185.8 0.9 copy-done.7
  186.7 4.6 %shard_map.142.refs_2_ = bf16[192,2048]{1,0:T(8,128)(2,1)} custom-call(s32[1]{0:T(128)} %bitcast.35.flag_ref, bf16[192,2048]{1,0:T(8,128)(2,1)} %get-tuple-element.32.keep_ref.refs_0_, bf16[192,2048]{1,0:T(8,128)(2,1)} %copy-done.7, bf16[1,2,192,2048]{3,2,1,0:T(8,128)(2,1)} %refs_0_.4, bf16[1,2,192,2048]{3,2,1,0:T(8,128)(2,1)} %refs_1_.4, ...), custom_call_target="tpu_custom_call" | custom-call | flops 7864320 | bytes 4718592 | tf_op jit(solution)/shard_map/pallas_call | solution.py:235
  191.3 0.9 collective-permute-start.13
  192.2 10.3 %collective-permute-done.15.recv_ref = bf16[192,2048]{1,0:T(8,128)(2,1)S(1)} collective-permute-done((bf16[192,2048]{1,0:T(8,128)(2,1)S(1)}, bf16[192,2048]{1,0:T(8,128)(2,1)S(1)}, u32[]{:S(2)}, u32[]{:S(2)}) %collective-permute-start.15) | collective-permute-done | bytes 786464 | tf_op jit(solution)/shard_map/ppermute | solution.py:24
  202.5 0.9 copy-done.8
  203.4 4.6 %shard_map.145.refs_0_ = bf16[192,2048]{1,0:T(8,128)(2,1)} custom-call(s32[1]{0:T(128)} %bitcast.35.flag_ref, bf16[192,2048]{1,0:T(8,128)(2,1)} %get-tuple-element.35.keep_ref, bf16[192,2048]{1,0:T(8,128)(2,1)} %copy-done.8, bf16[1,192,2048]{2,1,0:T(8,128)(2,1)} %refs_0_.5, bf16[1,192,2048]{2,1,0:T(8,128)(2,1)} %refs_1_.5, bf16[1,192,2048]{2,1,0:T(8,128)(2,1)} %refs_2_.5), custom_call_target="tpu_custom_call" | custom-call | flops 7864320 | bytes 4718592 | tf_op jit(solution)/shard_map/pallas_call | solution.py:235
  208.0 0.9 collective-permute-start.16
  208.9 11.5 %all-to-all-done.1 = bf16[32,24,2048]{2,1,0:T(8,128)(2,1)S(1)} async-done(((bf16[32,24,2048]{2,1,0:T(8,128)(2,1)}), bf16[32,24,2048]{2,1,0:T(8,128)(2,1)S(1)}, u32[]{:S(2)}, u32[]{:S(2)}) %all-to-all-start.1) | async-done | bytes 3145760 | tf_op jit(solution)/shard_map/all_to_all | solution.py:343
  220.5 2.3 fusion.2
  223.0 1.0 collective-permute-start.8
  224.1 2.8 %shard_map.143 = bf16[2,192,2048]{2,1,0:T(8,128)(2,1)} custom-call(s32[1]{0:T(128)} %bitcast.35.flag_ref, bf16[192,2048]{1,0:T(8,128)(2,1)} %shard_map.140.refs_0_, bf16[192,2048]{1,0:T(8,128)(2,1)} %collective-permute-done.10.refs_1_, bf16[192,2048]{1,0:T(8,128)(2,1)} %shard_map.142.refs_2_, bf16[192,2048]{1,0:T(8,128)(2,1)} %collective-permute-done.13.refs_3_, ...), custom_call_target="tpu_custom_call" | custom-call | flops 786432 | bytes 4718592 | tf_op jit(solution)/shard_map/pallas_call | solution.py:261
  226.9 15.6 %collective-permute-done.8 = bf16[64,2048]{1,0:T(8,128)(2,1)S(1)} collective-permute-done((bf16[64,2048]{1,0:T(8,128)(2,1)S(1)}, bf16[64,2048]{1,0:T(8,128)(2,1)S(1)}, u32[]{:S(2)}, u32[]{:S(2)}) %collective-permute-start.8) | collective-permute-done | bytes 262176 | tf_op jit(solution)/shard_map/ppermute | solution.py:24
  242.5 0.8 fusion.16
  243.3 2.1 shard_map.146
  (74 shorter events, 3.8 us)
Async XLA Ops:
  2.0 11.2 %collective-permute-start = (f32[32,16]{0,1:T(8,128)S(1)}, f32[32,16]{0,1:T(8,128)S(1)}, u32[]{:S(2)}, u32[]{:S(2)}) collective-permute-start(f32[32,16]{0,1:T(8,128)S(1)} %get-tuple-element.69), channel_id=1, source_target_pairs={{0,128},{128,0},{1,129},{129,1},{2,130},{130,2},{3,131},{131,3},{4... | collective-permute-start | bytes 6152 | tf_op jit(solution)/shard_map/ppermute | solution.py:24
  5.6 9.4 %collective-permute-start.1 = (bf16[32,2048]{1,0:T(8,128)(2,1)}, bf16[32,2048]{1,0:T(8,128)(2,1)S(1)}, u32[]{:S(2)}, u32[]{:S(2)}) collective-permute-start(bf16[32,2048]{1,0:T(8,128)(2,1)} %param.11), channel_id=1, source_target_pairs={{0,128},{128,0},{1,129},{129,1},{2,130},{130,2},{3,131},{131,3},{4... | collective-permute-start | bytes 393224 | tf_op jit(solution)/shard_map/ppermute | solution.py:24
  5.6 9.4 %collective-permute-start.2 = (bf16[32,2048]{1,0:T(8,128)(2,1)}, bf16[32,2048]{1,0:T(8,128)(2,1)S(1)}, u32[]{:S(2)}, u32[]{:S(2)}) collective-permute-start(bf16[32,2048]{1,0:T(8,128)(2,1)} %param.12), channel_id=1, source_target_pairs={{0,128},{128,0},{1,129},{129,1},{2,130},{130,2},{3,131},{131,3},{4... | collective-permute-start | bytes 393224 | tf_op jit(solution)/shard_map/ppermute | solution.py:24
  8.6 6.4 %copy-start.10 = (bf16[32,2048]{1,0:T(8,128)(2,1)S(1)}, bf16[32,2048]{1,0:T(8,128)(2,1)}, u32[]{:S(2)}) copy-start(bf16[32,2048]{1,0:T(8,128)(2,1)} %param.12) | copy-start | bytes 393220
  8.6 6.4 %copy-start.11 = (bf16[32,2048]{1,0:T(8,128)(2,1)S(1)}, bf16[32,2048]{1,0:T(8,128)(2,1)}, u32[]{:S(2)}) copy-start(bf16[32,2048]{1,0:T(8,128)(2,1)} %param.11) | copy-start | bytes 393220
  12.7 68.4 %collective-permute-start.3 = (bf16[3,192,2048]{2,1,0:T(8,128)(2,1)}, bf16[3,192,2048]{2,1,0:T(8,128)(2,1)S(1)}, u32[]{:S(2)}, u32[]{:S(2)}) collective-permute-start(bf16[3,192,2048]{2,1,0:T(8,128)(2,1)} %get-tuple-element.41.w_own), channel_id=1, source_target_pairs={{0,2},{2,0},{1,3},{3,1},{4,6},{6,4},{5,7},{7,5},{8,10},{10,8},{9,1... | collective-permute-start | bytes 7077896 | tf_op jit(solution)/shard_map/ppermute | solution.py:24
  13.1 4.5 %copy-start.12 = (pred[24,128]{1,0:T(8,128)(4,1)}, pred[24,128]{1,0:T(8,128)(4,1)S(1)}, u32[]{:S(2)}) copy-start(pred[24,128]{1,0:T(8,128)(4,1)S(1)} %broadcast_compare_fusion) | copy-start | bytes 9220
  13.2 4.4 %copy-start.14 = (s32[768]{0:T(1024)}, s32[768]{0:T(1024)S(1)}, u32[]{:S(2)}) copy-start(s32[768]{0:T(1024)S(1)} %eq.199) | copy-start | bytes 9220
  17.6 90.7 %all-to-all-start = ((bf16[32,24,2048]{2,1,0:T(8,128)(2,1)}), bf16[32,24,2048]{2,1,0:T(8,128)(2,1)}, u32[]{:S(2)}, u32[]{:S(2)}) async-start(bf16[32,24,2048]{2,1,0:T(8,128)(2,1)} %bitcast.28), calls=%async_computation | async-start | bytes 6291456 | tf_op jit(solution)/shard_map/all_to_all | solution.py:336
  30.2 50.9 %collective-permute-start.4 = (bf16[1,192,2048]{2,1,0:T(8,128)(2,1)S(1)}, bf16[1,192,2048]{2,1,0:T(8,128)(2,1)S(1)}, u32[]{:S(2)}, u32[]{:S(2)}) collective-permute-start(bf16[1,192,2048]{2,1,0:T(8,128)(2,1)S(1)} %slice_bitcast_fusion.1), channel_id=1, source_target_pairs={{0,2},{2,0},{1,3},{3,1},{4,6},{6,4},{5,7},{7,5},{8,10},{10,8},{9,1... | collective-permute-start | bytes 2359304 | tf_op jit(solution)/shard_map/ppermute | solution.py:24
  81.1 5.5 %copy-start.2 = (bf16[1,192,2048]{2,1,0:T(8,128)(2,1)}, bf16[1,192,2048]{2,1,0:T(8,128)(2,1)S(1)}, u32[]{:S(2)}) copy-start(bf16[1,192,2048]{2,1,0:T(8,128)(2,1)S(1)} %collective-permute-done.4._m.refs_4_) | copy-start | bytes 2359300
  81.1 5.5 %copy-start = (bf16[3,192,2048]{2,1,0:T(8,128)(2,1)}, bf16[3,192,2048]{2,1,0:T(8,128)(2,1)S(1)}, u32[]{:S(2)}) copy-start(bf16[3,192,2048]{2,1,0:T(8,128)(2,1)S(1)} %collective-permute-done.3.w_xl.refs_3_) | copy-start | bytes 7077892
  81.1 7.8 %copy-start.1 = (bf16[1,2,192,2048]{3,2,1,0:T(8,128)(2,1)S(1)}, bf16[1,2,192,2048]{3,2,1,0:T(8,128)(2,1)}, u32[]{:S(2)}) copy-start(bf16[1,2,192,2048]{3,2,1,0:T(8,128)(2,1)} %refs_2_.4) | copy-start | bytes 4718596
  86.5 21.9 %collective-permute-start.5 = (bf16[2,3,192,2048]{3,2,1,0:T(8,128)(2,1)}, bf16[2,3,192,2048]{3,2,1,0:T(8,128)(2,1)}, u32[]{:S(2)}, u32[]{:S(2)}) collective-permute-start(bf16[2,3,192,2048]{3,2,1,0:T(8,128)(2,1)} %pad_maximum_fusion), channel_id=1, source_target_pairs={{0,1},{1,0},{2,3},{3,2},{4,5},{5,4},{6,7},{7,6},{8,9},{9,8},{10,11... | collective-permute-start | bytes 14155784 | tf_op jit(solution)/shard_map/ppermute | solution.py:24
  89.0 19.4 %collective-permute-start.6 = (bf16[1,192,2048]{2,1,0:T(8,128)(2,1)S(1)}, bf16[1,192,2048]{2,1,0:T(8,128)(2,1)S(1)}, u32[]{:S(2)}, u32[]{:S(2)}) collective-permute-start(bf16[1,192,2048]{2,1,0:T(8,128)(2,1)S(1)} %slice_bitcast_fusion), channel_id=1, source_target_pairs={{0,2},{2,0},{1,3},{3,1},{4,6},{6,4},{5,7},{7,5},{8,10},{10,8},{9,1... | collective-permute-start | bytes 2359304 | tf_op jit(solution)/shard_map/ppermute | solution.py:24
  108.4 0.9 copy-start.3
  109.3 19.8 %copy-start.18 = (s32[64]{0:T(128)S(1)}, s32[64]{0:T(128)}, u32[]{:S(2)}) copy-start(s32[64]{0:T(128)} %param.15) | copy-start | bytes 772
  128.1 4.1 %collective-permute-start.7 = (bf16[384,2048]{1,0:T(8,128)(2,1)}, bf16[384,2048]{1,0:T(8,128)(2,1)S(1)}, u32[]{:S(2)}, u32[]{:S(2)}) collective-permute-start(bf16[384,2048]{1,0:T(8,128)(2,1)} %get-tuple-element.27), channel_id=1, source_target_pairs={{0,1},{1,0},{2,3},{3,2},{4,5},{5,4},{6,7},{7,6},{8,9},{9,8},{10,11... | collective-permute-start | bytes 4718600 | tf_op jit(solution)/shard_map/ppermute | solution.py:24
  132.3 1.1 copy-start.6
  137.4 83.1 %all-to-all-start.1 = ((bf16[32,24,2048]{2,1,0:T(8,128)(2,1)}), bf16[32,24,2048]{2,1,0:T(8,128)(2,1)S(1)}, u32[]{:S(2)}, u32[]{:S(2)}) async-start(bf16[32,24,2048]{2,1,0:T(8,128)(2,1)} %bitcast.36), calls=%async_computation.1 | async-start | bytes 6291456 | tf_op jit(solution)/shard_map/all_to_all | solution.py:343
  148.6 4.0 %collective-permute-start.11 = (bf16[384,2048]{1,0:T(8,128)(2,1)}, bf16[384,2048]{1,0:T(8,128)(2,1)S(1)}, u32[]{:S(2)}, u32[]{:S(2)}) collective-permute-start(bf16[384,2048]{1,0:T(8,128)(2,1)} %get-tuple-element.31), channel_id=1, source_target_pairs={{0,1},{1,0},{2,3},{3,2},{4,5},{5,4},{6,7},{7,6},{8,9},{9,8},{10,11... | collective-permute-start | bytes 4718600 | tf_op jit(solution)/shard_map/ppermute | solution.py:24
  149.3 8.2 %collective-permute-start.14 = (bf16[384,2048]{1,0:T(8,128)(2,1)}, bf16[384,2048]{1,0:T(8,128)(2,1)S(1)}, u32[]{:S(2)}, u32[]{:S(2)}) collective-permute-start(bf16[384,2048]{1,0:T(8,128)(2,1)} %get-tuple-element.34), channel_id=1, source_target_pairs={{0,1},{1,0},{2,3},{3,2},{4,5},{5,4},{6,7},{7,6},{8,9},{9,8},{10,11... | collective-permute-start | bytes 4718600 | tf_op jit(solution)/shard_map/ppermute | solution.py:24
  149.7 19.2 %collective-permute-start.9 = (bf16[192,2048]{1,0:T(8,128)(2,1)}, bf16[192,2048]{1,0:T(8,128)(2,1)S(1)}, u32[]{:S(2)}, u32[]{:S(2)}) collective-permute-start(bf16[192,2048]{1,0:T(8,128)(2,1)} %get-tuple-element.30), channel_id=1, source_target_pairs={{0,2},{2,0},{1,3},{3,1},{4,6},{6,4},{5,7},{7,5},{8,10},{10,8},{9,1... | collective-permute-start | bytes 2359304 | tf_op jit(solution)/shard_map/ppermute | solution.py:24
  152.6 1.1 copy-start.5
  157.2 28.6 %collective-permute-start.12 = (bf16[192,2048]{1,0:T(8,128)(2,1)}, bf16[192,2048]{1,0:T(8,128)(2,1)S(1)}, u32[]{:S(2)}, u32[]{:S(2)}) collective-permute-start(bf16[192,2048]{1,0:T(8,128)(2,1)} %get-tuple-element.33), channel_id=1, source_target_pairs={{0,2},{2,0},{1,3},{3,1},{4,6},{6,4},{5,7},{7,5},{8,10},{10,8},{9,1... | collective-permute-start | bytes 2359304 | tf_op jit(solution)/shard_map/ppermute | solution.py:24
  157.5 1.1 copy-start.4
  162.2 12.6 %copy-start.17 = (bf16[192,2048]{1,0:T(8,128)(2,1)S(1)}, bf16[192,2048]{1,0:T(8,128)(2,1)}, u32[]{:S(2)}) copy-start(bf16[192,2048]{1,0:T(8,128)(2,1)} %get-tuple-element.37) | copy-start | bytes 2359300
  162.2 13.0 %copy-start.13 = (pred[24,128]{1,0:T(8,128)(4,1)S(1)}, pred[24,128]{1,0:T(8,128)(4,1)}, u32[]{:S(2)}) copy-start(pred[24,128]{1,0:T(8,128)(4,1)} %copy-done.12) | copy-start | bytes 9220
  162.2 13.0 %copy-start.15 = (s32[768]{0:T(1024)S(1)}, s32[768]{0:T(1024)}, u32[]{:S(2)}) copy-start(s32[768]{0:T(1024)} %copy-done.14) | copy-start | bytes 9220
  162.2 13.0 %copy-start.16 = (bf16[32,128]{1,0:T(8,128)(2,1)S(1)}, bf16[32,128]{1,0:T(8,128)(2,1)}, u32[]{:S(2)}) copy-start(bf16[32,128]{1,0:T(8,128)(2,1)} %get-tuple-element.38) | copy-start | bytes 24580
  168.8 0.9 copy-start.9
  174.8 27.7 %collective-permute-start.15 = (bf16[192,2048]{1,0:T(8,128)(2,1)S(1)}, bf16[192,2048]{1,0:T(8,128)(2,1)S(1)}, u32[]{:S(2)}, u32[]{:S(2)}) collective-permute-start(bf16[192,2048]{1,0:T(8,128)(2,1)S(1)} %copy-done.17), channel_id=1, source_target_pairs={{0,2},{2,0},{1,3},{3,1},{4,6},{6,4},{5,7},{7,5},{8,10},{10,8},{9,1... | collective-permute-start | bytes 2359304 | tf_op jit(solution)/shard_map/ppermute | solution.py:24
  176.2 47.9 %collective-permute-start.10 = (bf16[192,2048]{1,0:T(8,128)(2,1)}, bf16[192,2048]{1,0:T(8,128)(2,1)}, u32[]{:S(2)}, u32[]{:S(2)}) collective-permute-start(bf16[192,2048]{1,0:T(8,128)(2,1)} %shard_map.140.refs_0_), channel_id=1, source_target_pairs={{0,130},{130,0},{2,128},{128,2},{1,131},{131,1},{3,129},{129,3},{4... | collective-permute-start | bytes 2359304 | tf_op jit(solution)/shard_map/ppermute | solution.py:351
  185.8 0.9 copy-start.7
  191.3 32.8 %collective-permute-start.13 = (bf16[192,2048]{1,0:T(8,128)(2,1)}, bf16[192,2048]{1,0:T(8,128)(2,1)}, u32[]{:S(2)}, u32[]{:S(2)}) collective-permute-start(bf16[192,2048]{1,0:T(8,128)(2,1)} %shard_map.142.refs_2_), channel_id=1, source_target_pairs={{0,128},{128,0},{1,129},{129,1},{2,130},{130,2},{3,131},{131,3},{4... | collective-permute-start | bytes 2359304 | tf_op jit(solution)/shard_map/ppermute | solution.py:24
  202.5 0.9 copy-start.8
  208.0 35.3 %collective-permute-start.16 = (bf16[192,2048]{1,0:T(8,128)(2,1)}, bf16[192,2048]{1,0:T(8,128)(2,1)}, u32[]{:S(2)}, u32[]{:S(2)}) collective-permute-start(bf16[192,2048]{1,0:T(8,128)(2,1)} %shard_map.145.refs_0_), channel_id=1, source_target_pairs={{0,128},{128,0},{1,129},{129,1},{2,130},{130,2},{3,131},{131,3},{4... | collective-permute-start | bytes 2359304 | tf_op jit(solution)/shard_map/ppermute | solution.py:24
  223.0 19.4 %collective-permute-start.8 = (bf16[64,2048]{1,0:T(8,128)(2,1)S(1)}, bf16[64,2048]{1,0:T(8,128)(2,1)S(1)}, u32[]{:S(2)}, u32[]{:S(2)}) collective-permute-start(bf16[64,2048]{1,0:T(8,128)(2,1)S(1)} %slice.251), channel_id=1, source_target_pairs={{0,128},{128,0},{1,129},{129,1},{2,130},{130,2},{3,131},{131,3},{4... | collective-permute-start | bytes 786440 | tf_op jit(solution)/shard_map/ppermute | solution.py:24
